TPU v7x, 32 devices: a whole 2x2x4 slice. The times are simulated.
32 devices in a mesh: gy: 4 (over y, core), gx: 8 (over z, x).
Axes of the slice: x: 2, y: 2, z: 4, core: 2. Of those that a mesh axis runs over, the one named last changes fastest.
Arguments:
- scan_features: bfloat16 [64, 248, 14336], P(None, 'gy', 'gx'), may hold values from -10 to 10
- occupancy: int32 [64, 248, 224], P(None, 'gy', 'gx'), may hold values from 0 to 1
- kernels: float32 [2, 576, 64], replicated, may hold values from -0.25 to 0.25
- kernel_m: float32 [2, 576, 64], replicated, may hold values from -0.0546875 to 0.0546875
- kernel_v: float32 [2, 576, 64], replicated, may hold values from 1.3516436e-05 to 0.00010813149
- norm_params: float32 [2, 2, 64], replicated, may hold values from -0.3 to 1.4, as said below
- norm_m: float32 [2, 2, 64], replicated, may hold values from -0.0546875 to 0.0546875
- norm_v: float32 [2, 2, 64], replicated, may hold values from 1.3516436e-05 to 0.00021626298
- cotangent: bfloat16 [64, 124, 7168], P(None, 'gy', 'gx'), may hold values from -8 to 8
Outputs:
- features: bfloat16 [64, 124, 7168], P(None, 'gy', 'gx')
- input_grad: bfloat16 [64, 248, 14336], P(None, 'gy', 'gx')
- grad_norm: float32 [], replicated
- new_kernels: float32 [2, 576, 64], replicated
- new_kernel_m: float32 [2, 576, 64], replicated
- new_kernel_v: float32 [2, 576, 64], replicated
- kernels_low: bfloat16 [2, 576, 64], replicated
- new_norm_params: float32 [2, 2, 64], replicated
- new_norm_m: float32 [2, 2, 64], replicated
- new_norm_v: float32 [2, 2, 64], replicated
Inputs may be any that keep to these rules, and one draw needn't show every extreme that they name: `norm_params`: gains at index 0, shifts at index 1.
All inputs are finite; a program needn't handle non-finite values.
Results may differ from a plain program's by a relative error of at most 0.0082.
Values may be sent and summed in bfloat16 or wider, within the bound.
No kernel may reach another device: no remote copies, remote signals or barrier semaphores. Data moves between devices by JAX's collectives and lax.ppermute only.
A program may use at most 384 MiB of HBM per device.

v0:
```python
import jax
import jax.numpy as jnp
from jax import lax
from jax.sharding import PartitionSpec as P

norm_eps = 1e-05
adam_beta = 0.5
adam_eps = 1e-08
step_count = 5
clip_limit = 1.0
kernel_rate = 0.04
norm_rate = 0.25
kernel_decay = 0.01


def shifted(block, axis, distance):
    devices = range(lax.axis_size(axis))
    route = [(i - distance, i) for i in devices if i - distance in devices]
    return lax.ppermute(block, axis, route)


def with_halo(array, sides, width):
    for axis, dim in sides:
        peers, length = (lax.axis_size(axis), array.shape[dim])
        up = [(i, (i + 1) % peers) for i in range(peers - 1)]
        down = [(j, i) for i, j in up]
        last = lax.slice_in_dim(array, length - width, length, axis=dim)
        first = lax.slice_in_dim(array, 0, width, axis=dim)
        before = lax.ppermute(last, axis, up)
        after = lax.ppermute(first, axis, down)
        array = jnp.concatenate([before, array, after], axis=dim)
    return array


def adam_step(weight_now, gradient, moment_one, moment_two, step_rate, decay_rate):
    first_new = adam_beta * moment_one + (1.0 - adam_beta) * gradient
    second_new = adam_beta * moment_two + (1.0 - adam_beta) * gradient * gradient
    correction = 1.0 - adam_beta**step_count
    update = first_new / correction / (jnp.sqrt(second_new / correction) + adam_eps)
    return (weight_now - step_rate * (update + decay_rate * weight_now), first_new, second_new)


def silu_slope(values):
    sigma = jax.nn.sigmoid(values)
    return sigma * (1.0 + values * (1.0 - sigma))


def patches(padded, out_rows, out_cols, stride):
    pieces = []
    for row_tap in range(3):
        for col_tap in range(3):
            pieces.append(
                padded[
                    :,
                    row_tap : row_tap + stride * (out_rows - 1) + 1 : stride,
                    col_tap : col_tap + stride * (out_cols - 1) + 1 : stride,
                    :,
                ]
            )
    return jnp.concatenate(pieces, axis=3)


def batch_stats(values, cell_count):
    summed = lax.psum(jnp.sum(values, axis=(0, 1, 2)), ("gy", "gx"))
    centre = summed / cell_count
    deviate = values - centre
    spread = lax.psum(jnp.sum(deviate * deviate, axis=(0, 1, 2)), ("gy", "gx")) / cell_count
    return (centre, spread)


def normalize(values, params, cell_count):
    centre, spread = batch_stats(values, cell_count)
    inverse = lax.rsqrt(spread + norm_eps)
    normed = (values - centre) * inverse
    return (normed, inverse, params[0] * normed + params[1], centre)


def norm_back(d_pre, normed, inverse, gain, shift_sum, gain_sum, cell_count):
    return (
        gain * inverse * (d_pre - shift_sum / cell_count - normed * (gain_sum / cell_count))
    ).astype(jnp.bfloat16)


def per_device(
    scan_features, occupancy, kernels, kernel_m, kernel_v, norm_params, norm_m, norm_v, cotangent
):
    scan_count, in_rows, flat_cols = scan_features.shape
    channels = kernels.shape[2]
    in_cols = flat_cols // channels
    out_rows = in_rows // 2
    out_cols = in_cols // 2
    rows_all = out_rows * lax.axis_size("gy")
    cols_all = out_cols * lax.axis_size("gx")
    cell_count = float(scan_count * rows_all * cols_all)
    live_mask = occupancy.astype(jnp.bfloat16)
    masked = (
        scan_features.reshape(scan_count, in_rows, in_cols, channels) * live_mask[..., None]
    ).reshape(scan_count, in_rows, flat_cols)
    kernels_now = kernels.astype(jnp.bfloat16)
    top_rim = shifted(masked[:, in_rows - 1 :], "gy", 1)
    extended = jnp.concatenate([top_rim, masked], axis=1).reshape(
        scan_count, in_rows + 1, in_cols, channels
    )
    left_rim = shifted(extended[:, :, in_cols - 1 :], "gx", 1)
    extended = jnp.concatenate([left_rim, extended], axis=2)
    first_cols = patches(extended, out_rows, out_cols, 2)
    conv_one = jnp.dot(first_cols, kernels_now[0], preferred_element_type=jnp.float32)
    normed_one, inverse_one, pre_one, centre_one = normalize(conv_one, norm_params[0], cell_count)
    hidden = jax.nn.silu(pre_one).astype(jnp.bfloat16)
    hidden_pad = with_halo(hidden, (("gy", 1), ("gx", 2)), 1)
    second_cols = patches(hidden_pad, out_rows, out_cols, 1)
    conv_two = jnp.dot(second_cols, kernels_now[1], preferred_element_type=jnp.float32)
    normed_two, inverse_two, pre_two, centre_two = normalize(conv_two, norm_params[1], cell_count)
    features = (
        jax.nn.silu(pre_two).astype(jnp.bfloat16).reshape(scan_count, out_rows, out_cols * channels)
    )
    upstream = cotangent.reshape(scan_count, out_rows, out_cols, channels).astype(jnp.float32)
    d_pre_two = upstream * silu_slope(pre_two)
    shift_two, gain_two = lax.psum(
        (jnp.sum(d_pre_two, axis=(0, 1, 2)), jnp.sum(d_pre_two * normed_two, axis=(0, 1, 2))),
        ("gy", "gx"),
    )
    d_conv_two = norm_back(
        d_pre_two, normed_two, inverse_two, norm_params[1, 0], shift_two, gain_two, cell_count
    )
    kernel_two = jnp.einsum(
        "bhwk,bhwd->kd", second_cols, d_conv_two, preferred_element_type=jnp.float32
    )
    grad_pad = with_halo(d_conv_two, (("gy", 1), ("gx", 2)), 1)
    back_pieces = []
    for row_tap in range(3):
        for col_tap in range(3):
            back_pieces.append(
                grad_pad[
                    :, 2 - row_tap : 2 - row_tap + out_rows, 2 - col_tap : 2 - col_tap + out_cols, :
                ]
            )
    back_cols = jnp.concatenate(back_pieces, axis=3)
    back_kernel = (
        kernels_now[1]
        .reshape(3, 3, channels, channels)
        .transpose(0, 1, 3, 2)
        .reshape(9 * channels, channels)
    )
    d_hidden = jnp.dot(back_cols, back_kernel, preferred_element_type=jnp.float32)
    d_pre_one = d_hidden * silu_slope(pre_one)
    local_shift = jnp.sum(d_pre_one, axis=(0, 1, 2))
    local_gain = jnp.sum(d_pre_one * normed_one, axis=(0, 1, 2))
    shift_one, gain_one = lax.psum((local_shift, local_gain), ("gy", "gx"))
    d_conv_one = norm_back(
        d_pre_one, normed_one, inverse_one, norm_params[0, 0], shift_one, gain_one, cell_count
    )
    kernel_one = jnp.einsum(
        "bhwk,bhwd->kd", first_cols, d_conv_one, preferred_element_type=jnp.float32
    )
    below_rim = shifted(d_conv_one[:, :1], "gy", -1)
    grad_ext = jnp.concatenate([d_conv_one, below_rim], axis=1)
    right_rim = shifted(grad_ext[:, :, :1], "gx", -1)
    grad_ext = jnp.concatenate([grad_ext, right_rim], axis=2)
    tap_kernel = (
        kernels_now[0]
        .reshape(9, channels, channels)
        .transpose(2, 0, 1)
        .reshape(channels, 9 * channels)
    )
    contrib = jnp.dot(grad_ext, tap_kernel, preferred_element_type=jnp.float32)
    contrib = contrib.reshape(scan_count, out_rows + 1, out_cols + 1, 3, 3, channels)
    selects = ([(1, 0)], [(0, 1), (2, 0)])
    row_blocks = []
    for row_par in range(2):
        col_blocks = []
        for col_par in range(2):
            summed = jnp.zeros((scan_count, out_rows, out_cols, channels), jnp.float32)
            for row_tap, row_off in selects[row_par]:
                for col_tap, col_off in selects[col_par]:
                    summed = (
                        summed
                        + contrib[
                            :,
                            row_off : row_off + out_rows,
                            col_off : col_off + out_cols,
                            row_tap,
                            col_tap,
                            :,
                        ]
                    )
            col_blocks.append(summed)
        row_blocks.append(
            jnp.stack(col_blocks, axis=3).reshape(scan_count, out_rows, in_cols, channels)
        )
    d_inputs = jnp.stack(row_blocks, axis=2).reshape(scan_count, in_rows, in_cols, channels)
    input_grad = (
        (d_inputs * occupancy.astype(jnp.float32)[..., None])
        .astype(jnp.bfloat16)
        .reshape(scan_count, in_rows, flat_cols)
    )
    kernel_one, kernel_two = lax.psum((kernel_one, kernel_two), ("gy", "gx"))
    kernel_grad = jnp.stack([kernel_one, kernel_two])
    norm_grad = jnp.stack([jnp.stack([gain_one, shift_one]), jnp.stack([gain_two, shift_two])])
    grad_norm = jnp.sqrt(jnp.sum(kernel_grad * kernel_grad) + jnp.sum(norm_grad * norm_grad))
    factor = jnp.minimum(1.0, clip_limit / grad_norm)
    new_kernels, new_kernel_m, new_kernel_v = adam_step(
        kernels, kernel_grad * factor, kernel_m, kernel_v, kernel_rate, kernel_decay
    )
    new_norm_params, new_norm_m, new_norm_v = adam_step(
        norm_params, norm_grad * factor, norm_m, norm_v, norm_rate, 0.0
    )
    return (
        features,
        input_grad,
        grad_norm,
        new_kernels,
        new_kernel_m,
        new_kernel_v,
        new_kernels.astype(jnp.bfloat16),
        new_norm_params,
        new_norm_m,
        new_norm_v,
    )


def solution(mesh):
    return jax.shard_map(
        per_device,
        mesh=mesh,
        in_specs=(
            P(None, "gy", "gx"),
            P(None, "gy", "gx"),
            P(),
            P(),
            P(),
            P(),
            P(),
            P(),
            P(None, "gy", "gx"),
        ),
        out_specs=(
            P(None, "gy", "gx"),
            P(None, "gy", "gx"),
            P(),
            P(),
            P(),
            P(),
            P(),
            P(),
            P(),
            P(),
        ),
        check_vma=False,
    )
```

profile of v0, /device:TPU:0, one launch (start us, length us, event | category | flops | bytes accessed | tf_op | source)
XLA Modules:
  0.0 1566.6 jit_solution(2716342254337984499)
XLA Ops:
  11.7 20.6 %mul.205 = bf16[64,62,28,64]{3,2,0,1:T(8,128)(2,1)} broadcast(bf16[64,62,28]{2,0,1:T(8,128)(2,1)S(1)} %copy.28), dimensions={0,1,2} | broadcast | bytes 14443520 | tf_op jit(solution)/shard_map/mul | solution.py:97
  32.3 41.4 %mul.206 = bf16[64,62,1792]{2,0,1:T(8,128)(2,1)} reshape(bf16[64,62,28,64]{3,2,0,1:T(8,128)(2,1)} %mul.205) | data formatting | bytes 28442624 | tf_op jit(solution)/shard_map/mul | solution.py:97
  94.0 43.7 %concatenate.67 = bf16[64,62,28,64]{3,2,0,1:T(8,128)(2,1)} reshape(bf16[64,62,1792]{2,0,1:T(8,128)(2,1)} %copy-done.3) | data formatting | bytes 28442624 | tf_op jit(solution)/shard_map/concatenate | solution.py:101
  139.8 29.3 %constant_dynamic-update-slice_fusion = (bf16[64,63,28,64]{3,0,2,1:T(8,128)(2,1)}, bf16[64,62,28,64]{3,0,2,1:T(8,128)(2,1)}) fusion(bf16[64,63,28,64]{3,0,2,1:T(8,128)(2,1)} %copy_dynamic-update-slice_fusion, bf16[64,62,28,64]{3,2,0,1:T(8,128)(2,1)} %concatenate.67), kind=kLoop, calls=%fused_computation.65 | loop fusion | bytes 89391104 | tf_op jit(solution)/shard_map/concatenate | solution.py:101
  174.9 19.2 %fusion.27 = (bf16[64,31,14,64]{3,0,2,1:T(8,128)(2,1)}, bf16[64,31,14,64]{3,0,2,1:T(8,128)(2,1)}, bf16[64,31,14,64]{3,0,2,1:T(8,128)(2,1)}, bf16[64,31,14,64]{3,0,2,1:T(8,128)(2,1)}) fusion(bf16[64,62,28,64]{3,0,2,1:T(8,128)(2,1)} %get-tuple-element.29), kind=kLoop, calls=%fused_computation.98 | loop fusion | bytes 28442624 | tf_op jit(solution)/shard_map/slice | solution.py:53
  205.0 20.6 %pad_maximum_fusion.1 = bf16[64,63,29,64]{3,0,2,1:T(8,128)(2,1)} fusion(bf16[64,63,28,64]{3,0,2,1:T(8,128)(2,1)} %get-tuple-element.28, bf16[64,63,1,64]{3,0,2,1:T(8,128)(2,1)S(1)} %collective-permute-done.1), kind=kLoop, calls=%fused_computation.1 | loop fusion | flops 7483392 | bytes 29933568 | tf_op jit(solution)/shard_map/concatenate | solution.py:105
  240.6 71.5 %concatenate.70 = bf16[64,31,14,576]{3,0,2,1:T(8,128)(2,1)} concatenate(bf16[64,31,14,64]{3,0,2,1:T(8,128)(2,1)} %get-tuple-element.35, bf16[64,31,14,64]{3,0,2,1:T(8,128)(2,1)} %get-tuple-element.37, bf16[64,31,14,64]{3,0,2,1:T(8,128)(2,1)} %get-tuple-element.36, bf16[64,31,14,64]{3,0,2,1:T(8,128)(2,1)} %get-tuple-element.34, bf16[64,31,14,64]{3,0,2,1:T(8,128)(2,1)} %get-tuple-element.41, ...), dimensions={3} | concatenate | bytes 63995904 | tf_op jit(solution)/shard_map/concatenate | solution.py:60
  312.2 21.0 %fusion.36 = (f32[64]{0:T(128)S(1)}, f32[64,31,14,64]{3,0,2,1:T(8,128)}) fusion(bf16[64,31,14,576]{3,0,2,1:T(8,128)(2,1)} %concatenate.70, bf16[2,576,64]{1,2,0:T(8,128)(2,1)S(1)} %convert_element_type.35), kind=kOutput, calls=%fused_computation.107 | convolution fusion | flops 2049646592 | bytes 39190784 | tf_op jit(solution)/shard_map/dot_general | solution.py:107
  333.2 40.6 %psum.70 = f32[64]{0:T(128)S(1)} all-reduce(f32[64]{0:T(128)S(1)} %get-tuple-element.82), channel_id=1, replica_groups=mesh['gy'=4,'gx'=8] {'gy','gx'}, use_global_device_ids=true, to_apply=%region_1.0 | all-reduce | flops 64 | bytes 512 | tf_op jit(solution)/shard_map/psum | solution.py:64
  382.5 40.1 %psum.71 = f32[64]{0:T(128)S(1)} all-reduce(f32[64]{0:T(128)S(1)} %multiply_reduce_fusion.3), channel_id=1, replica_groups=mesh['gy'=4,'gx'=8] {'gy','gx'}, use_global_device_ids=true, to_apply=%region_3.0 | all-reduce | flops 64 | bytes 512 | tf_op jit(solution)/shard_map/psum | solution.py:67
  452.2 20.7 %mul.236 = f32[64,62,28,64]{3,2,0,1:T(8,128)} broadcast(f32[64,62,28]{2,0,1:T(8,128)S(1)} %copy.43), dimensions={0,1,2} | broadcast | bytes 28887040 | tf_op jit(solution)/shard_map/mul | solution.py:193
  472.9 51.0 %mul.237 = f32[64,62,1792]{2,0,1:T(8,128)} reshape(f32[64,62,28,64]{3,2,0,1:T(8,128)} %mul.236) | data formatting | bytes 56885248 | tf_op jit(solution)/shard_map/mul | solution.py:193
  561.9 23.2 %fusion.30 = (bf16[64,31,14,64]{3,0,2,1:T(8,128)(2,1)}, bf16[64,31,14,64]{3,0,2,1:T(8,128)(2,1)}, bf16[64,31,14,64]{3,0,2,1:T(8,128)(2,1)}, bf16[64,31,14,64]{3,...) fusion(bf16[64,33,15,64]{3,0,2,1:T(8,128)(2,1)S(1)} %get-tuple-element.59, ...), kind=kLoop, calls=%fused_computation.101 | loop fusion | bytes 42663936 | tf_op jit(solution)/shard_map/slice | solution.py:53
  585.1 71.5 %concatenate.76 = bf16[64,31,14,576]{3,0,2,1:T(8,128)(2,1)} concatenate(bf16[64,31,14,64]{3,0,2,1:T(8,128)(2,1)} %get-tuple-element.87, bf16[64,31,14,64]{3,0,2,1:T(8,128)(2,1)} %get-tuple-element.68, bf16[64,31,14,64]{3,0,2,1:T(8,128)(2,1)} %get-tuple-element.51, bf16[64,31,14,64]{3,0,2,1:T(8,128)(2,1)} %get-tuple-element.88, bf16[64,31,14,64]{3,0,2,1:T(8,128)(2,1)} %copy-done.1, ...), dimensions={3} | concatenate | bytes 63995904 | tf_op jit(solution)/shard_map/concatenate | solution.py:60
  656.6 21.1 %fusion.37 = (f32[64]{0:T(128)S(1)}, f32[64,31,14,64]{3,0,2,1:T(8,128)}) fusion(bf16[64,31,14,576]{3,0,2,1:T(8,128)(2,1)} %concatenate.76, bf16[2,576,64]{1,2,0:T(8,128)(2,1)S(1)} %copy-done.6), kind=kOutput, calls=%fused_computation.108 | convolution fusion | flops 2049646592 | bytes 39190784 | tf_op jit(solution)/shard_map/dot_general | solution.py:112
  677.7 41.6 %psum.72 = f32[64]{0:T(128)S(1)} all-reduce(f32[64]{0:T(128)S(1)} %get-tuple-element.84), channel_id=1, replica_groups=mesh['gy'=4,'gx'=8] {'gy','gx'}, use_global_device_ids=true, to_apply=%region_5.6 | all-reduce | flops 64 | bytes 512 | tf_op jit(solution)/shard_map/psum | solution.py:64
  728.0 41.4 %psum.73 = f32[64]{0:T(128)S(1)} all-reduce(f32[64]{0:T(128)S(1)} %multiply_reduce_fusion.2), channel_id=1, replica_groups=mesh['gy'=4,'gx'=8] {'gy','gx'}, use_global_device_ids=true, to_apply=%region_7.8 | all-reduce | flops 64 | bytes 512 | tf_op jit(solution)/shard_map/psum | solution.py:67
  769.9 20.9 %fusion.21 = (f32[64]{0:T(128)S(1)}, f32[64]{0:T(128)S(1)}, f32[64,31,14,64]{3,0,2,1:T(8,128)}, bf16[64,31,14,64]{3,0,2,1:T(8,128)(2,1)}) fusion(f32[64]{0:T(128)S(1)} %get-tuple-element.81, f32[64,31,14,64]{3,0,2,1:T(8,128)} %get-tuple-element.85, f32[64]{0:T(128)S(1)} %broadcast_multiply_fusion.4, f32[64]{0:T(128)S(1)} %copy-done.26, f32[64]{0:T(128)S(1)} %copy-done.25, ...), kind=kLoop, calls=%fused_computation.94 | loop fusion | flops 30220160 | bytes 24888832 | tf_op jit(solution)/shard_map/reduce_sum | solution.py:120
  790.8 39.0 %all-reduce.1 = (f32[64]{0:T(128)S(1)}, f32[64]{0:T(128)S(1)}) all-reduce(f32[64]{0:T(128)S(1)} %get-tuple-element.13, f32[64]{0:T(128)S(1)} %get-tuple-element.12), channel_id=1, replica_groups=mesh['gy'=4,'gx'=8] {'gy','gx'}, use_global_device_ids=true, to_apply=%region_11.12 | all-reduce | flops 128 | bytes 1024 | tf_op jit(solution)/shard_map/psum | solution.py:119
  845.9 16.9 %convolution_bitcast_fusion = f32[1,576,64]{1,2,0:T(8,128)} fusion(bf16[64,31,14,576]{3,0,2,1:T(8,128)(2,1)} %concatenate.76, bf16[64,31,14,64]{3,0,2,1:T(8,128)(2,1)} %copy-done), kind=kOutput, calls=%fused_computation.46 | convolution fusion | flops 2047868928 | bytes 35700736 | tf_op jit(solution)/shard_map/bhwk,bhwd->kd/dot_general | solution.py:126
  862.8 16.9 %copy.31 = bf16[64,31,14,64]{3,2,0,1:T(8,128)(2,1)} copy(bf16[64,31,14,64]{3,0,2,1:T(8,128)(2,1)} %get-tuple-element.42) | data formatting | bytes 7110656 | tf_op jit(solution)/shard_map/convert_element_type | solution.py:115
  946.7 71.5 %concatenate.82 = bf16[64,31,14,576]{3,0,2,1:T(8,128)(2,1)} concatenate(bf16[64,31,14,64]{3,0,2,1:T(8,128)(2,1)} %get-tuple-element.48, bf16[64,31,14,64]{3,0,2,1:T(8,128)(2,1)} %get-tuple-element.64, bf16[64,31,14,64]{3,0,2,1:T(8,128)(2,1)} %get-tuple-element.45, bf16[64,31,14,64]{3,0,2,1:T(8,128)(2,1)} %get-tuple-element.47, bf16[64,31,14,64]{3,0,2,1:T(8,128)(2,1)} %copy-done, ...), dimensions={3} | concatenate | bytes 63995904 | tf_op jit(solution)/shard_map/concatenate | solution.py:138
  1018.3 25.0 %fusion.20 = (f32[64]{0:T(128)S(1)}, f32[64]{0:T(128)S(1)}, f32[64,31,14,64]{3,0,2,1:T(8,128)}) fusion(f32[64]{0:T(128)S(1)} %copy-done.19, f32[64,31,14,64]{3,0,2,1:T(8,128)} %get-tuple-element.83, f32[64]{0:T(128)S(1)} %copy-done.17, f32[64]{0:T(128)S(1)} %copy-done.22, f32[64]{0:T(128)S(1)} %copy-done.24, bf16[64,31,14,576]{3,0,2,1:T(8,128)(2,1)} %concatenate.82, ...), kind=kOutput, calls=%fused_computation.93 | convolution fusion | flops 2074533888 | bytes 46294528 | tf_op jit(solution)/shard_map/dot_general | solution.py:145
  1043.3 42.0 %all-reduce = (f32[64]{0:T(128)S(1)}, f32[64]{0:T(128)S(1)}) all-reduce(f32[64]{0:T(128)S(1)} %get-tuple-element.11, f32[64]{0:T(128)S(1)} %get-tuple-element.10), channel_id=1, replica_groups=mesh['gy'=4,'gx'=8] {'gy','gx'}, use_global_device_ids=true, to_apply=%region_15.16 | all-reduce | flops 128 | bytes 1024 | tf_op jit(solution)/shard_map/psum | solution.py:149
  1100.4 16.9 %convolution_bitcast_fusion.1 = f32[1,576,64]{1,2,0:T(8,128)} fusion(bf16[64,31,14,576]{3,0,2,1:T(8,128)(2,1)} %concatenate.70, bf16[64,31,14,64]{3,0,2,1:T(8,128)(2,1)} %copy-done.2), kind=kOutput, calls=%fused_computation.47 | convolution fusion | flops 2047868928 | bytes 35700736 | tf_op jit(solution)/shard_map/bhwk,bhwd->kd/dot_general | solution.py:153
  1120.3 124.1 %all-reduce.5.cloned.1.call-done = (f32[1,576,64]{1,2,0:T(8,128)}, f32[1,576,64]{1,2,0:T(8,128)}) async-done(((f32[1,576,64]{1,2,0:T(8,128)}, f32[1,576,64]{1,2,0:T(8,128)}), (f32[1,576,64]{1,2,0:T(8,128)}, f32[1,576,64]{1,2,0:T(8,128)})) %all-reduce.5.cloned.1.call-update) | async-done | bytes 294928 | tf_op jit(solution)/shard_map/psum | solution.py:197
  1250.2 49.6 %fusion.4 = f32[64,32,15,3,3,64]{5,0,4,3,2,1:T(8,128)} fusion(bf16[3,3,64,64,1,1]{3,2,1,0,5,4:T(8,128)(2,1)S(1)} %bitcast.128, bf16[64,32,1,64]{3,0,2,1:T(8,128)(2,1)S(1)} %collective-permute-done.11, bf16[64,1,14,64]{3,0,2,1:T(8,128)(2,1)S(1)} %collective-permute-done.10, bf16[64,31,14,64]{3,0,2,1:T(8,128)(2,1)} %copy-done.2), kind=kOutput, calls=%fused_computation.37 | convolution fusion | flops 2276720640 | bytes 74784768 | tf_op jit(solution)/shard_map/dot_general | solution.py:166
  1299.8 48.0 %slice_bitcast_fusion.2 = (f32[64,31,14,1,64]{4,0,2,1,3:T(8,128)}, f32[64,31,14,1,64]{4,0,2,1,3:T(8,128)}, f32[64,31,14,1,64]{4,0,2,1,3:T(8,128)}) fusion(f32[64,32,15,3,3,64]{5,0,4,3,2,1:T(8,128)} %fusion.4), kind=kLoop, calls=%fused_computation.15 | loop fusion | flops 7110656 | bytes 71106560 | tf_op jit(solution)/shard_map/stack;squeeze | solution.py:189
  1403.7 38.3 %pad_maximum_fusion = f32[64,31,2,28,64]{4,0,3,2,1:T(8,128)} fusion(f32[64,31,1,28,64]{4,0,3,2,1:T(8,128)} %bitcast.127, f32[64,31,1,28,64]{4,0,3,2,1:T(8,128)} %bitcast.126), kind=kLoop, calls=%fused_computation | loop fusion | flops 7110656 | bytes 56885248 | tf_op jit(solution)/shard_map/stack | solution.py:191
  1442.0 41.4 %copy.42 = f32[64,31,2,28,64]{4,3,0,2,1:T(8,128)} copy(f32[64,31,2,28,64]{4,0,3,2,1:T(8,128)} %pad_maximum_fusion) | data formatting | bytes 56885248 | tf_op jit(solution)/shard_map/stack | solution.py:191
  1483.5 50.9 %reshape.149 = f32[64,62,1792]{2,0,1:T(8,128)} reshape(f32[64,31,2,28,64]{4,3,0,2,1:T(8,128)} %copy.42) | data formatting | bytes 56885248 | tf_op jit(solution)/shard_map/reshape | solution.py:191
  1534.4 24.0 %multiply_convert_fusion = bf16[64,62,1792]{2,0,1:T(8,128)(2,1)} fusion(f32[64,62,1792]{2,0,1:T(8,128)} %reshape.149, f32[64,62,1792]{2,0,1:T(8,128)} %mul.237), kind=kLoop, calls=%fused_computation.4 | loop fusion | flops 14221312 | bytes 71106560 | tf_op jit(solution)/shard_map/convert_element_type | solution.py:194
  (150 shorter events, 305.3 us)
Async XLA Ops:
  7.2 1237.3 %all-reduce.5.cloned.1.call-start = ((), (), s32[]{:S(2)}) async-start(), calls=%async_computation | async-start | bytes 655360 | tf_op jit(solution)/shard_map/psum | solution.py:197
  91.5 46.8 %collective-permute-start = (bf16[64,1,1792]{2,0,1:T(8,128)(2,1)S(1)}, bf16[64,1,1792]{2,0,1:T(8,128)(2,1)S(1)}, u32[]{:S(2)}, u32[]{:S(2)}) collective-permute-start(bf16[64,1,1792]{2,0,1:T(8,128)(2,1)S(1)} %slice.242), channel_id=1, source_target_pairs={{0,8},{8,16},{16,24},{1,9},{9,17},{17,25},{2,10},{10,18},{18,26},{... | collective-permute-start | bytes 688136 | tf_op jit(solution)/shard_map/ppermute | solution.py:19
  137.7 299.3 %copy-start.5 = (bf16[2,576,64]{1,2,0:T(8,128)(2,1)}, bf16[2,576,64]{1,2,0:T(8,128)(2,1)S(1)}, u32[]{:S(2)}) copy-start(bf16[2,576,64]{1,2,0:T(8,128)(2,1)S(1)} %convert_element_type.35) | copy-start | bytes 442372
  138.3 284.3 %copy-start.21 = (f32[64]{0:T(128)}, f32[64]{0:T(128)S(1)}, u32[]{:S(2)}) copy-start(f32[64]{0:T(128)S(1)} %get-tuple-element.78) | copy-start | bytes 772
  138.3 284.3 %copy-start.23 = (f32[64]{0:T(128)}, f32[64]{0:T(128)S(1)}, u32[]{:S(2)}) copy-start(f32[64]{0:T(128)S(1)} %get-tuple-element.79) | copy-start | bytes 772
  170.4 34.6 %collective-permute-start.1 = (bf16[64,63,1,64]{3,0,2,1:T(8,128)(2,1)S(1)}, bf16[64,63,1,64]{3,0,2,1:T(8,128)(2,1)S(1)}, u32[]{:S(2)}, u32[]{:S(2)}) collective-permute-start(bf16[64,63,1,64]{3,0,2,1:T(8,128)(2,1)S(1)} %slice.243), channel_id=1, source_target_pairs={{0,1},{1,2},{2,3},{3,4},{4,5},{5,6},{6,7},{8,9},{9,10},{10,11},{11... | collective-permute-start | bytes 1548296 | tf_op jit(solution)/shard_map/ppermute | solution.py:19
  434.2 89.7 %collective-permute-start.2 = (bf16[64,1,14,64]{3,0,2,1:T(8,128)(2,1)}, bf16[64,1,14,64]{3,0,2,1:T(8,128)(2,1)S(1)}, u32[]{:S(2)}, u32[]{:S(2)}) collective-permute-start(bf16[64,1,14,64]{3,0,2,1:T(8,128)(2,1)} %get-tuple-element.69), channel_id=1, source_target_pairs={{0,8},{8,16},{16,24},{1,9},{9,17},{17,25},{2,10},{10,18},{18,26},{... | collective-permute-start | bytes 344072 | tf_op jit(solution)/shard_map/ppermute | solution.py:29
  435.7 88.2 %collective-permute-start.3 = (bf16[64,1,14,64]{3,0,2,1:T(8,128)(2,1)}, bf16[64,1,14,64]{3,0,2,1:T(8,128)(2,1)S(1)}, u32[]{:S(2)}, u32[]{:S(2)}) collective-permute-start(bf16[64,1,14,64]{3,0,2,1:T(8,128)(2,1)} %get-tuple-element.70), channel_id=1, source_target_pairs={{8,0},{16,8},{24,16},{9,1},{17,9},{25,17},{10,2},{18,10},{26,18},{... | collective-permute-start | bytes 344072 | tf_op jit(solution)/shard_map/ppermute | solution.py:30
  525.5 27.8 %collective-permute-start.4 = (bf16[64,33,1,64]{3,0,2,1:T(8,128)(2,1)S(1)}, bf16[64,33,1,64]{3,0,2,1:T(8,128)(2,1)S(1)}, u32[]{:S(2)}, u32[]{:S(2)}) collective-permute-start(bf16[64,33,1,64]{3,0,2,1:T(8,128)(2,1)S(1)} %get-tuple-element.62), channel_id=1, source_target_pairs={{0,1},{1,2},{2,3},{3,4},{4,5},{5,6},{6,7},{8,9},{9,10},{10,11},{11... | collective-permute-start | bytes 811016 | tf_op jit(solution)/shard_map/ppermute | solution.py:29
  529.8 23.5 %collective-permute-start.5 = (bf16[64,33,1,64]{3,0,2,1:T(8,128)(2,1)S(1)}, bf16[64,33,1,64]{3,0,2,1:T(8,128)(2,1)S(1)}, u32[]{:S(2)}, u32[]{:S(2)}) collective-permute-start(bf16[64,33,1,64]{3,0,2,1:T(8,128)(2,1)S(1)} %get-tuple-element.61), channel_id=1, source_target_pairs={{1,0},{2,1},{3,2},{4,3},{5,4},{6,5},{7,6},{9,8},{10,9},{11,10},{12... | collective-permute-start | bytes 811016 | tf_op jit(solution)/shard_map/ppermute | solution.py:30
  585.1 71.5 %copy-start.6 = (bf16[2,576,64]{1,2,0:T(8,128)(2,1)S(1)}, bf16[2,576,64]{1,2,0:T(8,128)(2,1)}, u32[]{:S(2)}) copy-start(bf16[2,576,64]{1,2,0:T(8,128)(2,1)} %copy-done.5) | copy-start | bytes 442372
  677.7 91.7 %copy-start.14 = (f32[2,2,64]{2,1,0:T(2,128)S(1)}, f32[2,2,64]{2,1,0:T(2,128)}, u32[]{:S(2)}) copy-start(f32[2,2,64]{2,1,0:T(2,128)} %param.14) | copy-start | bytes 3076
  677.7 92.2 %copy-start.25 = (f32[64]{0:T(128)S(1)}, f32[64]{0:T(128)}, u32[]{:S(2)}) copy-start(f32[64]{0:T(128)} %get-tuple-element.77) | copy-start | bytes 772
  677.7 92.2 %copy-start.26 = (f32[64]{0:T(128)S(1)}, f32[64]{0:T(128)}, u32[]{:S(2)}) copy-start(f32[64]{0:T(128)} %get-tuple-element.80) | copy-start | bytes 772
  843.3 48.1 %collective-permute-start.6 = (bf16[64,1,14,64]{3,0,2,1:T(8,128)(2,1)S(1)}, bf16[64,1,14,64]{3,0,2,1:T(8,128)(2,1)S(1)}, u32[]{:S(2)}, u32[]{:S(2)}) collective-permute-start(bf16[64,1,14,64]{3,0,2,1:T(8,128)(2,1)S(1)} %get-tuple-element.65), channel_id=1, source_target_pairs={{0,8},{8,16},{16,24},{1,9},{9,17},{17,25},{2,10},{10,18},{18,26},{... | collective-permute-start | bytes 344072 | tf_op jit(solution)/shard_map/ppermute | solution.py:29
  844.6 46.8 %collective-permute-start.7 = (bf16[64,1,14,64]{3,0,2,1:T(8,128)(2,1)S(1)}, bf16[64,1,14,64]{3,0,2,1:T(8,128)(2,1)S(1)}, u32[]{:S(2)}, u32[]{:S(2)}) collective-permute-start(bf16[64,1,14,64]{3,0,2,1:T(8,128)(2,1)S(1)} %get-tuple-element.66), channel_id=1, source_target_pairs={{8,0},{16,8},{24,16},{9,1},{17,9},{25,17},{10,2},{18,10},{26,18},{... | collective-permute-start | bytes 344072 | tf_op jit(solution)/shard_map/ppermute | solution.py:30
  893.0 17.5 %collective-permute-start.8 = (bf16[64,33,1,64]{3,0,2,1:T(8,128)(2,1)S(1)}, bf16[64,33,1,64]{3,0,2,1:T(8,128)(2,1)S(1)}, u32[]{:S(2)}, u32[]{:S(2)}) collective-permute-start(bf16[64,33,1,64]{3,0,2,1:T(8,128)(2,1)S(1)} %get-tuple-element.58), channel_id=1, source_target_pairs={{1,0},{2,1},{3,2},{4,3},{5,4},{6,5},{7,6},{9,8},{10,9},{11,10},{12... | collective-permute-start | bytes 811016 | tf_op jit(solution)/shard_map/ppermute | solution.py:30
  894.3 27.9 %collective-permute-start.9 = (bf16[64,33,1,64]{3,0,2,1:T(8,128)(2,1)S(1)}, bf16[64,33,1,64]{3,0,2,1:T(8,128)(2,1)S(1)}, u32[]{:S(2)}, u32[]{:S(2)}) collective-permute-start(bf16[64,33,1,64]{3,0,2,1:T(8,128)(2,1)S(1)} %get-tuple-element.57), channel_id=1, source_target_pairs={{0,1},{1,2},{2,3},{3,4},{4,5},{5,6},{6,7},{8,9},{9,10},{10,11},{11... | collective-permute-start | bytes 811016 | tf_op jit(solution)/shard_map/ppermute | solution.py:29
  946.7 71.6 %copy-start.12 = (bf16[3,3,64,64]{3,2,1,0:T(8,128)(2,1)S(1)}, bf16[3,3,64,64]{3,2,1,0:T(8,128)(2,1)}, u32[]{:S(2)}) copy-start(bf16[3,3,64,64]{3,2,1,0:T(8,128)(2,1)} %copy.34) | copy-start | bytes 221188
  946.7 71.6 %copy-start.17 = (f32[64]{0:T(128)S(1)}, f32[64]{0:T(128)}, u32[]{:S(2)}) copy-start(f32[64]{0:T(128)} %copy-done.16) | copy-start | bytes 772
  946.7 71.6 %copy-start.19 = (f32[64]{0:T(128)S(1)}, f32[64]{0:T(128)}, u32[]{:S(2)}) copy-start(f32[64]{0:T(128)} %copy-done.18) | copy-start | bytes 772
  946.7 71.6 %copy-start.22 = (f32[64]{0:T(128)S(1)}, f32[64]{0:T(128)}, u32[]{:S(2)}) copy-start(f32[64]{0:T(128)} %copy-done.21) | copy-start | bytes 772
  946.7 71.6 %copy-start.24 = (f32[64]{0:T(128)S(1)}, f32[64]{0:T(128)}, u32[]{:S(2)}) copy-start(f32[64]{0:T(128)} %copy-done.23) | copy-start | bytes 772
  1098.8 149.5 %copy-start.15 = (f32[2,2,64]{2,1,0:T(2,128)S(1)}, f32[2,2,64]{2,1,0:T(2,128)}, u32[]{:S(2)}) copy-start(f32[2,2,64]{2,1,0:T(2,128)} %param.14) | copy-start | bytes 3076
  1098.8 149.5 %copy-start.27 = (f32[2,2,64]{2,1,0:T(2,128)S(1)}, f32[2,2,64]{2,1,0:T(2,128)}, u32[]{:S(2)}) copy-start(f32[2,2,64]{2,1,0:T(2,128)} %param.15) | copy-start | bytes 3076
  1098.9 149.5 %copy-start.28 = (f32[2,2,64]{2,1,0:T(2,128)S(1)}, f32[2,2,64]{2,1,0:T(2,128)}, u32[]{:S(2)}) copy-start(f32[2,2,64]{2,1,0:T(2,128)} %param.16) | copy-start | bytes 3076
  1098.9 150.1 %copy-start.8 = (f32[2,576,64]{1,2,0:T(8,128)S(1)}, f32[2,576,64]{1,2,0:T(8,128)}, u32[]{:S(2)}) copy-start(f32[2,576,64]{1,2,0:T(8,128)} %param.11) | copy-start | bytes 884740
  1098.9 150.1 %copy-start.10 = (f32[2,576,64]{1,2,0:T(8,128)S(1)}, f32[2,576,64]{1,2,0:T(8,128)}, u32[]{:S(2)}) copy-start(f32[2,576,64]{1,2,0:T(8,128)} %param.12) | copy-start | bytes 884740
  1098.9 150.1 %copy-start.11 = (f32[2,576,64]{1,2,0:T(8,128)S(1)}, f32[2,576,64]{1,2,0:T(8,128)}, u32[]{:S(2)}) copy-start(f32[2,576,64]{1,2,0:T(8,128)} %param.13) | copy-start | bytes 884740
  1098.9 151.3 %copy-start.9 = (bf16[1,576,64]{2,1,0:T(8,128)(2,1)S(1)}, bf16[1,576,64]{2,1,0:T(8,128)(2,1)}, u32[]{:S(2)}) copy-start(bf16[1,576,64]{2,1,0:T(8,128)(2,1)} %copy.36) | copy-start | bytes 221188
  1098.9 19.0 %collective-permute-start.10 = (bf16[64,1,14,64]{3,0,2,1:T(8,128)(2,1)S(1)}, bf16[64,1,14,64]{3,0,2,1:T(8,128)(2,1)S(1)}, u32[]{:S(2)}, u32[]{:S(2)}) collective-permute-start(bf16[64,1,14,64]{3,0,2,1:T(8,128)(2,1)S(1)} %slice.262), channel_id=1, source_target_pairs={{8,0},{16,8},{24,16},{9,1},{17,9},{25,17},{10,2},{18,10},{26,18},{... | collective-permute-start | bytes 344072 | tf_op jit(solution)/shard_map/ppermute | solution.py:19
  1119.0 131.2 %collective-permute-start.11 = (bf16[64,32,1,64]{3,0,2,1:T(8,128)(2,1)S(1)}, bf16[64,32,1,64]{3,0,2,1:T(8,128)(2,1)S(1)}, u32[]{:S(2)}, u32[]{:S(2)}) collective-permute-start(bf16[64,32,1,64]{3,0,2,1:T(8,128)(2,1)S(1)} %pad_maximum_fusion.16), channel_id=1, source_target_pairs={{1,0},{2,1},{3,2},{4,3},{5,4},{6,5},{7,6},{9,8},{10,9},{11,10},{12... | collective-permute-start | bytes 786440 | tf_op jit(solution)/shard_map/ppermute | solution.py:19
  (14 other events, 384.7 us)
Sparse Core Ops, SparseCore 0:
  1117.4 127.0 all-reduce.4
where the time goes:
time: 1590 us; the launch traced here: 1570 us
  local copies, waits for them, and re-layouts  686 us (43%)
  other arithmetic  294 us (18%)
  blocking collectives  245 us (15%)
  matrix products  150 us (9%)
  waiting for transfers between devices  147 us (9%)
  starting transfers between devices  27.3 us (2%)
  between operations  17.3 us (1%)
    concatenate x2, local copies, waits for them, and re-layouts, patches(): return jnp.concatenate(pieces, axis=3)  143 us
    psum x1, waiting for transfers between devices, per_device(): kernel_one, kernel_two = lax.psum((kernel_one, kernel_two), ('gy', 'gx'))  124 us
    psum x2, blocking collectives, batch_stats(): summed = lax.psum(jnp.sum(values, axis=(0, 1, 2)), ('gy', 'gx'))  82.2 us
    psum x2, blocking collectives, batch_stats(): lax.psum(jnp.sum(deviate * deviate, axis=(0, 1, 2)), ('gy', 'gx'))  81.5 us
    concatenate x3, local copies, waits for them, and re-layouts, per_device(): jnp.concatenate([top_rim, masked], axis=1)  73.5 us
    mul x2, local copies, waits for them, and re-layouts, per_device(): d_inputs * occupancy.astype(jnp.float32)[..., None]  71.7 us
    concatenate x1, local copies, waits for them, and re-layouts, per_device(): back_cols = jnp.concatenate(back_pieces, axis=3)  71.5 us
    another operation x3, other arithmetic, per_device(): jnp.stack(col_blocks, axis=3)  70.1 us
  transfers between devices with their start and end apart: 13, of which 3 were waited for; matrix products, arithmetic and copies ran while one was open for 16% of the time, Pallas kernels for 0%

commit v1 on v0

v1 whole, which is shorter than its diff:
```python
import functools
import math

import jax
import jax.numpy as jnp
from jax import lax
from jax.experimental import pallas as pl
from jax.experimental.pallas import tpu as pltpu
from jax.sharding import PartitionSpec as P

norm_eps = 1e-05
adam_beta = 0.5
adam_eps = 1e-08
step_count = 5
clip_limit = 1.0
kernel_rate = 0.04
norm_rate = 0.25
kernel_decay = 0.01

f32, bf16 = (jnp.float32, jnp.bfloat16)
BOTH = ("gy", "gx")
S, C, L, BITS = (16, 64, 128, 13)


def params_of(limit=56):
    return pltpu.CompilerParams(
        dimension_semantics=("arbitrary",), vmem_limit_bytes=limit << 20
    )


def cost(microseconds):
    return pl.CostEstimate(
        flops=0, bytes_accessed=int(microseconds * 3.6e6), transcendentals=0
    )


def whole(shape):
    return pl.BlockSpec(shape, lambda g: (0,) * len(shape))


def scans(rows, lanes):
    return pl.BlockSpec((rows, S, lanes), lambda g: (0, g, 0))


def low_half(rows=S):
    return lax.broadcasted_iota(jnp.int32, (rows, L), 1) < C


def swap(x):
    return pltpu.roll(x, C, 1)


def fold(x):
    x = jnp.broadcast_to(x, (8, L))
    return (x + swap(x))[:1]


def pair(ref, row, t):
    return ref[row, :, t * L : (t + 1) * L]


def stats_of(st_ref, count):
    groups = 2 * st_ref.shape[0]
    means = st_ref[:, :L]
    mean = fold(jnp.sum(means, axis=0, keepdims=True)) / groups
    spread = st_ref[:, L:] + count * (means - mean) ** 2
    spread = fold(jnp.sum(spread, axis=0, keepdims=True)) / (groups * count)
    return (mean, lax.rsqrt(spread + norm_eps))


def sums_of(st_ref):
    both = jnp.sum(st_ref[...], axis=0, keepdims=True)
    return (fold(both[:, :L]), fold(both[:, L:]))


def merge_stats(step, mean, squares, count, run_ref):
    @pl.when(step == 0)
    def _():
        run_ref[0:1] = mean
        run_ref[1:2] = squares

    @pl.when(step > 0)
    def _():
        before = step.astype(f32)
        share = 1.0 / (before + 1.0)
        delta = mean - run_ref[0:1]
        run_ref[0:1] = run_ref[0:1] + delta * share
        run_ref[1:2] = run_ref[1:2] + squares + delta * delta * (count * before * share)


def send_stats(step, steps, run_ref, st_ref):
    @pl.when(step == steps - 1)
    def _():
        row = jnp.concatenate([run_ref[0:1], run_ref[1:2]], axis=1)
        st_ref[...] = jnp.broadcast_to(row, st_ref.shape)


def halves(x):
    return x[:8] + x[8:]


def prep_kernel(
    row_ref, col_ref, occ_ref, kt_ref, np_ref, bits_ref, xrow_ref, xcol_ref, w1_ref, w2_ref,
    w2b_ref, w1b_ref, np2_ref,
):
    cols, scan_count, rows = occ_ref.shape
    groups = bits_ref.shape[0]
    row_of = lax.broadcasted_iota(jnp.int32, (rows, groups * L), 0)
    group_of = lax.broadcasted_iota(jnp.int32, (rows, groups * L), 1) // L
    inner = row_of - group_of * BITS
    power = jnp.where(
        (inner >= 0) & (inner < BITS), (1 << jnp.clip(inner, 0, BITS)), 0
    ).astype(bf16)
    flat = occ_ref[...].astype(f32).astype(bf16).reshape(cols * scan_count, rows)
    words = jnp.dot(flat, power, preferred_element_type=f32).astype(jnp.int32)
    words = words.reshape(cols // 2, 2, scan_count, groups * L)
    low = low_half(scan_count)
    for g in range(groups):
        for t in range(cols // 2):
            lanes = slice(g * L, (g + 1) * L)
            word = jnp.where(low, words[t, 0, :, lanes], words[t, 1, :, lanes])
            bits_ref[g, :, t * L : (t + 1) * L] = word.astype(jnp.int16)

    def live(row, t):
        word = bits_ref[row // BITS, :, t * L : (t + 1) * L].astype(jnp.int32)
        return (word & (1 << (row % BITS))) != 0

    for t in range(cols // 2):
        x = row_ref[0, :, t * L : (t + 1) * L].astype(f32)
        xrow_ref[:, t * L : (t + 1) * L] = jnp.where(live(rows - 1, t), x, 0.0).astype(bf16)
    for i in range(rows // 2):
        even = jnp.where(live(2 * i, cols // 2 - 1), col_ref[2 * i].astype(f32), 0.0)
        odd = jnp.where(live(2 * i + 1, cols // 2 - 1), col_ref[2 * i + 1].astype(f32), 0.0)
        xcol_ref[i] = jnp.where(low, swap(even), odd).astype(bf16)
    back = [[kt_ref[l, :, k * C : (k + 1) * C] for k in range(9)] for l in range(2)]
    fore = [[jnp.transpose(b) for b in layer] for layer in back]
    none = jnp.zeros((C, C), f32)

    def put(ref, rows_of, cols_of, pick):
        for a in range(rows_of):
            blocks = [pick(a, b) for b in range(cols_of)]
            for k in range(0, cols_of, 2):
                two = jnp.concatenate(blocks[k : k + 2], axis=1).astype(bf16)
                ref[a * C : (a + 1) * C, k * C : (k + 2) * C] = two

    def tap(table, p, q):
        return table[3 * p + q] if 0 <= p < 3 and 0 <= q < 3 else none

    put(w1_ref, 30, 4, lambda a, b: tap(fore[0], a // 6 - 2 * (b // 2), a % 6 - 2 * (b % 2) - 1))
    put(w2_ref, 16, 4, lambda a, b: tap(fore[1], a // 4 - b // 2, a % 4 - b % 2))
    put(w2b_ref, 16, 4, lambda a, b: tap(back[1], b // 2 + 2 - a // 4, b % 2 + 2 - a % 4))
    put(w1b_ref, 12, 4, lambda a, b: tap(back[0], (1, 2, 0)[a // 4], b + 1 - 2 * (a % 4)))
    np2_ref[...] = jnp.concatenate([np_ref[...], np_ref[...]], axis=1)


def prepare(x, occ, kt, norm_params):
    rows, scan_count, lanes = x.shape
    cols = occ.shape[0]
    groups = -(-rows // BITS)
    full = lambda *shape: jax.ShapeDtypeStruct(shape, bf16)
    outs = [
        jax.ShapeDtypeStruct((groups, scan_count, lanes), jnp.int16),
        full(scan_count, lanes),
        full(rows // 2, scan_count, L),
        full(30 * C, 4 * C),
        full(16 * C, 4 * C),
        full(16 * C, 4 * C),
        full(12 * C, 4 * C),
        jax.ShapeDtypeStruct((4, L), f32),
    ]
    return pl.pallas_call(
        prep_kernel,
        grid=(1,),
        in_specs=[
            pl.BlockSpec((1, scan_count, lanes), lambda g: (rows - 1, 0, 0)),
            pl.BlockSpec((rows, scan_count, L), lambda g: (0, 0, lanes // L - 1)),
            whole(occ.shape),
            whole(kt.shape),
            whole((4, C)),
        ],
        out_specs=[whole(o.shape) for o in outs],
        out_shape=outs,
        compiler_params=params_of(),
        cost_estimate=cost(5),
        name="prepare",
    )(x, x, occ, kt, norm_params.reshape(4, C))


def conv_one_kernel(
    x_ref, bits_ref, xrow_ref, xcol_ref, w_ref, c_ref, st_ref, up_ref, down_ref, left_ref,
    right_ref, xs, run,
):
    step, steps = (pl.program_id(0), pl.num_programs(0))
    rows, tiles = (x_ref.shape[0], x_ref.shape[2] // L)
    out_rows, out_tiles = (rows // 2, tiles // 2)
    pairs = (out_rows + 1) // 2

    @pl.when(step == 0)
    def _():
        for k in range(rows + 1, 4 * pairs + 1):
            xs[k // 4, k % 4] = jnp.zeros_like(xs[0, 0])

    xs[0, 0, :, L:] = xrow_ref[...]
    for k in range(out_rows + 1):
        xs[2 * k // 4, 2 * k % 4, :, :L] = xcol_ref[k]
    for i in range(out_rows):
        k = 2 * i + 1
        xs[k // 4, k % 4, :, :L] = swap(xcol_ref[i + 1].astype(f32)).astype(bf16)

    def fill(t, _):
        lanes = pl.ds(pl.multiple_of(t * L, L), L)
        into = pl.ds(pl.multiple_of(t * L + L, L), L)
        for g in range(bits_ref.shape[0]):
            word = bits_ref[g, :, lanes].astype(jnp.int32)
            for r in range(g * BITS, min(rows, (g + 1) * BITS)):
                x = x_ref[r, :, lanes].astype(f32)
                x = jnp.where((word & (1 << (r - g * BITS))) != 0, x, 0.0)
                xs[(r + 1) // 4, (r + 1) % 4, :, into] = x.astype(bf16)
        return 0

    lax.fori_loop(0, tiles, fill, 0)
    total = jnp.zeros((8, L), f32)
    for t in range(out_tiles):
        lanes = slice(2 * t * L, (2 * t + 3) * L)
        pieces = [xs[0:pairs, q, :, lanes] for q in range(4)] + [xs[1 : pairs + 1, 0, :, lanes]]
        lhs = jnp.concatenate([p.reshape(pairs * S, 3 * L) for p in pieces], axis=1)
        acc = jnp.dot(lhs, w_ref[...], preferred_element_type=f32).reshape(pairs, S, 2 * L)
        for i in range(out_rows):
            block = acc[i // 2, :, (i % 2) * L : (i % 2 + 1) * L]
            c_ref[i, :, t * L : (t + 1) * L] = block
            total = total + halves(block)
    count = out_rows * out_tiles * S
    mean = jnp.sum(total, axis=0, keepdims=True) / count

    def square(i, acc):
        for t in range(out_tiles):
            d = pair(c_ref, i, t) - mean
            acc = acc + halves(d * d)
        return acc

    squares = lax.fori_loop(0, out_rows, square, jnp.zeros((8, L), f32))
    merge_stats(step, mean, jnp.sum(squares, axis=0, keepdims=True), float(count), run)
    send_stats(step, steps, run, st_ref)
    up_ref[...] = c_ref[0:3].astype(bf16)
    down_ref[...] = c_ref[out_rows - 2 : out_rows].astype(bf16)
    left_ref[...] = c_ref[:, :, :L].astype(bf16)
    right_ref[...] = c_ref[:, :, (out_tiles - 1) * L :].astype(bf16)


def conv_one(x, bits, xrow, xcol, w, devices):
    rows, scan_count, lanes = x.shape
    r, w_out = (rows // 2, lanes // 2)
    pairs = (r + 1) // 2
    shape = lambda dtype, *s: jax.ShapeDtypeStruct(s, dtype)
    return pl.pallas_call(
        conv_one_kernel,
        grid=(scan_count // S,),
        in_specs=[
            scans(rows, lanes),
            scans(bits.shape[0], lanes),
            pl.BlockSpec((S, lanes), lambda g: (g, 0)),
            scans(r + 1, L),
            whole(w.shape),
        ],
        out_specs=[
            scans(r, w_out),
            whole((devices, 2 * L)),
            scans(3, w_out),
            scans(2, w_out),
            scans(r, L),
            scans(r, L),
        ],
        out_shape=[
            shape(f32, r, scan_count, w_out),
            shape(f32, devices, 2 * L),
            shape(bf16, 3, scan_count, w_out),
            shape(bf16, 2, scan_count, w_out),
            shape(bf16, r, scan_count, L),
            shape(bf16, r, scan_count, L),
        ],
        scratch_shapes=[
            pltpu.VMEM((pairs + 1, 4, S, lanes + L), bf16),
            pltpu.VMEM((8, L), f32),
        ],
        compiler_params=params_of(),
        cost_estimate=cost(18),
        name="conv_one",
    )(x, bits, xrow, xcol, w)


def conv_two_kernel(
    flags, c_ref, up_ref, down_ref, left_ref, right_ref, st_ref, np_ref, w_ref, c2_ref, n1_ref,
    st2_ref, hs, run, *, count,
):
    step, steps = (pl.program_id(0), pl.num_programs(0))
    r, tiles = (c_ref.shape[0], c_ref.shape[2] // L)
    mean, inv = stats_of(st_ref, count)
    offset = -mean * inv
    scale = 0.5 * np_ref[0:1] * inv
    shift = 0.5 * (np_ref[0:1] * offset + np_ref[1:2])
    f_up, f_down, f_left, f_right = (flags[k].astype(f32) for k in range(4))

    def act(c, flag=None):
        c = c.astype(f32)
        h = c * scale + shift
        out = h + h * jnp.tanh(h)
        if flag is not None:
            out = out * flag
        return (out.astype(bf16), c * inv + offset)

    def own(i, _):
        row = i + 2
        for t in range(tiles):
            hid, n = act(pair(c_ref, i, t))
            hs[row // 2, row % 2, :, (t + 1) * L : (t + 2) * L] = hid
            n1_ref[i, :, t * L : (t + 1) * L] = n
        hid, _n = act(left_ref[row], f_left)
        hs[row // 2, row % 2, :, :L] = hid
        hid, n = act(right_ref[row], f_right)
        hs[row // 2, row % 2, :, (tiles + 1) * L :] = hid
        n1_ref[i, :, tiles * L :] = n
        return 0

    lax.fori_loop(0, r, own, 0)
    for row in [0, 1, r + 2, r + 3, r + 4]:
        src, k, flag = (up_ref, row, f_up) if row < 2 else (down_ref, row - r - 2, f_down)
        for t in range(tiles):
            hid, n = act(pair(src, k, t), flag)
            hs[row // 2, row % 2, :, (t + 1) * L : (t + 2) * L] = hid
            if row == r + 2:
                n1_ref[r, :, t * L : (t + 1) * L] = n
        hid, _n = act(left_ref[row], flag * f_left)
        hs[row // 2, row % 2, :, :L] = hid
        hid, n = act(right_ref[row], flag * f_right)
        hs[row // 2, row % 2, :, (tiles + 1) * L :] = hid
        if row == r + 2:
            n1_ref[r, :, tiles * L :] = n
    pairs = (r + 3) // 2
    low = low_half()
    for k in range(tiles + 1):
        lanes = slice(k * L, (k + 2) * L)
        pieces = [hs[a : a + pairs, b, :, lanes] for a in range(2) for b in range(2)]
        lhs = jnp.concatenate([p.reshape(pairs * S, 2 * L) for p in pieces], axis=1)
        acc = jnp.dot(lhs, w_ref[...], preferred_element_type=f32).reshape(pairs, S, 2 * L)
        for row in range(r + 3):
            c2_ref[row, :, k * L : (k + 1) * L] = acc[row // 2, :, (row % 2) * L : (row % 2 + 1) * L]

    def tile_of(row, k):
        if k == 0:
            return jnp.where(low, pair(c2_ref, row, tiles), pair(c2_ref, row, 0))
        return pair(c2_ref, row, k)

    def add(i, acc):
        for k in range(tiles):
            acc = acc + halves(tile_of(i + 1, k))
        return acc

    total = lax.fori_loop(0, r, add, jnp.zeros((8, L), f32))
    cells = r * tiles * S
    mean2 = jnp.sum(total, axis=0, keepdims=True) / cells

    def square(i, acc):
        for k in range(tiles):
            d = tile_of(i + 1, k) - mean2
            acc = acc + halves(d * d)
        return acc

    squares = lax.fori_loop(0, r, square, jnp.zeros((8, L), f32))
    merge_stats(step, mean2, jnp.sum(squares, axis=0, keepdims=True), float(cells), run)
    send_stats(step, steps, run, st2_ref)


def conv_two(flags, c1, up, down, left, right, st, np2, w, count):
    r, scan_count, lanes = c1.shape
    tiles = lanes // L
    devices = st.shape[0]
    return pl.pallas_call(
        functools.partial(conv_two_kernel, count=count),
        grid=(scan_count // S,),
        in_specs=[
            pl.BlockSpec(memory_space=pltpu.SMEM),
            scans(r, lanes),
            scans(2, lanes),
            scans(3, lanes),
            scans(r + 5, L),
            scans(r + 5, L),
            whole(st.shape),
            whole(np2.shape),
            whole(w.shape),
        ],
        out_specs=[scans(r + 3, lanes + L), scans(r + 1, lanes + L), whole((devices, 2 * L))],
        out_shape=[
            jax.ShapeDtypeStruct((r + 3, scan_count, lanes + L), f32),
            jax.ShapeDtypeStruct((r + 1, scan_count, lanes + L), f32),
            jax.ShapeDtypeStruct((devices, 2 * L), f32),
        ],
        scratch_shapes=[
            pltpu.VMEM(((r + 5) // 2, 2, S, lanes + 2 * L), bf16),
            pltpu.VMEM((8, L), f32),
        ],
        compiler_params=params_of(),
        cost_estimate=cost(16),
        name="conv_two",
    )(flags, c1, up, down, left, right, st, np2, w)


def output_kernel(
    c2_ref, st_ref, np_ref, cot_ref, up_ref, down_ref, left_ref, right_ref, feat_ref, d_ref,
    sum_ref, run, *, count,
):
    step, steps = (pl.program_id(0), pl.num_programs(0))
    r, tiles = (cot_ref.shape[0], cot_ref.shape[2] // L)
    packed = left_ref.shape[0]
    mean, inv = stats_of(st_ref, count)
    offset = -mean * inv
    scale = 0.5 * np_ref[2:3] * inv
    shift = 0.5 * (np_ref[2:3] * offset + np_ref[3:4])
    low = low_half()

    def line(row, cot_of, own_row, sums):
        far = row >= packed
        line_of = row - jnp.where(far, packed, 0)
        before = left_ref[line_of].astype(f32)
        before = jnp.where(far, swap(before), before)
        beyond = right_ref[line_of].astype(f32)
        beyond = jnp.where(far, swap(beyond), beyond)
        last = None
        for k in range(tiles + 1):
            here = cot_of(k).astype(f32) if k < tiles else beyond
            cot = swap(jnp.where(low, here, before))
            before = here
            c = pair(c2_ref, row, k)
            n = c * inv + offset
            h = c * scale + shift
            t = jnp.tanh(h)
            plus = 1.0 + t
            d = (0.5 * cot) * (plus * (1.0 + h * (1.0 - t)))
            d_ref[row, :, k * L : (k + 1) * L] = d
            if own_row is None:
                continue
            f = h * plus
            if k > 0:
                both = swap(jnp.where(low, f, last))
                feat_ref[own_row, :, (k - 1) * L : k * L] = both.astype(bf16)
            last = f
            if k == 0:
                d = jnp.where(low, 0.0, d)
            if k == tiles:
                d = jnp.where(low, d, 0.0)
            sums = (sums[0] + halves(d), sums[1] + halves(d * n))
        return sums

    def own(i, sums):
        return line(i + 1, lambda k: pair(cot_ref, i, k), i, sums)

    zero = jnp.zeros((8, L), f32)
    sums = lax.fori_loop(0, r, own, (zero, zero))
    line(0, lambda k: pair(up_ref, 0, k), None, None)
    for j in range(2):
        line(r + 1 + j, lambda k, j=j: pair(down_ref, j, k), None, None)
    add_sums(step, steps, sums, run, sum_ref)


def add_sums(step, steps, sums, run, sum_ref):
    row = jnp.concatenate([jnp.sum(s, axis=0, keepdims=True) for s in sums], axis=1)

    @pl.when(step == 0)
    def _():
        run[0:1] = row

    @pl.when(step > 0)
    def _():
        run[0:1] = run[0:1] + row

    @pl.when(step == steps - 1)
    def _():
        sum_ref[...] = jnp.broadcast_to(run[0:1], sum_ref.shape)


def output(c2, st, np2, cot, up, down, left, right, count):
    r, scan_count, lanes = cot.shape
    devices = st.shape[0]
    wide = lanes + L
    return pl.pallas_call(
        functools.partial(output_kernel, count=count),
        grid=(scan_count // S,),
        in_specs=[
            scans(r + 3, wide),
            whole(st.shape),
            whole(np2.shape),
            scans(r, lanes),
            scans(1, lanes),
            scans(2, lanes),
            scans(left.shape[0], L),
            scans(right.shape[0], L),
        ],
        out_specs=[scans(r, lanes), scans(r + 3, wide), whole((devices, 2 * L))],
        out_shape=[
            jax.ShapeDtypeStruct((r, scan_count, lanes), bf16),
            jax.ShapeDtypeStruct((r + 3, scan_count, wide), f32),
            jax.ShapeDtypeStruct((devices, 2 * L), f32),
        ],
        scratch_shapes=[pltpu.VMEM((8, 2 * L), f32)],
        compiler_params=params_of(),
        cost_estimate=cost(16),
        name="output",
    )(c2, st, np2, cot, up, down, left, right)


def back_two_kernel(
    flags, d_ref, c2_ref, n1_ref, st_ref, sum_ref, np_ref, w_ref, dp_ref, edge_ref, kg_ref,
    sum1_ref, ds, hs, grad, run, *, count,
):
    step, steps = (pl.program_id(0), pl.num_programs(0))
    r, tiles = (n1_ref.shape[0] - 1, n1_ref.shape[2] // L - 1)
    cells = 2.0 * count * st_ref.shape[0]
    mean, inv = stats_of(st_ref, count)
    shift_sum, gain_sum = sums_of(sum_ref)
    gain = np_ref[2:3] * inv
    c_n = -gain * inv * gain_sum / cells
    c_0 = -gain * shift_sum / cells - c_n * mean
    f_up, f_down, f_left, f_right = (flags[k].astype(f32) for k in range(4))
    low = low_half()
    left = jnp.where(low, f_left, 1.0)
    right = jnp.where(low, 1.0, f_right)

    def line(row, flag):
        for k in range(tiles + 1):
            d = pair(d_ref, row, k) * gain + (pair(c2_ref, row, k) * c_n + c_0)
            if k == 0:
                d = d * left
            if k == tiles:
                d = d * right
            if flag is not None:
                d = d * flag
            ds[row // 2, row % 2, :, k * L : (k + 1) * L] = d.astype(bf16)

    def own(i, _):
        line(i + 1, None)
        for t in range(tiles):
            h = 0.5 * (pair(n1_ref, i, t) * np_ref[0:1] + np_ref[1:2])
            hs[i, :, t * L : (t + 1) * L] = (h + h * jnp.tanh(h)).astype(bf16)
        return 0

    lax.fori_loop(0, r, own, 0)
    line(0, f_up)
    line(r + 1, f_down)
    line(r + 2, f_down)

    @pl.when(step == 0)
    def _():
        grad[...] = jnp.zeros_like(grad)

    total = None
    for t in range(tiles):
        lanes = slice(t * L, (t + 2) * L)
        rows = ds[:, :, :, lanes].reshape(r + 3, S, 2 * L)
        rhs = jnp.concatenate([rows[a : a + r].reshape(r * S, 2 * L) for a in range(3)], axis=1)
        lhs = hs[:, :, t * L : (t + 1) * L].reshape(r * S, L)
        part = lax.dot_general(lhs, rhs, (((0,), (0,)), ((), ())), preferred_element_type=f32)
        total = part if total is None else total + part
    grad[...] += total
    pairs = (r + 1) // 2
    sums = (jnp.zeros((8, L), f32), jnp.zeros((8, L), f32))
    for t in range(tiles):
        lanes = slice(t * L, (t + 2) * L)
        pieces = [ds[a : a + pairs, b, :, lanes] for a in range(2) for b in range(2)]
        lhs = jnp.concatenate([p.reshape(pairs * S, 2 * L) for p in pieces], axis=1)
        acc = jnp.dot(lhs, w_ref[...], preferred_element_type=f32).reshape(pairs, S, 2 * L)
        for i in range(r + 1):
            n = pair(n1_ref, i, t)
            h = 0.5 * (n * np_ref[0:1] + np_ref[1:2])
            tan = jnp.tanh(h)
            d = acc[i // 2, :, (i % 2) * L : (i % 2 + 1) * L]
            d = (0.5 * d) * ((1.0 + tan) * (1.0 + h * (1.0 - tan)))
            dp_ref[i, :, t * L : (t + 1) * L] = d
            if i < r:
                sums = (sums[0] + halves(d), sums[1] + halves(d * n))
    add_sums(step, steps, sums, run, sum1_ref)
    for i in range(pairs):
        both = jnp.where(low, pair(dp_ref, i, 0), swap(pair(dp_ref, pairs + i, 0)))
        edge_ref[i] = both.astype(bf16)

    @pl.when(step == steps - 1)
    def _():
        for p in range(3):
            for q in range(3):
                block = None
                for w in range(2):
                    at = (2 - p) * 4 * C + (w + 2 - q) * C
                    part = grad[w * C : (w + 1) * C, at : at + C]
                    block = part if block is None else block + part
                kg_ref[3 * p + q] = jnp.transpose(block)


def back_two(flags, d, c2, n1, st, sums, np2, w, count):
    r, scan_count, wide = n1.shape
    r, lanes = (r - 1, wide - L)
    devices = st.shape[0]
    return pl.pallas_call(
        functools.partial(back_two_kernel, count=count),
        grid=(scan_count // S,),
        in_specs=[
            pl.BlockSpec(memory_space=pltpu.SMEM),
            scans(r + 3, wide),
            scans(r + 3, wide),
            scans(r + 1, wide),
            whole(st.shape),
            whole(sums.shape),
            whole(np2.shape),
            whole(w.shape),
        ],
        out_specs=[
            scans(r + 1, lanes),
            scans((r + 1) // 2, L),
            whole((9, C, C)),
            whole((devices, 2 * L)),
        ],
        out_shape=[
            jax.ShapeDtypeStruct((r + 1, scan_count, lanes), f32),
            jax.ShapeDtypeStruct(((r + 1) // 2, scan_count, L), bf16),
            jax.ShapeDtypeStruct((9, C, C), f32),
            jax.ShapeDtypeStruct((devices, 2 * L), f32),
        ],
        scratch_shapes=[
            pltpu.VMEM(((r + 3) // 2, 2, S, wide), bf16),
            pltpu.VMEM((r, S, lanes), bf16),
            pltpu.VMEM((L, 12 * C), f32),
            pltpu.VMEM((8, 2 * L), f32),
        ],
        compiler_params=params_of(),
        cost_estimate=cost(18),
        name="back_two",
    )(flags, d, c2, n1, st, sums, np2, w)


def back_one_kernel(
    flags, dp_ref, edge_ref, n1_ref, x_ref, bits_ref, st_ref, sum_ref, np_ref, kg2_ref, ds, kg_ref,
    xm, grad, *, count,
):
    step, steps = (pl.program_id(0), pl.num_programs(0))
    r, tiles = (n1_ref.shape[0] - 1, n1_ref.shape[2] // L - 1)
    cells = 2.0 * count * st_ref.shape[0]
    _mean, inv = stats_of(st_ref, count)
    shift_sum, gain_sum = sums_of(sum_ref)
    gain = np_ref[0:1] * inv
    c_n = -gain * gain_sum / cells
    c_0 = -gain * shift_sum / cells
    f_down, f_right = (flags[1].astype(f32), flags[3].astype(f32))
    packed = edge_ref.shape[0]

    def line(i, flag):
        far = i >= packed
        beyond = edge_ref[i - jnp.where(far, packed, 0)].astype(f32)
        beyond = jnp.where(far, swap(beyond), beyond)
        for t in range(tiles + 1):
            d = pair(dp_ref, i, t) if t < tiles else beyond
            d = d * gain + (pair(n1_ref, i, t) * c_n + c_0)
            if t == tiles:
                d = d * f_right
            if flag is not None:
                d = d * flag
            ds[i, :, t * L : (t + 1) * L] = d.astype(bf16)

    def own(i, _):
        line(i, None)
        return 0

    lax.fori_loop(0, r, own, 0)
    line(r, f_down)

    def fill(t, _):
        lanes = pl.ds(pl.multiple_of(t * L, L), L)
        for g in range(bits_ref.shape[0]):
            word = bits_ref[g, :, lanes].astype(jnp.int32)
            for row in range(g * BITS, min(2 * r, (g + 1) * BITS)):
                x = x_ref[row, :, lanes].astype(f32)
                x = jnp.where((word & (1 << (row - g * BITS))) != 0, x, 0.0)
                xm[row % 2, row // 2, :, lanes] = x.astype(bf16)
        return 0

    lax.fori_loop(0, 2 * tiles, fill, 0)

    @pl.when(step == 0)
    def _():
        grad[...] = jnp.zeros_like(grad)

    turned = (((0,), (0,)), ((), ()))
    totals = [None, None, None]
    for t in range(tiles):
        lanes = slice(t * L, (t + 2) * L)
        xl = slice(2 * t * L, 2 * (t + 1) * L)
        rows = [ds[a : a + r, :, lanes].reshape(r * S, 2 * L) for a in range(2)]
        xe, xo = (xm[a, :, :, xl].reshape(r * S, 2 * L) for a in range(2))
        for k, (a, b) in enumerate(((xe, rows[0]), (xo, rows[0]), (xo, rows[1]))):
            part = lax.dot_general(a, b, turned, preferred_element_type=f32)
            totals[k] = part if totals[k] is None else totals[k] + part
    for k in range(3):
        grad[k] += totals[k]

    @pl.when(step == steps - 1)
    def _():
        blocks = []
        for p in range(3):
            g = (2, 0, 1)[p]
            for q in range(3):
                block = None
                for v in range(3):
                    u = q - 1 + 2 * v
                    if 0 <= u < 4:
                        part = grad[g, u * C : (u + 1) * C, v * C : (v + 1) * C]
                        block = part if block is None else block + part
                blocks.append(jnp.transpose(block))
        blocks += [kg2_ref[8]] + [kg2_ref[k] for k in range(8)]
        for a in range(9):
            kg_ref[a * C : (a + 1) * C] = jnp.concatenate(blocks[2 * a : 2 * a + 2], axis=1)
        if kg_ref.shape[0] > 9 * C:
            kg_ref[9 * C :] = jnp.zeros((kg_ref.shape[0] - 9 * C, L), f32)


def back_one(flags, dp, edge, n1, x, bits, st, sums, np2, kg2, count):
    rows, scan_count, lanes = x.shape
    r, tiles = (rows // 2, lanes // L // 2)
    devices = st.shape[0]
    share = 8 * -(-9 * C // (8 * devices))
    wide = (tiles + 1) * L
    return pl.pallas_call(
        functools.partial(back_one_kernel, count=count),
        grid=(scan_count // S,),
        in_specs=[
            pl.BlockSpec(memory_space=pltpu.SMEM),
            scans(r + 1, tiles * L),
            scans(edge.shape[0], L),
            scans(r + 1, wide),
            scans(rows, lanes),
            scans(bits.shape[0], lanes),
            whole(st.shape),
            whole(sums.shape),
            whole(np2.shape),
            whole(kg2.shape),
        ],
        out_specs=[scans(r + 1, wide), whole((devices * share, L))],
        out_shape=[
            jax.ShapeDtypeStruct((r + 1, scan_count, wide), bf16),
            jax.ShapeDtypeStruct((devices * share, L), f32),
        ],
        scratch_shapes=[
            pltpu.VMEM((2, r, S, lanes), bf16),
            pltpu.VMEM((3, 4 * C, 4 * C), f32),
        ],
        compiler_params=params_of(),
        cost_estimate=cost(16),
        name="back_one",
    )(flags, dp, edge, n1, x, bits, st, sums, np2, kg2)


def input_grad_kernel(ds, bits_ref, w_ref, *rest):
    ig_ref = rest[-1]
    r, tiles = (ds.shape[0] - 1, ds.shape[2] // L - 1)
    for t in range(tiles):
        lanes = slice(t * L, (t + 2) * L)
        rows = [ds[a : a + r, :, lanes].reshape(r * S, 2 * L) for a in range(2)]
        even = jnp.dot(rows[0], w_ref[: 4 * C], preferred_element_type=f32)
        odd = jnp.dot(
            jnp.concatenate(rows, axis=1), w_ref[4 * C :], preferred_element_type=f32
        )
        for k, block in enumerate((even, odd)):
            block = block.reshape(r, S, 2 * L)
            for h in range(2):
                xl = slice((2 * t + h) * L, (2 * t + h + 1) * L)
                for i in range(r):
                    row = 2 * i + k
                    word = bits_ref[row // BITS, :, xl].astype(jnp.int32)
                    live = (word & (1 << (row % BITS))) != 0
                    d = jnp.where(live, block[i, :, h * L : (h + 1) * L], 0.0)
                    ig_ref[row, :, xl] = d.astype(bf16)


def input_gradient(d, bits, w, part, before):
    r, scan_count, wide = d.shape
    rows, lanes = (2 * (r - 1), 2 * (wide - L))
    steps = scan_count // S // 2
    at = lambda n, m: pl.BlockSpec((n, S, m), lambda g: (0, g + part * steps, 0))
    earlier = () if before is None else (before,)
    return pl.pallas_call(
        input_grad_kernel,
        grid=(steps,),
        in_specs=[at(r, wide), at(bits.shape[0], lanes), whole(w.shape)]
        + [pl.BlockSpec(memory_space=pl.ANY)] * len(earlier),
        out_specs=at(rows, lanes),
        out_shape=jax.ShapeDtypeStruct((rows, scan_count, lanes), bf16),
        input_output_aliases={3: 0} if earlier else {},
        compiler_params=params_of(),
        cost_estimate=cost(7),
        name="input_gradient",
    )(d, bits, w, *earlier)


def adam_step(weight_now, gradient, moment_one, moment_two, step_rate, decay_rate):
    first_new = adam_beta * moment_one + (1.0 - adam_beta) * gradient
    second_new = adam_beta * moment_two + (1.0 - adam_beta) * gradient * gradient
    correction = 1.0 - adam_beta**step_count
    update = first_new / correction / (jnp.sqrt(second_new / correction) + adam_eps)
    return (weight_now - step_rate * (update + decay_rate * weight_now), first_new, second_new)


def update_kernel(
    g_ref, s1_ref, s2_ref, k_ref, km_ref, kv_ref, n_ref, nm_ref, nv_ref, gn_ref, ok_ref, okm_ref,
    okv_ref, olow_ref, on_ref, onm_ref, onv_ref,
):
    norm_rows = []
    for ref in (s1_ref, s2_ref):
        shift_sum, gain_sum = sums_of(ref)
        norm_rows += [gain_sum[:, :C], shift_sum[:, :C]]
    g_norm = jnp.concatenate(norm_rows, axis=0)
    squares = jnp.sum(jnp.sum(g_ref[: 9 * C] ** 2, axis=0, keepdims=True), axis=1, keepdims=True)
    squares = squares + jnp.sum(
        jnp.sum(g_norm * g_norm, axis=0, keepdims=True), axis=1, keepdims=True
    )
    norm = jnp.sqrt(squares)
    gn_ref[...] = norm
    factor = jnp.minimum(1.0, clip_limit / norm)
    on, onm, onv = adam_step(
        n_ref[...], g_norm * factor, nm_ref[...], nv_ref[...], norm_rate, 0.0
    )
    on_ref[...] = on
    onm_ref[...] = onm
    onv_ref[...] = onv
    for layer in range(2):
        for a in range(5):
            width = L if a < 4 else C
            at = slice(a * L, a * L + width)
            if a == 4:
                g = g_ref[4 * C : 5 * C, layer * C : (layer + 1) * C]
            else:
                first = (a + 5 * layer) * C
                g = g_ref[first : first + C, :]
            k, km, kv = adam_step(
                k_ref[layer, :, at], g * factor, km_ref[layer, :, at], kv_ref[layer, :, at],
                kernel_rate, kernel_decay,
            )
            ok_ref[layer, :, at] = k
            okm_ref[layer, :, at] = km
            okv_ref[layer, :, at] = kv
            olow_ref[layer, :, at] = k.astype(bf16)


def update(grads, sums1, sums2, kt, kmt, kvt, norm_params, norm_m, norm_v):
    flat = lambda a: a.reshape(4, C)
    big = jax.ShapeDtypeStruct(kt.shape, f32)
    small = jax.ShapeDtypeStruct((4, C), f32)
    outs = [
        jax.ShapeDtypeStruct((1, 1), f32), big, big, big,
        jax.ShapeDtypeStruct(kt.shape, bf16), small, small, small,
    ]
    args = [grads, sums1, sums2, kt, kmt, kvt, flat(norm_params), flat(norm_m), flat(norm_v)]
    return pl.pallas_call(
        update_kernel,
        grid=(1,),
        in_specs=[whole(a.shape) for a in args],
        out_specs=[whole(o.shape) for o in outs],
        out_shape=outs,
        compiler_params=params_of(),
        cost_estimate=cost(3),
        name="update",
    )(*args)


def shifted(block, axis, distance):
    devices = range(lax.axis_size(axis))
    route = [(i - distance, i) for i in devices if i - distance in devices]
    return lax.ppermute(block, axis, route)


def exchange(rows):
    return lax.all_to_all(rows, BOTH, 0, 0, tiled=True)


def per_device(
    scan_features, occupancy, kernels, kernel_m, kernel_v, norm_params, norm_m, norm_v, cotangent
):
    x = jnp.transpose(scan_features, (1, 0, 2))
    cot = jnp.transpose(cotangent, (1, 0, 2))
    occ = jnp.transpose(occupancy, (2, 0, 1))
    kt, kmt, kvt = (jnp.transpose(a, (0, 2, 1)) for a in (kernels, kernel_m, kernel_v))
    gy, gx = (lax.axis_size("gy"), lax.axis_size("gx"))
    devices = gy * gx
    y, z = (lax.axis_index("gy"), lax.axis_index("gx"))
    flags = jnp.stack([y > 0, y < gy - 1, z > 0, z < gx - 1]).astype(jnp.int32)
    rows, scan_count, lanes = x.shape
    r, tiles = (rows // 2, lanes // L // 2)
    count = float(scan_count * r * tiles)
    last = (tiles - 1) * L

    bits, xrow, xcol, w1, w2, w2b, w1b, np2 = prepare(x, occ, kt, norm_params)
    down = shifted(jnp.concatenate([xrow, cot[r - 1]], axis=1), "gy", 1)
    cot_down = shifted(cot[:2], "gy", -1)
    xrow_in, cot_up = (down[:, :lanes], down[None, :, lanes:])
    xcol_in = shifted(jnp.concatenate([xrow_in[None, :, lanes - L :], xcol], axis=0), "gx", 1)
    packed = (r + 3) // 2

    def cot_column(at, first):
        column = jnp.concatenate(
            [a[:, :, at : at + C] for a in (cot_up, cot, cot_down)], axis=0
        )
        pieces = [column[:packed], column[packed:]]
        return jnp.concatenate(pieces[::first], axis=2)

    cot_left = shifted(cot_column(last + C, -1), "gx", 1)
    cot_right = shifted(cot_column(0, 1), "gx", -1)

    c1, st1, up, down, left, right = conv_one(x, bits, xrow_in, xcol_in, w1, devices)
    down_in = shifted(up, "gy", -1)
    up_in = shifted(down, "gy", 1)
    lines = lambda own, at: jnp.concatenate(
        [up_in[:, :, at : at + L], own, down_in[:, :, at : at + L]], axis=0
    )
    left_in = shifted(lines(right, last), "gx", 1)
    right_in = shifted(lines(left, 0), "gx", -1)
    st1 = exchange(st1)

    c2, n1, st2 = conv_two(flags, c1, up_in, down_in, left_in, right_in, st1, np2, w2, count)
    st2 = exchange(st2)
    features, d2, sums2 = output(c2, st2, np2, cot, cot_up, cot_down, cot_left, cot_right, count)
    sums2 = exchange(sums2)
    d1, edge, kg2, sums1 = back_two(flags, d2, c2, n1, st2, sums2, np2, w2b, count)
    edge = shifted(edge, "gx", -1)
    sums1 = exchange(sums1)
    d1, grads = back_one(flags, d1, edge, n1, x, bits, st1, sums1, np2, kg2, count)
    share = grads.shape[0] // devices
    grads = exchange(grads)
    input_grad = input_gradient(d1, bits, w1b, 0, None)
    mine = jnp.sum(grads.reshape(devices, share, L), axis=0)
    grads = exchange(jnp.broadcast_to(mine[None], (devices, share, L)).reshape(-1, L))
    input_grad = input_gradient(d1, bits, w1b, 1, input_grad)
    norm, k, km, kv, low, n, nm, nv = update(
        grads, sums1, sums2, kt, kmt, kvt, norm_params, norm_m, norm_v
    )
    back = lambda a: jnp.transpose(a, (0, 2, 1))
    deep = lambda a: a.reshape(norm_params.shape)
    return (
        jnp.transpose(features, (1, 0, 2)),
        jnp.transpose(input_grad, (1, 0, 2)),
        norm.reshape(()),
        back(k),
        back(km),
        back(kv),
        back(low),
        deep(n),
        deep(nm),
        deep(nv),
    )


def solution(mesh):
    split = P(None, "gy", "gx")
    return jax.shard_map(
        per_device,
        mesh=mesh,
        in_specs=(split, split) + (P(),) * 6 + (split,),
        out_specs=(split, split) + (P(),) * 8,
        check_vma=False,
    )
```

time: 1590 us -> 269 us (0.17); the launches traced: 1570 us -> 268 us
  local copies, waits for them, and re-layouts: 686 us -> 15.1 us
  other arithmetic: 294 us -> 6.76 us
  blocking collectives: 245 us -> 53.9 us
  matrix products: 150 us -> 0 us
  Pallas kernels: 0 us -> 130 us
  waiting for transfers between devices: 147 us -> 19.3 us
  between operations: 17.3 us -> 0.91 us
    concatenate x6 -> x0, local copies, waits for them, and re-layouts: 288 us -> none  [the longest x2 143 us: patches(): return jnp.concatenate(pieces, axis=3)]
    psum x6 -> x0, blocking collectives: 245 us -> none  [the longest x2 82.2 us: batch_stats(): summed = lax.psum(jnp.sum(values, axis=(0, 1, 2)), ('gy', 'gx'))]
    dot_general x6 -> x0, matrix products: 150 us -> none  [the longest x1 49.6 us: per_device(): contrib = jnp.dot(grad_ext, tap_kernel, preferred_element_type=jnp.float32)]
    mul x5 -> x0, local copies, waits for them, and re-layouts: 134 us -> none  [the longest x2 71.7 us: per_device(): d_inputs * occupancy.astype(jnp.float32)[..., None]]
    pallas_call x0 -> x9, Pallas kernels: none -> 130 us  [the longest x1 27.8 us: back_one(): pl.pallas_call(functools.partial(back_one_kernel, count=count), grid=(sca...]
    psum x1 -> x0, waiting for transfers between devices: 124 us -> none  [per_device(): kernel_one, kernel_two = lax.psum((kernel_one, kernel_two), ('gy', 'gx'))]
    another operation x6 -> x0, other arithmetic: 108 us -> none  [the longest x3 70.1 us: per_device(): jnp.stack(col_blocks, axis=3)]
    slice x14 -> x7, local copies, waits for them, and re-layouts: 90.4 us -> 3.3 us  [the longest x3 1.6 us: cot_column(): a[:, :, at:at + C]]
  transfers between devices with their start and end apart: 13 -> 12, of which waited for: 3 -> 5; matrix products, arithmetic and copies ran while one was open for 16% -> 4% of each run, Pallas kernels for 0% -> 11%
where the time goes in v1:
time: 269 us; the launch traced here: 268 us
  Pallas kernels  130 us (48%)
  blocking collectives  53.9 us (20%)
  starting transfers between devices  42.5 us (16%)
  waiting for transfers between devices  19.3 us (7%)
  local copies, waits for them, and re-layouts  15.1 us (6%)
  other arithmetic  6.76 us (3%)
    all_to_all x4, blocking collectives, exchange(): return lax.all_to_all(rows, BOTH, 0, 0, tiled=True)  53.9 us
    ppermute x10, starting transfers between devices, shifted(): return lax.ppermute(block, axis, route)  29.9 us
    pallas_call x1, Pallas kernels, back_one(): pl.pallas_call(functools.partial(back_one_kernel, count=count), grid=(sca...  27.8 us
    pallas_call x1, Pallas kernels, output(): pl.pallas_call(functools.partial(output_kernel, count=count), grid=(scan_...  25.2 us
    pallas_call x1, Pallas kernels, conv_one(): pl.pallas_call(conv_one_kernel, grid=(scan_count // S,), in_specs=[scans(...  19.7 us
    pallas_call x1, Pallas kernels, back_two(): pl.pallas_call(functools.partial(back_two_kernel, count=count), grid=(sca...  19.1 us
    pallas_call x1, Pallas kernels, conv_two(): pl.pallas_call(functools.partial(conv_two_kernel, count=count), grid=(sca...  16.9 us
    pallas_call x2, Pallas kernels, input_gradient(): pl.pallas_call(input_grad_kernel, grid=(steps,), in_specs=[at(r, wide), a...  13.2 us
  transfers between devices with their start and end apart: 12, of which 5 were waited for; matrix products, arithmetic and copies ran while one was open for 4% of the time, Pallas kernels for 11%

profile of v1, /device:TPU:0, one launch (start us, length us, event | category | flops | bytes accessed | tf_op | source)
XLA Modules:
  0.0 268.2 jit_solution(15113357256810686499)
XLA Ops:
  1.6 4.9 %prepare.1 = (s16[5,64,1792]{2,1,0:T(8,128)(2,1)}, bf16[64,1792]{1,0:T(8,128)(2,1)}, bf16[31,64,128]{2,1,0:T(8,128)(2,1)}, bf16[1920,256]{1,0:T(8,128)(2,1)}, bf...) custom-call(bf16[62,64,1792]{2,1,0:T(8,128)(2,1)} %bitcast.47, ...), custom_call_target="tpu_custom_call" | custom-call | bytes 18000000 | tf_op jit(solution)/shard_map/prepare/pallas_call | solution.py:171
  7.4 2.4 collective-permute-start
  9.8 1.2 collective-permute-done
  12.1 4.3 %collective-permute-start.1 = (bf16[32,64,128]{2,1,0:T(8,128)(2,1)S(1)}, bf16[32,64,128]{2,1,0:T(8,128)(2,1)S(1)}, u32[]{:S(2)}, u32[]{:S(2)}) collective-permute-start(bf16[32,64,128]{2,1,0:T(8,128)(2,1)S(1)} %pad_maximum_fusion.2), channel_id=1, source_target_pairs={{0,1},{1,2},{2,3},{3,4},{4,5},{5,6},{6,7},{8,9},{9,10},{10,11},{11... | collective-permute-start | bytes 1572872 | tf_op jit(solution)/shard_map/ppermute | solution.py:872
  17.4 1.3 collective-permute-start.6
  18.7 1.4 fusion.2
  20.1 4.6 %collective-permute-done.6.down_ref = bf16[2,64,896]{2,1,0:T(8,128)(2,1)S(1)} collective-permute-done((bf16[2,64,896]{2,1,0:T(8,128)(2,1)S(1)}, bf16[2,64,896]{2,1,0:T(8,128)(2,1)S(1)}, u32[]{:S(2)}, u32[]{:S(2)}) %collective-permute-start.6) | collective-permute-done | bytes 229408 | tf_op jit(solution)/shard_map/ppermute | solution.py:872
  26.3 19.7 %conv_one.1 = (f32[31,64,896]{2,1,0:T(8,128)}, f32[32,256]{1,0:T(8,128)}, bf16[3,64,896]{2,1,0:T(8,128)(2,1)}, bf16[2,64,896]{2,1,0:T(8,128)(2,1)}, bf16[31,64,1...) custom-call(bf16[62,64,1792]{2,1,0:T(8,128)(2,1)} %bitcast.49, s16[5,64,1792]{2,1,0:T(8,128)(2,1)} %get-tuple-element.44.bits_ref, ...), custom_call_target="tpu_custom_call" | custom-call | bytes 64800000 | tf_op jit(solution)/shard_map/conv_one/pallas_call | solution.py:255
  46.0 7.4 %collective-permute-start.2 = (bf16[2,64,896]{2,1,0:T(8,128)(2,1)}, bf16[2,64,896]{2,1,0:T(8,128)(2,1)S(1)}, u32[]{:S(2)}, u32[]{:S(2)}) collective-permute-start(bf16[2,64,896]{2,1,0:T(8,128)(2,1)} %get-tuple-element.49), channel_id=1, source_target_pairs={{0,8},{8,16},{16,24},{1,9},{9,17},{17,25},{2,10},{10,18},{18,26},{... | collective-permute-start | bytes 688136 | tf_op jit(solution)/shard_map/ppermute | solution.py:872
  53.4 1.3 collective-permute-start.3
  54.8 2.4 collective-permute-done.3.down_ref
  57.2 1.2 pad_maximum_fusion
  58.4 3.5 %collective-permute-start.4 = (bf16[36,64,128]{2,1,0:T(8,128)(2,1)S(1)}, bf16[36,64,128]{2,1,0:T(8,128)(2,1)S(1)}, u32[]{:S(2)}, u32[]{:S(2)}) collective-permute-start(bf16[36,64,128]{2,1,0:T(8,128)(2,1)S(1)} %pad_maximum_fusion), channel_id=1, source_target_pairs={{0,1},{1,2},{2,3},{3,4},{4,5},{5,6},{6,7},{8,9},{9,10},{10,11},{11... | collective-permute-start | bytes 1769480 | tf_op jit(solution)/shard_map/ppermute | solution.py:872
  63.0 1.3 collective-permute-start.5
  65.3 1.3 collective-permute-start.8
  67.4 6.0 %collective-permute-start.7 = (bf16[17,64,128]{2,1,0:T(8,128)(2,1)}, bf16[17,64,128]{2,1,0:T(8,128)(2,1)}, u32[]{:S(2)}, u32[]{:S(2)}) collective-permute-start(bf16[17,64,128]{2,1,0:T(8,128)(2,1)} %fusion.1), channel_id=1, source_target_pairs={{0,1},{1,2},{2,3},{3,4},{4,5},{5,6},{6,7},{8,9},{9,10},{10,11},{11... | collective-permute-start | bytes 835592 | tf_op jit(solution)/shard_map/ppermute | solution.py:872
  73.4 1.4 copy.20
  74.8 10.0 %all-to-all-start = ((f32[32,1,256]{2,1,0:T(1,128)}), f32[32,1,256]{2,1,0:T(1,128)S(1)}, u32[]{:S(2)}, u32[]{:S(2)}) async-start(f32[32,1,256]{2,1,0:T(1,128)} %copy.20), calls=%async_computation | async-start | bytes 65536 | tf_op jit(solution)/shard_map/all_to_all | solution.py:876
  85.4 10.7 %all-to-all-done = f32[32,1,256]{2,1,0:T(1,128)S(1)} async-done(((f32[32,1,256]{2,1,0:T(1,128)}), f32[32,1,256]{2,1,0:T(1,128)S(1)}, u32[]{:S(2)}, u32[]{:S(2)}) %all-to-all-start) | async-done | bytes 32800 | tf_op jit(solution)/shard_map/all_to_all | solution.py:876
  97.8 16.9 %conv_two.1 = (f32[34,64,1024]{2,1,0:T(8,128)}, f32[32,64,1024]{2,1,0:T(8,128)}, f32[32,256]{1,0:T(8,128)}) custom-call(s32[4]{0:T(128)} %add_convert_fusion.flags, f32[31,64,896]{2,1,0:T(8,128)} %get-tuple-element.48.c_ref, bf16[2,64,896]{2,1,0:T(8,128)(2,1)} %copy-done.7, bf16[3,64,896]{2,1,0:T(8,128)(2,1)} %copy-done.4, bf16[36,64,128]{2,1,0:T(8,128)(2,1)} %copy-done.2, ...), custom_call_target="tpu_custom_call" | custom-call | bytes 57600000 | tf_op jit(solution)/shard_map/conv_two/pallas_call | solution.py:377
  115.5 18.7 %all_to_all.61 = f32[32,1,256]{2,1,0:T(1,128)S(1)} all-to-all(f32[32,1,256]{2,1,0:T(1,128)S(1)} %copy.21), channel_id=1, replica_groups=mesh['gy'=4,'gx'=8] {'gy','gx'}, dimensions={0} | all-to-all | bytes 65536 | tf_op jit(solution)/shard_map/all_to_all | solution.py:876
  135.5 25.2 %output.1 = (bf16[31,64,896]{2,1,0:T(8,128)(2,1)}, f32[34,64,1024]{2,1,0:T(8,128)}, f32[32,256]{1,0:T(8,128)}) custom-call(f32[34,64,1024]{2,1,0:T(8,128)} %get-tuple-element.56.c2_ref, f32[32,256]{1,0:T(8,128)} %bitcast.63, f32[4,128]{1,0:T(4,128)} %get-tuple-element.54.np_ref, bf16[31,64,896]{2,1,0:T(8,128)(2,1)} %bitcast.55, ...), custom_call_target="tpu_custom_call" | custom-call | bytes 57600000 | tf_op jit(solution)/shard_map/output/pallas_call | solution.py:484
  161.5 8.9 %all_to_all.62 = f32[32,1,256]{2,1,0:T(1,128)S(1)} all-to-all(f32[32,1,256]{2,1,0:T(1,128)S(1)} %copy.22), channel_id=1, replica_groups=mesh['gy'=4,'gx'=8] {'gy','gx'}, dimensions={0} | all-to-all | bytes 65536 | tf_op jit(solution)/shard_map/all_to_all | solution.py:876
  171.0 19.1 %back_two.1 = (f32[32,64,896]{2,1,0:T(8,128)}, bf16[16,64,128]{2,1,0:T(8,128)(2,1)}, f32[9,64,64]{2,1,0:T(8,128)}, f32[32,256]{1,0:T(8,128)}) custom-call(s32[4]{0:T(128)} %add_convert_fusion.flags, f32[34,64,1024]{2,1,0:T(8,128)} %get-tuple-element.59.d_ref, f32[34,64,1024]{2,1,0:T(8,128)} %get-tuple-element.56.c2_ref, ...), custom_call_target="tpu_custom_call" | custom-call | bytes 64800000 | tf_op jit(solution)/shard_map/back_two/pallas_call | solution.py:600
  190.1 1.3 collective-permute-start.9
  192.2 10.2 %all_to_all.63 = f32[32,1,256]{2,1,0:T(1,128)S(1)} all-to-all(f32[32,1,256]{2,1,0:T(1,128)S(1)} %copy.23), channel_id=1, replica_groups=mesh['gy'=4,'gx'=8] {'gy','gx'}, dimensions={0} | all-to-all | bytes 65536 | tf_op jit(solution)/shard_map/all_to_all | solution.py:876
  203.7 27.8 %back_one.1 = (bf16[32,64,1024]{2,1,0:T(8,128)(2,1)}, f32[768,128]{1,0:T(8,128)}) custom-call(s32[4]{0:T(128)} %add_convert_fusion.flags, f32[32,64,896]{2,1,0:T(8,128)} %get-tuple-element.63.dp_ref, bf16[16,64,128]{2,1,0:T(8,128)(2,1)} %copy-done.9, f32[32,64,1024]{2,1,0:T(8,128)} %get-tuple-element.60.n1_ref, bf16[62,64,1792]{2,1,0:T(8,128)(2,1)} %bitcast.50, ...), custom_call_target="tpu_custom_call" | custom-call | bytes 57600000 | tf_op jit(solution)/shard_map/back_one/pallas_call | solution.py:727
  231.5 16.2 %all_to_all.64 = f32[32,24,128]{2,1,0:T(8,128)S(1)} all-to-all(f32[32,24,128]{2,1,0:T(8,128)} %bitcast.60), channel_id=1, replica_groups=mesh['gy'=4,'gx'=8] {'gy','gx'}, dimensions={0} | all-to-all | bytes 786432 | tf_op jit(solution)/shard_map/all_to_all | solution.py:876
  248.5 2.6 all-to-all-start.5
  251.1 6.6 %input_gradient.2.rest_0_ = bf16[62,64,1792]{2,1,0:T(8,128)(2,1)} custom-call(bf16[32,64,1024]{2,1,0:T(8,128)(2,1)} %get-tuple-element.67.ds, s16[5,64,1792]{2,1,0:T(8,128)(2,1)} %get-tuple-element.44.bits_ref, bf16[768,256]{1,0:T(8,128)(2,1)} %get-tuple-element.68.w_ref), custom_call_target="tpu_custom_call" | custom-call | bytes 25200000 | tf_op jit(solution)/shard_map/input_gradient/pallas_call | solution.py:785
  257.7 6.6 %input_gradient.3 = bf16[62,64,1792]{2,1,0:T(8,128)(2,1)} custom-call(bf16[32,64,1024]{2,1,0:T(8,128)(2,1)} %get-tuple-element.67.ds, s16[5,64,1792]{2,1,0:T(8,128)(2,1)} %get-tuple-element.44.bits_ref, bf16[768,256]{1,0:T(8,128)(2,1)} %get-tuple-element.68.w_ref, bf16[62,64,1792]{2,1,0:T(8,128)(2,1)} %input_gradient.2.rest_0_), custom_call_target="tpu_custom_call", output_to_operand_aliasing={{}: (3, {})} | custom-call | bytes 25200000 | tf_op jit(solution)/shard_map/input_gradient/pallas_call | solution.py:785
  265.4 2.8 %update.1 = (f32[1,1]{1,0:T(1,128)}, f32[2,64,576]{2,1,0:T(8,128)}, f32[2,64,576]{2,1,0:T(8,128)}, f32[2,64,576]{2,1,0:T(8,128)}, bf16[2,64,576]{2,1,0:T(8,128)(...) custom-call(f32[768,128]{1,0:T(8,128)} %bitcast.56, f32[32,256]{1,0:T(8,128)} %bitcast.70, ...), custom_call_target="tpu_custom_call" | custom-call | bytes 10800000 | tf_op jit(solution)/shard_map/update/pallas_call | solution.py:857
  (52 shorter events, 18.2 us)
Async XLA Ops:
  7.4 3.6 %collective-permute-start = (bf16[64,2688]{1,0:T(8,128)(2,1)S(1)}, bf16[64,2688]{1,0:T(8,128)(2,1)S(1)}, u32[]{:S(2)}, u32[]{:S(2)}) collective-permute-start(bf16[64,2688]{1,0:T(8,128)(2,1)S(1)} %pad_maximum_fusion.3), channel_id=1, source_target_pairs={{0,8},{8,16},{16,24},{1,9},{9,17},{17,25},{2,10},{10,18},{18,26},{... | collective-permute-start | bytes 1032200 | tf_op jit(solution)/shard_map/ppermute | solution.py:872
  12.1 13.3 %collective-permute-start.1 = (bf16[32,64,128]{2,1,0:T(8,128)(2,1)S(1)}, bf16[32,64,128]{2,1,0:T(8,128)(2,1)S(1)}, u32[]{:S(2)}, u32[]{:S(2)}) collective-permute-start(bf16[32,64,128]{2,1,0:T(8,128)(2,1)S(1)} %pad_maximum_fusion.2), channel_id=1, source_target_pairs={{0,1},{1,2},{2,3},{3,4},{4,5},{5,6},{6,7},{8,9},{9,10},{10,11},{11... | collective-permute-start | bytes 1572872 | tf_op jit(solution)/shard_map/ppermute | solution.py:872
  17.4 7.3 %collective-permute-start.6 = (bf16[2,64,896]{2,1,0:T(8,128)(2,1)S(1)}, bf16[2,64,896]{2,1,0:T(8,128)(2,1)S(1)}, u32[]{:S(2)}, u32[]{:S(2)}) collective-permute-start(bf16[2,64,896]{2,1,0:T(8,128)(2,1)S(1)} %slice.89), channel_id=1, source_target_pairs={{8,0},{16,8},{24,16},{9,1},{17,9},{25,17},{10,2},{18,10},{26,18},{... | collective-permute-start | bytes 688136 | tf_op jit(solution)/shard_map/ppermute | solution.py:872
  24.7 21.3 %copy-start.6 = (bf16[2,64,896]{2,1,0:T(8,128)(2,1)}, bf16[2,64,896]{2,1,0:T(8,128)(2,1)S(1)}, u32[]{:S(2)}) copy-start(bf16[2,64,896]{2,1,0:T(8,128)(2,1)S(1)} %collective-permute-done.6.down_ref) | copy-start | bytes 688132
  25.5 0.8 copy-start.5
  46.0 8.7 %collective-permute-start.2 = (bf16[2,64,896]{2,1,0:T(8,128)(2,1)}, bf16[2,64,896]{2,1,0:T(8,128)(2,1)S(1)}, u32[]{:S(2)}, u32[]{:S(2)}) collective-permute-start(bf16[2,64,896]{2,1,0:T(8,128)(2,1)} %get-tuple-element.49), channel_id=1, source_target_pairs={{0,8},{8,16},{16,24},{1,9},{9,17},{17,25},{2,10},{10,18},{18,26},{... | collective-permute-start | bytes 688136 | tf_op jit(solution)/shard_map/ppermute | solution.py:872
  53.4 3.8 %collective-permute-start.3 = (bf16[3,64,896]{2,1,0:T(8,128)(2,1)}, bf16[3,64,896]{2,1,0:T(8,128)(2,1)S(1)}, u32[]{:S(2)}, u32[]{:S(2)}) collective-permute-start(bf16[3,64,896]{2,1,0:T(8,128)(2,1)} %get-tuple-element.50), channel_id=1, source_target_pairs={{8,0},{16,8},{24,16},{9,1},{17,9},{25,17},{10,2},{18,10},{26,18},{... | collective-permute-start | bytes 1032200 | tf_op jit(solution)/shard_map/ppermute | solution.py:872
  54.7 80.0 %copy-start.1 = (bf16[1,64,896]{2,1,0:T(8,128)(2,1)}, bf16[1,64,896]{2,1,0:T(8,128)(2,1)S(1)}, u32[]{:S(2)}) copy-start(bf16[1,64,896]{2,1,0:T(8,128)(2,1)S(1)} %slice_bitcast_fusion.up_ref) | copy-start | bytes 344068
  54.8 42.0 %copy-start.7 = (bf16[2,64,896]{2,1,0:T(8,128)(2,1)}, bf16[2,64,896]{2,1,0:T(8,128)(2,1)S(1)}, u32[]{:S(2)}) copy-start(bf16[2,64,896]{2,1,0:T(8,128)(2,1)S(1)} %collective-permute-done.2.up_ref) | copy-start | bytes 688132
  57.2 39.6 %copy-start.4 = (bf16[3,64,896]{2,1,0:T(8,128)(2,1)}, bf16[3,64,896]{2,1,0:T(8,128)(2,1)S(1)}, u32[]{:S(2)}) copy-start(bf16[3,64,896]{2,1,0:T(8,128)(2,1)S(1)} %collective-permute-done.3.down_ref) | copy-start | bytes 1032196
  58.4 38.3 %collective-permute-start.4 = (bf16[36,64,128]{2,1,0:T(8,128)(2,1)S(1)}, bf16[36,64,128]{2,1,0:T(8,128)(2,1)S(1)}, u32[]{:S(2)}, u32[]{:S(2)}) collective-permute-start(bf16[36,64,128]{2,1,0:T(8,128)(2,1)S(1)} %pad_maximum_fusion), channel_id=1, source_target_pairs={{0,1},{1,2},{2,3},{3,4},{4,5},{5,6},{6,7},{8,9},{9,10},{10,11},{11... | collective-permute-start | bytes 1769480 | tf_op jit(solution)/shard_map/ppermute | solution.py:872
  63.0 33.7 %collective-permute-start.5 = (bf16[36,64,128]{2,1,0:T(8,128)(2,1)S(1)}, bf16[36,64,128]{2,1,0:T(8,128)(2,1)S(1)}, u32[]{:S(2)}, u32[]{:S(2)}) collective-permute-start(bf16[36,64,128]{2,1,0:T(8,128)(2,1)S(1)} %pad_maximum_fusion.1), channel_id=1, source_target_pairs={{1,0},{2,1},{3,2},{4,3},{5,4},{6,5},{7,6},{9,8},{10,9},{11,10},{12... | collective-permute-start | bytes 1769480 | tf_op jit(solution)/shard_map/ppermute | solution.py:872
  65.3 69.5 %collective-permute-start.8 = (bf16[17,64,128]{2,1,0:T(8,128)(2,1)}, bf16[17,64,128]{2,1,0:T(8,128)(2,1)S(1)}, u32[]{:S(2)}, u32[]{:S(2)}) collective-permute-start(bf16[17,64,128]{2,1,0:T(8,128)(2,1)} %fusion), channel_id=1, source_target_pairs={{1,0},{2,1},{3,2},{4,3},{5,4},{6,5},{7,6},{9,8},{10,9},{11,10},{12... | collective-permute-start | bytes 835592 | tf_op jit(solution)/shard_map/ppermute | solution.py:872
  67.4 67.3 %collective-permute-start.7 = (bf16[17,64,128]{2,1,0:T(8,128)(2,1)}, bf16[17,64,128]{2,1,0:T(8,128)(2,1)}, u32[]{:S(2)}, u32[]{:S(2)}) collective-permute-start(bf16[17,64,128]{2,1,0:T(8,128)(2,1)} %fusion.1), channel_id=1, source_target_pairs={{0,1},{1,2},{2,3},{3,4},{4,5},{5,6},{6,7},{8,9},{9,10},{10,11},{11... | collective-permute-start | bytes 835592 | tf_op jit(solution)/shard_map/ppermute | solution.py:872
  74.8 21.3 %all-to-all-start = ((f32[32,1,256]{2,1,0:T(1,128)}), f32[32,1,256]{2,1,0:T(1,128)S(1)}, u32[]{:S(2)}, u32[]{:S(2)}) async-start(f32[32,1,256]{2,1,0:T(1,128)} %copy.20), calls=%async_computation | async-start | bytes 65536 | tf_op jit(solution)/shard_map/all_to_all | solution.py:876
  96.8 0.8 copy-start.2
  96.8 1.0 copy-start.3
  134.8 0.7 copy-start.8
  190.1 12.9 %collective-permute-start.9 = (bf16[16,64,128]{2,1,0:T(8,128)(2,1)}, bf16[16,64,128]{2,1,0:T(8,128)(2,1)S(1)}, u32[]{:S(2)}, u32[]{:S(2)}) collective-permute-start(bf16[16,64,128]{2,1,0:T(8,128)(2,1)} %get-tuple-element.64), channel_id=1, source_target_pairs={{1,0},{2,1},{3,2},{4,3},{5,4},{6,5},{7,6},{9,8},{10,9},{11,10},{12... | collective-permute-start | bytes 786440 | tf_op jit(solution)/shard_map/ppermute | solution.py:872
  203.0 0.7 copy-start.9
  248.5 16.1 %all-to-all-start.5 = ((f32[32,24,128]{2,1,0:T(8,128)}), f32[32,24,128]{2,1,0:T(8,128)S(1)}, u32[]{:S(2)}, u32[]{:S(2)}) async-start(f32[32,24,128]{2,1,0:T(8,128)} %broadcast_in_dim.14), calls=%async_computation.5 | async-start | bytes 786432 | tf_op jit(solution)/shard_map/all_to_all | solution.py:876
  264.7 0.7 copy-start

commit v2 on v1

v2 whole, which is shorter than its diff:
```python
import functools
import math

import jax
import jax.numpy as jnp
from jax import lax
from jax.experimental import pallas as pl
from jax.experimental.pallas import tpu as pltpu
from jax.sharding import PartitionSpec as P

norm_eps = 1e-05
adam_beta = 0.5
adam_eps = 1e-08
step_count = 5
clip_limit = 1.0
kernel_rate = 0.04
norm_rate = 0.25
kernel_decay = 0.01

f32, bf16 = (jnp.float32, jnp.bfloat16)
BOTH = ("gy", "gx")
S, C, L, BITS = (16, 64, 128, 13)


def params_of(limit=56):
    return pltpu.CompilerParams(
        dimension_semantics=("arbitrary",), vmem_limit_bytes=limit << 20
    )


def cost(microseconds):
    return pl.CostEstimate(
        flops=0, bytes_accessed=int(microseconds * 3.6e6), transcendentals=0
    )


def whole(shape):
    return pl.BlockSpec(shape, lambda g: (0,) * len(shape))


def scans(rows, lanes):
    return pl.BlockSpec((rows, S, lanes), lambda g: (0, g, 0))


def low_half(rows=S):
    return lax.broadcasted_iota(jnp.int32, (rows, L), 1) < C


def swap(x):
    return pltpu.roll(x, C, 1)


def fold(x):
    x = jnp.broadcast_to(x, (8, L))
    return (x + swap(x))[:1]


def live(word, row, x):
    bit = 1 << (row % BITS)
    if x.dtype == bf16:
        return jnp.where((word & jnp.int16(bit)) != 0, x, jnp.zeros_like(x))
    return jnp.where((word.astype(jnp.int32) & bit) != 0, x, 0.0)


def pair(ref, row, t):
    return ref[row, :, t * L : (t + 1) * L]


def stats_of(st_ref, count):
    groups = 2 * st_ref.shape[0]
    means = st_ref[:, 0, :]
    mean = fold(jnp.sum(means, axis=0, keepdims=True)) / groups
    spread = st_ref[:, 1, :] + count * (means - mean) ** 2
    spread = fold(jnp.sum(spread, axis=0, keepdims=True)) / (groups * count)
    return (mean, lax.rsqrt(spread + norm_eps))


def sums_of(st_ref):
    return tuple(fold(jnp.sum(st_ref[:, k, :], axis=0, keepdims=True)) for k in range(2))


def pilot_of(block):
    flat = block.reshape(-1, L)
    return jnp.sum(flat, axis=0, keepdims=True) / flat.shape[0]


def finish_stats(step, steps, pilot, sums, count, run_ref, st_ref):
    off, squares = (jnp.sum(s, axis=0, keepdims=True) for s in sums)
    mean = pilot + off / count
    squares = squares - off * off / count

    @pl.when(step == 0)
    def _():
        run_ref[0:1] = mean
        run_ref[1:2] = squares

    @pl.when(step > 0)
    def _():
        before = step.astype(f32)
        share = 1.0 / (before + 1.0)
        delta = mean - run_ref[0:1]
        run_ref[0:1] = run_ref[0:1] + delta * share
        run_ref[1:2] = run_ref[1:2] + squares + delta * delta * (count * before * share)

    @pl.when(step == steps - 1)
    def _():
        st_ref[...] = jnp.broadcast_to(run_ref[0:2][None], st_ref.shape)


def off_sums(blocks, pilot):
    sums = [jnp.zeros((8, L), f32), jnp.zeros((8, L), f32)]
    for block in blocks:
        d = block - pilot
        sums = [sums[0] + halves(d), sums[1] + halves(d * d)]
    return sums


def added(a, b):
    return b if a is None else [x + y for x, y in zip(a, b)]


def rim_of(first, second, row, low):
    half = first.shape[0]
    if row < half:
        return jnp.where(low, first[row].astype(f32), second[row].astype(f32))
    row = row - half
    return swap(jnp.where(low, second[row].astype(f32), first[row].astype(f32)))


def halves(x):
    return x[:8] + x[8:]


def occupancy_words(occ, groups, first):
    rows = occ.shape[1]
    shape = (rows, groups * L)
    group_of = lax.broadcasted_iota(jnp.int32, shape, 1) // L + first
    inner = lax.broadcasted_iota(jnp.int32, shape, 0) - group_of * BITS
    power = jnp.where(
        (inner >= 0) & (inner < BITS), (1 << jnp.clip(inner, 0, BITS)), 0
    ).astype(bf16)
    low = occ.astype(f32).astype(bf16)
    return jnp.dot(low, power, preferred_element_type=f32).astype(jnp.int32)


def edges_kernel(
    row_ref, col_ref, occ_ref, cot_last_ref, cot_first_ref, down_ref, up_ref, corner_ref, xcol_ref
):
    cols, scan_count, rows = occ_ref.shape
    lanes = row_ref.shape[2]
    groups = -(-rows // BITS)
    low = low_half(scan_count)
    words = occupancy_words(occ_ref[...].reshape(cols * scan_count, rows), 1, groups - 1)
    words = words.reshape(cols // 2, 2, scan_count, L)
    for t in range(cols // 2):
        word = jnp.where(low, words[t, 0], words[t, 1])
        x = live(word, rows - 1, row_ref[0, :, t * L : (t + 1) * L].astype(f32)).astype(bf16)
        down_ref[:, t * L : (t + 1) * L] = x
    corner_ref[...] = x
    down_ref[:, lanes:] = cot_last_ref[0]
    up_ref[...] = cot_first_ref[...]
    words = occupancy_words(occ_ref[cols - 1], groups, 0)
    for i in range(rows // 2):
        even, odd = (
            live(
                words[:, row // BITS * L : (row // BITS + 1) * L], row, col_ref[row].astype(f32)
            )
            for row in (2 * i, 2 * i + 1)
        )
        xcol_ref[i] = jnp.where(low, swap(even), odd).astype(bf16)


def edges(x, occ, cot):
    rows, scan_count, lanes = x.shape
    r, wide = (rows // 2, lanes // 2)
    outs = [
        jax.ShapeDtypeStruct((scan_count, lanes + wide), bf16),
        jax.ShapeDtypeStruct((2, scan_count, wide), bf16),
        jax.ShapeDtypeStruct((scan_count, L), bf16),
        jax.ShapeDtypeStruct((r, scan_count, L), bf16),
    ]
    return pl.pallas_call(
        edges_kernel,
        grid=(1,),
        in_specs=[
            pl.BlockSpec((1, scan_count, lanes), lambda g: (rows - 1, 0, 0)),
            pl.BlockSpec((rows, scan_count, L), lambda g: (0, 0, lanes // L - 1)),
            whole(occ.shape),
            pl.BlockSpec((1, scan_count, wide), lambda g: (r - 1, 0, 0)),
            pl.BlockSpec((2, scan_count, wide), lambda g: (0, 0, 0)),
        ],
        out_specs=[whole(o.shape) for o in outs],
        out_shape=outs,
        compiler_params=params_of(),
        cost_estimate=cost(3),
        name="edges",
    )(x, x, occ, cot, cot)


def prep_kernel(occ_ref, kt_ref, np_ref, bits_ref, w1_ref, w2_ref, w2b_ref, w1b_ref, np2_ref):
    cols, scan_count, rows = occ_ref.shape
    groups = bits_ref.shape[0]
    words = occupancy_words(occ_ref[...].reshape(cols * scan_count, rows), groups, 0)
    words = words.reshape(cols // 2, 2, scan_count, groups * L)
    low = low_half(scan_count)
    for g in range(groups):
        for t in range(cols // 2):
            lanes = slice(g * L, (g + 1) * L)
            word = jnp.where(low, words[t, 0, :, lanes], words[t, 1, :, lanes])
            bits_ref[g, :, t * L : (t + 1) * L] = word.astype(jnp.int16)
    back = [[kt_ref[l, :, k * C : (k + 1) * C] for k in range(9)] for l in range(2)]
    fore = [[jnp.transpose(b) for b in layer] for layer in back]
    none = jnp.zeros((C, C), f32)

    def put(ref, rows_of, cols_of, pick):
        for a in range(rows_of):
            blocks = [pick(a, b) for b in range(cols_of)]
            for k in range(0, cols_of, 2):
                two = jnp.concatenate(blocks[k : k + 2], axis=1).astype(bf16)
                ref[a * C : (a + 1) * C, k * C : (k + 2) * C] = two

    def tap(table, p, q):
        return table[3 * p + q] if 0 <= p < 3 and 0 <= q < 3 else none

    put(w1_ref, 30, 4, lambda a, b: tap(fore[0], a // 6 - 2 * (b // 2), a % 6 - 2 * (b % 2) - 1))
    put(w2_ref, 16, 4, lambda a, b: tap(fore[1], a // 4 - b // 2, a % 4 - b % 2))
    put(w2b_ref, 16, 4, lambda a, b: tap(back[1], b // 2 + 2 - a // 4, b % 2 + 2 - a % 4))
    put(w1b_ref, 12, 4, lambda a, b: tap(back[0], (1, 2, 0)[a // 4], b + 3 - 2 * (a % 4)))
    np2_ref[...] = jnp.concatenate([np_ref[...], np_ref[...]], axis=1)


def prepare(occ, kt, norm_params):
    cols, scan_count, rows = occ.shape
    full = lambda *shape: jax.ShapeDtypeStruct(shape, bf16)
    outs = [
        jax.ShapeDtypeStruct((-(-rows // BITS), scan_count, cols * C), jnp.int16),
        full(30 * C, 4 * C),
        full(16 * C, 4 * C),
        full(16 * C, 4 * C),
        full(12 * C, 4 * C),
        jax.ShapeDtypeStruct((4, L), f32),
    ]
    return pl.pallas_call(
        prep_kernel,
        grid=(1,),
        in_specs=[whole(occ.shape), whole(kt.shape), whole((4, C))],
        out_specs=[whole(o.shape) for o in outs],
        out_shape=outs,
        compiler_params=params_of(),
        cost_estimate=cost(4),
        name="prepare",
    )(occ, kt, norm_params.reshape(4, C))


def mask_tile(x_ref, bits_ref, t, xs, into):
    rows = x_ref.shape[0]
    for g in range(bits_ref.shape[0]):
        word = bits_ref[g, :, t * L : (t + 1) * L]
        for row in range(g * BITS, min(rows, (g + 1) * BITS)):
            x = live(word, row, pair(x_ref, row, t))
            xs[(row + 1) // 4, (row + 1) % 4, :, into * L : (into + 1) * L] = x


def clear_rows(rows, pairs, xs):
    for k in range(rows + 1, 4 * pairs + 1):
        xs[k // 4, k % 4] = jnp.zeros_like(xs[0, 0])


def conv_rows(xs, lanes, w, r):
    pairs = (r + 1) // 2
    pieces = [xs[0:pairs, q, :, lanes] for q in range(4)] + [xs[1 : pairs + 1, 0, :, lanes]]
    lhs = jnp.concatenate([p.reshape(pairs * S, p.shape[2]) for p in pieces], axis=1)
    acc = jnp.dot(lhs, w, preferred_element_type=f32).reshape(pairs, S, 2 * L)
    return [acc[i // 2, :, (i % 2) * L : (i % 2 + 1) * L] for i in range(r)]


def first_last_kernel(
    xa_ref, xb_ref, ba_ref, bb_ref, xrow_ref, xcol_ref, corner_ref, w_ref, c_ref, st_ref, er_ref,
    el_ref, edge_ref, xs, run,
):
    step, steps = (pl.program_id(0), pl.num_programs(0))
    rows, lanes = (xa_ref.shape[0], xrow_ref.shape[1] * 2 // 3)
    r = rows // 2
    low = low_half()

    @pl.when(step == 0)
    def _():
        clear_rows(rows, (r + 1) // 2, xs)

    xs[0, 0, :, L : 2 * L] = xrow_ref[:, :L]
    xs[0, 0, :, 2 * L :] = xrow_ref[:, lanes - 2 * L : lanes]
    xs[0, 0, :, :L] = corner_ref[...]
    for i in range(r):
        k = 2 * i + 2
        xs[k // 4, k % 4, :, :L] = xcol_ref[i]
        k = 2 * i + 1
        xs[k // 4, k % 4, :, :L] = swap(xcol_ref[i].astype(f32)).astype(bf16)
    mask_tile(xa_ref, ba_ref, 0, xs, 1)
    mask_tile(xb_ref, bb_ref, 0, xs, 2)
    mask_tile(xb_ref, bb_ref, 1, xs, 3)
    wide = 3 * L
    some = lambda a: jnp.concatenate(
        [w_ref[q * wide + a * L : q * wide + (a + 2) * L] for q in range(5)], axis=0
    )
    last = conv_rows(xs, slice(2 * L, 4 * L), some(0), r)
    first = conv_rows(xs, slice(0, 2 * L), some(1), r)
    edge = [jnp.where(low, b, a) for a, b in zip(first, last)]
    pilot = pilot_of(jnp.concatenate(edge[: r // 2], axis=0))
    for i in range(r):
        c_ref[i, :, :L] = first[i]
        c_ref[i, :, L:] = last[i]
        edge_ref[i] = edge[i].astype(bf16)
    finish_stats(step, steps, pilot, off_sums(edge, pilot), float(r * S), run, st_ref)
    half = er_ref.shape[0]
    for k in range(half):
        far = swap(edge[k + half]) if k + half < r else jnp.zeros((S, L), f32)
        er_ref[k] = jnp.where(low, edge[k], far).astype(bf16)
        el_ref[k] = jnp.where(low, far, edge[k]).astype(bf16)


def first_last(x, bits, down, xcol, corner, w):
    rows, scan_count, lanes = x.shape
    r = rows // 2
    shape = lambda dtype, *s: jax.ShapeDtypeStruct(s, dtype)
    at = lambda n, width, k: pl.BlockSpec((n, S, width), lambda g: (0, g, k))
    end = lanes // (2 * L) - 1
    return pl.pallas_call(
        first_last_kernel,
        grid=(scan_count // S,),
        in_specs=[
            at(rows, L, 0),
            at(rows, 2 * L, end),
            at(bits.shape[0], L, 0),
            at(bits.shape[0], 2 * L, end),
            pl.BlockSpec((S, down.shape[1]), lambda g: (g, 0)),
            scans(r, L),
            pl.BlockSpec((S, L), lambda g: (g, 0)),
            whole(w.shape),
        ],
        out_specs=[
            scans(r, 2 * L),
            whole((1, 2, L)),
            scans((r + 1) // 2, L),
            scans((r + 1) // 2, L),
            scans(r, L),
        ],
        out_shape=[
            shape(f32, r, scan_count, 2 * L),
            shape(f32, 1, 2, L),
            shape(bf16, (r + 1) // 2, scan_count, L),
            shape(bf16, (r + 1) // 2, scan_count, L),
            shape(bf16, r, scan_count, L),
        ],
        scratch_shapes=[
            pltpu.VMEM(((r + 1) // 2 + 1, 4, S, 4 * L), bf16),
            pltpu.VMEM((8, L), f32),
        ],
        compiler_params=params_of(),
        cost_estimate=cost(5),
        name="conv_one_ends",
    )(x, x, bits, bits, down, xcol, corner, w)


def conv_one_kernel(
    x_ref, bits_ref, xrow_ref, ends_ref, w_ref, c_ref, st_ref, up_ref, down_ref, xs, run
):
    step, steps = (pl.program_id(0), pl.num_programs(0))
    rows, tiles = (x_ref.shape[0], x_ref.shape[2] // L)
    r, inner = (rows // 2, tiles // 2 - 1)

    @pl.when(step == 0)
    def _():
        clear_rows(rows, (r + 1) // 2, xs)

    xs[0, 0] = xrow_ref[:, : tiles * L]
    sums, pilot = (None, None)
    filled = 0
    for t in range(inner):
        while filled < 2 * t + 3:
            mask_tile(x_ref, bits_ref, filled, xs, filled)
            filled += 1
        blocks = conv_rows(xs, slice(2 * t * L, (2 * t + 3) * L), w_ref[...], r)
        if pilot is None:
            pilot = pilot_of(jnp.concatenate(blocks[: r // 2], axis=0))
        sums = added(sums, off_sums(blocks, pilot))
        for i, block in enumerate(blocks):
            c_ref[i, :, t * L : (t + 1) * L] = block
    finish_stats(step, steps, pilot, sums, float(r * inner * S), run, st_ref)
    up_ref[...] = c_ref[0:3].astype(bf16)
    down_ref[...] = c_ref[r - 2 : r].astype(bf16)

    @pl.when(step == steps - 1)
    def _():
        own, more = (float(r * S) * steps * n for n in (inner, 1))
        delta = ends_ref[0, 0:1] - run[0:1]
        mean = run[0:1] + delta * (more / (own + more))
        squares = run[1:2] + ends_ref[0, 1:2] + delta * delta * (own * more / (own + more))
        row = jnp.concatenate([mean, squares], axis=0)
        st_ref[...] = jnp.broadcast_to(row[None], st_ref.shape)


def conv_one(x, bits, down, ends, w, devices):
    rows, scan_count, lanes = x.shape
    r, wide = (rows // 2, lanes // 2 - L)
    shape = lambda dtype, *s: jax.ShapeDtypeStruct(s, dtype)
    return pl.pallas_call(
        conv_one_kernel,
        grid=(scan_count // S,),
        in_specs=[
            scans(rows, lanes),
            scans(bits.shape[0], lanes),
            pl.BlockSpec((S, down.shape[1]), lambda g: (g, 0)),
            whole(ends.shape),
            whole(w.shape),
        ],
        out_specs=[
            scans(r, wide),
            whole((devices, 2, L)),
            scans(3, wide),
            scans(2, wide),
        ],
        out_shape=[
            shape(f32, r, scan_count, wide),
            shape(f32, devices, 2, L),
            shape(bf16, 3, scan_count, wide),
            shape(bf16, 2, scan_count, wide),
        ],
        scratch_shapes=[
            pltpu.VMEM(((r + 1) // 2 + 1, 4, S, lanes), bf16),
            pltpu.VMEM((8, L), f32),
        ],
        compiler_params=params_of(),
        cost_estimate=cost(13),
        name="conv_one",
    )(x, bits, down, ends, w)


def conv_two_kernel(
    flags, c_ref, ends_ref, up_ref, down_ref, left_ref, right_ref, st_ref, np_ref, w_ref, c2_ref,
    n1_ref, hid_ref, st2_ref, hs, rim, run, *, count,
):
    step, steps = (pl.program_id(0), pl.num_programs(0))
    r, tiles = (c_ref.shape[0], c_ref.shape[2] // L + 2)
    t_out = tiles - 1
    mean, inv = stats_of(st_ref, count)
    offset = -mean * inv
    scale = 0.5 * np_ref[0:1] * inv
    shift = 0.5 * (np_ref[0:1] * offset + np_ref[1:2])
    f_up, f_down, f_left, f_right = (flags[k].astype(f32) for k in range(4))
    low = low_half()
    left = jnp.where(low, f_left, 1.0)
    right = jnp.where(low, 1.0, f_right)
    for row in range(r):
        rim[row] = rim_of(left_ref, right_ref, row, low)

    def act(row, t):
        ends = (0, tiles - 1)
        if 2 <= row < r + 2:
            flag = None
            c = pair(ends_ref, row - 2, min(t, 1)) if t in ends else pair(c_ref, row - 2, t - 1)
            beyond = rim[row - 2] if t in ends else None
        else:
            src, k, flag = (up_ref, row, f_up) if row < 2 else (down_ref, row - r - 2, f_down)
            c = pair(src, k, tiles - 2 if t in ends else t - 1).astype(f32)
            beyond = pair(src, k, tiles - 1).astype(f32) if t in ends else None
        if t == 0:
            c = jnp.where(low, beyond, c)
        if t == tiles - 1:
            c = jnp.where(low, c, beyond)
        h = c * scale + shift
        out = h + h * jnp.tanh(h)
        if t == 0:
            out = out * left
        if t == tiles - 1:
            out = out * right
        if flag is not None:
            out = out * flag
        out = out.astype(bf16)
        hs[row // 2, row % 2, :, t * L : (t + 1) * L] = out
        if 1 <= row < r + 3:
            hid_ref[row - 1, :, t * L : (t + 1) * L] = out
        if 2 <= row < r + 3:
            n1_ref[row - 2, :, t * L : (t + 1) * L] = (c * inv + offset).astype(bf16)

    pairs = (r + 3) // 2
    sums, pilot = (None, None)
    for t in range(tiles):
        for row in range(r + 5):
            act(row, t)
        k = t - 1
        if k < 0:
            continue
        lanes = slice(k * L, (k + 2) * L)
        pieces = [hs[a : a + pairs, b, :, lanes] for a in range(2) for b in range(2)]
        lhs = jnp.concatenate([p.reshape(pairs * S, 2 * L) for p in pieces], axis=1)
        acc = jnp.dot(lhs, w_ref[...], preferred_element_type=f32).reshape(pairs, S, 2 * L)
        if pilot is None:
            pilot = pilot_of(acc[1 : r // 2, :, :L])
        blocks = []
        for row in range(r + 3):
            block = acc[row // 2, :, (row % 2) * L : (row % 2 + 1) * L]
            c2_ref[row, :, k * L : (k + 1) * L] = block
            if 0 < row <= r:
                blocks.append(block)
        sums = added(sums, off_sums(blocks, pilot))
    finish_stats(step, steps, pilot, sums, float(r * t_out * S), run, st2_ref)


def conv_two(flags, c1, ends, up, down, left, right, st, np2, w, count):
    r, scan_count, wide = c1.shape
    wide = wide + 2 * L
    lanes = wide - L
    devices = st.shape[0]
    return pl.pallas_call(
        functools.partial(conv_two_kernel, count=count),
        grid=(scan_count // S,),
        in_specs=[
            pl.BlockSpec(memory_space=pltpu.SMEM),
            scans(r, wide - 2 * L),
            scans(r, 2 * L),
            scans(2, wide),
            scans(3, wide),
            scans(left.shape[0], L),
            scans(right.shape[0], L),
            whole(st.shape),
            whole(np2.shape),
            whole(w.shape),
        ],
        out_specs=[
            scans(r + 3, lanes),
            scans(r + 1, wide),
            scans(r + 2, wide),
            whole((devices, 2, L)),
        ],
        out_shape=[
            jax.ShapeDtypeStruct((r + 3, scan_count, lanes), f32),
            jax.ShapeDtypeStruct((r + 1, scan_count, wide), bf16),
            jax.ShapeDtypeStruct((r + 2, scan_count, wide), bf16),
            jax.ShapeDtypeStruct((devices, 2, L), f32),
        ],
        scratch_shapes=[
            pltpu.VMEM(((r + 5) // 2, 2, S, wide), bf16),
            pltpu.VMEM((r, S, L), f32),
            pltpu.VMEM((8, L), f32),
        ],
        compiler_params=params_of(),
        cost_estimate=cost(14),
        name="conv_two",
    )(flags, c1, ends, up, down, left, right, st, np2, w)


def output_kernel(
    c2_ref, st_ref, np_ref, cot_ref, up_ref, down_ref, feat_ref, d_ref, sum_ref, run, *, count,
):
    step, steps = (pl.program_id(0), pl.num_programs(0))
    r, tiles = (cot_ref.shape[0], cot_ref.shape[2] // L)
    mean, inv = stats_of(st_ref, count)
    offset = -mean * inv
    scale = 0.5 * np_ref[2:3] * inv
    shift = 0.5 * (np_ref[2:3] * offset + np_ref[3:4])
    above = 2 * tiles

    def slope(c, cot):
        h = c * scale + shift
        t = jnp.tanh(h)
        plus = 1.0 + t
        return (h * plus, (0.5 * cot.astype(f32)) * (plus * (1.0 + h * (1.0 - t))))

    def own(i, sums):
        for t in range(tiles):
            c = pair(c2_ref, i + 1, t)
            f, d = slope(c, pair(cot_ref, i, t))
            feat_ref[i, :, t * L : (t + 1) * L] = f.astype(bf16)
            d_ref[i + 1, :, t * L : (t + 1) * L] = d
            sums = (sums[0] + halves(d), sums[1] + halves(d * (c * inv + offset)))
        return sums

    zero = jnp.zeros((8, L), f32)
    sums = lax.fori_loop(0, r, own, (zero, zero))
    for t in range(tiles):
        lanes = slice(t * L, (t + 1) * L)
        cot = up_ref[:, (above + t) * L : (above + t + 1) * L]
        d_ref[0, :, lanes] = slope(pair(c2_ref, 0, t), cot)[1]
        for k in range(2):
            row = r + 1 + k
            d_ref[row, :, lanes] = slope(pair(c2_ref, row, t), pair(down_ref, k, t))[1]
    add_sums(step, steps, sums, run, sum_ref)


def add_sums(step, steps, sums, run, sum_ref):
    rows = jnp.concatenate([jnp.sum(s, axis=0, keepdims=True) for s in sums], axis=0)

    @pl.when(step == 0)
    def _():
        run[0:2] = rows

    @pl.when(step > 0)
    def _():
        run[0:2] = run[0:2] + rows

    @pl.when(step == steps - 1)
    def _():
        sum_ref[...] = jnp.broadcast_to(run[0:2][None], sum_ref.shape)


def output(c2, st, np2, cot, up, down, count):
    r, scan_count, lanes = cot.shape
    devices = st.shape[0]
    return pl.pallas_call(
        functools.partial(output_kernel, count=count),
        grid=(scan_count // S,),
        in_specs=[
            scans(r + 3, lanes),
            whole(st.shape),
            whole(np2.shape),
            scans(r, lanes),
            pl.BlockSpec((S, up.shape[1]), lambda g: (g, 0)),
            scans(2, lanes),
        ],
        out_specs=[scans(r, lanes), scans(r + 3, lanes), whole((devices, 2, L))],
        out_shape=[
            jax.ShapeDtypeStruct((r, scan_count, lanes), bf16),
            jax.ShapeDtypeStruct((r + 3, scan_count, lanes), f32),
            jax.ShapeDtypeStruct((devices, 2, L), f32),
        ],
        scratch_shapes=[pltpu.VMEM((8, L), f32)],
        compiler_params=params_of(),
        cost_estimate=cost(12),
        name="output",
    )(c2, st, np2, cot, up, down)


def norm_back_two(flags, st_ref, sum_ref, np_ref, count, rows):
    cells = 2.0 * count * st_ref.shape[0]
    mean, inv = stats_of(st_ref, count)
    shift_sum, gain_sum = sums_of(sum_ref)
    gain = np_ref[2:3] * inv
    c_n = -gain * inv * gain_sum / cells
    c_0 = -gain * shift_sum / cells - c_n * mean
    f_up, f_down = (flags[k].astype(f32) for k in range(2))

    def back(row, d, c):
        d = d * gain + (c * c_n + c_0)
        if isinstance(row, int):
            if row == 0:
                d = d * f_up
            if row > rows:
                d = d * f_down
        return d

    return back


def rim_two_kernel(
    flags, da_ref, db_ref, ca_ref, cb_ref, st_ref, sum_ref, np_ref, er_ref, el_ref, *, count
):
    rows = da_ref.shape[0]
    back = norm_back_two(flags, st_ref, sum_ref, np_ref, count, rows - 3)
    low = low_half()
    half = rows // 2
    both = lambda row: jnp.where(
        low, back(row, da_ref[row], ca_ref[row]), back(row, db_ref[row], cb_ref[row])
    )
    for k in range(half):
        near, far = (both(k), swap(both(k + half)))
        el_ref[k] = jnp.where(low, near, far).astype(bf16)
        er_ref[k] = jnp.where(low, far, near).astype(bf16)


def rim_two(flags, d, c2, st, sums, np2, count):
    rows, scan_count, lanes = d.shape
    at = lambda k: pl.BlockSpec((rows, S, L), lambda g: (0, g, k))
    last = lanes // L - 1
    return pl.pallas_call(
        functools.partial(rim_two_kernel, count=count),
        grid=(scan_count // S,),
        in_specs=[
            pl.BlockSpec(memory_space=pltpu.SMEM), at(0), at(last), at(0), at(last),
            whole(st.shape), whole(sums.shape), whole(np2.shape),
        ],
        out_specs=[scans(rows // 2, L)] * 2,
        out_shape=[jax.ShapeDtypeStruct((rows // 2, scan_count, L), bf16)] * 2,
        compiler_params=params_of(),
        cost_estimate=cost(3),
        name="rim_two",
    )(flags, d, d, c2, c2, st, sums, np2)


def back_two_kernel(
    flags, d_ref, c2_ref, hid_ref, st_ref, sum_ref, np_ref, ds_ref, kg_ref, grad, *, count
):
    step, steps = (pl.program_id(0), pl.num_programs(0))
    r, tiles = (c2_ref.shape[0] - 3, c2_ref.shape[2] // L)
    back = norm_back_two(flags, st_ref, sum_ref, np_ref, count, r)

    @pl.when(step == 0)
    def _():
        grad[...] = jnp.zeros_like(grad)

    total = None
    for t in range(tiles):
        for row in range(r + 3):
            d = back(row, pair(d_ref, row, t), pair(c2_ref, row, t))
            ds_ref[row, :, t * L : (t + 1) * L] = d.astype(bf16)
        lanes = slice(t * L, (t + 2) * L)
        rhs = jnp.concatenate(
            [hid_ref[p : p + r, :, lanes].reshape(r * S, 2 * L) for p in range(3)], axis=1
        )
        lhs = ds_ref[1 : r + 1, :, t * L : (t + 1) * L].reshape(r * S, L)
        part = lax.dot_general(lhs, rhs, (((0,), (0,)), ((), ())), preferred_element_type=f32)
        total = part if total is None else total + part
    grad[...] += total

    @pl.when(step == steps - 1)
    def _():
        for p in range(3):
            for q in range(3):
                block = None
                for w in range(2):
                    at = 4 * p * C + (w + q) * C
                    part = grad[w * C : (w + 1) * C, at : at + C]
                    block = part if block is None else block + part
                kg_ref[3 * p + q] = block


def back_two(flags, d, c2, hid, st, sums, np2, count):
    r, scan_count, wide = hid.shape
    r, lanes = (r - 2, wide - L)
    return pl.pallas_call(
        functools.partial(back_two_kernel, count=count),
        grid=(scan_count // S,),
        in_specs=[
            pl.BlockSpec(memory_space=pltpu.SMEM),
            scans(r + 3, lanes),
            scans(r + 3, lanes),
            scans(r + 2, wide),
            whole(st.shape),
            whole(sums.shape),
            whole(np2.shape),
        ],
        out_specs=[scans(r + 3, lanes), whole((9, C, C))],
        out_shape=[
            jax.ShapeDtypeStruct((r + 3, scan_count, lanes), bf16),
            jax.ShapeDtypeStruct((9, C, C), f32),
        ],
        scratch_shapes=[pltpu.VMEM((L, 12 * C), f32)],
        compiler_params=params_of(),
        cost_estimate=cost(12),
        name="back_two",
    )(flags, d, c2, hid, st, sums, np2)


def hidden_kernel(
    ds_ref, left_ref, right_ref, n1_ref, np_ref, w_ref, dp_ref, edge_ref, sum1_ref, rim, run
):
    step, steps = (pl.program_id(0), pl.num_programs(0))
    r, tiles = (n1_ref.shape[0] - 1, n1_ref.shape[2] // L)
    pairs = (r + 1) // 2
    low = low_half()
    for row in range(r + 3):
        rim[row] = rim_of(right_ref, left_ref, row, low).astype(bf16)
    sums = None
    for t in range(tiles):
        parts = []
        for k in (t - 1, t):
            part = ds_ref[:, :, k * L : (k + 1) * L] if 0 <= k < tiles - 1 else rim[...]
            parts.append(part.reshape(pairs + 1, 2, S, L))
        pieces = [p[a : a + pairs, b] for a in range(2) for b in range(2) for p in parts]
        lhs = jnp.concatenate([p.reshape(pairs * S, L) for p in pieces], axis=1)
        acc = jnp.dot(lhs, w_ref[...], preferred_element_type=f32).reshape(pairs, S, 2 * L)
        part = [jnp.zeros((8, L), f32), jnp.zeros((8, L), f32)]
        for i in range(r + 1):
            n = pair(n1_ref, i, t).astype(f32)
            h = 0.5 * (n * np_ref[0:1] + np_ref[1:2])
            tan = jnp.tanh(h)
            d = acc[i // 2, :, (i % 2) * L : (i % 2 + 1) * L]
            d = (0.5 * d) * ((1.0 + tan) * (1.0 + h * (1.0 - tan)))
            dp_ref[i, :, t * L : (t + 1) * L] = d
            if i < r:
                if t == 0:
                    d = jnp.where(low, 0.0, d)
                if t == tiles - 1:
                    d = jnp.where(low, d, 0.0)
                part = [part[0] + halves(d), part[1] + halves(d * n)]
        sums = added(sums, part)
    add_sums(step, steps, sums, run, sum1_ref)
    for i in range(pairs):
        both = jnp.where(low, swap(pair(dp_ref, pairs + i, 0)), pair(dp_ref, i, 0))
        edge_ref[i] = both.astype(bf16)


def hidden_gradient(ds, left, right, n1, np2, w, devices):
    r, scan_count, wide = n1.shape
    r, lanes = (r - 1, wide - L)
    half = left.shape[0]
    return pl.pallas_call(
        hidden_kernel,
        grid=(scan_count // S,),
        in_specs=[
            scans(r + 3, lanes),
            scans(half, L),
            scans(half, L),
            scans(r + 1, wide),
            whole(np2.shape),
            whole(w.shape),
        ],
        out_specs=[
            scans(r + 1, wide),
            scans((r + 1) // 2, L),
            whole((devices, 2, L)),
        ],
        out_shape=[
            jax.ShapeDtypeStruct((r + 1, scan_count, wide), f32),
            jax.ShapeDtypeStruct(((r + 1) // 2, scan_count, L), bf16),
            jax.ShapeDtypeStruct((devices, 2, L), f32),
        ],
        scratch_shapes=[pltpu.VMEM((r + 3, S, L), bf16), pltpu.VMEM((8, L), f32)],
        compiler_params=params_of(),
        cost_estimate=cost(12),
        name="hidden_gradient",
    )(ds, left, right, n1, np2, w)


def back_one_kernel(
    flags, dp_ref, edge_ref, n1_ref, x_ref, bits_ref, st_ref, sum_ref, np_ref, kg2_ref, ds, kg_ref,
    xm, grad, *, count,
):
    step, steps = (pl.program_id(0), pl.num_programs(0))
    r, tiles = (n1_ref.shape[0] - 1, n1_ref.shape[2] // L - 1)
    cells = 2.0 * count * st_ref.shape[0]
    _mean, inv = stats_of(st_ref, count)
    shift_sum, gain_sum = sums_of(sum_ref)
    gain = np_ref[0:1] * inv
    c_n = -gain * gain_sum / cells
    c_0 = -gain * shift_sum / cells
    f_down, f_right = (flags[1].astype(f32), flags[3].astype(f32))
    packed = edge_ref.shape[0]
    low = low_half()
    right = jnp.where(low, 1.0, f_right)

    @pl.when(step == 0)
    def _():
        grad[...] = jnp.zeros_like(grad)

    def line(i, t):
        d = pair(dp_ref, i, t)
        if t == tiles:
            beyond = edge_ref[i % packed].astype(f32)
            d = jnp.where(low, d, swap(beyond) if i >= packed else beyond)
        d = d * gain + (pair(n1_ref, i, t).astype(f32) * c_n + c_0)
        if t == tiles:
            d = d * right
        if i == r:
            d = d * f_down
        ds[i, :, t * L : (t + 1) * L] = d.astype(bf16)

    turned = (((0,), (0,)), ((), ()))
    totals = [None, None, None]
    done = 0
    for t in range(tiles):
        while done < t + 2:
            for i in range(r + 1):
                line(i, done)
            done += 1
        for k in (2 * t, 2 * t + 1):
            for g in range(bits_ref.shape[0]):
                word = bits_ref[g, :, k * L : (k + 1) * L]
                for row in range(g * BITS, min(2 * r, (g + 1) * BITS)):
                    x = live(word, row, pair(x_ref, row, k))
                    xm[row % 2, row // 2, :, k * L : (k + 1) * L] = x
        lanes = slice(t * L, (t + 2) * L)
        xl = slice(2 * t * L, 2 * (t + 1) * L)
        rows = [ds[a : a + r, :, lanes].reshape(r * S, 2 * L) for a in range(2)]
        xe, xo = (xm[a, :, :, xl].reshape(r * S, 2 * L) for a in range(2))
        for k, (a, b) in enumerate(((xe, rows[0]), (xo, rows[0]), (xo, rows[1]))):
            part = lax.dot_general(a, b, turned, preferred_element_type=f32)
            totals[k] = part if totals[k] is None else totals[k] + part
    for k in range(3):
        grad[k] += totals[k]

    @pl.when(step == steps - 1)
    def _():
        blocks = []
        for p in range(3):
            g = (2, 0, 1)[p]
            for q in range(3):
                block = None
                for v in range(1, 4):
                    u = q - 3 + 2 * v
                    if 0 <= u < 4:
                        part = grad[g, u * C : (u + 1) * C, v * C : (v + 1) * C]
                        block = part if block is None else block + part
                blocks.append(jnp.transpose(block))
        blocks += [kg2_ref[8]] + [kg2_ref[k] for k in range(8)]
        for a in range(9):
            kg_ref[a * C : (a + 1) * C] = jnp.concatenate(blocks[2 * a : 2 * a + 2], axis=1)
        if kg_ref.shape[0] > 9 * C:
            kg_ref[9 * C :] = jnp.zeros((kg_ref.shape[0] - 9 * C, L), f32)


def back_one(flags, dp, edge, n1, x, bits, st, sums, np2, kg2, count):
    rows, scan_count, lanes = x.shape
    r, tiles = (rows // 2, lanes // L // 2)
    devices = st.shape[0]
    share = 8 * -(-9 * C // (8 * devices))
    wide = (tiles + 1) * L
    return pl.pallas_call(
        functools.partial(back_one_kernel, count=count),
        grid=(scan_count // S,),
        in_specs=[
            pl.BlockSpec(memory_space=pltpu.SMEM),
            scans(r + 1, wide),
            scans(edge.shape[0], L),
            scans(r + 1, wide),
            scans(rows, lanes),
            scans(bits.shape[0], lanes),
            whole(st.shape),
            whole(sums.shape),
            whole(np2.shape),
            whole(kg2.shape),
        ],
        out_specs=[scans(r + 1, wide), whole((devices * share, L))],
        out_shape=[
            jax.ShapeDtypeStruct((r + 1, scan_count, wide), bf16),
            jax.ShapeDtypeStruct((devices * share, L), f32),
        ],
        scratch_shapes=[
            pltpu.VMEM((2, r, S, lanes), bf16),
            pltpu.VMEM((3, 4 * C, 4 * C), f32),
        ],
        compiler_params=params_of(),
        cost_estimate=cost(16),
        name="back_one",
    )(flags, dp, edge, n1, x, bits, st, sums, np2, kg2)


def input_grad_kernel(ds, bits_ref, w_ref, *rest):
    ig_ref = rest[-1]
    r, tiles = (ds.shape[0] - 1, ds.shape[2] // L - 1)
    for t in range(tiles):
        lanes = slice(t * L, (t + 2) * L)
        rows = [ds[a : a + r, :, lanes].reshape(r * S, 2 * L) for a in range(2)]
        even = jnp.dot(rows[0], w_ref[: 4 * C], preferred_element_type=f32)
        odd = jnp.dot(
            jnp.concatenate(rows, axis=1), w_ref[4 * C :], preferred_element_type=f32
        )
        for k, block in enumerate((even, odd)):
            block = block.reshape(r, S, 2 * L)
            for h in range(2):
                xl = slice((2 * t + h) * L, (2 * t + h + 1) * L)
                for i in range(r):
                    row = 2 * i + k
                    d = block[i, :, h * L : (h + 1) * L].astype(bf16)
                    ig_ref[row, :, xl] = live(bits_ref[row // BITS, :, xl], row, d)


def input_gradient(d, bits, w, part, before):
    r, scan_count, wide = d.shape
    rows, lanes = (2 * (r - 1), 2 * (wide - L))
    steps = scan_count // S // 2
    at = lambda n, m: pl.BlockSpec((n, S, m), lambda g: (0, g + part * steps, 0))
    earlier = () if before is None else (before,)
    return pl.pallas_call(
        input_grad_kernel,
        grid=(steps,),
        in_specs=[at(r, wide), at(bits.shape[0], lanes), whole(w.shape)]
        + [pl.BlockSpec(memory_space=pl.ANY)] * len(earlier),
        out_specs=at(rows, lanes),
        out_shape=jax.ShapeDtypeStruct((rows, scan_count, lanes), bf16),
        input_output_aliases={3: 0} if earlier else {},
        compiler_params=params_of(),
        cost_estimate=cost(7),
        name="input_gradient",
    )(d, bits, w, *earlier)


def adam_step(weight_now, gradient, moment_one, moment_two, step_rate, decay_rate):
    first_new = adam_beta * moment_one + (1.0 - adam_beta) * gradient
    second_new = adam_beta * moment_two + (1.0 - adam_beta) * gradient * gradient
    correction = 1.0 - adam_beta**step_count
    update = first_new / correction / (jnp.sqrt(second_new / correction) + adam_eps)
    return (weight_now - step_rate * (update + decay_rate * weight_now), first_new, second_new)


def update_kernel(
    g_ref, s1_ref, s2_ref, k_ref, km_ref, kv_ref, n_ref, nm_ref, nv_ref, gn_ref, ok_ref, okm_ref,
    okv_ref, olow_ref, on_ref, onm_ref, onv_ref,
):
    norm_rows = []
    for ref in (s1_ref, s2_ref):
        shift_sum, gain_sum = sums_of(ref)
        norm_rows += [gain_sum[:, :C], shift_sum[:, :C]]
    g_norm = jnp.concatenate(norm_rows, axis=0)
    squares = jnp.sum(jnp.sum(g_ref[: 9 * C] ** 2, axis=0, keepdims=True), axis=1, keepdims=True)
    squares = squares + jnp.sum(
        jnp.sum(g_norm * g_norm, axis=0, keepdims=True), axis=1, keepdims=True
    )
    norm = jnp.sqrt(squares)
    gn_ref[...] = norm
    factor = jnp.minimum(1.0, clip_limit / norm)
    on, onm, onv = adam_step(
        n_ref[...], g_norm * factor, nm_ref[...], nv_ref[...], norm_rate, 0.0
    )
    on_ref[...] = on
    onm_ref[...] = onm
    onv_ref[...] = onv
    for layer in range(2):
        for a in range(5):
            width = L if a < 4 else C
            at = slice(a * L, a * L + width)
            if a == 4:
                g = g_ref[4 * C : 5 * C, layer * C : (layer + 1) * C]
            else:
                first = (a + 5 * layer) * C
                g = g_ref[first : first + C, :]
            k, km, kv = adam_step(
                k_ref[layer, :, at], g * factor, km_ref[layer, :, at], kv_ref[layer, :, at],
                kernel_rate, kernel_decay,
            )
            ok_ref[layer, :, at] = k
            okm_ref[layer, :, at] = km
            okv_ref[layer, :, at] = kv
            olow_ref[layer, :, at] = k.astype(bf16)


def update(grads, sums1, sums2, kt, kmt, kvt, norm_params, norm_m, norm_v):
    flat = lambda a: a.reshape(4, C)
    big = jax.ShapeDtypeStruct(kt.shape, f32)
    small = jax.ShapeDtypeStruct((4, C), f32)
    outs = [
        jax.ShapeDtypeStruct((1, 1), f32), big, big, big,
        jax.ShapeDtypeStruct(kt.shape, bf16), small, small, small,
    ]
    args = [grads, sums1, sums2, kt, kmt, kvt, flat(norm_params), flat(norm_m), flat(norm_v)]
    return pl.pallas_call(
        update_kernel,
        grid=(1,),
        in_specs=[whole(a.shape) for a in args],
        out_specs=[whole(o.shape) for o in outs],
        out_shape=outs,
        compiler_params=params_of(),
        cost_estimate=cost(3),
        name="update",
    )(*args)


def shifted(block, axis, distance):
    devices = range(lax.axis_size(axis))
    route = [(i - distance, i) for i in devices if i - distance in devices]
    return lax.ppermute(block, axis, route)


def exchange(rows):
    return lax.all_to_all(rows, BOTH, 0, 0, tiled=True)


def per_device(
    scan_features, occupancy, kernels, kernel_m, kernel_v, norm_params, norm_m, norm_v, cotangent
):
    x = jnp.transpose(scan_features, (1, 0, 2))
    cot = jnp.transpose(cotangent, (1, 0, 2))
    occ = jnp.transpose(occupancy, (2, 0, 1))
    kt, kmt, kvt = (jnp.transpose(a, (0, 2, 1)) for a in (kernels, kernel_m, kernel_v))
    gy, gx = (lax.axis_size("gy"), lax.axis_size("gx"))
    devices = gy * gx
    y, z = (lax.axis_index("gy"), lax.axis_index("gx"))
    flags = jnp.stack([y > 0, y < gy - 1, z > 0, z < gx - 1]).astype(jnp.int32)
    rows, scan_count, lanes = x.shape
    r, tiles = (rows // 2, lanes // L // 2)
    count = float(scan_count * r * tiles)
    last = (tiles - 1) * L

    down, cot_down, corner, xcol = edges(x, occ, cot)
    xcol = shifted(xcol, "gx", 1)
    down = shifted(down, "gy", 1)
    cot_down = shifted(cot_down, "gy", -1)
    corner = lax.ppermute(
        corner, BOTH, [(i, i + gx + 1) for i in range(devices - gx) if (i + 1) % gx]
    )
    bits, w1, w2, w2b, w1b, np2 = prepare(occ, kt, norm_params)

    ends, st1, going_right, going_left, edge = first_last(x, bits, down, xcol, corner, w1)
    left_in = shifted(going_right, "gx", 1)
    right_in = shifted(going_left, "gx", -1)
    c1, st1, up, low_rows = conv_one(x, bits, down, st1, w1, devices)
    half = (r + 1) // 2

    def beyond(a, b):
        near, far = (slice(0, C), slice(C, L))
        if a >= half:
            a, b, near, far = (a - half, b - half, far, near)
        return jnp.concatenate([left_in[a:b, :, near], right_in[a:b, :, far]], axis=2)

    up = jnp.concatenate([up, edge[:3], beyond(0, 3)], axis=2)
    low_rows = jnp.concatenate([low_rows, edge[r - 2 :], beyond(r - 2, r)], axis=2)
    down_in = shifted(up, "gy", -1)
    up_in = shifted(low_rows, "gy", 1)
    st1 = exchange(st1)

    c2, n1, hid, st2 = conv_two(
        flags, c1, ends, up_in, down_in, left_in, right_in, st1, np2, w2, count
    )
    st2 = exchange(st2)
    features, d2, sums2 = output(c2, st2, np2, cot, down, cot_down, count)
    sums2 = exchange(sums2)
    going_right, going_left = rim_two(flags, d2, c2, st2, sums2, np2, count)
    left_in = shifted(going_right, "gx", 1)
    right_in = shifted(going_left, "gx", -1)
    ds, kg2 = back_two(flags, d2, c2, hid, st2, sums2, np2, count)
    d1, edge, sums1 = hidden_gradient(ds, left_in, right_in, n1, np2, w2b, devices)
    edge = shifted(edge, "gx", -1)
    sums1 = exchange(sums1)
    d1, grads = back_one(flags, d1, edge, n1, x, bits, st1, sums1, np2, kg2, count)
    share = grads.shape[0] // devices
    grads = exchange(grads)
    input_grad = input_gradient(d1, bits, w1b, 0, None)
    mine = jnp.sum(grads.reshape(devices, share, L), axis=0)
    grads = exchange(jnp.broadcast_to(mine[None], (devices, share, L)).reshape(-1, L))
    input_grad = input_gradient(d1, bits, w1b, 1, input_grad)
    norm, k, km, kv, low, n, nm, nv = update(
        grads, sums1, sums2, kt, kmt, kvt, norm_params, norm_m, norm_v
    )
    back = lambda a: jnp.transpose(a, (0, 2, 1))
    deep = lambda a: a.reshape(norm_params.shape)
    return (
        jnp.transpose(features, (1, 0, 2)),
        jnp.transpose(input_grad, (1, 0, 2)),
        norm.reshape(()),
        back(k),
        back(km),
        back(kv),
        back(low),
        deep(n),
        deep(nm),
        deep(nv),
    )


def solution(mesh):
    split = P(None, "gy", "gx")
    return jax.shard_map(
        per_device,
        mesh=mesh,
        in_specs=(split, split) + (P(),) * 6 + (split,),
        out_specs=(split, split) + (P(),) * 8,
        check_vma=False,
    )
```

time: 269 us -> 219 us (0.81)
  Pallas kernels: 130 us -> 111 us
  blocking collectives: 53.9 us -> 39.9 us
  local copies, waits for them, and re-layouts: 15.1 us -> 7.13 us
  waiting for transfers between devices: 19.3 us -> 14.7 us
  other arithmetic: 6.76 us -> 2.79 us
    pallas_call x1 -> x5, Pallas kernels: 4.91 us -> 29.6 us  [the longest x1 11 us: hidden_gradient(): pl.pallas_call(hidden_kernel, grid=(scan_count // S,), in_specs=[scans(r...]
    all_to_all x4 -> x3, blocking collectives: 53.9 us -> 39.9 us  [exchange(): return lax.all_to_all(rows, BOTH, 0, 0, tiled=True)]
    pallas_call x1, Pallas kernels: 25.2 us -> 11.6 us  [output(): pl.pallas_call(functools.partial(output_kernel, count=count), grid=(scan_...]
    pallas_call x1, Pallas kernels: 27.8 us -> 16.3 us  [back_one(): pl.pallas_call(functools.partial(back_one_kernel, count=count), grid=(sca...]
    ppermute x10, waiting for transfers between devices: 8.21 us -> 0.08 us  [shifted(): return lax.ppermute(block, axis, route)]
    pallas_call x1, Pallas kernels: 19.1 us -> 11.1 us  [back_two(): pl.pallas_call(functools.partial(back_two_kernel, count=count), grid=(sca...]
    ppermute x10, starting transfers between devices: 29.9 us -> 23.3 us  [shifted(): return lax.ppermute(block, axis, route)]
    pallas_call x1, Pallas kernels: 19.7 us -> 13.3 us  [conv_one(): pl.pallas_call(conv_one_kernel, grid=(scan_count // S,), in_specs=[scans(...]
  transfers between devices with their start and end apart: 12 -> 14, of which waited for: 5 -> 5; matrix products, arithmetic and copies ran while one was open for 4% -> 2% of each run, Pallas kernels for 11% -> 25%
where the time goes in v2:
time: 219 us; the launch traced here: 218 us
  Pallas kernels  111 us (51%)
  starting transfers between devices  41.6 us (19%)
  blocking collectives  39.9 us (18%)
  waiting for transfers between devices  14.7 us (7%)
  local copies, waits for them, and re-layouts  7.13 us (3%)
  other arithmetic  2.79 us (1%)
    all_to_all x3, blocking collectives, exchange(): return lax.all_to_all(rows, BOTH, 0, 0, tiled=True)  39.9 us
    ppermute x10, starting transfers between devices, shifted(): return lax.ppermute(block, axis, route)  23.3 us
    pallas_call x1, Pallas kernels, back_one(): pl.pallas_call(functools.partial(back_one_kernel, count=count), grid=(sca...  16.3 us
    all_to_all x3, waiting for transfers between devices, exchange(): return lax.all_to_all(rows, BOTH, 0, 0, tiled=True)  13.9 us
    pallas_call x2, Pallas kernels, input_gradient(): pl.pallas_call(input_grad_kernel, grid=(steps,), in_specs=[at(r, wide), a...  13.4 us
    pallas_call x1, Pallas kernels, conv_one(): pl.pallas_call(conv_one_kernel, grid=(scan_count // S,), in_specs=[scans(...  13.3 us
    all_to_all x3, starting transfers between devices, exchange(): return lax.all_to_all(rows, BOTH, 0, 0, tiled=True)  13.2 us
    pallas_call x1, Pallas kernels, conv_two(): pl.pallas_call(functools.partial(conv_two_kernel, count=count), grid=(sca...  12.9 us
  transfers between devices with their start and end apart: 14, of which 5 were waited for; matrix products, arithmetic and copies ran while one was open for 2% of the time, Pallas kernels for 25%

profile of v2, /device:TPU:0, one launch (start us, length us, event | category | flops | bytes accessed | tf_op | source)
XLA Modules:
  0.0 218.1 jit_solution(13177905433187101194)
XLA Ops:
  0.6 3.3 %edges.1 = (bf16[64,2688]{1,0:T(8,128)(2,1)}, bf16[2,64,896]{2,1,0:T(8,128)(2,1)}, bf16[64,128]{1,0:T(8,128)(2,1)}, bf16[31,64,128]{2,1,0:T(8,128)(2,1)}) custom-call(bf16[62,64,1792]{2,1,0:T(8,128)(2,1)} %bitcast.25, bf16[62,64,1792]{2,1,0:T(8,128)(2,1)} %bitcast.26, s32[28,64,62]{2,1,0:T(8,128)} %bitcast.35, bf16[31,64,896]{2,1,0:T(8,128)(2,1)} %bitcast.32, ...), custom_call_target="tpu_custom_call" | custom-call | bytes 10800000 | tf_op jit(solution)/shard_map/edges/pallas_call | solution.py:182
  3.9 4.9 %collective-permute-start.1 = (bf16[31,64,128]{2,1,0:T(8,128)(2,1)}, bf16[31,64,128]{2,1,0:T(8,128)(2,1)S(1)}, u32[]{:S(2)}, u32[]{:S(2)}) collective-permute-start(bf16[31,64,128]{2,1,0:T(8,128)(2,1)} %get-tuple-element.55), channel_id=1, source_target_pairs={{0,1},{1,2},{2,3},{3,4},{4,5},{5,6},{6,7},{8,9},{9,10},{10,11},{11... | collective-permute-start | bytes 1523720 | tf_op jit(solution)/shard_map/ppermute | solution.py:1050
  8.8 1.5 collective-permute-start
  10.3 5.1 %collective-permute-start.2 = (bf16[64,128]{1,0:T(8,128)(2,1)}, bf16[64,128]{1,0:T(8,128)(2,1)S(1)}, u32[]{:S(2)}, u32[]{:S(2)}) collective-permute-start(bf16[64,128]{1,0:T(8,128)(2,1)} %get-tuple-element.56), channel_id=1, source_target_pairs={{0,9},{1,10},{2,11},{3,12},{4,13},{5,14},{6,15},{8,17},{9,18},{10,... | collective-permute-start | bytes 49160 | tf_op jit(solution)/shard_map/ppermute | solution.py:1077
  15.4 4.0 %prepare.1 = (s16[5,64,1792]{2,1,0:T(8,128)(2,1)}, bf16[1920,256]{1,0:T(8,128)(2,1)}, bf16[1024,256]{1,0:T(8,128)(2,1)}, bf16[1024,256]{1,0:T(8,128)(2,1)}, bf16[768,256]{1,0:T(8,128)(2,1)}, /*index=5*/f32[4,128]{1,0:T(4,128)}) custom-call(s32[28,64,62]{2,1,0:T(8,128)} %bitcast.36, f32[2,64,576]{2,1,0:T(8,128)} %bitcast.38, f32[4,64]{1,0:T(4,128)} %bitcast.43), custom_call_target="tpu_custom_call" | custom-call | bytes 14400000 | tf_op jit(solution)/shard_map/prepare/pallas_call | solution.py:243
  21.0 6.8 %conv_one_ends.1 = (f32[31,64,256]{2,1,0:T(8,128)}, f32[1,2,128]{2,1,0:T(2,128)}, bf16[16,64,128]{2,1,0:T(8,128)(2,1)}, bf16[16,64,128]{2,1,0:T(8,128)(2,1)}, bf16[31,64,128]{2,1,0:T(8,128)(2,1)}) custom-call(bf16[62,64,1792]{2,1,0:T(8,128)(2,1)} %bitcast.27, bf16[62,64,1792]{2,1,0:T(8,128)(2,1)} %bitcast.28, ...), custom_call_target="tpu_custom_call" | custom-call | bytes 18000000 | tf_op jit(solution)/shard_map/conv_one_ends/pallas_call | solution.py:327
  27.8 1.3 collective-permute-start.4
  29.1 4.7 %collective-permute-start.3 = (bf16[16,64,128]{2,1,0:T(8,128)(2,1)}, bf16[16,64,128]{2,1,0:T(8,128)(2,1)S(1)}, u32[]{:S(2)}, u32[]{:S(2)}) collective-permute-start(bf16[16,64,128]{2,1,0:T(8,128)(2,1)} %get-tuple-element.63), channel_id=1, source_target_pairs={{0,1},{1,2},{2,3},{3,4},{4,5},{5,6},{6,7},{8,9},{9,10},{10,11},{11... | collective-permute-start | bytes 786440 | tf_op jit(solution)/shard_map/ppermute | solution.py:1050
  34.6 13.3 %conv_one.1 = (f32[31,64,768]{2,1,0:T(8,128)}, f32[32,2,128]{2,1,0:T(2,128)}, bf16[3,64,768]{2,1,0:T(8,128)(2,1)}, bf16[2,64,768]{2,1,0:T(8,128)(2,1)}) custom-call(bf16[62,64,1792]{2,1,0:T(8,128)(2,1)} %bitcast.29, s16[5,64,1792]{2,1,0:T(8,128)(2,1)} %get-tuple-element.53.ba_ref.bb_ref.bits_ref, bf16[64,2688]{1,0:T(8,128)(2,1)} %copy-done, ...), custom_call_target="tpu_custom_call" | custom-call | bytes 46800000 | tf_op jit(solution)/shard_map/conv_one/pallas_call | solution.py:406
  49.3 1.3 collective-permute-start.6
  52.4 3.0 %collective-permute-start.5 = (bf16[2,64,1024]{2,1,0:T(8,128)(2,1)S(1)}, bf16[2,64,1024]{2,1,0:T(8,128)(2,1)S(1)}, u32[]{:S(2)}, u32[]{:S(2)}) collective-permute-start(bf16[2,64,1024]{2,1,0:T(8,128)(2,1)S(1)} %pad_maximum_fusion.1), channel_id=1, source_target_pairs={{0,8},{8,16},{16,24},{1,9},{9,17},{17,25},{2,10},{10,18},{18,26},{... | collective-permute-start | bytes 786440 | tf_op jit(solution)/shard_map/ppermute | solution.py:1050
  55.5 1.3 collective-permute-start.7
  56.8 8.0 %all-to-all-start = ((f32[32,2,128]{2,1,0:T(2,128)}), f32[32,2,128]{2,1,0:T(2,128)S(1)}, u32[]{:S(2)}, u32[]{:S(2)}) async-start(f32[32,2,128]{2,1,0:T(2,128)} %get-tuple-element.66), calls=%async_computation | async-start | bytes 65536 | tf_op jit(solution)/shard_map/all_to_all | solution.py:1054
  65.4 6.6 %all-to-all-done.st_ref = f32[32,2,128]{2,1,0:T(2,128)S(1)} async-done(((f32[32,2,128]{2,1,0:T(2,128)}), f32[32,2,128]{2,1,0:T(2,128)S(1)}, u32[]{:S(2)}, u32[]{:S(2)}) %all-to-all-start) | async-done | bytes 32800 | tf_op jit(solution)/shard_map/all_to_all | solution.py:1054
  72.9 12.9 %conv_two.1 = (f32[34,64,896]{2,1,0:T(8,128)}, bf16[32,64,1024]{2,1,0:T(8,128)(2,1)}, bf16[33,64,1024]{2,1,0:T(8,128)(2,1)}, f32[32,2,128]{2,1,0:T(2,128)}) custom-call(s32[4]{0:T(128)} %add_convert_fusion.flags, f32[31,64,768]{2,1,0:T(8,128)} %get-tuple-element.59.c_ref, f32[31,64,256]{2,1,0:T(8,128)} %get-tuple-element.60.ends_ref, ...), custom_call_target="tpu_custom_call" | custom-call | bytes 50400000 | tf_op jit(solution)/shard_map/conv_two/pallas_call | solution.py:514
  85.8 2.6 %all-to-all-start.1 = ((f32[32,2,128]{2,1,0:T(2,128)}), f32[32,2,128]{2,1,0:T(2,128)S(1)}, u32[]{:S(2)}, u32[]{:S(2)}) async-start(f32[32,2,128]{2,1,0:T(2,128)} %get-tuple-element.70), calls=%async_computation.1 | async-start | bytes 65536 | tf_op jit(solution)/shard_map/all_to_all | solution.py:1054
  88.4 7.2 %all-to-all-done.1.st_ref = f32[32,2,128]{2,1,0:T(2,128)S(1)} async-done(((f32[32,2,128]{2,1,0:T(2,128)}), f32[32,2,128]{2,1,0:T(2,128)S(1)}, u32[]{:S(2)}, u32[]{:S(2)}) %all-to-all-start.1) | async-done | bytes 32800 | tf_op jit(solution)/shard_map/all_to_all | solution.py:1054
  96.2 11.6 %output.1 = (bf16[31,64,896]{2,1,0:T(8,128)(2,1)}, f32[34,64,896]{2,1,0:T(8,128)}, f32[32,2,128]{2,1,0:T(2,128)}) custom-call(f32[34,64,896]{2,1,0:T(8,128)} %get-tuple-element.69.c2_ref.ca_ref.cb_ref, f32[32,2,128]{2,1,0:T(2,128)} %copy-done.2, f32[4,128]{1,0:T(4,128)} %get-tuple-element.67.np_ref, bf16[31,64,896]{2,1,0:T(8,128)(2,1)} %bitcast.34, ...), custom_call_target="tpu_custom_call" | custom-call | bytes 43200000 | tf_op jit(solution)/shard_map/output/pallas_call | solution.py:609
  107.8 10.4 %all_to_all.37.sum_ref.s2_ref = f32[32,2,128]{2,1,0:T(2,128)} all-to-all(f32[32,2,128]{2,1,0:T(2,128)} %get-tuple-element.75), channel_id=1, replica_groups=mesh['gy'=4,'gx'=8] {'gy','gx'}, dimensions={0} | all-to-all | bytes 65536 | tf_op jit(solution)/shard_map/all_to_all | solution.py:1054
  118.2 4.5 %rim_two.1 = (bf16[17,64,128]{2,1,0:T(8,128)(2,1)}, bf16[17,64,128]{2,1,0:T(8,128)(2,1)}) custom-call(s32[4]{0:T(128)} %add_convert_fusion.flags, f32[34,64,896]{2,1,0:T(8,128)} %get-tuple-element.73.d_ref.da_ref.db_ref, f32[34,64,896]{2,1,0:T(8,128)} %get-tuple-element.73.d_ref.da_ref.db_ref, f32[34,64,896]{2,1,0:T(8,128)} %get-tuple-element.69.c2_ref.ca_ref.cb_ref, ...), custom_call_target="tpu_custom_call" | custom-call | bytes 10800000 | tf_op jit(solution)/shard_map/rim_two/pallas_call | solution.py:674
  122.7 2.6 %collective-permute-start.8 = (bf16[17,64,128]{2,1,0:T(8,128)(2,1)}, bf16[17,64,128]{2,1,0:T(8,128)(2,1)S(1)}, u32[]{:S(2)}, u32[]{:S(2)}) collective-permute-start(bf16[17,64,128]{2,1,0:T(8,128)(2,1)} %get-tuple-element.77), channel_id=1, source_target_pairs={{0,1},{1,2},{2,3},{3,4},{4,5},{5,6},{6,7},{8,9},{9,10},{10,11},{11... | collective-permute-start | bytes 835592 | tf_op jit(solution)/shard_map/ppermute | solution.py:1050
  125.3 1.3 collective-permute-start.9
  126.6 11.1 %back_two.1 = (bf16[34,64,896]{2,1,0:T(8,128)(2,1)}, f32[9,64,64]{2,1,0:T(8,128)}) custom-call(s32[4]{0:T(128)} %add_convert_fusion.flags, f32[34,64,896]{2,1,0:T(8,128)} %get-tuple-element.73.d_ref.da_ref.db_ref, f32[34,64,896]{2,1,0:T(8,128)} %get-tuple-element.69.c2_ref.ca_ref.cb_ref, bf16[33,64,1024]{2,1,0:T(8,128)(2,1)} %get-tuple-element.74.hid_ref, ...), custom_call_target="tpu_custom_call" | custom-call | bytes 43200000 | tf_op jit(solution)/shard_map/back_two/pallas_call | solution.py:729
  138.5 11.0 %hidden_gradient.1 = (f32[32,64,1024]{2,1,0:T(8,128)}, bf16[16,64,128]{2,1,0:T(8,128)(2,1)}, f32[32,2,128]{2,1,0:T(2,128)}) custom-call(bf16[34,64,896]{2,1,0:T(8,128)(2,1)} %get-tuple-element.76.ds_ref, bf16[17,64,128]{2,1,0:T(8,128)(2,1)} %copy-done.8, bf16[17,64,128]{2,1,0:T(8,128)(2,1)} %copy-done.9, bf16[32,64,1024]{2,1,0:T(8,128)(2,1)} %get-tuple-element.79.n1_ref, ...), custom_call_target="tpu_custom_call" | custom-call | bytes 43200000 | tf_op jit(solution)/shard_map/hidden_gradient/pallas_call | solution.py:796
  149.6 1.5 collective-permute-start.10
  151.0 13.3 %all_to_all.38.sum_ref.s1_ref = f32[32,2,128]{2,1,0:T(2,128)} all-to-all(f32[32,2,128]{2,1,0:T(2,128)} %get-tuple-element.83), channel_id=1, replica_groups=mesh['gy'=4,'gx'=8] {'gy','gx'}, dimensions={0} | all-to-all | bytes 65536 | tf_op jit(solution)/shard_map/all_to_all | solution.py:1054
  165.0 16.3 %back_one.1 = (bf16[32,64,1024]{2,1,0:T(8,128)(2,1)}, f32[768,128]{1,0:T(8,128)}) custom-call(s32[4]{0:T(128)} %add_convert_fusion.flags, f32[32,64,1024]{2,1,0:T(8,128)} %get-tuple-element.81.dp_ref, bf16[16,64,128]{2,1,0:T(8,128)(2,1)} %copy-done.10, bf16[32,64,1024]{2,1,0:T(8,128)(2,1)} %get-tuple-element.79.n1_ref, bf16[62,64,1792]{2,1,0:T(8,128)(2,1)} %bitcast.30, ...), custom_call_target="tpu_custom_call" | custom-call | bytes 57600000 | tf_op jit(solution)/shard_map/back_one/pallas_call | solution.py:907
  181.3 16.2 %all_to_all.39 = f32[32,24,128]{2,1,0:T(8,128)S(1)} all-to-all(f32[32,24,128]{2,1,0:T(8,128)} %bitcast.40), channel_id=1, replica_groups=mesh['gy'=4,'gx'=8] {'gy','gx'}, dimensions={0} | all-to-all | bytes 786432 | tf_op jit(solution)/shard_map/all_to_all | solution.py:1054
  198.3 2.6 %all-to-all-start.5 = ((f32[32,24,128]{2,1,0:T(8,128)}), f32[32,24,128]{2,1,0:T(8,128)S(1)}, u32[]{:S(2)}, u32[]{:S(2)}) async-start(f32[32,24,128]{2,1,0:T(8,128)} %broadcast_in_dim.2), calls=%async_computation.5 | async-start | bytes 786432 | tf_op jit(solution)/shard_map/all_to_all | solution.py:1054
  200.9 6.7 %input_gradient.2.rest_0_ = bf16[62,64,1792]{2,1,0:T(8,128)(2,1)} custom-call(bf16[32,64,1024]{2,1,0:T(8,128)(2,1)} %get-tuple-element.85.ds, s16[5,64,1792]{2,1,0:T(8,128)(2,1)} %get-tuple-element.53.ba_ref.bb_ref.bits_ref, bf16[768,256]{1,0:T(8,128)(2,1)} %get-tuple-element.86.w_ref), custom_call_target="tpu_custom_call" | custom-call | bytes 25200000 | tf_op jit(solution)/shard_map/input_gradient/pallas_call | solution.py:963
  207.6 6.7 %input_gradient.3 = bf16[62,64,1792]{2,1,0:T(8,128)(2,1)} custom-call(bf16[32,64,1024]{2,1,0:T(8,128)(2,1)} %get-tuple-element.85.ds, s16[5,64,1792]{2,1,0:T(8,128)(2,1)} %get-tuple-element.53.ba_ref.bb_ref.bits_ref, bf16[768,256]{1,0:T(8,128)(2,1)} %get-tuple-element.86.w_ref, ...), custom_call_target="tpu_custom_call", output_to_operand_aliasing={{}: (3, {})} | custom-call | bytes 25200000 | tf_op jit(solution)/shard_map/input_gradient/pallas_call | solution.py:963
  215.2 2.8 %update.1 = (f32[1,1]{1,0:T(1,128)}, f32[2,64,576]{2,1,0:T(8,128)}, f32[2,64,576]{2,1,0:T(8,128)}, f32[2,64,576]{2,1,0:T(8,128)}, bf16[2,64,576]{2,1,0:T(8,128)(...) custom-call(f32[768,128]{1,0:T(8,128)} %bitcast.37, f32[32,2,128]{2,1,0:T(2,128)} %all_to_all.38.sum_ref.s1_ref, ...), custom_call_target="tpu_custom_call" | custom-call | bytes 10800000 | tf_op jit(solution)/shard_map/update/pallas_call | solution.py:1035
  (53 shorter events, 10.9 us)
Async XLA Ops:
  3.9 16.2 %collective-permute-start.1 = (bf16[31,64,128]{2,1,0:T(8,128)(2,1)}, bf16[31,64,128]{2,1,0:T(8,128)(2,1)S(1)}, u32[]{:S(2)}, u32[]{:S(2)}) collective-permute-start(bf16[31,64,128]{2,1,0:T(8,128)(2,1)} %get-tuple-element.55), channel_id=1, source_target_pairs={{0,1},{1,2},{2,3},{3,4},{4,5},{5,6},{6,7},{8,9},{9,10},{10,11},{11... | collective-permute-start | bytes 1523720 | tf_op jit(solution)/shard_map/ppermute | solution.py:1050
  8.8 11.3 %collective-permute-start = (bf16[64,2688]{1,0:T(8,128)(2,1)}, bf16[64,2688]{1,0:T(8,128)(2,1)S(1)}, u32[]{:S(2)}, u32[]{:S(2)}) collective-permute-start(bf16[64,2688]{1,0:T(8,128)(2,1)} %get-tuple-element.54), channel_id=1, source_target_pairs={{0,8},{8,16},{16,24},{1,9},{9,17},{17,25},{2,10},{10,18},{18,26},{... | collective-permute-start | bytes 1032200 | tf_op jit(solution)/shard_map/ppermute | solution.py:1050
  10.3 9.9 %collective-permute-start.2 = (bf16[64,128]{1,0:T(8,128)(2,1)}, bf16[64,128]{1,0:T(8,128)(2,1)S(1)}, u32[]{:S(2)}, u32[]{:S(2)}) collective-permute-start(bf16[64,128]{1,0:T(8,128)(2,1)} %get-tuple-element.56), channel_id=1, source_target_pairs={{0,9},{1,10},{2,11},{3,12},{4,13},{5,14},{6,15},{8,17},{9,18},{10,... | collective-permute-start | bytes 49160 | tf_op jit(solution)/shard_map/ppermute | solution.py:1077
  20.1 0.6 copy-start.13
  20.1 0.7 copy-start
  20.1 0.9 copy-start.3
  27.8 20.2 %collective-permute-start.4 = (bf16[16,64,128]{2,1,0:T(8,128)(2,1)}, bf16[16,64,128]{2,1,0:T(8,128)(2,1)S(1)}, u32[]{:S(2)}, u32[]{:S(2)}) collective-permute-start(bf16[16,64,128]{2,1,0:T(8,128)(2,1)} %get-tuple-element.64), channel_id=1, source_target_pairs={{1,0},{2,1},{3,2},{4,3},{5,4},{6,5},{7,6},{9,8},{10,9},{11,10},{12... | collective-permute-start | bytes 786440 | tf_op jit(solution)/shard_map/ppermute | solution.py:1050
  29.1 19.0 %collective-permute-start.3 = (bf16[16,64,128]{2,1,0:T(8,128)(2,1)}, bf16[16,64,128]{2,1,0:T(8,128)(2,1)S(1)}, u32[]{:S(2)}, u32[]{:S(2)}) collective-permute-start(bf16[16,64,128]{2,1,0:T(8,128)(2,1)} %get-tuple-element.63), channel_id=1, source_target_pairs={{0,1},{1,2},{2,3},{3,4},{4,5},{5,6},{6,7},{8,9},{9,10},{10,11},{11... | collective-permute-start | bytes 786440 | tf_op jit(solution)/shard_map/ppermute | solution.py:1050
  34.6 20.9 %copy-start.14 = (bf16[2,64,896]{2,1,0:T(8,128)(2,1)S(1)}, bf16[2,64,896]{2,1,0:T(8,128)(2,1)}, u32[]{:S(2)}) copy-start(bf16[2,64,896]{2,1,0:T(8,128)(2,1)} %get-tuple-element.71) | copy-start | bytes 688132
  48.0 24.1 %copy-start.4 = (bf16[16,64,128]{2,1,0:T(8,128)(2,1)}, bf16[16,64,128]{2,1,0:T(8,128)(2,1)S(1)}, u32[]{:S(2)}) copy-start(bf16[16,64,128]{2,1,0:T(8,128)(2,1)S(1)} %collective-permute-done.4.right_ref) | copy-start | bytes 786436
  48.1 24.0 %copy-start.5 = (bf16[16,64,128]{2,1,0:T(8,128)(2,1)}, bf16[16,64,128]{2,1,0:T(8,128)(2,1)S(1)}, u32[]{:S(2)}) copy-start(bf16[16,64,128]{2,1,0:T(8,128)(2,1)S(1)} %collective-permute-done.3.left_ref) | copy-start | bytes 786436
  49.3 22.8 %collective-permute-start.6 = (bf16[3,64,1024]{2,1,0:T(8,128)(2,1)S(1)}, bf16[3,64,1024]{2,1,0:T(8,128)(2,1)S(1)}, u32[]{:S(2)}, u32[]{:S(2)}) collective-permute-start(bf16[3,64,1024]{2,1,0:T(8,128)(2,1)S(1)} %pad_maximum_fusion), channel_id=1, source_target_pairs={{8,0},{16,8},{24,16},{9,1},{17,9},{25,17},{10,2},{18,10},{26,18},{... | collective-permute-start | bytes 1179656 | tf_op jit(solution)/shard_map/ppermute | solution.py:1050
  52.4 19.6 %collective-permute-start.5 = (bf16[2,64,1024]{2,1,0:T(8,128)(2,1)S(1)}, bf16[2,64,1024]{2,1,0:T(8,128)(2,1)S(1)}, u32[]{:S(2)}, u32[]{:S(2)}) collective-permute-start(bf16[2,64,1024]{2,1,0:T(8,128)(2,1)S(1)} %pad_maximum_fusion.1), channel_id=1, source_target_pairs={{0,8},{8,16},{16,24},{1,9},{9,17},{17,25},{2,10},{10,18},{18,26},{... | collective-permute-start | bytes 786440 | tf_op jit(solution)/shard_map/ppermute | solution.py:1050
  55.5 32.9 %collective-permute-start.7 = (bf16[2,64,896]{2,1,0:T(8,128)(2,1)S(1)}, bf16[2,64,896]{2,1,0:T(8,128)(2,1)S(1)}, u32[]{:S(2)}, u32[]{:S(2)}) collective-permute-start(bf16[2,64,896]{2,1,0:T(8,128)(2,1)S(1)} %copy-done.14), channel_id=1, source_target_pairs={{8,0},{16,8},{24,16},{9,1},{17,9},{25,17},{10,2},{18,10},{26,18},{... | collective-permute-start | bytes 688136 | tf_op jit(solution)/shard_map/ppermute | solution.py:1050
  56.8 15.2 %all-to-all-start = ((f32[32,2,128]{2,1,0:T(2,128)}), f32[32,2,128]{2,1,0:T(2,128)S(1)}, u32[]{:S(2)}, u32[]{:S(2)}) async-start(f32[32,2,128]{2,1,0:T(2,128)} %get-tuple-element.66), calls=%async_computation | async-start | bytes 65536 | tf_op jit(solution)/shard_map/all_to_all | solution.py:1054
  72.0 0.6 copy-start.7
  72.0 0.7 copy-start.11
  72.0 0.8 copy-start.6
  85.8 9.8 %all-to-all-start.1 = ((f32[32,2,128]{2,1,0:T(2,128)}), f32[32,2,128]{2,1,0:T(2,128)S(1)}, u32[]{:S(2)}, u32[]{:S(2)}) async-start(f32[32,2,128]{2,1,0:T(2,128)} %get-tuple-element.70), calls=%async_computation.1 | async-start | bytes 65536 | tf_op jit(solution)/shard_map/all_to_all | solution.py:1054
  88.4 7.2 %copy-start.12 = (bf16[2,64,896]{2,1,0:T(8,128)(2,1)}, bf16[2,64,896]{2,1,0:T(8,128)(2,1)S(1)}, u32[]{:S(2)}) copy-start(bf16[2,64,896]{2,1,0:T(8,128)(2,1)S(1)} %collective-permute-done.7.down_ref) | copy-start | bytes 688132
  95.5 0.6 copy-start.2
  122.7 15.0 %collective-permute-start.8 = (bf16[17,64,128]{2,1,0:T(8,128)(2,1)}, bf16[17,64,128]{2,1,0:T(8,128)(2,1)S(1)}, u32[]{:S(2)}, u32[]{:S(2)}) collective-permute-start(bf16[17,64,128]{2,1,0:T(8,128)(2,1)} %get-tuple-element.77), channel_id=1, source_target_pairs={{0,1},{1,2},{2,3},{3,4},{4,5},{5,6},{6,7},{8,9},{9,10},{10,11},{11... | collective-permute-start | bytes 835592 | tf_op jit(solution)/shard_map/ppermute | solution.py:1050
  125.3 12.5 %collective-permute-start.9 = (bf16[17,64,128]{2,1,0:T(8,128)(2,1)}, bf16[17,64,128]{2,1,0:T(8,128)(2,1)S(1)}, u32[]{:S(2)}, u32[]{:S(2)}) collective-permute-start(bf16[17,64,128]{2,1,0:T(8,128)(2,1)} %get-tuple-element.78), channel_id=1, source_target_pairs={{1,0},{2,1},{3,2},{4,3},{5,4},{6,5},{7,6},{9,8},{10,9},{11,10},{12... | collective-permute-start | bytes 835592 | tf_op jit(solution)/shard_map/ppermute | solution.py:1050
  137.7 0.7 copy-start.8
  137.7 0.8 copy-start.9
  149.6 14.8 %collective-permute-start.10 = (bf16[16,64,128]{2,1,0:T(8,128)(2,1)}, bf16[16,64,128]{2,1,0:T(8,128)(2,1)S(1)}, u32[]{:S(2)}, u32[]{:S(2)}) collective-permute-start(bf16[16,64,128]{2,1,0:T(8,128)(2,1)} %get-tuple-element.82), channel_id=1, source_target_pairs={{1,0},{2,1},{3,2},{4,3},{5,4},{6,5},{7,6},{9,8},{10,9},{11,10},{12... | collective-permute-start | bytes 786440 | tf_op jit(solution)/shard_map/ppermute | solution.py:1050
  164.3 0.7 copy-start.10
  198.3 16.1 %all-to-all-start.5 = ((f32[32,24,128]{2,1,0:T(8,128)}), f32[32,24,128]{2,1,0:T(8,128)S(1)}, u32[]{:S(2)}, u32[]{:S(2)}) async-start(f32[32,24,128]{2,1,0:T(8,128)} %broadcast_in_dim.2), calls=%async_computation.5 | async-start | bytes 786432 | tf_op jit(solution)/shard_map/all_to_all | solution.py:1054
  214.5 0.8 copy-start.1

commit v3 on v2

--- a/solution.py
+++ b/solution.py
@@ -22,7 +22,7 @@
 S, C, L, BITS = (16, 64, 128, 13)
 
 
-def params_of(limit=56):
+def params_of(limit=20):
     return pltpu.CompilerParams(
         dimension_semantics=("arbitrary",), vmem_limit_bytes=limit << 20
     )
@@ -40,6 +40,21 @@
 
 def scans(rows, lanes):
     return pl.BlockSpec((rows, S, lanes), lambda g: (0, g, 0))
+
+
+def resident(shape, dtype):
+    return pltpu.VMEM(shape, dtype)
+
+
+held = pl.BlockSpec(memory_space=pltpu.VMEM)
+
+
+def hbm(array):
+    return pltpu.with_memory_space_constraint(array, pltpu.HBM)
+
+
+def part_of(ref, step):
+    return ref.at[:, pl.ds(pl.multiple_of(step * S, S), S), :]
 
 
 def low_half(rows=S):
@@ -194,7 +209,7 @@
         compiler_params=params_of(),
         cost_estimate=cost(3),
         name="edges",
-    )(x, x, occ, cot, cot)
+    )(hbm(x), hbm(x), hbm(occ), hbm(cot), hbm(cot))
 
 
 def prep_kernel(occ_ref, kt_ref, np_ref, bits_ref, w1_ref, w2_ref, w2b_ref, w1b_ref, np2_ref):
@@ -249,7 +264,7 @@
         compiler_params=params_of(),
         cost_estimate=cost(4),
         name="prepare",
-    )(occ, kt, norm_params.reshape(4, C))
+    )(hbm(occ), kt, norm_params.reshape(4, C))
 
 
 def mask_tile(x_ref, bits_ref, t, xs, into):
@@ -274,134 +289,62 @@
     return [acc[i // 2, :, (i % 2) * L : (i % 2 + 1) * L] for i in range(r)]
 
 
-def first_last_kernel(
-    xa_ref, xb_ref, ba_ref, bb_ref, xrow_ref, xcol_ref, corner_ref, w_ref, c_ref, st_ref, er_ref,
-    el_ref, edge_ref, xs, run,
+def conv_one_kernel(
+    x_ref, bits_ref, xrow_ref, xcol_ref, corner_ref, w_ref, c_ref, st_ref, up_ref, down_ref,
+    edge_ref, xs, run,
 ):
     step, steps = (pl.program_id(0), pl.num_programs(0))
-    rows, lanes = (xa_ref.shape[0], xrow_ref.shape[1] * 2 // 3)
-    r = rows // 2
+    c_ref = part_of(c_ref, step)
+    rows, tiles = (x_ref.shape[0], x_ref.shape[2] // L)
+    r, t_out = (rows // 2, tiles // 2 + 1)
     low = low_half()
 
     @pl.when(step == 0)
     def _():
         clear_rows(rows, (r + 1) // 2, xs)
 
-    xs[0, 0, :, L : 2 * L] = xrow_ref[:, :L]
-    xs[0, 0, :, 2 * L :] = xrow_ref[:, lanes - 2 * L : lanes]
+    xs[0, 0, :, L:] = xrow_ref[:, : tiles * L]
     xs[0, 0, :, :L] = corner_ref[...]
     for i in range(r):
         k = 2 * i + 2
         xs[k // 4, k % 4, :, :L] = xcol_ref[i]
         k = 2 * i + 1
         xs[k // 4, k % 4, :, :L] = swap(xcol_ref[i].astype(f32)).astype(bf16)
-    mask_tile(xa_ref, ba_ref, 0, xs, 1)
-    mask_tile(xb_ref, bb_ref, 0, xs, 2)
-    mask_tile(xb_ref, bb_ref, 1, xs, 3)
     wide = 3 * L
     some = lambda a: jnp.concatenate(
         [w_ref[q * wide + a * L : q * wide + (a + 2) * L] for q in range(5)], axis=0
     )
-    last = conv_rows(xs, slice(2 * L, 4 * L), some(0), r)
-    first = conv_rows(xs, slice(0, 2 * L), some(1), r)
-    edge = [jnp.where(low, b, a) for a, b in zip(first, last)]
-    pilot = pilot_of(jnp.concatenate(edge[: r // 2], axis=0))
-    for i in range(r):
-        c_ref[i, :, :L] = first[i]
-        c_ref[i, :, L:] = last[i]
-        edge_ref[i] = edge[i].astype(bf16)
-    finish_stats(step, steps, pilot, off_sums(edge, pilot), float(r * S), run, st_ref)
-    half = er_ref.shape[0]
-    for k in range(half):
-        far = swap(edge[k + half]) if k + half < r else jnp.zeros((S, L), f32)
-        er_ref[k] = jnp.where(low, edge[k], far).astype(bf16)
-        el_ref[k] = jnp.where(low, far, edge[k]).astype(bf16)
-
-
-def first_last(x, bits, down, xcol, corner, w):
-    rows, scan_count, lanes = x.shape
-    r = rows // 2
-    shape = lambda dtype, *s: jax.ShapeDtypeStruct(s, dtype)
-    at = lambda n, width, k: pl.BlockSpec((n, S, width), lambda g: (0, g, k))
-    end = lanes // (2 * L) - 1
-    return pl.pallas_call(
-        first_last_kernel,
-        grid=(scan_count // S,),
-        in_specs=[
-            at(rows, L, 0),
-            at(rows, 2 * L, end),
-            at(bits.shape[0], L, 0),
-            at(bits.shape[0], 2 * L, end),
-            pl.BlockSpec((S, down.shape[1]), lambda g: (g, 0)),
-            scans(r, L),
-            pl.BlockSpec((S, L), lambda g: (g, 0)),
-            whole(w.shape),
-        ],
-        out_specs=[
-            scans(r, 2 * L),
-            whole((1, 2, L)),
-            scans((r + 1) // 2, L),
-            scans((r + 1) // 2, L),
-            scans(r, L),
-        ],
-        out_shape=[
-            shape(f32, r, scan_count, 2 * L),
-            shape(f32, 1, 2, L),
-            shape(bf16, (r + 1) // 2, scan_count, L),
-            shape(bf16, (r + 1) // 2, scan_count, L),
-            shape(bf16, r, scan_count, L),
-        ],
-        scratch_shapes=[
-            pltpu.VMEM(((r + 1) // 2 + 1, 4, S, 4 * L), bf16),
-            pltpu.VMEM((8, L), f32),
-        ],
-        compiler_params=params_of(),
-        cost_estimate=cost(5),
-        name="conv_one_ends",
-    )(x, x, bits, bits, down, xcol, corner, w)
-
-
-def conv_one_kernel(
-    x_ref, bits_ref, xrow_ref, ends_ref, w_ref, c_ref, st_ref, up_ref, down_ref, xs, run
-):
-    step, steps = (pl.program_id(0), pl.num_programs(0))
-    rows, tiles = (x_ref.shape[0], x_ref.shape[2] // L)
-    r, inner = (rows // 2, tiles // 2 - 1)
-
-    @pl.when(step == 0)
-    def _():
-        clear_rows(rows, (r + 1) // 2, xs)
-
-    xs[0, 0] = xrow_ref[:, : tiles * L]
-    sums, pilot = (None, None)
+    sums, pilot, first = (None, None, None)
     filled = 0
-    for t in range(inner):
-        while filled < 2 * t + 3:
-            mask_tile(x_ref, bits_ref, filled, xs, filled)
+    for t in range(t_out):
+        while filled < min(tiles, 2 * t + 1):
+            mask_tile(x_ref, bits_ref, filled, xs, filled + 1)
             filled += 1
-        blocks = conv_rows(xs, slice(2 * t * L, (2 * t + 3) * L), w_ref[...], r)
-        if pilot is None:
-            pilot = pilot_of(jnp.concatenate(blocks[: r // 2], axis=0))
-        sums = added(sums, off_sums(blocks, pilot))
+        if t == 0:
+            blocks = conv_rows(xs, slice(0, 2 * L), some(1), r)
+            first = blocks
+        elif t == t_out - 1:
+            blocks = conv_rows(xs, slice((tiles - 1) * L, (tiles + 1) * L), some(0), r)
+        else:
+            blocks = conv_rows(xs, slice((2 * t - 1) * L, (2 * t + 2) * L), w_ref[...], r)
         for i, block in enumerate(blocks):
             c_ref[i, :, t * L : (t + 1) * L] = block
-    finish_stats(step, steps, pilot, sums, float(r * inner * S), run, st_ref)
+        if t == 1:
+            pilot = pilot_of(jnp.concatenate(blocks[: r // 2], axis=0))
+        if t == t_out - 1:
+            blocks = [jnp.where(low, b, pair(c_ref, i, 0)) for i, b in enumerate(blocks)]
+            for i in range(r):
+                edge_ref[i] = blocks[i].astype(bf16)
+        if t > 0:
+            sums = added(sums, off_sums(blocks, pilot))
+    finish_stats(step, steps, pilot, sums, float(r * (t_out - 1) * S), run, st_ref)
     up_ref[...] = c_ref[0:3].astype(bf16)
     down_ref[...] = c_ref[r - 2 : r].astype(bf16)
 
-    @pl.when(step == steps - 1)
-    def _():
-        own, more = (float(r * S) * steps * n for n in (inner, 1))
-        delta = ends_ref[0, 0:1] - run[0:1]
-        mean = run[0:1] + delta * (more / (own + more))
-        squares = run[1:2] + ends_ref[0, 1:2] + delta * delta * (own * more / (own + more))
-        row = jnp.concatenate([mean, squares], axis=0)
-        st_ref[...] = jnp.broadcast_to(row[None], st_ref.shape)
-
-
-def conv_one(x, bits, down, ends, w, devices):
+
+def conv_one(x, bits, down, xcol, corner, w, devices):
     rows, scan_count, lanes = x.shape
-    r, wide = (rows // 2, lanes // 2 - L)
+    r, wide = (rows // 2, lanes // 2 + L)
     shape = lambda dtype, *s: jax.ShapeDtypeStruct(s, dtype)
     return pl.pallas_call(
         conv_one_kernel,
@@ -410,37 +353,67 @@
             scans(rows, lanes),
             scans(bits.shape[0], lanes),
             pl.BlockSpec((S, down.shape[1]), lambda g: (g, 0)),
-            whole(ends.shape),
+            scans(r, L),
+            pl.BlockSpec((S, L), lambda g: (g, 0)),
             whole(w.shape),
         ],
-        out_specs=[
-            scans(r, wide),
-            whole((devices, 2, L)),
-            scans(3, wide),
-            scans(2, wide),
-        ],
+        out_specs=[held, whole((devices, 2, L)), scans(3, wide), scans(2, wide), scans(r, L)],
         out_shape=[
-            shape(f32, r, scan_count, wide),
+            resident((r, scan_count, wide), f32),
             shape(f32, devices, 2, L),
             shape(bf16, 3, scan_count, wide),
             shape(bf16, 2, scan_count, wide),
+            shape(bf16, r, scan_count, L),
         ],
         scratch_shapes=[
-            pltpu.VMEM(((r + 1) // 2 + 1, 4, S, lanes), bf16),
+            pltpu.VMEM(((r + 1) // 2 + 1, 4, S, lanes + L), bf16),
             pltpu.VMEM((8, L), f32),
         ],
         compiler_params=params_of(),
         cost_estimate=cost(13),
         name="conv_one",
-    )(x, bits, down, ends, w)
+    )(hbm(x), bits, down, xcol, corner, w)
+
+
+def pack_kernel(up_ref, edge_ref, down_ref, er_ref, el_ref):
+    r, half = (edge_ref.shape[0], er_ref.shape[0])
+    last = up_ref.shape[2] // L - 1
+    low = low_half()
+
+    def both(row):
+        if 2 <= row < r + 2:
+            return edge_ref[row - 2].astype(f32)
+        src, k = (up_ref, row) if row < 2 else (down_ref, row - r - 2)
+        return jnp.where(low, pair(src, k, last).astype(f32), pair(src, k, 0).astype(f32))
+
+    for k in range(half):
+        near, far = (both(k), swap(both(k + half)))
+        er_ref[k] = jnp.where(low, near, far).astype(bf16)
+        el_ref[k] = jnp.where(low, far, near).astype(bf16)
+
+
+def pack_edges(up, edge, down):
+    r, scan_count, _lanes = edge.shape
+    wide = up.shape[2]
+    return pl.pallas_call(
+        pack_kernel,
+        grid=(scan_count // S,),
+        in_specs=[scans(2, wide), scans(r, L), scans(3, wide)],
+        out_specs=[scans((r + 5) // 2, L)] * 2,
+        out_shape=[jax.ShapeDtypeStruct(((r + 5) // 2, scan_count, L), bf16)] * 2,
+        compiler_params=params_of(),
+        cost_estimate=cost(2),
+        name="pack_edges",
+    )(up, edge, down)
 
 
 def conv_two_kernel(
-    flags, c_ref, ends_ref, up_ref, down_ref, left_ref, right_ref, st_ref, np_ref, w_ref, c2_ref,
-    n1_ref, hid_ref, st2_ref, hs, rim, run, *, count,
+    flags, c_ref, up_ref, down_ref, left_ref, right_ref, st_ref, np_ref, w_ref, c2_ref, n1_ref,
+    hid_ref, st2_ref, hs, rim, run, *, count,
 ):
     step, steps = (pl.program_id(0), pl.num_programs(0))
-    r, tiles = (c_ref.shape[0], c_ref.shape[2] // L + 2)
+    c_ref, c2_ref, n1_ref = (part_of(a, step) for a in (c_ref, c2_ref, n1_ref))
+    r, tiles = (c_ref.shape[0], c_ref.shape[2] // L)
     t_out = tiles - 1
     mean, inv = stats_of(st_ref, count)
     offset = -mean * inv
@@ -450,23 +423,21 @@
     low = low_half()
     left = jnp.where(low, f_left, 1.0)
     right = jnp.where(low, 1.0, f_right)
-    for row in range(r):
+    for row in range(r + 5):
         rim[row] = rim_of(left_ref, right_ref, row, low)
 
     def act(row, t):
-        ends = (0, tiles - 1)
-        if 2 <= row < r + 2:
-            flag = None
-            c = pair(ends_ref, row - 2, min(t, 1)) if t in ends else pair(c_ref, row - 2, t - 1)
-            beyond = rim[row - 2] if t in ends else None
+        if row < 2:
+            c, flag = (pair(up_ref, row, t), f_up)
+        elif row < r + 2:
+            c, flag = (pair(c_ref, row - 2, t), None)
         else:
-            src, k, flag = (up_ref, row, f_up) if row < 2 else (down_ref, row - r - 2, f_down)
-            c = pair(src, k, tiles - 2 if t in ends else t - 1).astype(f32)
-            beyond = pair(src, k, tiles - 1).astype(f32) if t in ends else None
+            c, flag = (pair(down_ref, row - r - 2, t), f_down)
+        c = c.astype(f32)
         if t == 0:
-            c = jnp.where(low, beyond, c)
+            c = jnp.where(low, rim[row], c)
         if t == tiles - 1:
-            c = jnp.where(low, c, beyond)
+            c = jnp.where(low, c, rim[row])
         h = c * scale + shift
         out = h + h * jnp.tanh(h)
         if t == 0:
@@ -506,9 +477,8 @@
     finish_stats(step, steps, pilot, sums, float(r * t_out * S), run, st2_ref)
 
 
-def conv_two(flags, c1, ends, up, down, left, right, st, np2, w, count):
+def conv_two(flags, c1, up, down, left, right, st, np2, w, count):
     r, scan_count, wide = c1.shape
-    wide = wide + 2 * L
     lanes = wide - L
     devices = st.shape[0]
     return pl.pallas_call(
@@ -516,8 +486,7 @@
         grid=(scan_count // S,),
         in_specs=[
             pl.BlockSpec(memory_space=pltpu.SMEM),
-            scans(r, wide - 2 * L),
-            scans(r, 2 * L),
+            held,
             scans(2, wide),
             scans(3, wide),
             scans(left.shape[0], L),
@@ -526,33 +495,29 @@
             whole(np2.shape),
             whole(w.shape),
         ],
-        out_specs=[
-            scans(r + 3, lanes),
-            scans(r + 1, wide),
-            scans(r + 2, wide),
-            whole((devices, 2, L)),
-        ],
+        out_specs=[held, held, scans(r + 2, wide), whole((devices, 2, L))],
         out_shape=[
-            jax.ShapeDtypeStruct((r + 3, scan_count, lanes), f32),
-            jax.ShapeDtypeStruct((r + 1, scan_count, wide), bf16),
-            jax.ShapeDtypeStruct((r + 2, scan_count, wide), bf16),
+            resident((r + 3, scan_count, lanes), f32),
+            resident((r + 1, scan_count, wide), bf16),
+            pltpu.HBM((r + 2, scan_count, wide), bf16),
             jax.ShapeDtypeStruct((devices, 2, L), f32),
         ],
         scratch_shapes=[
             pltpu.VMEM(((r + 5) // 2, 2, S, wide), bf16),
-            pltpu.VMEM((r, S, L), f32),
+            pltpu.VMEM((r + 5, S, L), f32),
             pltpu.VMEM((8, L), f32),
         ],
         compiler_params=params_of(),
         cost_estimate=cost(14),
         name="conv_two",
-    )(flags, c1, ends, up, down, left, right, st, np2, w)
+    )(flags, c1, up, down, left, right, st, np2, w)
 
 
 def output_kernel(
     c2_ref, st_ref, np_ref, cot_ref, up_ref, down_ref, feat_ref, d_ref, sum_ref, run, *, count,
 ):
     step, steps = (pl.program_id(0), pl.num_programs(0))
+    c2_ref, d_ref = (part_of(a, step) for a in (c2_ref, d_ref))
     r, tiles = (cot_ref.shape[0], cot_ref.shape[2] // L)
     mean, inv = stats_of(st_ref, count)
     offset = -mean * inv
@@ -610,24 +575,24 @@
         functools.partial(output_kernel, count=count),
         grid=(scan_count // S,),
         in_specs=[
-            scans(r + 3, lanes),
+            held,
             whole(st.shape),
             whole(np2.shape),
             scans(r, lanes),
             pl.BlockSpec((S, up.shape[1]), lambda g: (g, 0)),
             scans(2, lanes),
         ],
-        out_specs=[scans(r, lanes), scans(r + 3, lanes), whole((devices, 2, L))],
+        out_specs=[scans(r, lanes), held, whole((devices, 2, L))],
         out_shape=[
             jax.ShapeDtypeStruct((r, scan_count, lanes), bf16),
-            jax.ShapeDtypeStruct((r + 3, scan_count, lanes), f32),
+            resident((r + 3, scan_count, lanes), f32),
             jax.ShapeDtypeStruct((devices, 2, L), f32),
         ],
         scratch_shapes=[pltpu.VMEM((8, L), f32)],
         compiler_params=params_of(),
         cost_estimate=cost(12),
         name="output",
-    )(c2, st, np2, cot, up, down)
+    )(c2, st, np2, hbm(cot), up, down)
 
 
 def norm_back_two(flags, st_ref, sum_ref, np_ref, count, rows):
@@ -652,15 +617,15 @@
 
 
 def rim_two_kernel(
-    flags, da_ref, db_ref, ca_ref, cb_ref, st_ref, sum_ref, np_ref, er_ref, el_ref, *, count
+    flags, d_ref, c_ref, st_ref, sum_ref, np_ref, er_ref, el_ref, *, count
 ):
-    rows = da_ref.shape[0]
+    d_ref, c_ref = (part_of(a, pl.program_id(0)) for a in (d_ref, c_ref))
+    rows, last = (d_ref.shape[0], d_ref.shape[2] // L - 1)
     back = norm_back_two(flags, st_ref, sum_ref, np_ref, count, rows - 3)
     low = low_half()
     half = rows // 2
-    both = lambda row: jnp.where(
-        low, back(row, da_ref[row], ca_ref[row]), back(row, db_ref[row], cb_ref[row])
-    )
+    column = lambda row, t: back(row, pair(d_ref, row, t), pair(c_ref, row, t))
+    both = lambda row: jnp.where(low, column(row, 0), column(row, last))
     for k in range(half):
         near, far = (both(k), swap(both(k + half)))
         el_ref[k] = jnp.where(low, near, far).astype(bf16)
@@ -669,27 +634,26 @@
 
 def rim_two(flags, d, c2, st, sums, np2, count):
     rows, scan_count, lanes = d.shape
-    at = lambda k: pl.BlockSpec((rows, S, L), lambda g: (0, g, k))
-    last = lanes // L - 1
     return pl.pallas_call(
         functools.partial(rim_two_kernel, count=count),
         grid=(scan_count // S,),
         in_specs=[
-            pl.BlockSpec(memory_space=pltpu.SMEM), at(0), at(last), at(0), at(last),
-            whole(st.shape), whole(sums.shape), whole(np2.shape),
+            pl.BlockSpec(memory_space=pltpu.SMEM), held, held, whole(st.shape),
+            whole(sums.shape), whole(np2.shape),
         ],
         out_specs=[scans(rows // 2, L)] * 2,
         out_shape=[jax.ShapeDtypeStruct((rows // 2, scan_count, L), bf16)] * 2,
         compiler_params=params_of(),
         cost_estimate=cost(3),
         name="rim_two",
-    )(flags, d, d, c2, c2, st, sums, np2)
+    )(flags, d, c2, st, sums, np2)
 
 
 def back_two_kernel(
     flags, d_ref, c2_ref, hid_ref, st_ref, sum_ref, np_ref, ds_ref, kg_ref, grad, *, count
 ):
     step, steps = (pl.program_id(0), pl.num_programs(0))
+    d_ref, c2_ref, ds_ref = (part_of(a, step) for a in (d_ref, c2_ref, ds_ref))
     r, tiles = (c2_ref.shape[0] - 3, c2_ref.shape[2] // L)
     back = norm_back_two(flags, st_ref, sum_ref, np_ref, count, r)
 
@@ -731,29 +695,30 @@
         grid=(scan_count // S,),
         in_specs=[
             pl.BlockSpec(memory_space=pltpu.SMEM),
-            scans(r + 3, lanes),
-            scans(r + 3, lanes),
+            held,
+            held,
             scans(r + 2, wide),
             whole(st.shape),
             whole(sums.shape),
             whole(np2.shape),
         ],
-        out_specs=[scans(r + 3, lanes), whole((9, C, C))],
+        out_specs=[held, whole((9, C, C))],
         out_shape=[
-            jax.ShapeDtypeStruct((r + 3, scan_count, lanes), bf16),
+            resident((r + 3, scan_count, lanes), bf16),
             jax.ShapeDtypeStruct((9, C, C), f32),
         ],
         scratch_shapes=[pltpu.VMEM((L, 12 * C), f32)],
         compiler_params=params_of(),
         cost_estimate=cost(12),
         name="back_two",
-    )(flags, d, c2, hid, st, sums, np2)
+    )(flags, d, c2, hbm(hid), st, sums, np2)
 
 
 def hidden_kernel(
     ds_ref, left_ref, right_ref, n1_ref, np_ref, w_ref, dp_ref, edge_ref, sum1_ref, rim, run
 ):
     step, steps = (pl.program_id(0), pl.num_programs(0))
+    ds_ref, n1_ref, dp_ref = (part_of(a, step) for a in (ds_ref, n1_ref, dp_ref))
     r, tiles = (n1_ref.shape[0] - 1, n1_ref.shape[2] // L)
     pairs = (r + 1) // 2
     low = low_half()
@@ -797,20 +762,20 @@
         hidden_kernel,
         grid=(scan_count // S,),
         in_specs=[
-            scans(r + 3, lanes),
+            held,
             scans(half, L),
             scans(half, L),
-            scans(r + 1, wide),
+            held,
             whole(np2.shape),
             whole(w.shape),
         ],
         out_specs=[
-            scans(r + 1, wide),
+            held,
             scans((r + 1) // 2, L),
             whole((devices, 2, L)),
         ],
         out_shape=[
-            jax.ShapeDtypeStruct((r + 1, scan_count, wide), f32),
+            resident((r + 1, scan_count, wide), f32),
             jax.ShapeDtypeStruct(((r + 1) // 2, scan_count, L), bf16),
             jax.ShapeDtypeStruct((devices, 2, L), f32),
         ],
@@ -826,6 +791,7 @@
     xm, grad, *, count,
 ):
     step, steps = (pl.program_id(0), pl.num_programs(0))
+    dp_ref, n1_ref = (part_of(a, step) for a in (dp_ref, n1_ref))
     r, tiles = (n1_ref.shape[0] - 1, n1_ref.shape[2] // L - 1)
     cells = 2.0 * count * st_ref.shape[0]
     _mean, inv = stats_of(st_ref, count)
@@ -909,9 +875,9 @@
         grid=(scan_count // S,),
         in_specs=[
             pl.BlockSpec(memory_space=pltpu.SMEM),
-            scans(r + 1, wide),
+            held,
             scans(edge.shape[0], L),
-            scans(r + 1, wide),
+            held,
             scans(rows, lanes),
             scans(bits.shape[0], lanes),
             whole(st.shape),
@@ -921,7 +887,7 @@
         ],
         out_specs=[scans(r + 1, wide), whole((devices * share, L))],
         out_shape=[
-            jax.ShapeDtypeStruct((r + 1, scan_count, wide), bf16),
+            pltpu.HBM((r + 1, scan_count, wide), bf16),
             jax.ShapeDtypeStruct((devices * share, L), f32),
         ],
         scratch_shapes=[
@@ -931,7 +897,7 @@
         compiler_params=params_of(),
         cost_estimate=cost(16),
         name="back_one",
-    )(flags, dp, edge, n1, x, bits, st, sums, np2, kg2)
+    )(flags, dp, edge, n1, hbm(x), bits, st, sums, np2, kg2)
 
 
 def input_grad_kernel(ds, bits_ref, w_ref, *rest):
@@ -971,7 +937,29 @@
         compiler_params=params_of(),
         cost_estimate=cost(7),
         name="input_gradient",
-    )(d, bits, w, *earlier)
+    )(hbm(d), hbm(bits), w, *earlier)
+
+
+def share_kernel(g_ref, out_ref):
+    devices, share, _lanes = g_ref.shape
+    total = g_ref[0]
+    for k in range(1, devices):
+        total = total + g_ref[k]
+    for k in range(devices):
+        out_ref[k] = total
+
+
+def sum_share(grads, share):
+    shape = (grads.shape[0] // share, share, L)
+    return pl.pallas_call(
+        share_kernel,
+        in_specs=[held],
+        out_specs=held,
+        out_shape=jax.ShapeDtypeStruct(shape, f32),
+        compiler_params=pltpu.CompilerParams(vmem_limit_bytes=8 << 20),
+        cost_estimate=cost(1),
+        name="sum_share",
+    )(grads.reshape(shape)).reshape(grads.shape)
 
 
 def adam_step(weight_now, gradient, moment_one, moment_two, step_rate, decay_rate):
@@ -1079,26 +1067,17 @@
     )
     bits, w1, w2, w2b, w1b, np2 = prepare(occ, kt, norm_params)
 
-    ends, st1, going_right, going_left, edge = first_last(x, bits, down, xcol, corner, w1)
+    xcol, cot_down, flags = lax.optimization_barrier((xcol, cot_down, flags))
+    c1, st1, up, low_rows, edge = conv_one(x, bits, down, xcol, corner, w1, devices)
+    down_in = shifted(up, "gy", -1)
+    up_in = shifted(low_rows, "gy", 1)
+    going_right, going_left = pack_edges(up_in, edge, down_in)
     left_in = shifted(going_right, "gx", 1)
     right_in = shifted(going_left, "gx", -1)
-    c1, st1, up, low_rows = conv_one(x, bits, down, st1, w1, devices)
-    half = (r + 1) // 2
-
-    def beyond(a, b):
-        near, far = (slice(0, C), slice(C, L))
-        if a >= half:
-            a, b, near, far = (a - half, b - half, far, near)
-        return jnp.concatenate([left_in[a:b, :, near], right_in[a:b, :, far]], axis=2)
-
-    up = jnp.concatenate([up, edge[:3], beyond(0, 3)], axis=2)
-    low_rows = jnp.concatenate([low_rows, edge[r - 2 :], beyond(r - 2, r)], axis=2)
-    down_in = shifted(up, "gy", -1)
-    up_in = shifted(low_rows, "gy", 1)
     st1 = exchange(st1)
 
     c2, n1, hid, st2 = conv_two(
-        flags, c1, ends, up_in, down_in, left_in, right_in, st1, np2, w2, count
+        flags, c1, up_in, down_in, left_in, right_in, st1, np2, w2, count
     )
     st2 = exchange(st2)
     features, d2, sums2 = output(c2, st2, np2, cot, down, cot_down, count)
@@ -1114,8 +1093,7 @@
     share = grads.shape[0] // devices
     grads = exchange(grads)
     input_grad = input_gradient(d1, bits, w1b, 0, None)
-    mine = jnp.sum(grads.reshape(devices, share, L), axis=0)
-    grads = exchange(jnp.broadcast_to(mine[None], (devices, share, L)).reshape(-1, L))
+    grads = exchange(sum_share(grads, share))
     input_grad = input_gradient(d1, bits, w1b, 1, input_grad)
     norm, k, km, kv, low, n, nm, nv = update(
         grads, sums1, sums2, kt, kmt, kvt, norm_params, norm_m, norm_v

time: 219 us -> 187 us (0.85)
  Pallas kernels: 111 us -> 83.6 us
  blocking collectives: 39.9 us -> 64.7 us
  starting transfers between devices: 41.6 us -> 31.3 us
  waiting for transfers between devices: 14.7 us -> 5.62 us
  local copies, waits for them, and re-layouts: 7.13 us -> 0.03 us
  other arithmetic: 2.79 us -> 0.08 us
    all_to_all x3 -> x5, blocking collectives: 39.9 us -> 64.7 us  [exchange(): return lax.all_to_all(rows, BOTH, 0, 0, tiled=True)]
    all_to_all x3 -> x1, waiting for transfers between devices: 13.9 us -> 0.29 us  [exchange(): return lax.all_to_all(rows, BOTH, 0, 0, tiled=True)]
    all_to_all x3 -> x1, starting transfers between devices: 13.2 us -> 2.59 us  [exchange(): return lax.all_to_all(rows, BOTH, 0, 0, tiled=True)]
    pallas_call x2 -> x3, Pallas kernels: 17.8 us -> 8.97 us  [the longest x1 7.51 us: hidden_gradient(): pl.pallas_call(hidden_kernel, grid=(scan_count // S,), in_specs=[held, sc...]
    ppermute x10, waiting for transfers between devices: 0.08 us -> 5.16 us  [shifted(): return lax.ppermute(block, axis, route)]
    unnamed x30 -> x14, local copies, waits for them, and re-layouts: 4.6 us -> 0.03 us
    pallas_call x1, Pallas kernels: 11.1 us -> 6.97 us  [back_two(): pl.pallas_call(functools.partial(back_two_kernel, count=count), grid=(sca...]
    pallas_call x1, Pallas kernels: 12.9 us -> 9.34 us  [conv_two(): pl.pallas_call(functools.partial(conv_two_kernel, count=count), grid=(sca...]
  transfers between devices with their start and end apart: 14 -> 12, of which waited for: 5 -> 5; matrix products, arithmetic and copies ran while one was open for 2% -> 0% of each run, Pallas kernels for 25% -> 12%
where the time goes in v3:
time: 187 us; the launch traced here: 186 us
  Pallas kernels  83.6 us (45%)
  blocking collectives  64.7 us (35%)
  starting transfers between devices  31.3 us (17%)
  waiting for transfers between devices  5.62 us (3%)
    all_to_all x5, blocking collectives, exchange(): return lax.all_to_all(rows, BOTH, 0, 0, tiled=True)  64.7 us
    ppermute x10, starting transfers between devices, shifted(): return lax.ppermute(block, axis, route)  23 us
    pallas_call x1, Pallas kernels, back_one(): pl.pallas_call(functools.partial(back_one_kernel, count=count), grid=(sca...  14.6 us
    pallas_call x2, Pallas kernels, input_gradient(): pl.pallas_call(input_grad_kernel, grid=(steps,), in_specs=[at(r, wide), a...  13.2 us
    pallas_call x1, Pallas kernels, conv_one(): pl.pallas_call(conv_one_kernel, grid=(scan_count // S,), in_specs=[scans(...  13 us
    pallas_call x1, Pallas kernels, conv_two(): pl.pallas_call(functools.partial(conv_two_kernel, count=count), grid=(sca...  9.34 us
    pallas_call x1, Pallas kernels, output(): pl.pallas_call(functools.partial(output_kernel, count=count), grid=(scan_...  8.83 us
    pallas_call x1, Pallas kernels, hidden_gradient(): pl.pallas_call(hidden_kernel, grid=(scan_count // S,), in_specs=[held, sc...  7.51 us
  transfers between devices with their start and end apart: 12, of which 5 were waited for; matrix products, arithmetic and copies ran while one was open for 0% of the time, Pallas kernels for 12%

profile of v3, /device:TPU:0, one launch (start us, length us, event | category | flops | bytes accessed | tf_op | source)
XLA Modules:
  0.0 186.2 jit_solution(5050918228224397169)
XLA Ops:
  0.7 3.1 %edges.1 = (bf16[64,2688]{1,0:T(8,128)(2,1)}, bf16[2,64,896]{2,1,0:T(8,128)(2,1)}, bf16[64,128]{1,0:T(8,128)(2,1)S(1)}, bf16[31,64,128]{2,1,0:T(8,128)(2,1)S(1)}) custom-call(bf16[62,64,1792]{2,1,0:T(8,128)(2,1)} %bitcast.35, bf16[62,64,1792]{2,1,0:T(8,128)(2,1)} %bitcast.36, s32[28,64,62]{2,1,0:T(8,128)} %bitcast.43, bf16[31,64,896]{2,1,0:T(8,128)(2,1)} %bitcast.40, ...), custom_call_target="tpu_custom_call" | custom-call | bytes 10800000 | tf_op jit(solution)/shard_map/edges/pallas_call | solution.py:197
  3.8 4.9 %collective-permute-start = (bf16[31,64,128]{2,1,0:T(8,128)(2,1)S(1)}, bf16[31,64,128]{2,1,0:T(8,128)(2,1)S(1)}, u32[]{:S(2)}, u32[]{:S(2)}) collective-permute-start(bf16[31,64,128]{2,1,0:T(8,128)(2,1)S(1)} %get-tuple-element.54), channel_id=1, source_target_pairs={{0,1},{1,2},{2,3},{3,4},{4,5},{5,6},{6,7},{8,9},{9,10},{10,11},{11... | collective-permute-start | bytes 1523720 | tf_op jit(solution)/shard_map/ppermute | solution.py:1038
  8.7 1.5 collective-permute-start.2
  10.2 1.3 collective-permute-start.1
  11.5 5.7 %collective-permute-start.3 = (bf16[64,128]{1,0:T(8,128)(2,1)S(1)}, bf16[64,128]{1,0:T(8,128)(2,1)S(1)}, u32[]{:S(2)}, u32[]{:S(2)}) collective-permute-start(bf16[64,128]{1,0:T(8,128)(2,1)S(1)} %get-tuple-element.60), channel_id=1, source_target_pairs={{0,9},{1,10},{2,11},{3,12},{4,13},{5,14},{6,15},{8,17},{9,18},{10,... | collective-permute-start | bytes 49160 | tf_op jit(solution)/shard_map/ppermute | solution.py:1065
  17.3 2.2 %prepare.1 = (s16[5,64,1792]{2,1,0:T(8,128)(2,1)S(1)}, bf16[1920,256]{1,0:T(8,128)(2,1)S(1)}, bf16[1024,256]{1,0:T(8,128)(2,1)S(1)}, bf16[1024,256]{1,0:T(8,128)...) custom-call(s32[28,64,62]{2,1,0:T(8,128)} %bitcast.44, f32[2,64,576]{2,1,0:T(8,128)S(1)} %bitcast.26, ...), custom_call_target="tpu_custom_call" | custom-call | bytes 14400000 | tf_op jit(solution)/shard_map/prepare/pallas_call | solution.py:258
  19.8 13.0 %conv_one.1 = (f32[31,64,1024]{2,1,0:T(8,128)S(1)}, f32[32,2,128]{2,1,0:T(2,128)S(1)}, bf16[3,64,1024]{2,1,0:T(8,128)(2,1)S(1)}, bf16[2,64,1024]{2,1,0:T(8,128)(2,1)S(1)}, bf16[31,64,128]{2,1,0:T(8,128)(2,1)S(1)}) custom-call(bf16[62,64,1792]{2,1,0:T(8,128)(2,1)} %bitcast.37, s16[5,64,1792]{2,1,0:T(8,128)(2,1)S(1)} %get-tuple-element.57.bits_ref, ...), custom_call_target="tpu_custom_call" | custom-call | bytes 46800000 | tf_op jit(solution)/shard_map/conv_one/pallas_call | solution.py:349
  32.8 1.3 collective-permute-start.5
  34.1 4.1 %collective-permute-start.4 = (bf16[2,64,1024]{2,1,0:T(8,128)(2,1)S(1)}, bf16[2,64,1024]{2,1,0:T(8,128)(2,1)S(1)}, u32[]{:S(2)}, u32[]{:S(2)}) collective-permute-start(bf16[2,64,1024]{2,1,0:T(8,128)(2,1)S(1)} %get-tuple-element.63), channel_id=1, source_target_pairs={{0,8},{8,16},{16,24},{1,9},{9,17},{17,25},{2,10},{10,18},{18,26},{... | collective-permute-start | bytes 786440 | tf_op jit(solution)/shard_map/ppermute | solution.py:1038
  38.3 1.1 collective-permute-done.4.up_ref
  40.1 3.4 %collective-permute-start.6 = (bf16[18,64,128]{2,1,0:T(8,128)(2,1)S(1)}, bf16[18,64,128]{2,1,0:T(8,128)(2,1)S(1)}, u32[]{:S(2)}, u32[]{:S(2)}) collective-permute-start(bf16[18,64,128]{2,1,0:T(8,128)(2,1)S(1)} %get-tuple-element.66), channel_id=1, source_target_pairs={{0,1},{1,2},{2,3},{3,4},{4,5},{5,6},{6,7},{8,9},{9,10},{10,11},{11... | collective-permute-start | bytes 884744 | tf_op jit(solution)/shard_map/ppermute | solution.py:1038
  43.5 1.3 collective-permute-start.7
  44.8 18.9 %all_to_all.37.st_ref = f32[32,2,128]{2,1,0:T(2,128)S(1)} all-to-all(f32[32,2,128]{2,1,0:T(2,128)S(1)} %get-tuple-element.68), channel_id=1, replica_groups=mesh['gy'=4,'gx'=8] {'gy','gx'}, dimensions={0} | all-to-all | bytes 65536 | tf_op jit(solution)/shard_map/all_to_all | solution.py:1042
  63.7 9.3 %conv_two.1 = (f32[34,64,896]{2,1,0:T(8,128)S(1)}, bf16[32,64,1024]{2,1,0:T(8,128)(2,1)S(1)}, bf16[33,64,1024]{2,1,0:T(8,128)(2,1)}, f32[32,2,128]{2,1,0:T(2,128)S(1)}) custom-call(s32[4]{0:T(128)S(1)} %add_convert_fusion.flags, f32[31,64,1024]{2,1,0:T(8,128)S(1)} %get-tuple-element.62.c_ref, bf16[2,64,1024]{2,1,0:T(8,128)(2,1)S(1)} %collective-permute-done.4.up_ref, ...), custom_call_target="tpu_custom_call" | custom-call | bytes 50400000 | tf_op jit(solution)/shard_map/conv_two/pallas_call | solution.py:484
  73.0 8.9 %all_to_all.38.st_ref = f32[32,2,128]{2,1,0:T(2,128)S(1)} all-to-all(f32[32,2,128]{2,1,0:T(2,128)S(1)} %get-tuple-element.72), channel_id=1, replica_groups=mesh['gy'=4,'gx'=8] {'gy','gx'}, dimensions={0} | all-to-all | bytes 65536 | tf_op jit(solution)/shard_map/all_to_all | solution.py:1042
  81.9 8.8 %output.1 = (bf16[31,64,896]{2,1,0:T(8,128)(2,1)}, f32[34,64,896]{2,1,0:T(8,128)S(1)}, f32[32,2,128]{2,1,0:T(2,128)S(1)}) custom-call(f32[34,64,896]{2,1,0:T(8,128)S(1)} %get-tuple-element.71.c2_ref.c_ref, f32[32,2,128]{2,1,0:T(2,128)S(1)} %all_to_all.38.st_ref, f32[4,128]{1,0:T(4,128)S(1)} %get-tuple-element.69.np_ref, bf16[31,64,896]{2,1,0:T(8,128)(2,1)} %bitcast.42, ...), custom_call_target="tpu_custom_call" | custom-call | bytes 43200000 | tf_op jit(solution)/shard_map/output/pallas_call | solution.py:574
  90.7 8.9 %all_to_all.39.sum_ref.s2_ref = f32[32,2,128]{2,1,0:T(2,128)S(1)} all-to-all(f32[32,2,128]{2,1,0:T(2,128)S(1)} %get-tuple-element.77), channel_id=1, replica_groups=mesh['gy'=4,'gx'=8] {'gy','gx'}, dimensions={0} | all-to-all | bytes 65536 | tf_op jit(solution)/shard_map/all_to_all | solution.py:1042
  99.6 1.9 rim_two.1
  101.4 2.6 %collective-permute-start.8 = (bf16[17,64,128]{2,1,0:T(8,128)(2,1)S(1)}, bf16[17,64,128]{2,1,0:T(8,128)(2,1)S(1)}, u32[]{:S(2)}, u32[]{:S(2)}) collective-permute-start(bf16[17,64,128]{2,1,0:T(8,128)(2,1)S(1)} %get-tuple-element.79), channel_id=1, source_target_pairs={{0,1},{1,2},{2,3},{3,4},{4,5},{5,6},{6,7},{8,9},{9,10},{10,11},{11... | collective-permute-start | bytes 835592 | tf_op jit(solution)/shard_map/ppermute | solution.py:1038
  104.0 1.3 collective-permute-start.9
  105.3 7.0 %back_two.1 = (bf16[34,64,896]{2,1,0:T(8,128)(2,1)S(1)}, f32[9,64,64]{2,1,0:T(8,128)S(1)}) custom-call(s32[4]{0:T(128)S(1)} %add_convert_fusion.flags, f32[34,64,896]{2,1,0:T(8,128)S(1)} %get-tuple-element.75.d_ref, f32[34,64,896]{2,1,0:T(8,128)S(1)} %get-tuple-element.71.c2_ref.c_ref, bf16[33,64,1024]{2,1,0:T(8,128)(2,1)} %get-tuple-element.76.hid_ref, ...), custom_call_target="tpu_custom_call" | custom-call | bytes 43200000 | tf_op jit(solution)/shard_map/back_two/pallas_call | solution.py:693
  112.3 3.9 %collective-permute-done.8.left_ref = bf16[17,64,128]{2,1,0:T(8,128)(2,1)S(1)} collective-permute-done((bf16[17,64,128]{2,1,0:T(8,128)(2,1)S(1)}, bf16[17,64,128]{2,1,0:T(8,128)(2,1)S(1)}, u32[]{:S(2)}, u32[]{:S(2)}) %collective-permute-start.8) | collective-permute-done | bytes 278560 | tf_op jit(solution)/shard_map/ppermute | solution.py:1038
  116.2 7.5 %hidden_gradient.1 = (f32[32,64,1024]{2,1,0:T(8,128)S(1)}, bf16[16,64,128]{2,1,0:T(8,128)(2,1)S(1)}, f32[32,2,128]{2,1,0:T(2,128)S(1)}) custom-call(bf16[34,64,896]{2,1,0:T(8,128)(2,1)S(1)} %get-tuple-element.78.ds_ref, bf16[17,64,128]{2,1,0:T(8,128)(2,1)S(1)} %collective-permute-done.8.left_ref, bf16[17,64,128]{2,1,0:T(8,128)(2,1)S(1)} %collective-permute-done.9.right_ref, ...), custom_call_target="tpu_custom_call" | custom-call | bytes 43200000 | tf_op jit(solution)/shard_map/hidden_gradient/pallas_call | solution.py:761
  123.7 1.3 collective-permute-start.10
  125.0 12.8 %all_to_all.40.sum_ref.s1_ref = f32[32,2,128]{2,1,0:T(2,128)S(1)} all-to-all(f32[32,2,128]{2,1,0:T(2,128)S(1)} %get-tuple-element.85), channel_id=1, replica_groups=mesh['gy'=4,'gx'=8] {'gy','gx'}, dimensions={0} | all-to-all | bytes 65536 | tf_op jit(solution)/shard_map/all_to_all | solution.py:1042
  137.8 14.6 %back_one.1 = (bf16[32,64,1024]{2,1,0:T(8,128)(2,1)}, f32[768,128]{1,0:T(8,128)S(1)}) custom-call(s32[4]{0:T(128)S(1)} %add_convert_fusion.flags, f32[32,64,1024]{2,1,0:T(8,128)S(1)} %get-tuple-element.83.dp_ref, bf16[16,64,128]{2,1,0:T(8,128)(2,1)S(1)} %collective-permute-done.10.edge_ref, bf16[32,64,1024]{2,1,0:T(8,128)(2,1)S(1)} %get-tuple-element.81.n1_ref, ...), custom_call_target="tpu_custom_call" | custom-call | bytes 57600000 | tf_op jit(solution)/shard_map/back_one/pallas_call | solution.py:873
  152.5 15.2 %all_to_all.41.g_ref = f32[32,24,128]{2,1,0:T(8,128)S(1)} all-to-all(f32[32,24,128]{2,1,0:T(8,128)S(1)} %bitcast.28), channel_id=1, replica_groups=mesh['gy'=4,'gx'=8] {'gy','gx'}, dimensions={0} | all-to-all | bytes 786432 | tf_op jit(solution)/shard_map/all_to_all | solution.py:1042
  167.7 0.8 sum_share.1
  168.5 2.6 %all-to-all-start.5 = ((f32[32,24,128]{2,1,0:T(8,128)}), f32[32,24,128]{2,1,0:T(8,128)S(1)}, u32[]{:S(2)}, u32[]{:S(2)}) async-start(f32[32,24,128]{2,1,0:T(8,128)} %sum_share.1), calls=%async_computation.5 | async-start | bytes 786432 | tf_op jit(solution)/shard_map/all_to_all | solution.py:1042
  171.1 6.6 %input_gradient.2.rest_0_ = bf16[62,64,1792]{2,1,0:T(8,128)(2,1)} custom-call(bf16[32,64,1024]{2,1,0:T(8,128)(2,1)} %get-tuple-element.87.ds, s16[5,64,1792]{2,1,0:T(8,128)(2,1)} %copy-done, bf16[768,256]{1,0:T(8,128)(2,1)S(1)} %get-tuple-element.88.w_ref), custom_call_target="tpu_custom_call" | custom-call | bytes 25200000 | tf_op jit(solution)/shard_map/input_gradient/pallas_call | solution.py:929
  177.7 6.6 %input_gradient.3 = bf16[62,64,1792]{2,1,0:T(8,128)(2,1)} custom-call(bf16[32,64,1024]{2,1,0:T(8,128)(2,1)} %get-tuple-element.87.ds, s16[5,64,1792]{2,1,0:T(8,128)(2,1)} %copy-done, bf16[768,256]{1,0:T(8,128)(2,1)S(1)} %get-tuple-element.88.w_ref, bf16[62,64,1792]{2,1,0:T(8,128)(2,1)} %input_gradient.2.rest_0_), custom_call_target="tpu_custom_call", output_to_operand_aliasing={{}: (3, {})} | custom-call | bytes 25200000 | tf_op jit(solution)/shard_map/input_gradient/pallas_call | solution.py:929
  184.7 1.5 update.1
  (26 shorter events, 1.4 us)
Async XLA Ops:
  0.6 16.6 %copy-start.1 = (f32[2,576,64]{1,2,0:T(8,128)S(1)}, f32[2,576,64]{1,2,0:T(8,128)}, u32[]{:S(2)}) copy-start(f32[2,576,64]{1,2,0:T(8,128)} %param.11) | copy-start | bytes 884740
  0.7 16.6 %copy-start.4 = (f32[2,2,64]{2,1,0:T(2,128)S(1)}, f32[2,2,64]{2,1,0:T(2,128)}, u32[]{:S(2)}) copy-start(f32[2,2,64]{2,1,0:T(2,128)} %param.14) | copy-start | bytes 3076
  3.8 15.8 %collective-permute-start = (bf16[31,64,128]{2,1,0:T(8,128)(2,1)S(1)}, bf16[31,64,128]{2,1,0:T(8,128)(2,1)S(1)}, u32[]{:S(2)}, u32[]{:S(2)}) collective-permute-start(bf16[31,64,128]{2,1,0:T(8,128)(2,1)S(1)} %get-tuple-element.54), channel_id=1, source_target_pairs={{0,1},{1,2},{2,3},{3,4},{4,5},{5,6},{6,7},{8,9},{9,10},{10,11},{11... | collective-permute-start | bytes 1523720 | tf_op jit(solution)/shard_map/ppermute | solution.py:1038
  8.7 11.1 %collective-permute-start.2 = (bf16[64,2688]{1,0:T(8,128)(2,1)}, bf16[64,2688]{1,0:T(8,128)(2,1)S(1)}, u32[]{:S(2)}, u32[]{:S(2)}) collective-permute-start(bf16[64,2688]{1,0:T(8,128)(2,1)} %get-tuple-element.58), channel_id=1, source_target_pairs={{0,8},{8,16},{16,24},{1,9},{9,17},{17,25},{2,10},{10,18},{18,26},{... | collective-permute-start | bytes 1032200 | tf_op jit(solution)/shard_map/ppermute | solution.py:1038
  10.2 9.3 %collective-permute-start.1 = (bf16[2,64,896]{2,1,0:T(8,128)(2,1)}, bf16[2,64,896]{2,1,0:T(8,128)(2,1)S(1)}, u32[]{:S(2)}, u32[]{:S(2)}) collective-permute-start(bf16[2,64,896]{2,1,0:T(8,128)(2,1)} %get-tuple-element.55), channel_id=1, source_target_pairs={{8,0},{16,8},{24,16},{9,1},{17,9},{25,17},{10,2},{18,10},{26,18},{... | collective-permute-start | bytes 688136 | tf_op jit(solution)/shard_map/ppermute | solution.py:1038
  11.5 8.3 %collective-permute-start.3 = (bf16[64,128]{1,0:T(8,128)(2,1)S(1)}, bf16[64,128]{1,0:T(8,128)(2,1)S(1)}, u32[]{:S(2)}, u32[]{:S(2)}) collective-permute-start(bf16[64,128]{1,0:T(8,128)(2,1)S(1)} %get-tuple-element.60), channel_id=1, source_target_pairs={{0,9},{1,10},{2,11},{3,12},{4,13},{5,14},{6,15},{8,17},{9,18},{10,... | collective-permute-start | bytes 49160 | tf_op jit(solution)/shard_map/ppermute | solution.py:1065
  19.4 118.4 %copy-start = (s16[5,64,1792]{2,1,0:T(8,128)(2,1)}, s16[5,64,1792]{2,1,0:T(8,128)(2,1)S(1)}, u32[]{:S(2)}) copy-start(s16[5,64,1792]{2,1,0:T(8,128)(2,1)S(1)} %get-tuple-element.57.bits_ref) | copy-start | bytes 3440644
  32.8 6.6 %collective-permute-start.5 = (bf16[3,64,1024]{2,1,0:T(8,128)(2,1)S(1)}, bf16[3,64,1024]{2,1,0:T(8,128)(2,1)S(1)}, u32[]{:S(2)}, u32[]{:S(2)}) collective-permute-start(bf16[3,64,1024]{2,1,0:T(8,128)(2,1)S(1)} %get-tuple-element.64), channel_id=1, source_target_pairs={{8,0},{16,8},{24,16},{9,1},{17,9},{25,17},{10,2},{18,10},{26,18},{... | collective-permute-start | bytes 1179656 | tf_op jit(solution)/shard_map/ppermute | solution.py:1038
  34.1 5.3 %collective-permute-start.4 = (bf16[2,64,1024]{2,1,0:T(8,128)(2,1)S(1)}, bf16[2,64,1024]{2,1,0:T(8,128)(2,1)S(1)}, u32[]{:S(2)}, u32[]{:S(2)}) collective-permute-start(bf16[2,64,1024]{2,1,0:T(8,128)(2,1)S(1)} %get-tuple-element.63), channel_id=1, source_target_pairs={{0,8},{8,16},{16,24},{1,9},{9,17},{17,25},{2,10},{10,18},{18,26},{... | collective-permute-start | bytes 786440 | tf_op jit(solution)/shard_map/ppermute | solution.py:1038
  40.1 23.6 %collective-permute-start.6 = (bf16[18,64,128]{2,1,0:T(8,128)(2,1)S(1)}, bf16[18,64,128]{2,1,0:T(8,128)(2,1)S(1)}, u32[]{:S(2)}, u32[]{:S(2)}) collective-permute-start(bf16[18,64,128]{2,1,0:T(8,128)(2,1)S(1)} %get-tuple-element.66), channel_id=1, source_target_pairs={{0,1},{1,2},{2,3},{3,4},{4,5},{5,6},{6,7},{8,9},{9,10},{10,11},{11... | collective-permute-start | bytes 884744 | tf_op jit(solution)/shard_map/ppermute | solution.py:1038
  43.5 20.2 %collective-permute-start.7 = (bf16[18,64,128]{2,1,0:T(8,128)(2,1)S(1)}, bf16[18,64,128]{2,1,0:T(8,128)(2,1)S(1)}, u32[]{:S(2)}, u32[]{:S(2)}) collective-permute-start(bf16[18,64,128]{2,1,0:T(8,128)(2,1)S(1)} %get-tuple-element.67), channel_id=1, source_target_pairs={{1,0},{2,1},{3,2},{4,3},{5,4},{6,5},{7,6},{9,8},{10,9},{11,10},{12... | collective-permute-start | bytes 884744 | tf_op jit(solution)/shard_map/ppermute | solution.py:1038
  101.4 14.7 %collective-permute-start.8 = (bf16[17,64,128]{2,1,0:T(8,128)(2,1)S(1)}, bf16[17,64,128]{2,1,0:T(8,128)(2,1)S(1)}, u32[]{:S(2)}, u32[]{:S(2)}) collective-permute-start(bf16[17,64,128]{2,1,0:T(8,128)(2,1)S(1)} %get-tuple-element.79), channel_id=1, source_target_pairs={{0,1},{1,2},{2,3},{3,4},{4,5},{5,6},{6,7},{8,9},{9,10},{10,11},{11... | collective-permute-start | bytes 835592 | tf_op jit(solution)/shard_map/ppermute | solution.py:1038
  104.0 12.1 %collective-permute-start.9 = (bf16[17,64,128]{2,1,0:T(8,128)(2,1)S(1)}, bf16[17,64,128]{2,1,0:T(8,128)(2,1)S(1)}, u32[]{:S(2)}, u32[]{:S(2)}) collective-permute-start(bf16[17,64,128]{2,1,0:T(8,128)(2,1)S(1)} %get-tuple-element.80), channel_id=1, source_target_pairs={{1,0},{2,1},{3,2},{4,3},{5,4},{6,5},{7,6},{9,8},{10,9},{11,10},{12... | collective-permute-start | bytes 835592 | tf_op jit(solution)/shard_map/ppermute | solution.py:1038
  123.7 14.1 %collective-permute-start.10 = (bf16[16,64,128]{2,1,0:T(8,128)(2,1)S(1)}, bf16[16,64,128]{2,1,0:T(8,128)(2,1)S(1)}, u32[]{:S(2)}, u32[]{:S(2)}) collective-permute-start(bf16[16,64,128]{2,1,0:T(8,128)(2,1)S(1)} %get-tuple-element.84), channel_id=1, source_target_pairs={{1,0},{2,1},{3,2},{4,3},{5,4},{6,5},{7,6},{9,8},{10,9},{11,10},{12... | collective-permute-start | bytes 786440 | tf_op jit(solution)/shard_map/ppermute | solution.py:1038
  168.5 16.1 %all-to-all-start.5 = ((f32[32,24,128]{2,1,0:T(8,128)}), f32[32,24,128]{2,1,0:T(8,128)S(1)}, u32[]{:S(2)}, u32[]{:S(2)}) async-start(f32[32,24,128]{2,1,0:T(8,128)} %sum_share.1), calls=%async_computation.5 | async-start | bytes 786432 | tf_op jit(solution)/shard_map/all_to_all | solution.py:1042
  177.7 7.0 %copy-start.2 = (f32[2,576,64]{1,2,0:T(8,128)S(1)}, f32[2,576,64]{1,2,0:T(8,128)}, u32[]{:S(2)}) copy-start(f32[2,576,64]{1,2,0:T(8,128)} %param.12) | copy-start | bytes 884740
  177.7 7.0 %copy-start.3 = (f32[2,576,64]{1,2,0:T(8,128)S(1)}, f32[2,576,64]{1,2,0:T(8,128)}, u32[]{:S(2)}) copy-start(f32[2,576,64]{1,2,0:T(8,128)} %param.13) | copy-start | bytes 884740
  177.7 7.0 %copy-start.5 = (f32[2,2,64]{2,1,0:T(2,128)S(1)}, f32[2,2,64]{2,1,0:T(2,128)}, u32[]{:S(2)}) copy-start(f32[2,2,64]{2,1,0:T(2,128)} %param.15) | copy-start | bytes 3076
  177.7 7.0 %copy-start.6 = (f32[2,2,64]{2,1,0:T(2,128)S(1)}, f32[2,2,64]{2,1,0:T(2,128)}, u32[]{:S(2)}) copy-start(f32[2,2,64]{2,1,0:T(2,128)} %param.16) | copy-start | bytes 3076

commit v4 on v2

--- a/solution.py
+++ b/solution.py
@@ -19,10 +19,10 @@
 
 f32, bf16 = (jnp.float32, jnp.bfloat16)
 BOTH = ("gy", "gx")
-S, C, L, BITS = (16, 64, 128, 13)
-
-
-def params_of(limit=56):
+S, S2, C, L, BITS = (16, 32, 64, 128, 13)
+
+
+def params_of(limit=20):
     return pltpu.CompilerParams(
         dimension_semantics=("arbitrary",), vmem_limit_bytes=limit << 20
     )
@@ -38,8 +38,27 @@
     return pl.BlockSpec(shape, lambda g: (0,) * len(shape))
 
 
-def scans(rows, lanes):
-    return pl.BlockSpec((rows, S, lanes), lambda g: (0, g, 0))
+def scans(rows, lanes, n=S):
+    return pl.BlockSpec((rows, n, lanes), lambda g: (0, g, 0))
+
+
+def more(rows, lanes):
+    return scans(rows, lanes, S2)
+
+
+def resident(shape, dtype):
+    return pltpu.VMEM(shape, dtype)
+
+
+held = pl.BlockSpec(memory_space=pltpu.VMEM)
+
+
+def hbm(array):
+    return pltpu.with_memory_space_constraint(array, pltpu.HBM)
+
+
+def part_of(ref, step, n=S):
+    return ref.at[:, pl.ds(pl.multiple_of(step * n, n), n), :]
 
 
 def low_half(rows=S):
@@ -128,7 +147,10 @@
 
 
 def halves(x):
-    return x[:8] + x[8:]
+    total = x[:8]
+    for k in range(8, x.shape[0], 8):
+        total = total + x[k : k + 8]
+    return total
 
 
 def occupancy_words(occ, groups, first):
@@ -194,7 +216,7 @@
         compiler_params=params_of(),
         cost_estimate=cost(3),
         name="edges",
-    )(x, x, occ, cot, cot)
+    )(hbm(x), hbm(x), hbm(occ), hbm(cot), hbm(cot))
 
 
 def prep_kernel(occ_ref, kt_ref, np_ref, bits_ref, w1_ref, w2_ref, w2b_ref, w1b_ref, np2_ref):
@@ -249,7 +271,7 @@
         compiler_params=params_of(),
         cost_estimate=cost(4),
         name="prepare",
-    )(occ, kt, norm_params.reshape(4, C))
+    )(hbm(occ), kt, norm_params.reshape(4, C))
 
 
 def mask_tile(x_ref, bits_ref, t, xs, into):
@@ -266,10 +288,11 @@
         xs[k // 4, k % 4] = jnp.zeros_like(xs[0, 0])
 
 
-def conv_rows(xs, lanes, w, r):
+def conv_rows(xs, lanes, w, r, before=()):
     pairs = (r + 1) // 2
     pieces = [xs[0:pairs, q, :, lanes] for q in range(4)] + [xs[1 : pairs + 1, 0, :, lanes]]
-    lhs = jnp.concatenate([p.reshape(pairs * S, p.shape[2]) for p in pieces], axis=1)
+    pieces = [p.reshape(pairs * S, p.shape[2]) for p in pieces]
+    lhs = jnp.concatenate(list(before) + pieces, axis=1)
     acc = jnp.dot(lhs, w, preferred_element_type=f32).reshape(pairs, S, 2 * L)
     return [acc[i // 2, :, (i % 2) * L : (i % 2 + 1) * L] for i in range(r)]
 
@@ -279,6 +302,7 @@
     el_ref, edge_ref, xs, run,
 ):
     step, steps = (pl.program_id(0), pl.num_programs(0))
+    c_ref = part_of(c_ref, step)
     rows, lanes = (xa_ref.shape[0], xrow_ref.shape[1] * 2 // 3)
     r = rows // 2
     low = low_half()
@@ -287,23 +311,24 @@
     def _():
         clear_rows(rows, (r + 1) // 2, xs)
 
-    xs[0, 0, :, L : 2 * L] = xrow_ref[:, :L]
-    xs[0, 0, :, 2 * L :] = xrow_ref[:, lanes - 2 * L : lanes]
-    xs[0, 0, :, :L] = corner_ref[...]
-    for i in range(r):
-        k = 2 * i + 2
-        xs[k // 4, k % 4, :, :L] = xcol_ref[i]
-        k = 2 * i + 1
-        xs[k // 4, k % 4, :, :L] = swap(xcol_ref[i].astype(f32)).astype(bf16)
-    mask_tile(xa_ref, ba_ref, 0, xs, 1)
-    mask_tile(xb_ref, bb_ref, 0, xs, 2)
-    mask_tile(xb_ref, bb_ref, 1, xs, 3)
+    xs[0, 0, :, :L] = xrow_ref[:, :L]
+    xs[0, 0, :, L:] = xrow_ref[:, lanes - 2 * L : lanes]
+    mask_tile(xa_ref, ba_ref, 0, xs, 0)
+    mask_tile(xb_ref, bb_ref, 0, xs, 1)
+    mask_tile(xb_ref, bb_ref, 1, xs, 2)
     wide = 3 * L
-    some = lambda a: jnp.concatenate(
-        [w_ref[q * wide + a * L : q * wide + (a + 2) * L] for q in range(5)], axis=0
-    )
-    last = conv_rows(xs, slice(2 * L, 4 * L), some(0), r)
-    first = conv_rows(xs, slice(0, 2 * L), some(1), r)
+    rows_of = lambda q, a, b: w_ref[q * wide + a * C : q * wide + b * C]
+    w = jnp.concatenate([rows_of(q, 0, 4) for q in range(5)], axis=0)
+    last = conv_rows(xs, slice(L, 3 * L), w, r)
+    pairs = (r + 1) // 2
+    none = jnp.zeros((S, L), bf16)
+    beside = [corner_ref[...]] + [xcol_ref[i] for i in range(r)] + [none]
+    w = [jnp.zeros((C, 2 * L), bf16)] + [rows_of(q, 3, 4) for q in range(5)]
+    w = jnp.concatenate(w + [rows_of(q, 4, 6) for q in range(5)], axis=0)
+    more_lhs = [
+        jnp.concatenate([beside[2 * m + k] for m in range(pairs)], axis=0) for k in range(3)
+    ]
+    first = conv_rows(xs, slice(0, L), w, r, more_lhs)
     edge = [jnp.where(low, b, a) for a, b in zip(first, last)]
     pilot = pilot_of(jnp.concatenate(edge[: r // 2], axis=0))
     for i in range(r):
@@ -338,33 +363,34 @@
             whole(w.shape),
         ],
         out_specs=[
-            scans(r, 2 * L),
+            held,
             whole((1, 2, L)),
             scans((r + 1) // 2, L),
             scans((r + 1) // 2, L),
             scans(r, L),
         ],
         out_shape=[
-            shape(f32, r, scan_count, 2 * L),
+            resident((r, scan_count, 2 * L), f32),
             shape(f32, 1, 2, L),
             shape(bf16, (r + 1) // 2, scan_count, L),
             shape(bf16, (r + 1) // 2, scan_count, L),
             shape(bf16, r, scan_count, L),
         ],
         scratch_shapes=[
-            pltpu.VMEM(((r + 1) // 2 + 1, 4, S, 4 * L), bf16),
+            pltpu.VMEM(((r + 1) // 2 + 1, 4, S, 3 * L), bf16),
             pltpu.VMEM((8, L), f32),
         ],
         compiler_params=params_of(),
-        cost_estimate=cost(5),
+        cost_estimate=cost(4),
         name="conv_one_ends",
-    )(x, x, bits, bits, down, xcol, corner, w)
+    )(hbm(x), hbm(x), hbm(bits), hbm(bits), down, xcol, corner, w)
 
 
 def conv_one_kernel(
     x_ref, bits_ref, xrow_ref, ends_ref, w_ref, c_ref, st_ref, up_ref, down_ref, xs, run
 ):
     step, steps = (pl.program_id(0), pl.num_programs(0))
+    c_ref = part_of(c_ref, step)
     rows, tiles = (x_ref.shape[0], x_ref.shape[2] // L)
     r, inner = (rows // 2, tiles // 2 - 1)
 
@@ -413,14 +439,9 @@
             whole(ends.shape),
             whole(w.shape),
         ],
-        out_specs=[
-            scans(r, wide),
-            whole((devices, 2, L)),
-            scans(3, wide),
-            scans(2, wide),
-        ],
+        out_specs=[held, whole((devices, 2, L)), scans(3, wide), scans(2, wide)],
         out_shape=[
-            shape(f32, r, scan_count, wide),
+            resident((r, scan_count, wide), f32),
             shape(f32, devices, 2, L),
             shape(bf16, 3, scan_count, wide),
             shape(bf16, 2, scan_count, wide),
@@ -430,16 +451,49 @@
             pltpu.VMEM((8, L), f32),
         ],
         compiler_params=params_of(),
-        cost_estimate=cost(13),
+        cost_estimate=cost(11),
         name="conv_one",
-    )(x, bits, down, ends, w)
+    )(hbm(x), hbm(bits), down, ends, w)
+
+
+def pack_kernel(up_ref, down_ref, edge_ref, left_ref, right_ref, up_out, down_out):
+    r, wide = (edge_ref.shape[0], up_ref.shape[2])
+    low = low_half()
+    for src, out, first in ((up_ref, up_out, 0), (down_ref, down_out, r - 2)):
+        out[:, :, :wide] = src[...]
+        for k in range(src.shape[0]):
+            out[k, :, wide : wide + L] = edge_ref[first + k]
+            out[k, :, wide + L :] = rim_of(left_ref, right_ref, first + k, low).astype(bf16)
+
+
+def pack_rows(up, down, edge, left, right):
+    r, scan_count, _lanes = edge.shape
+    wide = up.shape[2]
+    return pl.pallas_call(
+        pack_kernel,
+        grid=(scan_count // S,),
+        in_specs=[
+            scans(3, wide), scans(2, wide), scans(r, L), scans(left.shape[0], L),
+            scans(right.shape[0], L),
+        ],
+        out_specs=[scans(3, wide + 2 * L), scans(2, wide + 2 * L)],
+        out_shape=[
+            jax.ShapeDtypeStruct((n, scan_count, wide + 2 * L), bf16) for n in (3, 2)
+        ],
+        compiler_params=params_of(),
+        cost_estimate=cost(1),
+        name="pack_rows",
+    )(up, down, edge, left, right)
 
 
 def conv_two_kernel(
     flags, c_ref, ends_ref, up_ref, down_ref, left_ref, right_ref, st_ref, np_ref, w_ref, c2_ref,
-    n1_ref, hid_ref, st2_ref, hs, rim, run, *, count,
+    n1_ref, hid_ref, st2_ref, rim, run, *, count,
 ):
     step, steps = (pl.program_id(0), pl.num_programs(0))
+    c_ref, ends_ref, c2_ref, n1_ref = (
+        part_of(a, step, S2) for a in (c_ref, ends_ref, c2_ref, n1_ref)
+    )
     r, tiles = (c_ref.shape[0], c_ref.shape[2] // L + 2)
     t_out = tiles - 1
     mean, inv = stats_of(st_ref, count)
@@ -447,22 +501,22 @@
     scale = 0.5 * np_ref[0:1] * inv
     shift = 0.5 * (np_ref[0:1] * offset + np_ref[1:2])
     f_up, f_down, f_left, f_right = (flags[k].astype(f32) for k in range(4))
-    low = low_half()
+    low = low_half(S2)
     left = jnp.where(low, f_left, 1.0)
     right = jnp.where(low, 1.0, f_right)
     for row in range(r):
         rim[row] = rim_of(left_ref, right_ref, row, low)
 
     def act(row, t):
-        ends = (0, tiles - 1)
+        at_end = t in (0, tiles - 1)
         if 2 <= row < r + 2:
             flag = None
-            c = pair(ends_ref, row - 2, min(t, 1)) if t in ends else pair(c_ref, row - 2, t - 1)
-            beyond = rim[row - 2] if t in ends else None
+            c = pair(ends_ref, row - 2, min(t, 1)) if at_end else pair(c_ref, row - 2, t - 1)
+            beyond = rim[row - 2] if at_end else None
         else:
             src, k, flag = (up_ref, row, f_up) if row < 2 else (down_ref, row - r - 2, f_down)
-            c = pair(src, k, tiles - 2 if t in ends else t - 1).astype(f32)
-            beyond = pair(src, k, tiles - 1).astype(f32) if t in ends else None
+            c = pair(src, k, tiles - 2 if at_end else t - 1).astype(f32)
+            beyond = pair(src, k, tiles - 1).astype(f32) if at_end else None
         if t == 0:
             c = jnp.where(low, beyond, c)
         if t == tiles - 1:
@@ -476,9 +530,7 @@
         if flag is not None:
             out = out * flag
         out = out.astype(bf16)
-        hs[row // 2, row % 2, :, t * L : (t + 1) * L] = out
-        if 1 <= row < r + 3:
-            hid_ref[row - 1, :, t * L : (t + 1) * L] = out
+        hid_ref[row, :, t * L : (t + 1) * L] = out
         if 2 <= row < r + 3:
             n1_ref[row - 2, :, t * L : (t + 1) * L] = (c * inv + offset).astype(bf16)
 
@@ -491,9 +543,12 @@
         if k < 0:
             continue
         lanes = slice(k * L, (k + 2) * L)
-        pieces = [hs[a : a + pairs, b, :, lanes] for a in range(2) for b in range(2)]
-        lhs = jnp.concatenate([p.reshape(pairs * S, 2 * L) for p in pieces], axis=1)
-        acc = jnp.dot(lhs, w_ref[...], preferred_element_type=f32).reshape(pairs, S, 2 * L)
+        pieces = [
+            jnp.concatenate([hid_ref[2 * m + a, :, lanes] for m in range(pairs)], axis=0)
+            for a in range(4)
+        ]
+        lhs = jnp.concatenate(pieces, axis=1)
+        acc = jnp.dot(lhs, w_ref[...], preferred_element_type=f32).reshape(pairs, S2, 2 * L)
         if pilot is None:
             pilot = pilot_of(acc[1 : r // 2, :, :L])
         blocks = []
@@ -503,7 +558,7 @@
             if 0 < row <= r:
                 blocks.append(block)
         sums = added(sums, off_sums(blocks, pilot))
-    finish_stats(step, steps, pilot, sums, float(r * t_out * S), run, st2_ref)
+    finish_stats(step, steps, pilot, sums, float(r * t_out * S2), run, st2_ref)
 
 
 def conv_two(flags, c1, ends, up, down, left, right, st, np2, w, count):
@@ -513,34 +568,28 @@
     devices = st.shape[0]
     return pl.pallas_call(
         functools.partial(conv_two_kernel, count=count),
-        grid=(scan_count // S,),
+        grid=(scan_count // S2,),
         in_specs=[
             pl.BlockSpec(memory_space=pltpu.SMEM),
-            scans(r, wide - 2 * L),
-            scans(r, 2 * L),
-            scans(2, wide),
-            scans(3, wide),
-            scans(left.shape[0], L),
-            scans(right.shape[0], L),
+            held,
+            held,
+            more(2, wide),
+            more(3, wide),
+            more(left.shape[0], L),
+            more(right.shape[0], L),
             whole(st.shape),
             whole(np2.shape),
             whole(w.shape),
         ],
-        out_specs=[
-            scans(r + 3, lanes),
-            scans(r + 1, wide),
-            scans(r + 2, wide),
-            whole((devices, 2, L)),
-        ],
+        out_specs=[held, held, more(r + 5, wide), whole((devices, 2, L))],
         out_shape=[
-            jax.ShapeDtypeStruct((r + 3, scan_count, lanes), f32),
-            jax.ShapeDtypeStruct((r + 1, scan_count, wide), bf16),
-            jax.ShapeDtypeStruct((r + 2, scan_count, wide), bf16),
+            resident((r + 3, scan_count, lanes), f32),
+            resident((r + 1, scan_count, wide), bf16),
+            pltpu.HBM((r + 5, scan_count, wide), bf16),
             jax.ShapeDtypeStruct((devices, 2, L), f32),
         ],
         scratch_shapes=[
-            pltpu.VMEM(((r + 5) // 2, 2, S, wide), bf16),
-            pltpu.VMEM((r, S, L), f32),
+            pltpu.VMEM((r, S2, L), f32),
             pltpu.VMEM((8, L), f32),
         ],
         compiler_params=params_of(),
@@ -553,6 +602,7 @@
     c2_ref, st_ref, np_ref, cot_ref, up_ref, down_ref, feat_ref, d_ref, sum_ref, run, *, count,
 ):
     step, steps = (pl.program_id(0), pl.num_programs(0))
+    c2_ref, d_ref = (part_of(a, step, S2) for a in (c2_ref, d_ref))
     r, tiles = (cot_ref.shape[0], cot_ref.shape[2] // L)
     mean, inv = stats_of(st_ref, count)
     offset = -mean * inv
@@ -562,21 +612,20 @@
 
     def slope(c, cot):
         h = c * scale + shift
-        t = jnp.tanh(h)
-        plus = 1.0 + t
-        return (h * plus, (0.5 * cot.astype(f32)) * (plus * (1.0 + h * (1.0 - t))))
-
-    def own(i, sums):
-        for t in range(tiles):
+        s = 1.0 + jnp.tanh(h)
+        f = h * s
+        return (f, cot.astype(f32) * (s + f * (2.0 - s)))
+
+    sums = None
+    for t in range(tiles):
+        part = [jnp.zeros((8, L), f32), jnp.zeros((8, L), f32)]
+        for i in range(r):
             c = pair(c2_ref, i + 1, t)
             f, d = slope(c, pair(cot_ref, i, t))
             feat_ref[i, :, t * L : (t + 1) * L] = f.astype(bf16)
             d_ref[i + 1, :, t * L : (t + 1) * L] = d
-            sums = (sums[0] + halves(d), sums[1] + halves(d * (c * inv + offset)))
-        return sums
-
-    zero = jnp.zeros((8, L), f32)
-    sums = lax.fori_loop(0, r, own, (zero, zero))
+            part = [part[0] + halves(d), part[1] + halves(d * c)]
+        sums = added(sums, part)
     for t in range(tiles):
         lanes = slice(t * L, (t + 1) * L)
         cot = up_ref[:, (above + t) * L : (above + t + 1) * L]
@@ -584,6 +633,7 @@
         for k in range(2):
             row = r + 1 + k
             d_ref[row, :, lanes] = slope(pair(c2_ref, row, t), pair(down_ref, k, t))[1]
+    sums = (0.5 * sums[0], (0.5 * inv) * (sums[1] - mean * sums[0]))
     add_sums(step, steps, sums, run, sum_ref)
 
 
@@ -608,26 +658,26 @@
     devices = st.shape[0]
     return pl.pallas_call(
         functools.partial(output_kernel, count=count),
-        grid=(scan_count // S,),
+        grid=(scan_count // S2,),
         in_specs=[
-            scans(r + 3, lanes),
+            held,
             whole(st.shape),
             whole(np2.shape),
-            scans(r, lanes),
-            pl.BlockSpec((S, up.shape[1]), lambda g: (g, 0)),
-            scans(2, lanes),
-        ],
-        out_specs=[scans(r, lanes), scans(r + 3, lanes), whole((devices, 2, L))],
+            more(r, lanes),
+            pl.BlockSpec((S2, up.shape[1]), lambda g: (g, 0)),
+            more(2, lanes),
+        ],
+        out_specs=[more(r, lanes), held, whole((devices, 2, L))],
         out_shape=[
             jax.ShapeDtypeStruct((r, scan_count, lanes), bf16),
-            jax.ShapeDtypeStruct((r + 3, scan_count, lanes), f32),
+            resident((r + 3, scan_count, lanes), f32),
             jax.ShapeDtypeStruct((devices, 2, L), f32),
         ],
         scratch_shapes=[pltpu.VMEM((8, L), f32)],
         compiler_params=params_of(),
         cost_estimate=cost(12),
         name="output",
-    )(c2, st, np2, cot, up, down)
+    )(c2, st, np2, hbm(cot), up, down)
 
 
 def norm_back_two(flags, st_ref, sum_ref, np_ref, count, rows):
@@ -637,6 +687,7 @@
     gain = np_ref[2:3] * inv
     c_n = -gain * inv * gain_sum / cells
     c_0 = -gain * shift_sum / cells - c_n * mean
+    gain = 0.5 * gain
     f_up, f_down = (flags[k].astype(f32) for k in range(2))
 
     def back(row, d, c):
@@ -652,15 +703,15 @@
 
 
 def rim_two_kernel(
-    flags, da_ref, db_ref, ca_ref, cb_ref, st_ref, sum_ref, np_ref, er_ref, el_ref, *, count
+    flags, d_ref, c_ref, st_ref, sum_ref, np_ref, er_ref, el_ref, *, count
 ):
-    rows = da_ref.shape[0]
+    d_ref, c_ref = (part_of(a, pl.program_id(0), S2) for a in (d_ref, c_ref))
+    rows, last = (d_ref.shape[0], d_ref.shape[2] // L - 1)
     back = norm_back_two(flags, st_ref, sum_ref, np_ref, count, rows - 3)
-    low = low_half()
+    low = low_half(S2)
     half = rows // 2
-    both = lambda row: jnp.where(
-        low, back(row, da_ref[row], ca_ref[row]), back(row, db_ref[row], cb_ref[row])
-    )
+    column = lambda row, t: back(row, pair(d_ref, row, t), pair(c_ref, row, t))
+    both = lambda row: jnp.where(low, column(row, 0), column(row, last))
     for k in range(half):
         near, far = (both(k), swap(both(k + half)))
         el_ref[k] = jnp.where(low, near, far).astype(bf16)
@@ -669,27 +720,26 @@
 
 def rim_two(flags, d, c2, st, sums, np2, count):
     rows, scan_count, lanes = d.shape
-    at = lambda k: pl.BlockSpec((rows, S, L), lambda g: (0, g, k))
-    last = lanes // L - 1
     return pl.pallas_call(
         functools.partial(rim_two_kernel, count=count),
-        grid=(scan_count // S,),
+        grid=(scan_count // S2,),
         in_specs=[
-            pl.BlockSpec(memory_space=pltpu.SMEM), at(0), at(last), at(0), at(last),
-            whole(st.shape), whole(sums.shape), whole(np2.shape),
-        ],
-        out_specs=[scans(rows // 2, L)] * 2,
+            pl.BlockSpec(memory_space=pltpu.SMEM), held, held, whole(st.shape),
+            whole(sums.shape), whole(np2.shape),
+        ],
+        out_specs=[more(rows // 2, L)] * 2,
         out_shape=[jax.ShapeDtypeStruct((rows // 2, scan_count, L), bf16)] * 2,
         compiler_params=params_of(),
         cost_estimate=cost(3),
         name="rim_two",
-    )(flags, d, d, c2, c2, st, sums, np2)
+    )(flags, d, c2, st, sums, np2)
 
 
 def back_two_kernel(
     flags, d_ref, c2_ref, hid_ref, st_ref, sum_ref, np_ref, ds_ref, kg_ref, grad, *, count
 ):
     step, steps = (pl.program_id(0), pl.num_programs(0))
+    d_ref, c2_ref, ds_ref = (part_of(a, step) for a in (d_ref, c2_ref, ds_ref))
     r, tiles = (c2_ref.shape[0] - 3, c2_ref.shape[2] // L)
     back = norm_back_two(flags, st_ref, sum_ref, np_ref, count, r)
 
@@ -704,7 +754,7 @@
             ds_ref[row, :, t * L : (t + 1) * L] = d.astype(bf16)
         lanes = slice(t * L, (t + 2) * L)
         rhs = jnp.concatenate(
-            [hid_ref[p : p + r, :, lanes].reshape(r * S, 2 * L) for p in range(3)], axis=1
+            [hid_ref[p + 1 : p + 1 + r, :, lanes].reshape(r * S, 2 * L) for p in range(3)], axis=1
         )
         lhs = ds_ref[1 : r + 1, :, t * L : (t + 1) * L].reshape(r * S, L)
         part = lax.dot_general(lhs, rhs, (((0,), (0,)), ((), ())), preferred_element_type=f32)
@@ -725,40 +775,42 @@
 
 def back_two(flags, d, c2, hid, st, sums, np2, count):
     r, scan_count, wide = hid.shape
-    r, lanes = (r - 2, wide - L)
+    r, lanes = (r - 5, wide - L)
     return pl.pallas_call(
         functools.partial(back_two_kernel, count=count),
         grid=(scan_count // S,),
         in_specs=[
             pl.BlockSpec(memory_space=pltpu.SMEM),
-            scans(r + 3, lanes),
-            scans(r + 3, lanes),
-            scans(r + 2, wide),
+            held,
+            held,
+            scans(r + 5, wide),
             whole(st.shape),
             whole(sums.shape),
             whole(np2.shape),
         ],
-        out_specs=[scans(r + 3, lanes), whole((9, C, C))],
+        out_specs=[held, whole((9, C, C))],
         out_shape=[
-            jax.ShapeDtypeStruct((r + 3, scan_count, lanes), bf16),
+            resident((r + 3, scan_count, lanes), bf16),
             jax.ShapeDtypeStruct((9, C, C), f32),
         ],
         scratch_shapes=[pltpu.VMEM((L, 12 * C), f32)],
         compiler_params=params_of(),
         cost_estimate=cost(12),
         name="back_two",
-    )(flags, d, c2, hid, st, sums, np2)
+    )(flags, d, c2, hbm(hid), st, sums, np2)
 
 
 def hidden_kernel(
     ds_ref, left_ref, right_ref, n1_ref, np_ref, w_ref, dp_ref, edge_ref, sum1_ref, rim, run
 ):
     step, steps = (pl.program_id(0), pl.num_programs(0))
+    ds_ref, n1_ref, dp_ref = (part_of(a, step) for a in (ds_ref, n1_ref, dp_ref))
     r, tiles = (n1_ref.shape[0] - 1, n1_ref.shape[2] // L)
     pairs = (r + 1) // 2
     low = low_half()
     for row in range(r + 3):
         rim[row] = rim_of(right_ref, left_ref, row, low).astype(bf16)
+    scale, shift = (0.5 * np_ref[0:1], 0.5 * np_ref[1:2])
     sums = None
     for t in range(tiles):
         parts = []
@@ -771,10 +823,9 @@
         part = [jnp.zeros((8, L), f32), jnp.zeros((8, L), f32)]
         for i in range(r + 1):
             n = pair(n1_ref, i, t).astype(f32)
-            h = 0.5 * (n * np_ref[0:1] + np_ref[1:2])
-            tan = jnp.tanh(h)
-            d = acc[i // 2, :, (i % 2) * L : (i % 2 + 1) * L]
-            d = (0.5 * d) * ((1.0 + tan) * (1.0 + h * (1.0 - tan)))
+            h = n * scale + shift
+            s = 1.0 + jnp.tanh(h)
+            d = acc[i // 2, :, (i % 2) * L : (i % 2 + 1) * L] * (s + h * s * (2.0 - s))
             dp_ref[i, :, t * L : (t + 1) * L] = d
             if i < r:
                 if t == 0:
@@ -783,7 +834,7 @@
                     d = jnp.where(low, d, 0.0)
                 part = [part[0] + halves(d), part[1] + halves(d * n)]
         sums = added(sums, part)
-    add_sums(step, steps, sums, run, sum1_ref)
+    add_sums(step, steps, [0.5 * x for x in sums], run, sum1_ref)
     for i in range(pairs):
         both = jnp.where(low, swap(pair(dp_ref, pairs + i, 0)), pair(dp_ref, i, 0))
         edge_ref[i] = both.astype(bf16)
@@ -797,20 +848,20 @@
         hidden_kernel,
         grid=(scan_count // S,),
         in_specs=[
-            scans(r + 3, lanes),
+            held,
             scans(half, L),
             scans(half, L),
-            scans(r + 1, wide),
+            held,
             whole(np2.shape),
             whole(w.shape),
         ],
         out_specs=[
-            scans(r + 1, wide),
+            held,
             scans((r + 1) // 2, L),
             whole((devices, 2, L)),
         ],
         out_shape=[
-            jax.ShapeDtypeStruct((r + 1, scan_count, wide), f32),
+            resident((r + 1, scan_count, wide), f32),
             jax.ShapeDtypeStruct(((r + 1) // 2, scan_count, L), bf16),
             jax.ShapeDtypeStruct((devices, 2, L), f32),
         ],
@@ -823,9 +874,10 @@
 
 def back_one_kernel(
     flags, dp_ref, edge_ref, n1_ref, x_ref, bits_ref, st_ref, sum_ref, np_ref, kg2_ref, ds, kg_ref,
-    xm, grad, *, count,
+    xm, grad, flat, *, count,
 ):
     step, steps = (pl.program_id(0), pl.num_programs(0))
+    dp_ref, n1_ref = (part_of(a, step) for a in (dp_ref, n1_ref))
     r, tiles = (n1_ref.shape[0] - 1, n1_ref.shape[2] // L - 1)
     cells = 2.0 * count * st_ref.shape[0]
     _mean, inv = stats_of(st_ref, count)
@@ -833,6 +885,7 @@
     gain = np_ref[0:1] * inv
     c_n = -gain * gain_sum / cells
     c_0 = -gain * shift_sum / cells
+    gain = 0.5 * gain
     f_down, f_right = (flags[1].astype(f32), flags[3].astype(f32))
     packed = edge_ref.shape[0]
     low = low_half()
@@ -893,9 +946,12 @@
                 blocks.append(jnp.transpose(block))
         blocks += [kg2_ref[8]] + [kg2_ref[k] for k in range(8)]
         for a in range(9):
-            kg_ref[a * C : (a + 1) * C] = jnp.concatenate(blocks[2 * a : 2 * a + 2], axis=1)
-        if kg_ref.shape[0] > 9 * C:
-            kg_ref[9 * C :] = jnp.zeros((kg_ref.shape[0] - 9 * C, L), f32)
+            flat[a * C : (a + 1) * C] = jnp.concatenate(blocks[2 * a : 2 * a + 2], axis=1)
+        if flat.shape[0] > 9 * C:
+            flat[9 * C :] = jnp.zeros((flat.shape[0] - 9 * C, L), f32)
+        devices, share, _lanes = kg_ref.shape
+        for k in range(devices):
+            kg_ref[k] = flat[k * share : (k + 1) * share].astype(bf16)
 
 
 def back_one(flags, dp, edge, n1, x, bits, st, sums, np2, kg2, count):
@@ -909,9 +965,9 @@
         grid=(scan_count // S,),
         in_specs=[
             pl.BlockSpec(memory_space=pltpu.SMEM),
-            scans(r + 1, wide),
+            held,
             scans(edge.shape[0], L),
-            scans(r + 1, wide),
+            held,
             scans(rows, lanes),
             scans(bits.shape[0], lanes),
             whole(st.shape),
@@ -919,19 +975,20 @@
             whole(np2.shape),
             whole(kg2.shape),
         ],
-        out_specs=[scans(r + 1, wide), whole((devices * share, L))],
+        out_specs=[scans(r + 1, wide), whole((devices, share, L))],
         out_shape=[
-            jax.ShapeDtypeStruct((r + 1, scan_count, wide), bf16),
-            jax.ShapeDtypeStruct((devices * share, L), f32),
+            pltpu.HBM((r + 1, scan_count, wide), bf16),
+            jax.ShapeDtypeStruct((devices, share, L), bf16),
         ],
         scratch_shapes=[
             pltpu.VMEM((2, r, S, lanes), bf16),
             pltpu.VMEM((3, 4 * C, 4 * C), f32),
+            pltpu.VMEM((devices * share, L), f32),
         ],
         compiler_params=params_of(),
         cost_estimate=cost(16),
         name="back_one",
-    )(flags, dp, edge, n1, x, bits, st, sums, np2, kg2)
+    )(flags, dp, edge, n1, hbm(x), hbm(bits), st, sums, np2, kg2)
 
 
 def input_grad_kernel(ds, bits_ref, w_ref, *rest):
@@ -971,7 +1028,29 @@
         compiler_params=params_of(),
         cost_estimate=cost(7),
         name="input_gradient",
-    )(d, bits, w, *earlier)
+    )(hbm(d), hbm(bits), w, *earlier)
+
+
+def share_kernel(g_ref, out_ref):
+    devices = g_ref.shape[0]
+    total = g_ref[0].astype(f32)
+    for k in range(1, devices):
+        total = total + g_ref[k].astype(f32)
+    total = total.astype(bf16)
+    for k in range(devices):
+        out_ref[k] = total
+
+
+def sum_share(grads):
+    return pl.pallas_call(
+        share_kernel,
+        in_specs=[held],
+        out_specs=held,
+        out_shape=jax.ShapeDtypeStruct(grads.shape, bf16),
+        compiler_params=pltpu.CompilerParams(vmem_limit_bytes=8 << 20),
+        cost_estimate=cost(1),
+        name="sum_share",
+    )(grads)
 
 
 def adam_step(weight_now, gradient, moment_one, moment_two, step_rate, decay_rate):
@@ -984,14 +1063,17 @@
 
 def update_kernel(
     g_ref, s1_ref, s2_ref, k_ref, km_ref, kv_ref, n_ref, nm_ref, nv_ref, gn_ref, ok_ref, okm_ref,
-    okv_ref, olow_ref, on_ref, onm_ref, onv_ref,
+    okv_ref, olow_ref, on_ref, onm_ref, onv_ref, flat,
 ):
+    devices, share, _lanes = g_ref.shape
+    for k in range(devices):
+        flat[k * share : (k + 1) * share] = g_ref[k].astype(f32)
     norm_rows = []
     for ref in (s1_ref, s2_ref):
         shift_sum, gain_sum = sums_of(ref)
         norm_rows += [gain_sum[:, :C], shift_sum[:, :C]]
     g_norm = jnp.concatenate(norm_rows, axis=0)
-    squares = jnp.sum(jnp.sum(g_ref[: 9 * C] ** 2, axis=0, keepdims=True), axis=1, keepdims=True)
+    squares = jnp.sum(jnp.sum(flat[: 9 * C] ** 2, axis=0, keepdims=True), axis=1, keepdims=True)
     squares = squares + jnp.sum(
         jnp.sum(g_norm * g_norm, axis=0, keepdims=True), axis=1, keepdims=True
     )
@@ -1009,10 +1091,10 @@
             width = L if a < 4 else C
             at = slice(a * L, a * L + width)
             if a == 4:
-                g = g_ref[4 * C : 5 * C, layer * C : (layer + 1) * C]
+                g = flat[4 * C : 5 * C, layer * C : (layer + 1) * C]
             else:
                 first = (a + 5 * layer) * C
-                g = g_ref[first : first + C, :]
+                g = flat[first : first + C, :]
             k, km, kv = adam_step(
                 k_ref[layer, :, at], g * factor, km_ref[layer, :, at], kv_ref[layer, :, at],
                 kernel_rate, kernel_decay,
@@ -1038,6 +1120,7 @@
         in_specs=[whole(a.shape) for a in args],
         out_specs=[whole(o.shape) for o in outs],
         out_shape=outs,
+        scratch_shapes=[pltpu.VMEM((grads.shape[0] * grads.shape[1], L), f32)],
         compiler_params=params_of(),
         cost_estimate=cost(3),
         name="update",
@@ -1079,20 +1162,12 @@
     )
     bits, w1, w2, w2b, w1b, np2 = prepare(occ, kt, norm_params)
 
+    xcol, cot_down, flags = lax.optimization_barrier((xcol, cot_down, flags))
     ends, st1, going_right, going_left, edge = first_last(x, bits, down, xcol, corner, w1)
     left_in = shifted(going_right, "gx", 1)
     right_in = shifted(going_left, "gx", -1)
     c1, st1, up, low_rows = conv_one(x, bits, down, st1, w1, devices)
-    half = (r + 1) // 2
-
-    def beyond(a, b):
-        near, far = (slice(0, C), slice(C, L))
-        if a >= half:
-            a, b, near, far = (a - half, b - half, far, near)
-        return jnp.concatenate([left_in[a:b, :, near], right_in[a:b, :, far]], axis=2)
-
-    up = jnp.concatenate([up, edge[:3], beyond(0, 3)], axis=2)
-    low_rows = jnp.concatenate([low_rows, edge[r - 2 :], beyond(r - 2, r)], axis=2)
+    up, low_rows = pack_rows(up, low_rows, edge, left_in, right_in)
     down_in = shifted(up, "gy", -1)
     up_in = shifted(low_rows, "gy", 1)
     st1 = exchange(st1)
@@ -1111,11 +1186,10 @@
     edge = shifted(edge, "gx", -1)
     sums1 = exchange(sums1)
     d1, grads = back_one(flags, d1, edge, n1, x, bits, st1, sums1, np2, kg2, count)
-    share = grads.shape[0] // devices
     grads = exchange(grads)
     input_grad = input_gradient(d1, bits, w1b, 0, None)
-    mine = jnp.sum(grads.reshape(devices, share, L), axis=0)
-    grads = exchange(jnp.broadcast_to(mine[None], (devices, share, L)).reshape(-1, L))
+    grads, input_grad = lax.optimization_barrier((sum_share(grads), input_grad))
+    grads = exchange(grads)
     input_grad = input_gradient(d1, bits, w1b, 1, input_grad)
     norm, k, km, kv, low, n, nm, nv = update(
         grads, sums1, sums2, kt, kmt, kvt, norm_params, norm_m, norm_v

time: 219 us -> 172 us (0.79)
  Pallas kernels: 111 us -> 82.4 us
  waiting for transfers between devices: 14.7 us -> 7.49 us
  starting transfers between devices: 41.6 us -> 35 us
  local copies, waits for them, and re-layouts: 7.13 us -> 1.07 us
  blocking collectives: 39.9 us -> 44.6 us
  other arithmetic: 2.79 us -> 0.08 us
    all_to_all x3 -> x2, waiting for transfers between devices: 13.9 us -> 3.82 us  [exchange(): return lax.all_to_all(rows, BOTH, 0, 0, tiled=True)]
    all_to_all x3 -> x2, starting transfers between devices: 13.2 us -> 6.45 us  [exchange(): return lax.all_to_all(rows, BOTH, 0, 0, tiled=True)]
    pallas_call x1, Pallas kernels: 11.6 us -> 6.69 us  [output(): pl.pallas_call(functools.partial(output_kernel, count=count), grid=(scan_...]
    all_to_all x3 -> x4, blocking collectives: 39.9 us -> 44.6 us  [exchange(): return lax.all_to_all(rows, BOTH, 0, 0, tiled=True)]
    pallas_call x1, Pallas kernels: 12.9 us -> 8.61 us  [conv_two(): pl.pallas_call(functools.partial(conv_two_kernel, count=count), grid=(sca...]
    pallas_call x1, Pallas kernels: 11.1 us -> 7 us  [back_two(): pl.pallas_call(functools.partial(back_two_kernel, count=count), grid=(sca...]
    ppermute x10, waiting for transfers between devices: 0.08 us -> 3.66 us  [shifted(): return lax.ppermute(block, axis, route)]
    unnamed x30 -> x14, local copies, waits for them, and re-layouts: 4.6 us -> 1.07 us
  transfers between devices with their start and end apart: 14 -> 13, of which waited for: 5 -> 3; matrix products, arithmetic and copies ran while one was open for 2% -> 0% of each run, Pallas kernels for 25% -> 20%
where the time goes in v4:
time: 172 us
  Pallas kernels  82.4 us (48%)
  blocking collectives  44.6 us (26%)
  starting transfers between devices  35 us (20%)
  waiting for transfers between devices  7.49 us (4%)
    all_to_all x4, blocking collectives, exchange(): return lax.all_to_all(rows, BOTH, 0, 0, tiled=True)  44.6 us
    ppermute x10, starting transfers between devices, shifted(): return lax.ppermute(block, axis, route)  22.8 us
    pallas_call x1, Pallas kernels, back_one(): pl.pallas_call(functools.partial(back_one_kernel, count=count), grid=(sca...  14.6 us
    pallas_call x2, Pallas kernels, input_gradient(): pl.pallas_call(input_grad_kernel, grid=(steps,), in_specs=[at(r, wide), a...  13.2 us
    pallas_call x1, Pallas kernels, conv_one(): pl.pallas_call(conv_one_kernel, grid=(scan_count // S,), in_specs=[scans(...  11.5 us
    pallas_call x1, Pallas kernels, conv_two(): pl.pallas_call(functools.partial(conv_two_kernel, count=count), grid=(sca...  8.61 us
    pallas_call x1, Pallas kernels, back_two(): pl.pallas_call(functools.partial(back_two_kernel, count=count), grid=(sca...  7 us
    pallas_call x1, Pallas kernels, hidden_gradient(): pl.pallas_call(hidden_kernel, grid=(scan_count // S,), in_specs=[held, sc...  6.86 us
  transfers between devices with their start and end apart: 13, of which 3 were waited for; matrix products, arithmetic and copies ran while one was open for 0% of the time, Pallas kernels for 20%

profile of v4, /device:TPU:0, one launch (start us, length us, event | category | flops | bytes accessed | tf_op | source)
XLA Modules:
  0.0 171.5 jit_solution(13775195545738461274)
XLA Ops:
  0.7 2.4 %edges.1 = (bf16[64,2688]{1,0:T(8,128)(2,1)S(1)}, bf16[2,64,896]{2,1,0:T(8,128)(2,1)S(1)}, bf16[64,128]{1,0:T(8,128)(2,1)S(1)}, bf16[31,64,128]{2,1,0:T(8,128)(2,1)S(1)}) custom-call(bf16[62,64,1792]{2,1,0:T(8,128)(2,1)} %bitcast.31, bf16[62,64,1792]{2,1,0:T(8,128)(2,1)} %bitcast.32, s32[28,64,62]{2,1,0:T(8,128)} %bitcast.41, bf16[31,64,896]{2,1,0:T(8,128)(2,1)} %bitcast.38, ...), custom_call_target="tpu_custom_call" | custom-call | bytes 10800000 | tf_op jit(solution)/shard_map/edges/pallas_call | solution.py:204
  3.1 4.9 %collective-permute-start = (bf16[31,64,128]{2,1,0:T(8,128)(2,1)S(1)}, bf16[31,64,128]{2,1,0:T(8,128)(2,1)S(1)}, u32[]{:S(2)}, u32[]{:S(2)}) collective-permute-start(bf16[31,64,128]{2,1,0:T(8,128)(2,1)S(1)} %get-tuple-element.60), channel_id=1, source_target_pairs={{0,1},{1,2},{2,3},{3,4},{4,5},{5,6},{6,7},{8,9},{9,10},{10,11},{11... | collective-permute-start | bytes 1523720 | tf_op jit(solution)/shard_map/ppermute | solution.py:1133
  8.0 1.5 collective-permute-start.2
  9.4 1.3 collective-permute-start.1
  10.7 5.7 %collective-permute-start.3 = (bf16[64,128]{1,0:T(8,128)(2,1)S(1)}, bf16[64,128]{1,0:T(8,128)(2,1)S(1)}, u32[]{:S(2)}, u32[]{:S(2)}) collective-permute-start(bf16[64,128]{1,0:T(8,128)(2,1)S(1)} %get-tuple-element.66), channel_id=1, source_target_pairs={{0,9},{1,10},{2,11},{3,12},{4,13},{5,14},{6,15},{8,17},{9,18},{10,... | collective-permute-start | bytes 49160 | tf_op jit(solution)/shard_map/ppermute | solution.py:1160
  16.6 2.2 %prepare.1 = (s16[5,64,1792]{2,1,0:T(8,128)(2,1)S(1)}, bf16[1920,256]{1,0:T(8,128)(2,1)S(1)}, bf16[1024,256]{1,0:T(8,128)(2,1)S(1)}, bf16[1024,256]{1,0:T(8,128)...) custom-call(s32[28,64,62]{2,1,0:T(8,128)} %bitcast.42, f32[2,64,576]{2,1,0:T(8,128)S(1)} %bitcast.23, ...), custom_call_target="tpu_custom_call" | custom-call | bytes 14400000 | tf_op jit(solution)/shard_map/prepare/pallas_call | solution.py:265
  19.8 5.0 %conv_one_ends.1 = (f32[31,64,256]{2,1,0:T(8,128)S(1)}, f32[1,2,128]{2,1,0:T(2,128)S(1)}, bf16[16,64,128]{2,1,0:T(8,128)(2,1)S(1)}, bf16[16,64,128]{2,1,0:T(8,128)(2,1)S(1)}, bf16[31,64,128]{2,1,0:T(8,128)(2,1)S(1)}) custom-call(bf16[62,64,1792]{2,1,0:T(8,128)(2,1)} %bitcast.33, bf16[62,64,1792]{2,1,0:T(8,128)(2,1)} %bitcast.34, ...), custom_call_target="tpu_custom_call" | custom-call | bytes 14400000 | tf_op jit(solution)/shard_map/conv_one_ends/pallas_call | solution.py:352
  24.8 3.5 %collective-permute-start.4 = (bf16[16,64,128]{2,1,0:T(8,128)(2,1)S(1)}, bf16[16,64,128]{2,1,0:T(8,128)(2,1)S(1)}, u32[]{:S(2)}, u32[]{:S(2)}) collective-permute-start(bf16[16,64,128]{2,1,0:T(8,128)(2,1)S(1)} %get-tuple-element.74), channel_id=1, source_target_pairs={{0,1},{1,2},{2,3},{3,4},{4,5},{5,6},{6,7},{8,9},{9,10},{10,11},{11... | collective-permute-start | bytes 786440 | tf_op jit(solution)/shard_map/ppermute | solution.py:1133
  28.3 1.3 collective-permute-start.5
  29.6 11.5 %conv_one.1 = (f32[31,64,768]{2,1,0:T(8,128)S(1)}, f32[32,2,128]{2,1,0:T(2,128)S(1)}, bf16[3,64,768]{2,1,0:T(8,128)(2,1)S(1)}, bf16[2,64,768]{2,1,0:T(8,128)(2,1)S(1)}) custom-call(bf16[62,64,1792]{2,1,0:T(8,128)(2,1)} %bitcast.35, s16[5,64,1792]{2,1,0:T(8,128)(2,1)} %copy-done, bf16[64,2688]{1,0:T(8,128)(2,1)S(1)} %collective-permute-done.2.xrow_ref.up_ref, ...), custom_call_target="tpu_custom_call" | custom-call | bytes 39600000 | tf_op jit(solution)/shard_map/conv_one/pallas_call | solution.py:432
  43.1 3.7 %collective-permute-start.6 = (bf16[2,64,1024]{2,1,0:T(8,128)(2,1)S(1)}, bf16[2,64,1024]{2,1,0:T(8,128)(2,1)S(1)}, u32[]{:S(2)}, u32[]{:S(2)}) collective-permute-start(bf16[2,64,1024]{2,1,0:T(8,128)(2,1)S(1)} %get-tuple-element.76), channel_id=1, source_target_pairs={{0,8},{8,16},{16,24},{1,9},{9,17},{17,25},{2,10},{10,18},{18,26},{... | collective-permute-start | bytes 786440 | tf_op jit(solution)/shard_map/ppermute | solution.py:1133
  46.8 14.0 %all_to_all.30.st_ref = f32[32,2,128]{2,1,0:T(2,128)S(1)} all-to-all(f32[32,2,128]{2,1,0:T(2,128)S(1)} %get-tuple-element.78), channel_id=1, replica_groups=mesh['gy'=4,'gx'=8] {'gy','gx'}, dimensions={0} | all-to-all | bytes 65536 | tf_op jit(solution)/shard_map/all_to_all | solution.py:1137
  60.8 8.6 %conv_two.1 = (f32[34,64,896]{2,1,0:T(8,128)S(1)}, bf16[32,64,1024]{2,1,0:T(8,128)(2,1)S(1)}, bf16[36,64,1024]{2,1,0:T(8,128)(2,1)}, f32[32,2,128]{2,1,0:T(2,128)S(1)}) custom-call(s32[4]{0:T(128)S(1)} %add_convert_fusion.flags, f32[31,64,768]{2,1,0:T(8,128)S(1)} %get-tuple-element.69.c_ref, f32[31,64,256]{2,1,0:T(8,128)S(1)} %get-tuple-element.70.ends_ref, ...), custom_call_target="tpu_custom_call" | custom-call | bytes 50400000 | tf_op jit(solution)/shard_map/conv_two/pallas_call | solution.py:569
  69.4 8.9 %all_to_all.31.st_ref = f32[32,2,128]{2,1,0:T(2,128)S(1)} all-to-all(f32[32,2,128]{2,1,0:T(2,128)S(1)} %get-tuple-element.82), channel_id=1, replica_groups=mesh['gy'=4,'gx'=8] {'gy','gx'}, dimensions={0} | all-to-all | bytes 65536 | tf_op jit(solution)/shard_map/all_to_all | solution.py:1137
  78.3 6.7 %output.1 = (bf16[31,64,896]{2,1,0:T(8,128)(2,1)}, f32[34,64,896]{2,1,0:T(8,128)S(1)}, f32[32,2,128]{2,1,0:T(2,128)S(1)}) custom-call(f32[34,64,896]{2,1,0:T(8,128)S(1)} %get-tuple-element.81.c2_ref.c_ref, f32[32,2,128]{2,1,0:T(2,128)S(1)} %all_to_all.31.st_ref, f32[4,128]{1,0:T(4,128)S(1)} %get-tuple-element.79.np_ref, bf16[31,64,896]{2,1,0:T(8,128)(2,1)} %bitcast.40, ...), custom_call_target="tpu_custom_call" | custom-call | bytes 43200000 | tf_op jit(solution)/shard_map/output/pallas_call | solution.py:659
  85.0 8.9 %all_to_all.32.sum_ref.s2_ref = f32[32,2,128]{2,1,0:T(2,128)S(1)} all-to-all(f32[32,2,128]{2,1,0:T(2,128)S(1)} %get-tuple-element.87), channel_id=1, replica_groups=mesh['gy'=4,'gx'=8] {'gy','gx'}, dimensions={0} | all-to-all | bytes 65536 | tf_op jit(solution)/shard_map/all_to_all | solution.py:1137
  93.8 1.4 rim_two.1
  95.2 2.6 %collective-permute-start.8 = (bf16[17,64,128]{2,1,0:T(8,128)(2,1)S(1)}, bf16[17,64,128]{2,1,0:T(8,128)(2,1)S(1)}, u32[]{:S(2)}, u32[]{:S(2)}) collective-permute-start(bf16[17,64,128]{2,1,0:T(8,128)(2,1)S(1)} %get-tuple-element.89), channel_id=1, source_target_pairs={{0,1},{1,2},{2,3},{3,4},{4,5},{5,6},{6,7},{8,9},{9,10},{10,11},{11... | collective-permute-start | bytes 835592 | tf_op jit(solution)/shard_map/ppermute | solution.py:1133
  97.8 1.5 collective-permute-start.9
  99.3 7.0 %back_two.1 = (bf16[34,64,896]{2,1,0:T(8,128)(2,1)S(1)}, f32[9,64,64]{2,1,0:T(8,128)S(1)}) custom-call(s32[4]{0:T(128)S(1)} %add_convert_fusion.flags, f32[34,64,896]{2,1,0:T(8,128)S(1)} %get-tuple-element.85.d_ref, f32[34,64,896]{2,1,0:T(8,128)S(1)} %get-tuple-element.81.c2_ref.c_ref, bf16[36,64,1024]{2,1,0:T(8,128)(2,1)} %get-tuple-element.86.hid_ref, ...), custom_call_target="tpu_custom_call" | custom-call | bytes 43200000 | tf_op jit(solution)/shard_map/back_two/pallas_call | solution.py:779
  106.3 3.6 %collective-permute-done.8.left_ref = bf16[17,64,128]{2,1,0:T(8,128)(2,1)S(1)} collective-permute-done((bf16[17,64,128]{2,1,0:T(8,128)(2,1)S(1)}, bf16[17,64,128]{2,1,0:T(8,128)(2,1)S(1)}, u32[]{:S(2)}, u32[]{:S(2)}) %collective-permute-start.8) | collective-permute-done | bytes 278560 | tf_op jit(solution)/shard_map/ppermute | solution.py:1133
  109.9 6.9 %hidden_gradient.1 = (f32[32,64,1024]{2,1,0:T(8,128)S(1)}, bf16[16,64,128]{2,1,0:T(8,128)(2,1)S(1)}, f32[32,2,128]{2,1,0:T(2,128)S(1)}) custom-call(bf16[34,64,896]{2,1,0:T(8,128)(2,1)S(1)} %get-tuple-element.88.ds_ref, bf16[17,64,128]{2,1,0:T(8,128)(2,1)S(1)} %collective-permute-done.8.left_ref, bf16[17,64,128]{2,1,0:T(8,128)(2,1)S(1)} %collective-permute-done.9.right_ref, ...), custom_call_target="tpu_custom_call" | custom-call | bytes 43200000 | tf_op jit(solution)/shard_map/hidden_gradient/pallas_call | solution.py:847
  116.8 1.3 collective-permute-start.10
  118.1 12.8 %all_to_all.33.sum_ref.s1_ref = f32[32,2,128]{2,1,0:T(2,128)S(1)} all-to-all(f32[32,2,128]{2,1,0:T(2,128)S(1)} %get-tuple-element.95), channel_id=1, replica_groups=mesh['gy'=4,'gx'=8] {'gy','gx'}, dimensions={0} | all-to-all | bytes 65536 | tf_op jit(solution)/shard_map/all_to_all | solution.py:1137
  131.0 14.6 %back_one.1 = (bf16[32,64,1024]{2,1,0:T(8,128)(2,1)}, bf16[32,24,128]{2,1,0:T(8,128)(2,1)}) custom-call(s32[4]{0:T(128)S(1)} %add_convert_fusion.flags, f32[32,64,1024]{2,1,0:T(8,128)S(1)} %get-tuple-element.93.dp_ref, bf16[16,64,128]{2,1,0:T(8,128)(2,1)S(1)} %collective-permute-done.10.edge_ref, bf16[32,64,1024]{2,1,0:T(8,128)(2,1)S(1)} %get-tuple-element.91.n1_ref, ...), custom_call_target="tpu_custom_call" | custom-call | bytes 57600000 | tf_op jit(solution)/shard_map/back_one/pallas_call | solution.py:963
  145.5 2.6 %all-to-all-start.4 = ((bf16[32,24,128]{2,1,0:T(8,128)(2,1)}), bf16[32,24,128]{2,1,0:T(8,128)(2,1)S(1)}, u32[]{:S(2)}, u32[]{:S(2)}) async-start(bf16[32,24,128]{2,1,0:T(8,128)(2,1)} %get-tuple-element.99), calls=%async_computation.4 | async-start | bytes 393216 | tf_op jit(solution)/shard_map/all_to_all | solution.py:1137
  148.1 6.6 %input_gradient.2.rest_0_ = bf16[62,64,1792]{2,1,0:T(8,128)(2,1)} custom-call(bf16[32,64,1024]{2,1,0:T(8,128)(2,1)} %get-tuple-element.97.ds, s16[5,64,1792]{2,1,0:T(8,128)(2,1)} %copy-done, bf16[768,256]{1,0:T(8,128)(2,1)S(1)} %get-tuple-element.98.w_ref), custom_call_target="tpu_custom_call" | custom-call | bytes 25200000 | tf_op jit(solution)/shard_map/input_gradient/pallas_call | solution.py:1020
  154.7 2.0 %all-to-all-done.4.g_ref = bf16[32,24,128]{2,1,0:T(8,128)(2,1)S(1)} async-done(((bf16[32,24,128]{2,1,0:T(8,128)(2,1)}), bf16[32,24,128]{2,1,0:T(8,128)(2,1)S(1)}, u32[]{:S(2)}, u32[]{:S(2)}) %all-to-all-start.4) | async-done | bytes 196640 | tf_op jit(solution)/shard_map/all_to_all | solution.py:1137
  157.4 3.9 %all-to-all-start.5 = ((bf16[32,24,128]{2,1,0:T(8,128)(2,1)}), bf16[32,24,128]{2,1,0:T(8,128)(2,1)S(1)}, u32[]{:S(2)}, u32[]{:S(2)}) async-start(bf16[32,24,128]{2,1,0:T(8,128)(2,1)} %sum_share.1), calls=%async_computation.5 | async-start | bytes 393216 | tf_op jit(solution)/shard_map/all_to_all | solution.py:1137
  161.3 6.6 %input_gradient.3 = bf16[62,64,1792]{2,1,0:T(8,128)(2,1)} custom-call(bf16[32,64,1024]{2,1,0:T(8,128)(2,1)} %get-tuple-element.97.ds, s16[5,64,1792]{2,1,0:T(8,128)(2,1)} %copy-done, bf16[768,256]{1,0:T(8,128)(2,1)S(1)} %get-tuple-element.98.w_ref, bf16[62,64,1792]{2,1,0:T(8,128)(2,1)} %input_gradient.2.rest_0_), custom_call_target="tpu_custom_call", output_to_operand_aliasing={{}: (3, {})} | custom-call | bytes 25200000 | tf_op jit(solution)/shard_map/input_gradient/pallas_call | solution.py:1020
  168.0 1.9 %all-to-all-done.5.g_ref = bf16[32,24,128]{2,1,0:T(8,128)(2,1)S(1)} async-done(((bf16[32,24,128]{2,1,0:T(8,128)(2,1)}), bf16[32,24,128]{2,1,0:T(8,128)(2,1)S(1)}, u32[]{:S(2)}, u32[]{:S(2)}) %all-to-all-start.5) | async-done | bytes 196640 | tf_op jit(solution)/shard_map/all_to_all | solution.py:1137
  169.8 1.7 update.1
  (28 shorter events, 3.8 us)
Async XLA Ops:
  0.6 15.9 %copy-start.1 = (f32[2,576,64]{1,2,0:T(8,128)S(1)}, f32[2,576,64]{1,2,0:T(8,128)}, u32[]{:S(2)}) copy-start(f32[2,576,64]{1,2,0:T(8,128)} %param.11) | copy-start | bytes 884740
  0.7 15.9 %copy-start.4 = (f32[2,2,64]{2,1,0:T(2,128)S(1)}, f32[2,2,64]{2,1,0:T(2,128)}, u32[]{:S(2)}) copy-start(f32[2,2,64]{2,1,0:T(2,128)} %param.14) | copy-start | bytes 3076
  3.1 16.7 %collective-permute-start = (bf16[31,64,128]{2,1,0:T(8,128)(2,1)S(1)}, bf16[31,64,128]{2,1,0:T(8,128)(2,1)S(1)}, u32[]{:S(2)}, u32[]{:S(2)}) collective-permute-start(bf16[31,64,128]{2,1,0:T(8,128)(2,1)S(1)} %get-tuple-element.60), channel_id=1, source_target_pairs={{0,1},{1,2},{2,3},{3,4},{4,5},{5,6},{6,7},{8,9},{9,10},{10,11},{11... | collective-permute-start | bytes 1523720 | tf_op jit(solution)/shard_map/ppermute | solution.py:1133
  8.0 11.8 %collective-permute-start.2 = (bf16[64,2688]{1,0:T(8,128)(2,1)S(1)}, bf16[64,2688]{1,0:T(8,128)(2,1)S(1)}, u32[]{:S(2)}, u32[]{:S(2)}) collective-permute-start(bf16[64,2688]{1,0:T(8,128)(2,1)S(1)} %get-tuple-element.64), channel_id=1, source_target_pairs={{0,8},{8,16},{16,24},{1,9},{9,17},{17,25},{2,10},{10,18},{18,26},{... | collective-permute-start | bytes 1032200 | tf_op jit(solution)/shard_map/ppermute | solution.py:1133
  9.4 10.3 %collective-permute-start.1 = (bf16[2,64,896]{2,1,0:T(8,128)(2,1)S(1)}, bf16[2,64,896]{2,1,0:T(8,128)(2,1)S(1)}, u32[]{:S(2)}, u32[]{:S(2)}) collective-permute-start(bf16[2,64,896]{2,1,0:T(8,128)(2,1)S(1)} %get-tuple-element.61), channel_id=1, source_target_pairs={{8,0},{16,8},{24,16},{9,1},{17,9},{25,17},{10,2},{18,10},{26,18},{... | collective-permute-start | bytes 688136 | tf_op jit(solution)/shard_map/ppermute | solution.py:1133
  10.7 9.0 %collective-permute-start.3 = (bf16[64,128]{1,0:T(8,128)(2,1)S(1)}, bf16[64,128]{1,0:T(8,128)(2,1)S(1)}, u32[]{:S(2)}, u32[]{:S(2)}) collective-permute-start(bf16[64,128]{1,0:T(8,128)(2,1)S(1)} %get-tuple-element.66), channel_id=1, source_target_pairs={{0,9},{1,10},{2,11},{3,12},{4,13},{5,14},{6,15},{8,17},{9,18},{10,... | collective-permute-start | bytes 49160 | tf_op jit(solution)/shard_map/ppermute | solution.py:1160
  18.7 1.0 copy-start
  24.8 16.4 %collective-permute-start.4 = (bf16[16,64,128]{2,1,0:T(8,128)(2,1)S(1)}, bf16[16,64,128]{2,1,0:T(8,128)(2,1)S(1)}, u32[]{:S(2)}, u32[]{:S(2)}) collective-permute-start(bf16[16,64,128]{2,1,0:T(8,128)(2,1)S(1)} %get-tuple-element.74), channel_id=1, source_target_pairs={{0,1},{1,2},{2,3},{3,4},{4,5},{5,6},{6,7},{8,9},{9,10},{10,11},{11... | collective-permute-start | bytes 786440 | tf_op jit(solution)/shard_map/ppermute | solution.py:1133
  28.3 12.9 %collective-permute-start.5 = (bf16[16,64,128]{2,1,0:T(8,128)(2,1)S(1)}, bf16[16,64,128]{2,1,0:T(8,128)(2,1)S(1)}, u32[]{:S(2)}, u32[]{:S(2)}) collective-permute-start(bf16[16,64,128]{2,1,0:T(8,128)(2,1)S(1)} %get-tuple-element.75), channel_id=1, source_target_pairs={{1,0},{2,1},{3,2},{4,3},{5,4},{6,5},{7,6},{9,8},{10,9},{11,10},{12... | collective-permute-start | bytes 786440 | tf_op jit(solution)/shard_map/ppermute | solution.py:1133
  41.8 19.1 %collective-permute-start.7 = (bf16[3,64,1024]{2,1,0:T(8,128)(2,1)S(1)}, bf16[3,64,1024]{2,1,0:T(8,128)(2,1)S(1)}, u32[]{:S(2)}, u32[]{:S(2)}) collective-permute-start(bf16[3,64,1024]{2,1,0:T(8,128)(2,1)S(1)} %get-tuple-element.77), channel_id=1, source_target_pairs={{8,0},{16,8},{24,16},{9,1},{17,9},{25,17},{10,2},{18,10},{26,18},{... | collective-permute-start | bytes 1179656 | tf_op jit(solution)/shard_map/ppermute | solution.py:1133
  43.1 17.8 %collective-permute-start.6 = (bf16[2,64,1024]{2,1,0:T(8,128)(2,1)S(1)}, bf16[2,64,1024]{2,1,0:T(8,128)(2,1)S(1)}, u32[]{:S(2)}, u32[]{:S(2)}) collective-permute-start(bf16[2,64,1024]{2,1,0:T(8,128)(2,1)S(1)} %get-tuple-element.76), channel_id=1, source_target_pairs={{0,8},{8,16},{16,24},{1,9},{9,17},{17,25},{2,10},{10,18},{18,26},{... | collective-permute-start | bytes 786440 | tf_op jit(solution)/shard_map/ppermute | solution.py:1133
  95.2 14.7 %collective-permute-start.8 = (bf16[17,64,128]{2,1,0:T(8,128)(2,1)S(1)}, bf16[17,64,128]{2,1,0:T(8,128)(2,1)S(1)}, u32[]{:S(2)}, u32[]{:S(2)}) collective-permute-start(bf16[17,64,128]{2,1,0:T(8,128)(2,1)S(1)} %get-tuple-element.89), channel_id=1, source_target_pairs={{0,1},{1,2},{2,3},{3,4},{4,5},{5,6},{6,7},{8,9},{9,10},{10,11},{11... | collective-permute-start | bytes 835592 | tf_op jit(solution)/shard_map/ppermute | solution.py:1133
  97.8 12.1 %collective-permute-start.9 = (bf16[17,64,128]{2,1,0:T(8,128)(2,1)S(1)}, bf16[17,64,128]{2,1,0:T(8,128)(2,1)S(1)}, u32[]{:S(2)}, u32[]{:S(2)}) collective-permute-start(bf16[17,64,128]{2,1,0:T(8,128)(2,1)S(1)} %get-tuple-element.90), channel_id=1, source_target_pairs={{1,0},{2,1},{3,2},{4,3},{5,4},{6,5},{7,6},{9,8},{10,9},{11,10},{12... | collective-permute-start | bytes 835592 | tf_op jit(solution)/shard_map/ppermute | solution.py:1133
  116.8 14.1 %collective-permute-start.10 = (bf16[16,64,128]{2,1,0:T(8,128)(2,1)S(1)}, bf16[16,64,128]{2,1,0:T(8,128)(2,1)S(1)}, u32[]{:S(2)}, u32[]{:S(2)}) collective-permute-start(bf16[16,64,128]{2,1,0:T(8,128)(2,1)S(1)} %get-tuple-element.94), channel_id=1, source_target_pairs={{1,0},{2,1},{3,2},{4,3},{5,4},{6,5},{7,6},{9,8},{10,9},{11,10},{12... | collective-permute-start | bytes 786440 | tf_op jit(solution)/shard_map/ppermute | solution.py:1133
  145.5 11.1 %all-to-all-start.4 = ((bf16[32,24,128]{2,1,0:T(8,128)(2,1)}), bf16[32,24,128]{2,1,0:T(8,128)(2,1)S(1)}, u32[]{:S(2)}, u32[]{:S(2)}) async-start(bf16[32,24,128]{2,1,0:T(8,128)(2,1)} %get-tuple-element.99), calls=%async_computation.4 | async-start | bytes 393216 | tf_op jit(solution)/shard_map/all_to_all | solution.py:1137
  157.4 12.4 %all-to-all-start.5 = ((bf16[32,24,128]{2,1,0:T(8,128)(2,1)}), bf16[32,24,128]{2,1,0:T(8,128)(2,1)S(1)}, u32[]{:S(2)}, u32[]{:S(2)}) async-start(bf16[32,24,128]{2,1,0:T(8,128)(2,1)} %sum_share.1), calls=%async_computation.5 | async-start | bytes 393216 | tf_op jit(solution)/shard_map/all_to_all | solution.py:1137
  161.3 8.6 %copy-start.2 = (f32[2,576,64]{1,2,0:T(8,128)S(1)}, f32[2,576,64]{1,2,0:T(8,128)}, u32[]{:S(2)}) copy-start(f32[2,576,64]{1,2,0:T(8,128)} %param.12) | copy-start | bytes 884740
  161.3 8.5 %copy-start.3 = (f32[2,576,64]{1,2,0:T(8,128)S(1)}, f32[2,576,64]{1,2,0:T(8,128)}, u32[]{:S(2)}) copy-start(f32[2,576,64]{1,2,0:T(8,128)} %param.13) | copy-start | bytes 884740
  161.3 8.5 %copy-start.5 = (f32[2,2,64]{2,1,0:T(2,128)S(1)}, f32[2,2,64]{2,1,0:T(2,128)}, u32[]{:S(2)}) copy-start(f32[2,2,64]{2,1,0:T(2,128)} %param.15) | copy-start | bytes 3076
  161.3 8.5 %copy-start.6 = (f32[2,2,64]{2,1,0:T(2,128)S(1)}, f32[2,2,64]{2,1,0:T(2,128)}, u32[]{:S(2)}) copy-start(f32[2,2,64]{2,1,0:T(2,128)} %param.16) | copy-start | bytes 3076

commit v5 on v4

--- a/solution.py
+++ b/solution.py
@@ -53,8 +53,20 @@
 held = pl.BlockSpec(memory_space=pltpu.VMEM)
 
 
+def vmem(array):
+    return pltpu.with_memory_space_constraint(array, pltpu.VMEM)
+
+
 def hbm(array):
     return pltpu.with_memory_space_constraint(array, pltpu.HBM)
+
+
+def inside():
+    flags = []
+    for axis in BOTH:
+        at = lax.axis_index(axis)
+        flags += [at > 0, at < lax.axis_size(axis) - 1]
+    return [jnp.where(flag, 1.0, 0.0) for flag in flags]
 
 
 def part_of(ref, step, n=S):
@@ -298,12 +310,12 @@
 
 
 def first_last_kernel(
-    xa_ref, xb_ref, ba_ref, bb_ref, xrow_ref, xcol_ref, corner_ref, w_ref, c_ref, st_ref, er_ref,
-    el_ref, edge_ref, xs, run,
+    x_ref, bits_ref, xrow_ref, xcol_ref, corner_ref, w_ref, c_ref, st_ref, er_ref, el_ref,
+    edge_ref, xs, run,
 ):
     step, steps = (pl.program_id(0), pl.num_programs(0))
-    c_ref = part_of(c_ref, step)
-    rows, lanes = (xa_ref.shape[0], xrow_ref.shape[1] * 2 // 3)
+    c_ref, x_ref, bits_ref = (part_of(a, step) for a in (c_ref, x_ref, bits_ref))
+    rows, lanes = (x_ref.shape[0], x_ref.shape[2])
     r = rows // 2
     low = low_half()
 
@@ -313,9 +325,9 @@
 
     xs[0, 0, :, :L] = xrow_ref[:, :L]
     xs[0, 0, :, L:] = xrow_ref[:, lanes - 2 * L : lanes]
-    mask_tile(xa_ref, ba_ref, 0, xs, 0)
-    mask_tile(xb_ref, bb_ref, 0, xs, 1)
-    mask_tile(xb_ref, bb_ref, 1, xs, 2)
+    mask_tile(x_ref, bits_ref, 0, xs, 0)
+    mask_tile(x_ref, bits_ref, lanes // L - 2, xs, 1)
+    mask_tile(x_ref, bits_ref, lanes // L - 1, xs, 2)
     wide = 3 * L
     rows_of = lambda q, a, b: w_ref[q * wide + a * C : q * wide + b * C]
     w = jnp.concatenate([rows_of(q, 0, 4) for q in range(5)], axis=0)
@@ -347,16 +359,12 @@
     rows, scan_count, lanes = x.shape
     r = rows // 2
     shape = lambda dtype, *s: jax.ShapeDtypeStruct(s, dtype)
-    at = lambda n, width, k: pl.BlockSpec((n, S, width), lambda g: (0, g, k))
-    end = lanes // (2 * L) - 1
     return pl.pallas_call(
         first_last_kernel,
         grid=(scan_count // S,),
         in_specs=[
-            at(rows, L, 0),
-            at(rows, 2 * L, end),
-            at(bits.shape[0], L, 0),
-            at(bits.shape[0], 2 * L, end),
+            held,
+            held,
             pl.BlockSpec((S, down.shape[1]), lambda g: (g, 0)),
             scans(r, L),
             pl.BlockSpec((S, L), lambda g: (g, 0)),
@@ -383,14 +391,14 @@
         compiler_params=params_of(),
         cost_estimate=cost(4),
         name="conv_one_ends",
-    )(hbm(x), hbm(x), hbm(bits), hbm(bits), down, xcol, corner, w)
+    )(vmem(x), vmem(bits), down, xcol, corner, w)
 
 
 def conv_one_kernel(
     x_ref, bits_ref, xrow_ref, ends_ref, w_ref, c_ref, st_ref, up_ref, down_ref, xs, run
 ):
     step, steps = (pl.program_id(0), pl.num_programs(0))
-    c_ref = part_of(c_ref, step)
+    c_ref, x_ref, bits_ref = (part_of(a, step) for a in (c_ref, x_ref, bits_ref))
     rows, tiles = (x_ref.shape[0], x_ref.shape[2] // L)
     r, inner = (rows // 2, tiles // 2 - 1)
 
@@ -433,8 +441,8 @@
         conv_one_kernel,
         grid=(scan_count // S,),
         in_specs=[
-            scans(rows, lanes),
-            scans(bits.shape[0], lanes),
+            held,
+            held,
             pl.BlockSpec((S, down.shape[1]), lambda g: (g, 0)),
             whole(ends.shape),
             whole(w.shape),
@@ -453,7 +461,7 @@
         compiler_params=params_of(),
         cost_estimate=cost(11),
         name="conv_one",
-    )(hbm(x), hbm(bits), down, ends, w)
+    )(vmem(x), vmem(bits), down, ends, w)
 
 
 def pack_kernel(up_ref, down_ref, edge_ref, left_ref, right_ref, up_out, down_out):
@@ -487,7 +495,7 @@
 
 
 def conv_two_kernel(
-    flags, c_ref, ends_ref, up_ref, down_ref, left_ref, right_ref, st_ref, np_ref, w_ref, c2_ref,
+    c_ref, ends_ref, up_ref, down_ref, left_ref, right_ref, st_ref, np_ref, w_ref, c2_ref,
     n1_ref, hid_ref, st2_ref, rim, run, *, count,
 ):
     step, steps = (pl.program_id(0), pl.num_programs(0))
@@ -500,7 +508,7 @@
     offset = -mean * inv
     scale = 0.5 * np_ref[0:1] * inv
     shift = 0.5 * (np_ref[0:1] * offset + np_ref[1:2])
-    f_up, f_down, f_left, f_right = (flags[k].astype(f32) for k in range(4))
+    f_up, f_down, f_left, f_right = inside()
     low = low_half(S2)
     left = jnp.where(low, f_left, 1.0)
     right = jnp.where(low, 1.0, f_right)
@@ -561,7 +569,7 @@
     finish_stats(step, steps, pilot, sums, float(r * t_out * S2), run, st2_ref)
 
 
-def conv_two(flags, c1, ends, up, down, left, right, st, np2, w, count):
+def conv_two(c1, ends, up, down, left, right, st, np2, w, count):
     r, scan_count, wide = c1.shape
     wide = wide + 2 * L
     lanes = wide - L
@@ -570,7 +578,6 @@
         functools.partial(conv_two_kernel, count=count),
         grid=(scan_count // S2,),
         in_specs=[
-            pl.BlockSpec(memory_space=pltpu.SMEM),
             held,
             held,
             more(2, wide),
@@ -595,14 +602,14 @@
         compiler_params=params_of(),
         cost_estimate=cost(14),
         name="conv_two",
-    )(flags, c1, ends, up, down, left, right, st, np2, w)
+    )(c1, ends, up, down, left, right, st, np2, w)
 
 
 def output_kernel(
     c2_ref, st_ref, np_ref, cot_ref, up_ref, down_ref, feat_ref, d_ref, sum_ref, run, *, count,
 ):
     step, steps = (pl.program_id(0), pl.num_programs(0))
-    c2_ref, d_ref = (part_of(a, step, S2) for a in (c2_ref, d_ref))
+    c2_ref, d_ref, cot_ref = (part_of(a, step, S2) for a in (c2_ref, d_ref, cot_ref))
     r, tiles = (cot_ref.shape[0], cot_ref.shape[2] // L)
     mean, inv = stats_of(st_ref, count)
     offset = -mean * inv
@@ -663,7 +670,7 @@
             held,
             whole(st.shape),
             whole(np2.shape),
-            more(r, lanes),
+            held,
             pl.BlockSpec((S2, up.shape[1]), lambda g: (g, 0)),
             more(2, lanes),
         ],
@@ -677,10 +684,10 @@
         compiler_params=params_of(),
         cost_estimate=cost(12),
         name="output",
-    )(c2, st, np2, hbm(cot), up, down)
-
-
-def norm_back_two(flags, st_ref, sum_ref, np_ref, count, rows):
+    )(c2, st, np2, vmem(cot), up, down)
+
+
+def norm_back_two(st_ref, sum_ref, np_ref, count, rows):
     cells = 2.0 * count * st_ref.shape[0]
     mean, inv = stats_of(st_ref, count)
     shift_sum, gain_sum = sums_of(sum_ref)
@@ -688,7 +695,7 @@
     c_n = -gain * inv * gain_sum / cells
     c_0 = -gain * shift_sum / cells - c_n * mean
     gain = 0.5 * gain
-    f_up, f_down = (flags[k].astype(f32) for k in range(2))
+    f_up, f_down = inside()[:2]
 
     def back(row, d, c):
         d = d * gain + (c * c_n + c_0)
@@ -703,11 +710,11 @@
 
 
 def rim_two_kernel(
-    flags, d_ref, c_ref, st_ref, sum_ref, np_ref, er_ref, el_ref, *, count
+    d_ref, c_ref, st_ref, sum_ref, np_ref, er_ref, el_ref, *, count
 ):
     d_ref, c_ref = (part_of(a, pl.program_id(0), S2) for a in (d_ref, c_ref))
     rows, last = (d_ref.shape[0], d_ref.shape[2] // L - 1)
-    back = norm_back_two(flags, st_ref, sum_ref, np_ref, count, rows - 3)
+    back = norm_back_two(st_ref, sum_ref, np_ref, count, rows - 3)
     low = low_half(S2)
     half = rows // 2
     column = lambda row, t: back(row, pair(d_ref, row, t), pair(c_ref, row, t))
@@ -718,13 +725,13 @@
         er_ref[k] = jnp.where(low, far, near).astype(bf16)
 
 
-def rim_two(flags, d, c2, st, sums, np2, count):
+def rim_two(d, c2, st, sums, np2, count):
     rows, scan_count, lanes = d.shape
     return pl.pallas_call(
         functools.partial(rim_two_kernel, count=count),
         grid=(scan_count // S2,),
         in_specs=[
-            pl.BlockSpec(memory_space=pltpu.SMEM), held, held, whole(st.shape),
+            held, held, whole(st.shape),
             whole(sums.shape), whole(np2.shape),
         ],
         out_specs=[more(rows // 2, L)] * 2,
@@ -732,16 +739,16 @@
         compiler_params=params_of(),
         cost_estimate=cost(3),
         name="rim_two",
-    )(flags, d, c2, st, sums, np2)
+    )(d, c2, st, sums, np2)
 
 
 def back_two_kernel(
-    flags, d_ref, c2_ref, hid_ref, st_ref, sum_ref, np_ref, ds_ref, kg_ref, grad, *, count
+    d_ref, c2_ref, hid_ref, st_ref, sum_ref, np_ref, ds_ref, kg_ref, grad, *, count
 ):
     step, steps = (pl.program_id(0), pl.num_programs(0))
-    d_ref, c2_ref, ds_ref = (part_of(a, step) for a in (d_ref, c2_ref, ds_ref))
+    d_ref, c2_ref, ds_ref = (part_of(a, step, S2) for a in (d_ref, c2_ref, ds_ref))
     r, tiles = (c2_ref.shape[0] - 3, c2_ref.shape[2] // L)
-    back = norm_back_two(flags, st_ref, sum_ref, np_ref, count, r)
+    back = norm_back_two(st_ref, sum_ref, np_ref, count, r)
 
     @pl.when(step == 0)
     def _():
@@ -752,12 +759,17 @@
         for row in range(r + 3):
             d = back(row, pair(d_ref, row, t), pair(c2_ref, row, t))
             ds_ref[row, :, t * L : (t + 1) * L] = d.astype(bf16)
-        lanes = slice(t * L, (t + 2) * L)
-        rhs = jnp.concatenate(
-            [hid_ref[p + 1 : p + 1 + r, :, lanes].reshape(r * S, 2 * L) for p in range(3)], axis=1
+        own = [ds_ref[i + 1, :, t * L : (t + 1) * L] for i in range(r)]
+        none = jnp.zeros_like(own[0])
+        lhs = jnp.concatenate(
+            [
+                jnp.transpose(jnp.concatenate([none] * p + own + [none] * (2 - p), axis=0))
+                for p in range(3)
+            ],
+            axis=0,
         )
-        lhs = ds_ref[1 : r + 1, :, t * L : (t + 1) * L].reshape(r * S, L)
-        part = lax.dot_general(lhs, rhs, (((0,), (0,)), ((), ())), preferred_element_type=f32)
+        rhs = hid_ref[1 : r + 3, :, t * L : (t + 2) * L].reshape((r + 2) * S2, 2 * L)
+        part = jnp.dot(lhs, rhs, preferred_element_type=f32)
         total = part if total is None else total + part
     grad[...] += total
 
@@ -767,23 +779,22 @@
             for q in range(3):
                 block = None
                 for w in range(2):
-                    at = 4 * p * C + (w + q) * C
-                    part = grad[w * C : (w + 1) * C, at : at + C]
+                    at = (2 * p + w) * C
+                    part = grad[at : at + C, (w + q) * C : (w + q + 1) * C]
                     block = part if block is None else block + part
                 kg_ref[3 * p + q] = block
 
 
-def back_two(flags, d, c2, hid, st, sums, np2, count):
+def back_two(d, c2, hid, st, sums, np2, count):
     r, scan_count, wide = hid.shape
     r, lanes = (r - 5, wide - L)
     return pl.pallas_call(
         functools.partial(back_two_kernel, count=count),
-        grid=(scan_count // S,),
+        grid=(scan_count // S2,),
         in_specs=[
-            pl.BlockSpec(memory_space=pltpu.SMEM),
-            held,
-            held,
-            scans(r + 5, wide),
+            held,
+            held,
+            more(r + 5, wide),
             whole(st.shape),
             whole(sums.shape),
             whole(np2.shape),
@@ -793,91 +804,125 @@
             resident((r + 3, scan_count, lanes), bf16),
             jax.ShapeDtypeStruct((9, C, C), f32),
         ],
-        scratch_shapes=[pltpu.VMEM((L, 12 * C), f32)],
+        scratch_shapes=[pltpu.VMEM((6 * C, 4 * C), f32)],
         compiler_params=params_of(),
         cost_estimate=cost(12),
         name="back_two",
-    )(flags, d, c2, hbm(hid), st, sums, np2)
-
-
-def hidden_kernel(
-    ds_ref, left_ref, right_ref, n1_ref, np_ref, w_ref, dp_ref, edge_ref, sum1_ref, rim, run
+    )(d, c2, hbm(hid), st, sums, np2)
+
+
+def hidden_tile(t, parts, n1_ref, np_ref, w_ref, dp_ref, into, first, last):
+    r = n1_ref.shape[0] - 1
+    pairs, n_scans = ((r + 1) // 2, n1_ref.shape[1])
+    low = low_half(n_scans)
+    scale, shift = (0.5 * np_ref[0:1], 0.5 * np_ref[1:2])
+    parts = [p.reshape(pairs + 1, 2, n_scans, L) for p in parts]
+    pieces = [p[a : a + pairs, b] for a in range(2) for b in range(2) for p in parts]
+    lhs = jnp.concatenate([p.reshape(pairs * n_scans, L) for p in pieces], axis=1)
+    acc = jnp.dot(lhs, w_ref[...], preferred_element_type=f32).reshape(pairs, n_scans, 2 * L)
+    sums = [jnp.zeros((8, L), f32), jnp.zeros((8, L), f32)]
+    for i in range(r + 1):
+        n = pair(n1_ref, i, t).astype(f32)
+        h = n * scale + shift
+        s = 1.0 + jnp.tanh(h)
+        d = acc[i // 2, :, (i % 2) * L : (i % 2 + 1) * L] * (s + h * s * (2.0 - s))
+        dp_ref[i, :, into * L : (into + 1) * L] = d
+        if i < r:
+            if first:
+                d = jnp.where(low, 0.0, d)
+            if last:
+                d = jnp.where(low, d, 0.0)
+            sums = [sums[0] + halves(d), sums[1] + halves(d * n)]
+    return sums
+
+
+def hidden_kernel(ds_ref, n1_ref, np_ref, w_ref, dp_ref, sum_ref, run):
+    step, steps = (pl.program_id(0), pl.num_programs(0))
+    ds_ref, n1_ref, dp_ref = (part_of(a, step) for a in (ds_ref, n1_ref, dp_ref))
+    sums = None
+    for t in range(1, n1_ref.shape[2] // L - 1):
+        parts = [ds_ref[:, :, k * L : (k + 1) * L] for k in (t - 1, t)]
+        sums = added(
+            sums, hidden_tile(t, parts, n1_ref, np_ref, w_ref, dp_ref, t - 1, False, False)
+        )
+    add_sums(step, steps, [0.5 * x for x in sums], run, sum_ref)
+
+
+def hidden_gradient(ds, n1, np2, w):
+    r, scan_count, wide = n1.shape
+    return pl.pallas_call(
+        hidden_kernel,
+        grid=(scan_count // S,),
+        in_specs=[held, held, whole(np2.shape), whole(w.shape)],
+        out_specs=[held, whole((1, 2, L))],
+        out_shape=[
+            resident((r, scan_count, wide - 2 * L), f32),
+            jax.ShapeDtypeStruct((1, 2, L), f32),
+        ],
+        scratch_shapes=[pltpu.VMEM((8, L), f32)],
+        compiler_params=params_of(),
+        cost_estimate=cost(6),
+        name="hidden_gradient",
+    )(ds, n1, np2, w)
+
+
+def hidden_ends_kernel(
+    ds_ref, left_ref, right_ref, n1_ref, np_ref, w_ref, inner_ref, dp_ref, edge_ref, sum_ref, rim,
+    run,
 ):
     step, steps = (pl.program_id(0), pl.num_programs(0))
-    ds_ref, n1_ref, dp_ref = (part_of(a, step) for a in (ds_ref, n1_ref, dp_ref))
+    ds_ref, n1_ref, dp_ref = (part_of(a, step, S2) for a in (ds_ref, n1_ref, dp_ref))
     r, tiles = (n1_ref.shape[0] - 1, n1_ref.shape[2] // L)
-    pairs = (r + 1) // 2
-    low = low_half()
+    low = low_half(S2)
     for row in range(r + 3):
         rim[row] = rim_of(right_ref, left_ref, row, low).astype(bf16)
-    scale, shift = (0.5 * np_ref[0:1], 0.5 * np_ref[1:2])
-    sums = None
-    for t in range(tiles):
-        parts = []
-        for k in (t - 1, t):
-            part = ds_ref[:, :, k * L : (k + 1) * L] if 0 <= k < tiles - 1 else rim[...]
-            parts.append(part.reshape(pairs + 1, 2, S, L))
-        pieces = [p[a : a + pairs, b] for a in range(2) for b in range(2) for p in parts]
-        lhs = jnp.concatenate([p.reshape(pairs * S, L) for p in pieces], axis=1)
-        acc = jnp.dot(lhs, w_ref[...], preferred_element_type=f32).reshape(pairs, S, 2 * L)
-        part = [jnp.zeros((8, L), f32), jnp.zeros((8, L), f32)]
-        for i in range(r + 1):
-            n = pair(n1_ref, i, t).astype(f32)
-            h = n * scale + shift
-            s = 1.0 + jnp.tanh(h)
-            d = acc[i // 2, :, (i % 2) * L : (i % 2 + 1) * L] * (s + h * s * (2.0 - s))
-            dp_ref[i, :, t * L : (t + 1) * L] = d
-            if i < r:
-                if t == 0:
-                    d = jnp.where(low, 0.0, d)
-                if t == tiles - 1:
-                    d = jnp.where(low, d, 0.0)
-                part = [part[0] + halves(d), part[1] + halves(d * n)]
-        sums = added(sums, part)
-    add_sums(step, steps, [0.5 * x for x in sums], run, sum1_ref)
-    for i in range(pairs):
-        both = jnp.where(low, swap(pair(dp_ref, pairs + i, 0)), pair(dp_ref, i, 0))
+    first, last = (ds_ref[:, :, k * L : (k + 1) * L] for k in (0, tiles - 2))
+    args = (n1_ref, np_ref, w_ref, dp_ref)
+    sums = hidden_tile(0, [rim[...], first], *args, 0, True, False)
+    sums = added(sums, hidden_tile(tiles - 1, [last, rim[...]], *args, 1, False, True))
+    sums = [0.5 * jnp.sum(x, axis=0, keepdims=True) for x in sums]
+    sums = [x + inner_ref[0, k : k + 1] / steps for k, x in enumerate(sums)]
+    add_sums(step, steps, sums, run, sum_ref)
+    half = edge_ref.shape[0]
+    for i in range(half):
+        both = jnp.where(low, swap(pair(dp_ref, half + i, 0)), pair(dp_ref, i, 0))
         edge_ref[i] = both.astype(bf16)
 
 
-def hidden_gradient(ds, left, right, n1, np2, w, devices):
-    r, scan_count, wide = n1.shape
-    r, lanes = (r - 1, wide - L)
+def hidden_ends(ds, left, right, n1, np2, w, inner, devices):
+    r, scan_count, _wide = n1.shape
     half = left.shape[0]
     return pl.pallas_call(
-        hidden_kernel,
-        grid=(scan_count // S,),
+        hidden_ends_kernel,
+        grid=(scan_count // S2,),
         in_specs=[
             held,
-            scans(half, L),
-            scans(half, L),
+            more(half, L),
+            more(half, L),
             held,
             whole(np2.shape),
             whole(w.shape),
-        ],
-        out_specs=[
-            held,
-            scans((r + 1) // 2, L),
-            whole((devices, 2, L)),
-        ],
+            whole(inner.shape),
+        ],
+        out_specs=[held, more(r // 2, L), whole((devices, 2, L))],
         out_shape=[
-            resident((r + 1, scan_count, wide), f32),
-            jax.ShapeDtypeStruct(((r + 1) // 2, scan_count, L), bf16),
+            resident((r, scan_count, 2 * L), f32),
+            jax.ShapeDtypeStruct((r // 2, scan_count, L), bf16),
             jax.ShapeDtypeStruct((devices, 2, L), f32),
         ],
-        scratch_shapes=[pltpu.VMEM((r + 3, S, L), bf16), pltpu.VMEM((8, L), f32)],
-        compiler_params=params_of(),
-        cost_estimate=cost(12),
-        name="hidden_gradient",
-    )(ds, left, right, n1, np2, w)
+        scratch_shapes=[pltpu.VMEM((r + 2, S2, L), bf16), pltpu.VMEM((8, L), f32)],
+        compiler_params=params_of(),
+        cost_estimate=cost(3),
+        name="hidden_gradient_ends",
+    )(ds, left, right, n1, np2, w, inner)
 
 
 def back_one_kernel(
-    flags, dp_ref, edge_ref, n1_ref, x_ref, bits_ref, st_ref, sum_ref, np_ref, kg2_ref, ds, kg_ref,
+    dp_ref, ends_ref, edge_ref, n1_ref, x_ref, bits_ref, st_ref, sum_ref, np_ref, kg2_ref, ds, kg_ref,
     xm, grad, flat, *, count,
 ):
     step, steps = (pl.program_id(0), pl.num_programs(0))
-    dp_ref, n1_ref = (part_of(a, step) for a in (dp_ref, n1_ref))
+    dp_ref, ends_ref, n1_ref = (part_of(a, step) for a in (dp_ref, ends_ref, n1_ref))
     r, tiles = (n1_ref.shape[0] - 1, n1_ref.shape[2] // L - 1)
     cells = 2.0 * count * st_ref.shape[0]
     _mean, inv = stats_of(st_ref, count)
@@ -886,7 +931,7 @@
     c_n = -gain * gain_sum / cells
     c_0 = -gain * shift_sum / cells
     gain = 0.5 * gain
-    f_down, f_right = (flags[1].astype(f32), flags[3].astype(f32))
+    f_down, f_right = inside()[1::2]
     packed = edge_ref.shape[0]
     low = low_half()
     right = jnp.where(low, 1.0, f_right)
@@ -896,7 +941,7 @@
         grad[...] = jnp.zeros_like(grad)
 
     def line(i, t):
-        d = pair(dp_ref, i, t)
+        d = pair(ends_ref, i, min(t, 1)) if t in (0, tiles) else pair(dp_ref, i, t - 1)
         if t == tiles:
             beyond = edge_ref[i % packed].astype(f32)
             d = jnp.where(low, d, swap(beyond) if i >= packed else beyond)
@@ -907,43 +952,52 @@
             d = d * f_down
         ds[i, :, t * L : (t + 1) * L] = d.astype(bf16)
 
-    turned = (((0,), (0,)), ((), ()))
-    totals = [None, None, None]
-    done = 0
-    for t in range(tiles):
-        while done < t + 2:
-            for i in range(r + 1):
-                line(i, done)
-            done += 1
-        for k in (2 * t, 2 * t + 1):
+    def turned(t, first):
+        return jnp.transpose(ds[first : first + r, :, t * L : (t + 1) * L].reshape(r * S, L))
+
+    columns = []
+    total_even, total_odd = (None, None)
+    for t in range(tiles + 1):
+        for i in range(r + 1):
+            line(i, t)
+        columns.append([turned(t, 0), turned(t, 1)])
+        if t == 0:
+            continue
+        k = t - 1
+        for a in (2 * k, 2 * k + 1):
             for g in range(bits_ref.shape[0]):
-                word = bits_ref[g, :, k * L : (k + 1) * L]
+                word = bits_ref[g, :, a * L : (a + 1) * L]
                 for row in range(g * BITS, min(2 * r, (g + 1) * BITS)):
-                    x = live(word, row, pair(x_ref, row, k))
-                    xm[row % 2, row // 2, :, k * L : (k + 1) * L] = x
-        lanes = slice(t * L, (t + 2) * L)
-        xl = slice(2 * t * L, 2 * (t + 1) * L)
-        rows = [ds[a : a + r, :, lanes].reshape(r * S, 2 * L) for a in range(2)]
+                    x = live(word, row, pair(x_ref, row, a))
+                    xm[row % 2, row // 2, :, a * L : (a + 1) * L] = x
+        xl = slice(2 * k * L, 2 * (k + 1) * L)
         xe, xo = (xm[a, :, :, xl].reshape(r * S, 2 * L) for a in range(2))
-        for k, (a, b) in enumerate(((xe, rows[0]), (xo, rows[0]), (xo, rows[1]))):
-            part = lax.dot_general(a, b, turned, preferred_element_type=f32)
-            totals[k] = part if totals[k] is None else totals[k] + part
-    for k in range(3):
-        grad[k] += totals[k]
+        here, below = (
+            jnp.concatenate([columns[k][a][C:], columns[t][a]], axis=0) for a in range(2)
+        )
+        even = jnp.dot(here, xe, preferred_element_type=f32)
+        odd = jnp.dot(
+            jnp.concatenate([here, below], axis=0), xo, preferred_element_type=f32
+        )
+        total_even = even if total_even is None else total_even + even
+        total_odd = odd if total_odd is None else total_odd + odd
+    grad[: 3 * C] += total_even
+    grad[3 * C :] += total_odd
 
     @pl.when(step == steps - 1)
     def _():
         blocks = []
         for p in range(3):
-            g = (2, 0, 1)[p]
+            first = (6, 0, 3)[p] * C
             for q in range(3):
                 block = None
                 for v in range(1, 4):
                     u = q - 3 + 2 * v
                     if 0 <= u < 4:
-                        part = grad[g, u * C : (u + 1) * C, v * C : (v + 1) * C]
+                        at = first + (v - 1) * C
+                        part = grad[at : at + C, u * C : (u + 1) * C]
                         block = part if block is None else block + part
-                blocks.append(jnp.transpose(block))
+                blocks.append(block)
         blocks += [kg2_ref[8]] + [kg2_ref[k] for k in range(8)]
         for a in range(9):
             flat[a * C : (a + 1) * C] = jnp.concatenate(blocks[2 * a : 2 * a + 2], axis=1)
@@ -954,7 +1008,7 @@
             kg_ref[k] = flat[k * share : (k + 1) * share].astype(bf16)
 
 
-def back_one(flags, dp, edge, n1, x, bits, st, sums, np2, kg2, count):
+def back_one(dp, ends, edge, n1, x, bits, st, sums, np2, kg2, count):
     rows, scan_count, lanes = x.shape
     r, tiles = (rows // 2, lanes // L // 2)
     devices = st.shape[0]
@@ -964,7 +1018,7 @@
         functools.partial(back_one_kernel, count=count),
         grid=(scan_count // S,),
         in_specs=[
-            pl.BlockSpec(memory_space=pltpu.SMEM),
+            held,
             held,
             scans(edge.shape[0], L),
             held,
@@ -982,13 +1036,13 @@
         ],
         scratch_shapes=[
             pltpu.VMEM((2, r, S, lanes), bf16),
-            pltpu.VMEM((3, 4 * C, 4 * C), f32),
+            pltpu.VMEM((9 * C, 4 * C), f32),
             pltpu.VMEM((devices * share, L), f32),
         ],
         compiler_params=params_of(),
         cost_estimate=cost(16),
         name="back_one",
-    )(flags, dp, edge, n1, hbm(x), hbm(bits), st, sums, np2, kg2)
+    )(dp, ends, edge, n1, hbm(x), hbm(bits), st, sums, np2, kg2)
 
 
 def input_grad_kernel(ds, bits_ref, w_ref, *rest):
@@ -1146,8 +1200,6 @@
     kt, kmt, kvt = (jnp.transpose(a, (0, 2, 1)) for a in (kernels, kernel_m, kernel_v))
     gy, gx = (lax.axis_size("gy"), lax.axis_size("gx"))
     devices = gy * gx
-    y, z = (lax.axis_index("gy"), lax.axis_index("gx"))
-    flags = jnp.stack([y > 0, y < gy - 1, z > 0, z < gx - 1]).astype(jnp.int32)
     rows, scan_count, lanes = x.shape
     r, tiles = (rows // 2, lanes // L // 2)
     count = float(scan_count * r * tiles)
@@ -1162,7 +1214,7 @@
     )
     bits, w1, w2, w2b, w1b, np2 = prepare(occ, kt, norm_params)
 
-    xcol, cot_down, flags = lax.optimization_barrier((xcol, cot_down, flags))
+    xcol, cot_down = lax.optimization_barrier((xcol, cot_down))
     ends, st1, going_right, going_left, edge = first_last(x, bits, down, xcol, corner, w1)
     left_in = shifted(going_right, "gx", 1)
     right_in = shifted(going_left, "gx", -1)
@@ -1173,19 +1225,20 @@
     st1 = exchange(st1)
 
     c2, n1, hid, st2 = conv_two(
-        flags, c1, ends, up_in, down_in, left_in, right_in, st1, np2, w2, count
+        c1, ends, up_in, down_in, left_in, right_in, st1, np2, w2, count
     )
     st2 = exchange(st2)
     features, d2, sums2 = output(c2, st2, np2, cot, down, cot_down, count)
     sums2 = exchange(sums2)
-    going_right, going_left = rim_two(flags, d2, c2, st2, sums2, np2, count)
+    going_right, going_left = rim_two(d2, c2, st2, sums2, np2, count)
     left_in = shifted(going_right, "gx", 1)
     right_in = shifted(going_left, "gx", -1)
-    ds, kg2 = back_two(flags, d2, c2, hid, st2, sums2, np2, count)
-    d1, edge, sums1 = hidden_gradient(ds, left_in, right_in, n1, np2, w2b, devices)
+    ds, kg2 = back_two(d2, c2, hid, st2, sums2, np2, count)
+    d1, sums1 = hidden_gradient(ds, n1, np2, w2b)
+    d1_ends, edge, sums1 = hidden_ends(ds, left_in, right_in, n1, np2, w2b, sums1, devices)
     edge = shifted(edge, "gx", -1)
     sums1 = exchange(sums1)
-    d1, grads = back_one(flags, d1, edge, n1, x, bits, st1, sums1, np2, kg2, count)
+    d1, grads = back_one(d1, d1_ends, edge, n1, x, bits, st1, sums1, np2, kg2, count)
     grads = exchange(grads)
     input_grad = input_gradient(d1, bits, w1b, 0, None)
     grads, input_grad = lax.optimization_barrier((sum_share(grads), input_grad))

time: 172 us -> 163 us (0.948)
  Pallas kernels: 82.4 us -> 76.2 us
  waiting for transfers between devices: 7.49 us -> 4.87 us
    pallas_call x3 -> x4, Pallas kernels: 23.4 us -> 20.5 us  [the longest x1 9.63 us: conv_one(): pl.pallas_call(conv_one_kernel, grid=(scan_count // S,), in_specs=[held,...]
    ppermute x10, waiting for transfers between devices: 3.66 us -> 0.97 us  [shifted(): return lax.ppermute(block, axis, route)]
  transfers between devices with their start and end apart: 13 -> 13, of which waited for: 3 -> 5; matrix products, arithmetic and copies ran while one was open for 0% -> 0% of each run, Pallas kernels for 20% -> 23%
where the time goes in v5:
time: 163 us
  Pallas kernels  76.2 us (47%)
  blocking collectives  45 us (28%)
  starting transfers between devices  35.4 us (22%)
  waiting for transfers between devices  4.87 us (3%)
    all_to_all x4, blocking collectives, exchange(): return lax.all_to_all(rows, BOTH, 0, 0, tiled=True)  45 us
    ppermute x10, starting transfers between devices, shifted(): return lax.ppermute(block, axis, route)  23.2 us
    pallas_call x1, Pallas kernels, back_one(): pl.pallas_call(functools.partial(back_one_kernel, count=count), grid=(sca...  13.6 us
    pallas_call x2, Pallas kernels, input_gradient(): pl.pallas_call(input_grad_kernel, grid=(steps,), in_specs=[at(r, wide), a...  13.3 us
    pallas_call x1, Pallas kernels, conv_one(): pl.pallas_call(conv_one_kernel, grid=(scan_count // S,), in_specs=[held,...  9.63 us
    pallas_call x1, Pallas kernels, conv_two(): pl.pallas_call(functools.partial(conv_two_kernel, count=count), grid=(sca...  8.14 us
    pallas_call x1, Pallas kernels, back_two(): pl.pallas_call(functools.partial(back_two_kernel, count=count), grid=(sca...  6.85 us
    all_to_all x2, starting transfers between devices, exchange(): return lax.all_to_all(rows, BOTH, 0, 0, tiled=True)  6.51 us
  transfers between devices with their start and end apart: 13, of which 5 were waited for; matrix products, arithmetic and copies ran while one was open for 0% of the time, Pallas kernels for 23%

profile of v5, /device:TPU:0, one launch (start us, length us, event | category | flops | bytes accessed | tf_op | source)
XLA Modules:
  0.0 162.5 jit_solution(14406141072943505196)
XLA Ops:
  0.7 2.5 %edges.1 = (bf16[64,2688]{1,0:T(8,128)(2,1)S(1)}, bf16[2,64,896]{2,1,0:T(8,128)(2,1)S(1)}, bf16[64,128]{1,0:T(8,128)(2,1)S(1)}, bf16[31,64,128]{2,1,0:T(8,128)(2,1)S(1)}) custom-call(bf16[62,64,1792]{2,1,0:T(8,128)(2,1)} %bitcast.19, bf16[62,64,1792]{2,1,0:T(8,128)(2,1)} %bitcast.20, s32[28,64,62]{2,1,0:T(8,128)} %bitcast.38, bf16[31,64,896]{2,1,0:T(8,128)(2,1)} %bitcast.26, ...), custom_call_target="tpu_custom_call" | custom-call | bytes 10800000 | tf_op jit(solution)/shard_map/edges/pallas_call | solution.py:216
  3.2 5.1 %collective-permute-start.1 = (bf16[31,64,128]{2,1,0:T(8,128)(2,1)S(1)}, bf16[31,64,128]{2,1,0:T(8,128)(2,1)S(1)}, u32[]{:S(2)}, u32[]{:S(2)}) collective-permute-start(bf16[31,64,128]{2,1,0:T(8,128)(2,1)S(1)} %get-tuple-element.63), channel_id=1, source_target_pairs={{0,1},{1,2},{2,3},{3,4},{4,5},{5,6},{6,7},{8,9},{9,10},{10,11},{11... | collective-permute-start | bytes 1523720 | tf_op jit(solution)/shard_map/ppermute | solution.py:1187
  8.4 1.5 collective-permute-start
  9.9 1.3 collective-permute-start.2
  11.2 5.7 %collective-permute-start.3 = (bf16[64,128]{1,0:T(8,128)(2,1)S(1)}, bf16[64,128]{1,0:T(8,128)(2,1)S(1)}, u32[]{:S(2)}, u32[]{:S(2)}) collective-permute-start(bf16[64,128]{1,0:T(8,128)(2,1)S(1)} %get-tuple-element.66), channel_id=1, source_target_pairs={{0,9},{1,10},{2,11},{3,12},{4,13},{5,14},{6,15},{8,17},{9,18},{10,... | collective-permute-start | bytes 49160 | tf_op jit(solution)/shard_map/ppermute | solution.py:1212
  16.9 2.2 %prepare.1 = (s16[5,64,1792]{2,1,0:T(8,128)(2,1)S(1)}, bf16[1920,256]{1,0:T(8,128)(2,1)S(1)}, bf16[1024,256]{1,0:T(8,128)(2,1)S(1)}, bf16[1024,256]{1,0:T(8,128)...) custom-call(s32[28,64,62]{2,1,0:T(8,128)} %bitcast.39, f32[2,64,576]{2,1,0:T(8,128)S(1)} %bitcast.29, ...), custom_call_target="tpu_custom_call" | custom-call | bytes 14400000 | tf_op jit(solution)/shard_map/prepare/pallas_call | solution.py:277
  19.5 3.5 %conv_one_ends.1 = (f32[31,64,256]{2,1,0:T(8,128)S(1)}, f32[1,2,128]{2,1,0:T(2,128)S(1)}, bf16[16,64,128]{2,1,0:T(8,128)(2,1)S(1)}, bf16[16,64,128]{2,1,0:T(8,128)(2,1)S(1)}, bf16[31,64,128]{2,1,0:T(8,128)(2,1)S(1)}) custom-call(bf16[62,64,1792]{2,1,0:T(8,128)(2,1)S(1)} %bitcast.24, s16[5,64,1792]{2,1,0:T(8,128)(2,1)S(1)} %get-tuple-element.61.bits_ref, ...), custom_call_target="tpu_custom_call" | custom-call | bytes 14400000 | tf_op jit(solution)/shard_map/conv_one_ends/pallas_call | solution.py:362
  23.1 4.3 %collective-permute-start.4 = (bf16[16,64,128]{2,1,0:T(8,128)(2,1)S(1)}, bf16[16,64,128]{2,1,0:T(8,128)(2,1)S(1)}, u32[]{:S(2)}, u32[]{:S(2)}) collective-permute-start(bf16[16,64,128]{2,1,0:T(8,128)(2,1)S(1)} %get-tuple-element.74), channel_id=1, source_target_pairs={{0,1},{1,2},{2,3},{3,4},{4,5},{5,6},{6,7},{8,9},{9,10},{10,11},{11... | collective-permute-start | bytes 786440 | tf_op jit(solution)/shard_map/ppermute | solution.py:1187
  27.3 1.3 collective-permute-start.5
  28.6 9.6 %conv_one.1 = (f32[31,64,768]{2,1,0:T(8,128)S(1)}, f32[32,2,128]{2,1,0:T(2,128)S(1)}, bf16[3,64,768]{2,1,0:T(8,128)(2,1)S(1)}, bf16[2,64,768]{2,1,0:T(8,128)(2,1)S(1)}) custom-call(bf16[62,64,1792]{2,1,0:T(8,128)(2,1)S(1)} %bitcast.25, s16[5,64,1792]{2,1,0:T(8,128)(2,1)S(1)} %get-tuple-element.61.bits_ref, ...), custom_call_target="tpu_custom_call" | custom-call | bytes 39600000 | tf_op jit(solution)/shard_map/conv_one/pallas_call | solution.py:440
  39.6 1.3 collective-permute-start.7
  40.9 3.0 %collective-permute-start.6 = (bf16[2,64,1024]{2,1,0:T(8,128)(2,1)S(1)}, bf16[2,64,1024]{2,1,0:T(8,128)(2,1)S(1)}, u32[]{:S(2)}, u32[]{:S(2)}) collective-permute-start(bf16[2,64,1024]{2,1,0:T(8,128)(2,1)S(1)} %get-tuple-element.76), channel_id=1, source_target_pairs={{0,8},{8,16},{16,24},{1,9},{9,17},{17,25},{2,10},{10,18},{18,26},{... | collective-permute-start | bytes 786440 | tf_op jit(solution)/shard_map/ppermute | solution.py:1187
  43.9 14.3 %all_to_all.30.st_ref = f32[32,2,128]{2,1,0:T(2,128)S(1)} all-to-all(f32[32,2,128]{2,1,0:T(2,128)S(1)} %get-tuple-element.78), channel_id=1, replica_groups=mesh['gy'=4,'gx'=8] {'gy','gx'}, dimensions={0} | all-to-all | bytes 65536 | tf_op jit(solution)/shard_map/all_to_all | solution.py:1191
  58.2 8.1 %conv_two.1 = (f32[34,64,896]{2,1,0:T(8,128)S(1)}, bf16[32,64,1024]{2,1,0:T(8,128)(2,1)S(1)}, bf16[36,64,1024]{2,1,0:T(8,128)(2,1)}, f32[32,2,128]{2,1,0:T(2,128)S(1)}) custom-call(f32[31,64,768]{2,1,0:T(8,128)S(1)} %get-tuple-element.69.c_ref, f32[31,64,256]{2,1,0:T(8,128)S(1)} %get-tuple-element.70.ends_ref, ...), custom_call_target="tpu_custom_call" | custom-call | bytes 50400000 | tf_op jit(solution)/shard_map/conv_two/pallas_call | solution.py:577
  66.4 8.9 %all_to_all.31.st_ref = f32[32,2,128]{2,1,0:T(2,128)S(1)} all-to-all(f32[32,2,128]{2,1,0:T(2,128)S(1)} %get-tuple-element.82), channel_id=1, replica_groups=mesh['gy'=4,'gx'=8] {'gy','gx'}, dimensions={0} | all-to-all | bytes 65536 | tf_op jit(solution)/shard_map/all_to_all | solution.py:1191
  75.2 5.3 %output.1 = (bf16[31,64,896]{2,1,0:T(8,128)(2,1)}, f32[34,64,896]{2,1,0:T(8,128)S(1)}, f32[32,2,128]{2,1,0:T(2,128)S(1)}) custom-call(f32[34,64,896]{2,1,0:T(8,128)S(1)} %get-tuple-element.81.c2_ref.c_ref, f32[32,2,128]{2,1,0:T(2,128)S(1)} %all_to_all.31.st_ref, f32[4,128]{1,0:T(4,128)S(1)} %get-tuple-element.79.np_ref, bf16[31,64,896]{2,1,0:T(8,128)(2,1)S(1)} %bitcast.28, ...), custom_call_target="tpu_custom_call" | custom-call | bytes 43200000 | tf_op jit(solution)/shard_map/output/pallas_call | solution.py:666
  80.5 8.9 %all_to_all.32.sum_ref.s2_ref = f32[32,2,128]{2,1,0:T(2,128)S(1)} all-to-all(f32[32,2,128]{2,1,0:T(2,128)S(1)} %get-tuple-element.87), channel_id=1, replica_groups=mesh['gy'=4,'gx'=8] {'gy','gx'}, dimensions={0} | all-to-all | bytes 65536 | tf_op jit(solution)/shard_map/all_to_all | solution.py:1191
  90.2 2.6 %collective-permute-start.8 = (bf16[17,64,128]{2,1,0:T(8,128)(2,1)S(1)}, bf16[17,64,128]{2,1,0:T(8,128)(2,1)S(1)}, u32[]{:S(2)}, u32[]{:S(2)}) collective-permute-start(bf16[17,64,128]{2,1,0:T(8,128)(2,1)S(1)} %get-tuple-element.92), channel_id=1, source_target_pairs={{0,1},{1,2},{2,3},{3,4},{4,5},{5,6},{6,7},{8,9},{9,10},{10,11},{11... | collective-permute-start | bytes 835592 | tf_op jit(solution)/shard_map/ppermute | solution.py:1187
  92.8 1.5 collective-permute-start.9
  94.3 6.8 %back_two.1 = (bf16[34,64,896]{2,1,0:T(8,128)(2,1)S(1)}, f32[9,64,64]{2,1,0:T(8,128)S(1)}) custom-call(f32[34,64,896]{2,1,0:T(8,128)S(1)} %get-tuple-element.85.d_ref, f32[34,64,896]{2,1,0:T(8,128)S(1)} %get-tuple-element.81.c2_ref.c_ref, bf16[36,64,1024]{2,1,0:T(8,128)(2,1)} %get-tuple-element.86.hid_ref, f32[32,2,128]{2,1,0:T(2,128)S(1)} %all_to_all.31.st_ref, ...), custom_call_target="tpu_custom_call" | custom-call | bytes 43200000 | tf_op jit(solution)/shard_map/back_two/pallas_call | solution.py:791
  101.2 4.9 %hidden_gradient.1 = (f32[32,64,768]{2,1,0:T(8,128)S(1)}, f32[1,2,128]{2,1,0:T(2,128)S(1)}) custom-call(bf16[34,64,896]{2,1,0:T(8,128)(2,1)S(1)} %get-tuple-element.88.ds_ref, bf16[32,64,1024]{2,1,0:T(8,128)(2,1)S(1)} %get-tuple-element.89.n1_ref, f32[4,128]{1,0:T(4,128)S(1)} %get-tuple-element.79.np_ref, bf16[1024,256]{1,0:T(8,128)(2,1)S(1)} %get-tuple-element.90.w_ref), custom_call_target="tpu_custom_call" | custom-call | bytes 21600000 | tf_op jit(solution)/shard_map/hidden_gradient/pallas_call | solution.py:853
  106.1 2.4 %hidden_gradient_ends.1 = (f32[32,64,256]{2,1,0:T(8,128)S(1)}, bf16[16,64,128]{2,1,0:T(8,128)(2,1)S(1)}, f32[32,2,128]{2,1,0:T(2,128)S(1)}) custom-call(bf16[34,64,896]{2,1,0:T(8,128)(2,1)S(1)} %get-tuple-element.88.ds_ref, bf16[17,64,128]{2,1,0:T(8,128)(2,1)S(1)} %collective-permute-done.8.left_ref, ...), custom_call_target="tpu_custom_call" | custom-call | bytes 10800000 | tf_op jit(solution)/shard_map/hidden_gradient_ends/pallas_call | solution.py:895
  108.5 1.3 collective-permute-start.10
  109.8 13.0 %all_to_all.33.sum_ref.s1_ref = f32[32,2,128]{2,1,0:T(2,128)S(1)} all-to-all(f32[32,2,128]{2,1,0:T(2,128)S(1)} %get-tuple-element.97), channel_id=1, replica_groups=mesh['gy'=4,'gx'=8] {'gy','gx'}, dimensions={0} | all-to-all | bytes 65536 | tf_op jit(solution)/shard_map/all_to_all | solution.py:1191
  122.8 13.6 %back_one.1 = (bf16[32,64,1024]{2,1,0:T(8,128)(2,1)}, bf16[32,24,128]{2,1,0:T(8,128)(2,1)}) custom-call(f32[32,64,768]{2,1,0:T(8,128)S(1)} %get-tuple-element.91.dp_ref, f32[32,64,256]{2,1,0:T(8,128)S(1)} %get-tuple-element.95.ends_ref, bf16[16,64,128]{2,1,0:T(8,128)(2,1)S(1)} %collective-permute-done.10.edge_ref, ...), custom_call_target="tpu_custom_call" | custom-call | bytes 57600000 | tf_op jit(solution)/shard_map/back_one/pallas_call | solution.py:1017
  136.5 2.6 %all-to-all-start.4 = ((bf16[32,24,128]{2,1,0:T(8,128)(2,1)}), bf16[32,24,128]{2,1,0:T(8,128)(2,1)S(1)}, u32[]{:S(2)}, u32[]{:S(2)}) async-start(bf16[32,24,128]{2,1,0:T(8,128)(2,1)} %get-tuple-element.101), calls=%async_computation.4 | async-start | bytes 393216 | tf_op jit(solution)/shard_map/all_to_all | solution.py:1191
  139.1 6.6 %input_gradient.2.rest_0_ = bf16[62,64,1792]{2,1,0:T(8,128)(2,1)} custom-call(bf16[32,64,1024]{2,1,0:T(8,128)(2,1)} %get-tuple-element.99.ds, s16[5,64,1792]{2,1,0:T(8,128)(2,1)} %copy-done.1, bf16[768,256]{1,0:T(8,128)(2,1)S(1)} %get-tuple-element.100.w_ref), custom_call_target="tpu_custom_call" | custom-call | bytes 25200000 | tf_op jit(solution)/shard_map/input_gradient/pallas_call | solution.py:1074
  145.7 1.9 %all-to-all-done.4.g_ref = bf16[32,24,128]{2,1,0:T(8,128)(2,1)S(1)} async-done(((bf16[32,24,128]{2,1,0:T(8,128)(2,1)}), bf16[32,24,128]{2,1,0:T(8,128)(2,1)S(1)}, u32[]{:S(2)}, u32[]{:S(2)}) %all-to-all-start.4) | async-done | bytes 196640 | tf_op jit(solution)/shard_map/all_to_all | solution.py:1191
  148.3 3.9 %all-to-all-start.5 = ((bf16[32,24,128]{2,1,0:T(8,128)(2,1)}), bf16[32,24,128]{2,1,0:T(8,128)(2,1)S(1)}, u32[]{:S(2)}, u32[]{:S(2)}) async-start(bf16[32,24,128]{2,1,0:T(8,128)(2,1)} %sum_share.1), calls=%async_computation.5 | async-start | bytes 393216 | tf_op jit(solution)/shard_map/all_to_all | solution.py:1191
  152.3 6.7 %input_gradient.3 = bf16[62,64,1792]{2,1,0:T(8,128)(2,1)} custom-call(bf16[32,64,1024]{2,1,0:T(8,128)(2,1)} %get-tuple-element.99.ds, s16[5,64,1792]{2,1,0:T(8,128)(2,1)} %copy-done.1, bf16[768,256]{1,0:T(8,128)(2,1)S(1)} %get-tuple-element.100.w_ref, bf16[62,64,1792]{2,1,0:T(8,128)(2,1)} %input_gradient.2.rest_0_), custom_call_target="tpu_custom_call", output_to_operand_aliasing={{}: (3, {})} | custom-call | bytes 25200000 | tf_op jit(solution)/shard_map/input_gradient/pallas_call | solution.py:1074
  159.0 1.8 %all-to-all-done.5.g_ref = bf16[32,24,128]{2,1,0:T(8,128)(2,1)S(1)} async-done(((bf16[32,24,128]{2,1,0:T(8,128)(2,1)}), bf16[32,24,128]{2,1,0:T(8,128)(2,1)S(1)}, u32[]{:S(2)}, u32[]{:S(2)}) %all-to-all-start.5) | async-done | bytes 196640 | tf_op jit(solution)/shard_map/all_to_all | solution.py:1191
  160.8 1.7 %update.1 = (f32[1,1]{1,0:T(1,128)}, f32[2,64,576]{2,1,0:T(8,128)}, f32[2,64,576]{2,1,0:T(8,128)}, f32[2,64,576]{2,1,0:T(8,128)}, bf16[2,64,576]{2,1,0:T(8,128)(...) custom-call(bf16[32,24,128]{2,1,0:T(8,128)(2,1)S(1)} %all-to-all-done.5.g_ref, ...), custom_call_target="tpu_custom_call" | custom-call | bytes 10800000 | tf_op jit(solution)/shard_map/update/pallas_call | solution.py:1171
  (39 shorter events, 3.3 us)
Async XLA Ops:
  0.6 18.9 %slice-start = ((s8[14221312]{0:T(1024)(128)(4,1)}), s8[4194304]{0:T(1024)(128)(4,1)S(1)}, s32[]{:S(2)}) async-start(s8[14221312]{0:T(1024)(128)(4,1)} %bitcast.22), calls=%async_computation.6 | async-start | bytes 8388608
  0.7 16.2 %copy-start.2 = (f32[2,576,64]{1,2,0:T(8,128)S(1)}, f32[2,576,64]{1,2,0:T(8,128)}, u32[]{:S(2)}) copy-start(f32[2,576,64]{1,2,0:T(8,128)} %param.11) | copy-start | bytes 884740
  0.7 16.2 %copy-start.5 = (f32[2,2,64]{2,1,0:T(2,128)S(1)}, f32[2,2,64]{2,1,0:T(2,128)}, u32[]{:S(2)}) copy-start(f32[2,2,64]{2,1,0:T(2,128)} %param.14) | copy-start | bytes 3076
  0.7 18.8 %slice-start.1 = ((s8[14221312]{0:T(1024)(128)(4,1)}), s8[4194304]{0:T(1024)(128)(4,1)S(1)}, s32[]{:S(2)}) async-start(s8[14221312]{0:T(1024)(128)(4,1)} %bitcast.22), calls=%async_computation.7 | async-start | bytes 8388608
  0.7 18.8 %slice-start.2 = ((s8[14221312]{0:T(1024)(128)(4,1)}), s8[4194304]{0:T(1024)(128)(4,1)S(1)}, s32[]{:S(2)}) async-start(s8[14221312]{0:T(1024)(128)(4,1)} %bitcast.22), calls=%async_computation.8 | async-start | bytes 8388608
  0.7 18.8 %slice-start.3 = ((s8[14221312]{0:T(1024)(128)(4,1)}), s8[1638400]{0:T(1024)(128)(4,1)S(1)}, s32[]{:S(2)}) async-start(s8[14221312]{0:T(1024)(128)(4,1)} %bitcast.22), calls=%async_computation.9 | async-start | bytes 3276800
  3.2 16.1 %collective-permute-start.1 = (bf16[31,64,128]{2,1,0:T(8,128)(2,1)S(1)}, bf16[31,64,128]{2,1,0:T(8,128)(2,1)S(1)}, u32[]{:S(2)}, u32[]{:S(2)}) collective-permute-start(bf16[31,64,128]{2,1,0:T(8,128)(2,1)S(1)} %get-tuple-element.63), channel_id=1, source_target_pairs={{0,1},{1,2},{2,3},{3,4},{4,5},{5,6},{6,7},{8,9},{9,10},{10,11},{11... | collective-permute-start | bytes 1523720 | tf_op jit(solution)/shard_map/ppermute | solution.py:1187
  8.4 11.1 %collective-permute-start = (bf16[64,2688]{1,0:T(8,128)(2,1)S(1)}, bf16[64,2688]{1,0:T(8,128)(2,1)S(1)}, u32[]{:S(2)}, u32[]{:S(2)}) collective-permute-start(bf16[64,2688]{1,0:T(8,128)(2,1)S(1)} %get-tuple-element.62), channel_id=1, source_target_pairs={{0,8},{8,16},{16,24},{1,9},{9,17},{17,25},{2,10},{10,18},{18,26},{... | collective-permute-start | bytes 1032200 | tf_op jit(solution)/shard_map/ppermute | solution.py:1187
  9.9 9.2 %collective-permute-start.2 = (bf16[2,64,896]{2,1,0:T(8,128)(2,1)S(1)}, bf16[2,64,896]{2,1,0:T(8,128)(2,1)S(1)}, u32[]{:S(2)}, u32[]{:S(2)}) collective-permute-start(bf16[2,64,896]{2,1,0:T(8,128)(2,1)S(1)} %get-tuple-element.64), channel_id=1, source_target_pairs={{8,0},{16,8},{24,16},{9,1},{17,9},{25,17},{10,2},{18,10},{26,18},{... | collective-permute-start | bytes 688136 | tf_op jit(solution)/shard_map/ppermute | solution.py:1187
  11.2 8.3 %collective-permute-start.3 = (bf16[64,128]{1,0:T(8,128)(2,1)S(1)}, bf16[64,128]{1,0:T(8,128)(2,1)S(1)}, u32[]{:S(2)}, u32[]{:S(2)}) collective-permute-start(bf16[64,128]{1,0:T(8,128)(2,1)S(1)} %get-tuple-element.66), channel_id=1, source_target_pairs={{0,9},{1,10},{2,11},{3,12},{4,13},{5,14},{6,15},{8,17},{9,18},{10,... | collective-permute-start | bytes 49160 | tf_op jit(solution)/shard_map/ppermute | solution.py:1212
  19.1 9.6 %copy-start.1 = (s16[5,64,1792]{2,1,0:T(8,128)(2,1)}, s16[5,64,1792]{2,1,0:T(8,128)(2,1)S(1)}, u32[]{:S(2)}) copy-start(s16[5,64,1792]{2,1,0:T(8,128)(2,1)S(1)} %get-tuple-element.61.bits_ref) | copy-start | bytes 3440644
  23.1 15.9 %collective-permute-start.4 = (bf16[16,64,128]{2,1,0:T(8,128)(2,1)S(1)}, bf16[16,64,128]{2,1,0:T(8,128)(2,1)S(1)}, u32[]{:S(2)}, u32[]{:S(2)}) collective-permute-start(bf16[16,64,128]{2,1,0:T(8,128)(2,1)S(1)} %get-tuple-element.74), channel_id=1, source_target_pairs={{0,1},{1,2},{2,3},{3,4},{4,5},{5,6},{6,7},{8,9},{9,10},{10,11},{11... | collective-permute-start | bytes 786440 | tf_op jit(solution)/shard_map/ppermute | solution.py:1187
  27.3 11.7 %collective-permute-start.5 = (bf16[16,64,128]{2,1,0:T(8,128)(2,1)S(1)}, bf16[16,64,128]{2,1,0:T(8,128)(2,1)S(1)}, u32[]{:S(2)}, u32[]{:S(2)}) collective-permute-start(bf16[16,64,128]{2,1,0:T(8,128)(2,1)S(1)} %get-tuple-element.75), channel_id=1, source_target_pairs={{1,0},{2,1},{3,2},{4,3},{5,4},{6,5},{7,6},{9,8},{10,9},{11,10},{12... | collective-permute-start | bytes 786440 | tf_op jit(solution)/shard_map/ppermute | solution.py:1187
  39.6 18.7 %collective-permute-start.7 = (bf16[3,64,1024]{2,1,0:T(8,128)(2,1)S(1)}, bf16[3,64,1024]{2,1,0:T(8,128)(2,1)S(1)}, u32[]{:S(2)}, u32[]{:S(2)}) collective-permute-start(bf16[3,64,1024]{2,1,0:T(8,128)(2,1)S(1)} %get-tuple-element.77), channel_id=1, source_target_pairs={{8,0},{16,8},{24,16},{9,1},{17,9},{25,17},{10,2},{18,10},{26,18},{... | collective-permute-start | bytes 1179656 | tf_op jit(solution)/shard_map/ppermute | solution.py:1187
  40.9 17.4 %collective-permute-start.6 = (bf16[2,64,1024]{2,1,0:T(8,128)(2,1)S(1)}, bf16[2,64,1024]{2,1,0:T(8,128)(2,1)S(1)}, u32[]{:S(2)}, u32[]{:S(2)}) collective-permute-start(bf16[2,64,1024]{2,1,0:T(8,128)(2,1)S(1)} %get-tuple-element.76), channel_id=1, source_target_pairs={{0,8},{8,16},{16,24},{1,9},{9,17},{17,25},{2,10},{10,18},{18,26},{... | collective-permute-start | bytes 786440 | tf_op jit(solution)/shard_map/ppermute | solution.py:1187
  58.2 17.0 %copy-start = (bf16[64,31,896]{2,0,1:T(8,128)(2,1)S(1)}, bf16[64,31,896]{2,0,1:T(8,128)(2,1)}, u32[]{:S(2)}) copy-start(bf16[64,31,896]{2,0,1:T(8,128)(2,1)} %param.17) | copy-start | bytes 10665988
  90.2 15.9 %collective-permute-start.8 = (bf16[17,64,128]{2,1,0:T(8,128)(2,1)S(1)}, bf16[17,64,128]{2,1,0:T(8,128)(2,1)S(1)}, u32[]{:S(2)}, u32[]{:S(2)}) collective-permute-start(bf16[17,64,128]{2,1,0:T(8,128)(2,1)S(1)} %get-tuple-element.92), channel_id=1, source_target_pairs={{0,1},{1,2},{2,3},{3,4},{4,5},{5,6},{6,7},{8,9},{9,10},{10,11},{11... | collective-permute-start | bytes 835592 | tf_op jit(solution)/shard_map/ppermute | solution.py:1187
  92.8 13.3 %collective-permute-start.9 = (bf16[17,64,128]{2,1,0:T(8,128)(2,1)S(1)}, bf16[17,64,128]{2,1,0:T(8,128)(2,1)S(1)}, u32[]{:S(2)}, u32[]{:S(2)}) collective-permute-start(bf16[17,64,128]{2,1,0:T(8,128)(2,1)S(1)} %get-tuple-element.93), channel_id=1, source_target_pairs={{1,0},{2,1},{3,2},{4,3},{5,4},{6,5},{7,6},{9,8},{10,9},{11,10},{12... | collective-permute-start | bytes 835592 | tf_op jit(solution)/shard_map/ppermute | solution.py:1187
  108.5 14.3 %collective-permute-start.10 = (bf16[16,64,128]{2,1,0:T(8,128)(2,1)S(1)}, bf16[16,64,128]{2,1,0:T(8,128)(2,1)S(1)}, u32[]{:S(2)}, u32[]{:S(2)}) collective-permute-start(bf16[16,64,128]{2,1,0:T(8,128)(2,1)S(1)} %get-tuple-element.96), channel_id=1, source_target_pairs={{1,0},{2,1},{3,2},{4,3},{5,4},{6,5},{7,6},{9,8},{10,9},{11,10},{12... | collective-permute-start | bytes 786440 | tf_op jit(solution)/shard_map/ppermute | solution.py:1187
  136.5 11.1 %all-to-all-start.4 = ((bf16[32,24,128]{2,1,0:T(8,128)(2,1)}), bf16[32,24,128]{2,1,0:T(8,128)(2,1)S(1)}, u32[]{:S(2)}, u32[]{:S(2)}) async-start(bf16[32,24,128]{2,1,0:T(8,128)(2,1)} %get-tuple-element.101), calls=%async_computation.4 | async-start | bytes 393216 | tf_op jit(solution)/shard_map/all_to_all | solution.py:1191
  148.3 12.5 %all-to-all-start.5 = ((bf16[32,24,128]{2,1,0:T(8,128)(2,1)}), bf16[32,24,128]{2,1,0:T(8,128)(2,1)S(1)}, u32[]{:S(2)}, u32[]{:S(2)}) async-start(bf16[32,24,128]{2,1,0:T(8,128)(2,1)} %sum_share.1), calls=%async_computation.5 | async-start | bytes 393216 | tf_op jit(solution)/shard_map/all_to_all | solution.py:1191
  152.3 8.6 %copy-start.3 = (f32[2,576,64]{1,2,0:T(8,128)S(1)}, f32[2,576,64]{1,2,0:T(8,128)}, u32[]{:S(2)}) copy-start(f32[2,576,64]{1,2,0:T(8,128)} %param.12) | copy-start | bytes 884740
  152.3 8.5 %copy-start.4 = (f32[2,576,64]{1,2,0:T(8,128)S(1)}, f32[2,576,64]{1,2,0:T(8,128)}, u32[]{:S(2)}) copy-start(f32[2,576,64]{1,2,0:T(8,128)} %param.13) | copy-start | bytes 884740
  152.3 8.5 %copy-start.6 = (f32[2,2,64]{2,1,0:T(2,128)S(1)}, f32[2,2,64]{2,1,0:T(2,128)}, u32[]{:S(2)}) copy-start(f32[2,2,64]{2,1,0:T(2,128)} %param.15) | copy-start | bytes 3076
  152.3 8.5 %copy-start.7 = (f32[2,2,64]{2,1,0:T(2,128)S(1)}, f32[2,2,64]{2,1,0:T(2,128)}, u32[]{:S(2)}) copy-start(f32[2,2,64]{2,1,0:T(2,128)} %param.16) | copy-start | bytes 3076

commit v6 on v5

--- a/solution.py
+++ b/solution.py
@@ -488,7 +488,7 @@
         out_shape=[
             jax.ShapeDtypeStruct((n, scan_count, wide + 2 * L), bf16) for n in (3, 2)
         ],
-        compiler_params=params_of(),
+        compiler_params=params_of(10),
         cost_estimate=cost(1),
         name="pack_rows",
     )(up, down, edge, left, right)
@@ -499,8 +499,8 @@
     n1_ref, hid_ref, st2_ref, rim, run, *, count,
 ):
     step, steps = (pl.program_id(0), pl.num_programs(0))
-    c_ref, ends_ref, c2_ref, n1_ref = (
-        part_of(a, step, S2) for a in (c_ref, ends_ref, c2_ref, n1_ref)
+    c_ref, ends_ref, c2_ref, n1_ref, hid_ref = (
+        part_of(a, step, S2) for a in (c_ref, ends_ref, c2_ref, n1_ref, hid_ref)
     )
     r, tiles = (c_ref.shape[0], c_ref.shape[2] // L + 2)
     t_out = tiles - 1
@@ -588,18 +588,18 @@
             whole(np2.shape),
             whole(w.shape),
         ],
-        out_specs=[held, held, more(r + 5, wide), whole((devices, 2, L))],
+        out_specs=[held, held, held, whole((devices, 2, L))],
         out_shape=[
             resident((r + 3, scan_count, lanes), f32),
             resident((r + 1, scan_count, wide), bf16),
-            pltpu.HBM((r + 5, scan_count, wide), bf16),
+            resident((r + 5, scan_count, wide), bf16),
             jax.ShapeDtypeStruct((devices, 2, L), f32),
         ],
         scratch_shapes=[
             pltpu.VMEM((r, S2, L), f32),
             pltpu.VMEM((8, L), f32),
         ],
-        compiler_params=params_of(),
+        compiler_params=params_of(10),
         cost_estimate=cost(14),
         name="conv_two",
     )(c1, ends, up, down, left, right, st, np2, w)
@@ -681,7 +681,7 @@
             jax.ShapeDtypeStruct((devices, 2, L), f32),
         ],
         scratch_shapes=[pltpu.VMEM((8, L), f32)],
-        compiler_params=params_of(),
+        compiler_params=params_of(10),
         cost_estimate=cost(12),
         name="output",
     )(c2, st, np2, vmem(cot), up, down)
@@ -736,7 +736,7 @@
         ],
         out_specs=[more(rows // 2, L)] * 2,
         out_shape=[jax.ShapeDtypeStruct((rows // 2, scan_count, L), bf16)] * 2,
-        compiler_params=params_of(),
+        compiler_params=params_of(10),
         cost_estimate=cost(3),
         name="rim_two",
     )(d, c2, st, sums, np2)
@@ -746,7 +746,9 @@
     d_ref, c2_ref, hid_ref, st_ref, sum_ref, np_ref, ds_ref, kg_ref, grad, *, count
 ):
     step, steps = (pl.program_id(0), pl.num_programs(0))
-    d_ref, c2_ref, ds_ref = (part_of(a, step, S2) for a in (d_ref, c2_ref, ds_ref))
+    d_ref, c2_ref, ds_ref, hid_ref = (
+        part_of(a, step, S2) for a in (d_ref, c2_ref, ds_ref, hid_ref)
+    )
     r, tiles = (c2_ref.shape[0] - 3, c2_ref.shape[2] // L)
     back = norm_back_two(st_ref, sum_ref, np_ref, count, r)
 
@@ -794,7 +796,7 @@
         in_specs=[
             held,
             held,
-            more(r + 5, wide),
+            held,
             whole(st.shape),
             whole(sums.shape),
             whole(np2.shape),
@@ -805,10 +807,10 @@
             jax.ShapeDtypeStruct((9, C, C), f32),
         ],
         scratch_shapes=[pltpu.VMEM((6 * C, 4 * C), f32)],
-        compiler_params=params_of(),
+        compiler_params=params_of(10),
         cost_estimate=cost(12),
         name="back_two",
-    )(d, c2, hbm(hid), st, sums, np2)
+    )(d, c2, hid, st, sums, np2)
 
 
 def hidden_tile(t, parts, n1_ref, np_ref, w_ref, dp_ref, into, first, last):
@@ -860,7 +862,7 @@
             jax.ShapeDtypeStruct((1, 2, L), f32),
         ],
         scratch_shapes=[pltpu.VMEM((8, L), f32)],
-        compiler_params=params_of(),
+        compiler_params=params_of(10),
         cost_estimate=cost(6),
         name="hidden_gradient",
     )(ds, n1, np2, w)
@@ -911,7 +913,7 @@
             jax.ShapeDtypeStruct((devices, 2, L), f32),
         ],
         scratch_shapes=[pltpu.VMEM((r + 2, S2, L), bf16), pltpu.VMEM((8, L), f32)],
-        compiler_params=params_of(),
+        compiler_params=params_of(10),
         cost_estimate=cost(3),
         name="hidden_gradient_ends",
     )(ds, left, right, n1, np2, w, inner)

time: 163 us -> 160 us (0.982)
  Pallas kernels: 76.2 us -> 73 us
    pallas_call x1, Pallas kernels: 6.85 us -> 5.11 us  [back_two(): pl.pallas_call(functools.partial(back_two_kernel, count=count), grid=(sca...]
  transfers between devices with their start and end apart: 13 -> 13, of which waited for: 5 -> 6; matrix products, arithmetic and copies ran while one was open for 0% -> 0% of each run, Pallas kernels for 23% -> 22%
where the time goes in v6:
time: 160 us
  Pallas kernels  73 us (46%)
  blocking collectives  44.9 us (28%)
  starting transfers between devices  35.4 us (22%)
  waiting for transfers between devices  5.46 us (3%)
    all_to_all x4, blocking collectives, exchange(): return lax.all_to_all(rows, BOTH, 0, 0, tiled=True)  44.9 us
    ppermute x10, starting transfers between devices, shifted(): return lax.ppermute(block, axis, route)  23.2 us
    pallas_call x1, Pallas kernels, back_one(): pl.pallas_call(functools.partial(back_one_kernel, count=count), grid=(sca...  13.6 us
    pallas_call x2, Pallas kernels, input_gradient(): pl.pallas_call(input_grad_kernel, grid=(steps,), in_specs=[at(r, wide), a...  13.3 us
    pallas_call x1, Pallas kernels, conv_one(): pl.pallas_call(conv_one_kernel, grid=(scan_count // S,), in_specs=[held,...  9.64 us
    pallas_call x1, Pallas kernels, conv_two(): pl.pallas_call(functools.partial(conv_two_kernel, count=count), grid=(sca...  6.69 us
    all_to_all x2, starting transfers between devices, exchange(): return lax.all_to_all(rows, BOTH, 0, 0, tiled=True)  6.51 us
    ppermute x1, starting transfers between devices, per_device(): lax.ppermute(corner, BOTH, [(i, i + gx + 1) for i in range(devices - gx)...  5.72 us
  transfers between devices with their start and end apart: 13, of which 6 were waited for; matrix products, arithmetic and copies ran while one was open for 0% of the time, Pallas kernels for 22%

profile of v6, /device:TPU:0, one launch (start us, length us, event | category | flops | bytes accessed | tf_op | source)
XLA Modules:
  0.0 159.8 jit_solution(17464721004503353290)
XLA Ops:
  0.7 2.5 %edges.1 = (bf16[64,2688]{1,0:T(8,128)(2,1)S(1)}, bf16[2,64,896]{2,1,0:T(8,128)(2,1)S(1)}, bf16[64,128]{1,0:T(8,128)(2,1)S(1)}, bf16[31,64,128]{2,1,0:T(8,128)(2,1)S(1)}) custom-call(bf16[62,64,1792]{2,1,0:T(8,128)(2,1)} %bitcast.19, bf16[62,64,1792]{2,1,0:T(8,128)(2,1)} %bitcast.20, s32[28,64,62]{2,1,0:T(8,128)} %bitcast.38, bf16[31,64,896]{2,1,0:T(8,128)(2,1)} %bitcast.26, ...), custom_call_target="tpu_custom_call" | custom-call | bytes 10800000 | tf_op jit(solution)/shard_map/edges/pallas_call | solution.py:216
  3.2 5.1 %collective-permute-start.1 = (bf16[31,64,128]{2,1,0:T(8,128)(2,1)S(1)}, bf16[31,64,128]{2,1,0:T(8,128)(2,1)S(1)}, u32[]{:S(2)}, u32[]{:S(2)}) collective-permute-start(bf16[31,64,128]{2,1,0:T(8,128)(2,1)S(1)} %get-tuple-element.63), channel_id=1, source_target_pairs={{0,1},{1,2},{2,3},{3,4},{4,5},{5,6},{6,7},{8,9},{9,10},{10,11},{11... | collective-permute-start | bytes 1523720 | tf_op jit(solution)/shard_map/ppermute | solution.py:1189
  8.4 1.5 collective-permute-start
  9.9 1.3 collective-permute-start.2
  11.2 5.7 %collective-permute-start.3 = (bf16[64,128]{1,0:T(8,128)(2,1)S(1)}, bf16[64,128]{1,0:T(8,128)(2,1)S(1)}, u32[]{:S(2)}, u32[]{:S(2)}) collective-permute-start(bf16[64,128]{1,0:T(8,128)(2,1)S(1)} %get-tuple-element.66), channel_id=1, source_target_pairs={{0,9},{1,10},{2,11},{3,12},{4,13},{5,14},{6,15},{8,17},{9,18},{10,... | collective-permute-start | bytes 49160 | tf_op jit(solution)/shard_map/ppermute | solution.py:1214
  16.9 2.2 %prepare.1 = (s16[5,64,1792]{2,1,0:T(8,128)(2,1)S(1)}, bf16[1920,256]{1,0:T(8,128)(2,1)S(1)}, bf16[1024,256]{1,0:T(8,128)(2,1)S(1)}, bf16[1024,256]{1,0:T(8,128)...) custom-call(s32[28,64,62]{2,1,0:T(8,128)} %bitcast.39, f32[2,64,576]{2,1,0:T(8,128)S(1)} %bitcast.29, ...), custom_call_target="tpu_custom_call" | custom-call | bytes 14400000 | tf_op jit(solution)/shard_map/prepare/pallas_call | solution.py:277
  19.5 3.5 %conv_one_ends.1 = (f32[31,64,256]{2,1,0:T(8,128)S(1)}, f32[1,2,128]{2,1,0:T(2,128)S(1)}, bf16[16,64,128]{2,1,0:T(8,128)(2,1)S(1)}, bf16[16,64,128]{2,1,0:T(8,128)(2,1)S(1)}, bf16[31,64,128]{2,1,0:T(8,128)(2,1)S(1)}) custom-call(bf16[62,64,1792]{2,1,0:T(8,128)(2,1)S(1)} %bitcast.24, s16[5,64,1792]{2,1,0:T(8,128)(2,1)S(1)} %get-tuple-element.61.bits_ref, ...), custom_call_target="tpu_custom_call" | custom-call | bytes 14400000 | tf_op jit(solution)/shard_map/conv_one_ends/pallas_call | solution.py:362
  23.0 4.3 %collective-permute-start.4 = (bf16[16,64,128]{2,1,0:T(8,128)(2,1)S(1)}, bf16[16,64,128]{2,1,0:T(8,128)(2,1)S(1)}, u32[]{:S(2)}, u32[]{:S(2)}) collective-permute-start(bf16[16,64,128]{2,1,0:T(8,128)(2,1)S(1)} %get-tuple-element.74), channel_id=1, source_target_pairs={{0,1},{1,2},{2,3},{3,4},{4,5},{5,6},{6,7},{8,9},{9,10},{10,11},{11... | collective-permute-start | bytes 786440 | tf_op jit(solution)/shard_map/ppermute | solution.py:1189
  27.3 1.3 collective-permute-start.5
  28.6 9.6 %conv_one.1 = (f32[31,64,768]{2,1,0:T(8,128)S(1)}, f32[32,2,128]{2,1,0:T(2,128)S(1)}, bf16[3,64,768]{2,1,0:T(8,128)(2,1)S(1)}, bf16[2,64,768]{2,1,0:T(8,128)(2,1)S(1)}) custom-call(bf16[62,64,1792]{2,1,0:T(8,128)(2,1)S(1)} %bitcast.25, s16[5,64,1792]{2,1,0:T(8,128)(2,1)S(1)} %get-tuple-element.61.bits_ref, ...), custom_call_target="tpu_custom_call" | custom-call | bytes 39600000 | tf_op jit(solution)/shard_map/conv_one/pallas_call | solution.py:440
  39.6 1.3 collective-permute-start.7
  40.9 3.0 %collective-permute-start.6 = (bf16[2,64,1024]{2,1,0:T(8,128)(2,1)S(1)}, bf16[2,64,1024]{2,1,0:T(8,128)(2,1)S(1)}, u32[]{:S(2)}, u32[]{:S(2)}) collective-permute-start(bf16[2,64,1024]{2,1,0:T(8,128)(2,1)S(1)} %get-tuple-element.76), channel_id=1, source_target_pairs={{0,8},{8,16},{16,24},{1,9},{9,17},{17,25},{2,10},{10,18},{18,26},{... | collective-permute-start | bytes 786440 | tf_op jit(solution)/shard_map/ppermute | solution.py:1189
  43.9 14.3 %all_to_all.30.st_ref = f32[32,2,128]{2,1,0:T(2,128)S(1)} all-to-all(f32[32,2,128]{2,1,0:T(2,128)S(1)} %get-tuple-element.78), channel_id=1, replica_groups=mesh['gy'=4,'gx'=8] {'gy','gx'}, dimensions={0} | all-to-all | bytes 65536 | tf_op jit(solution)/shard_map/all_to_all | solution.py:1193
  58.2 6.7 %conv_two.1 = (f32[34,64,896]{2,1,0:T(8,128)S(1)}, bf16[32,64,1024]{2,1,0:T(8,128)(2,1)S(1)}, bf16[36,64,1024]{2,1,0:T(8,128)(2,1)S(1)}, f32[32,2,128]{2,1,0:T(2,128)S(1)}) custom-call(f32[31,64,768]{2,1,0:T(8,128)S(1)} %get-tuple-element.69.c_ref, f32[31,64,256]{2,1,0:T(8,128)S(1)} %get-tuple-element.70.ends_ref, ...), custom_call_target="tpu_custom_call" | custom-call | bytes 50400000 | tf_op jit(solution)/shard_map/conv_two/pallas_call | solution.py:577
  64.9 8.9 %all_to_all.31.st_ref = f32[32,2,128]{2,1,0:T(2,128)S(1)} all-to-all(f32[32,2,128]{2,1,0:T(2,128)S(1)} %get-tuple-element.82), channel_id=1, replica_groups=mesh['gy'=4,'gx'=8] {'gy','gx'}, dimensions={0} | all-to-all | bytes 65536 | tf_op jit(solution)/shard_map/all_to_all | solution.py:1193
  73.8 5.3 %output.1 = (bf16[31,64,896]{2,1,0:T(8,128)(2,1)}, f32[34,64,896]{2,1,0:T(8,128)S(1)}, f32[32,2,128]{2,1,0:T(2,128)S(1)}) custom-call(f32[34,64,896]{2,1,0:T(8,128)S(1)} %get-tuple-element.81.c2_ref.c_ref, f32[32,2,128]{2,1,0:T(2,128)S(1)} %all_to_all.31.st_ref, f32[4,128]{1,0:T(4,128)S(1)} %get-tuple-element.79.np_ref, bf16[31,64,896]{2,1,0:T(8,128)(2,1)S(1)} %bitcast.28, ...), custom_call_target="tpu_custom_call" | custom-call | bytes 43200000 | tf_op jit(solution)/shard_map/output/pallas_call | solution.py:666
  79.1 8.9 %all_to_all.32.sum_ref.s2_ref = f32[32,2,128]{2,1,0:T(2,128)S(1)} all-to-all(f32[32,2,128]{2,1,0:T(2,128)S(1)} %get-tuple-element.87), channel_id=1, replica_groups=mesh['gy'=4,'gx'=8] {'gy','gx'}, dimensions={0} | all-to-all | bytes 65536 | tf_op jit(solution)/shard_map/all_to_all | solution.py:1193
  88.8 2.6 %collective-permute-start.8 = (bf16[17,64,128]{2,1,0:T(8,128)(2,1)S(1)}, bf16[17,64,128]{2,1,0:T(8,128)(2,1)S(1)}, u32[]{:S(2)}, u32[]{:S(2)}) collective-permute-start(bf16[17,64,128]{2,1,0:T(8,128)(2,1)S(1)} %get-tuple-element.92), channel_id=1, source_target_pairs={{0,1},{1,2},{2,3},{3,4},{4,5},{5,6},{6,7},{8,9},{9,10},{10,11},{11... | collective-permute-start | bytes 835592 | tf_op jit(solution)/shard_map/ppermute | solution.py:1189
  91.4 1.5 collective-permute-start.9
  92.9 5.1 %back_two.1 = (bf16[34,64,896]{2,1,0:T(8,128)(2,1)S(1)}, f32[9,64,64]{2,1,0:T(8,128)S(1)}) custom-call(f32[34,64,896]{2,1,0:T(8,128)S(1)} %get-tuple-element.85.d_ref, f32[34,64,896]{2,1,0:T(8,128)S(1)} %get-tuple-element.81.c2_ref.c_ref, bf16[36,64,1024]{2,1,0:T(8,128)(2,1)S(1)} %get-tuple-element.86.hid_ref, f32[32,2,128]{2,1,0:T(2,128)S(1)} %all_to_all.31.st_ref, ...), custom_call_target="tpu_custom_call" | custom-call | bytes 43200000 | tf_op jit(solution)/shard_map/back_two/pallas_call | solution.py:793
  98.0 4.9 %hidden_gradient.1 = (f32[32,64,768]{2,1,0:T(8,128)S(1)}, f32[1,2,128]{2,1,0:T(2,128)S(1)}) custom-call(bf16[34,64,896]{2,1,0:T(8,128)(2,1)S(1)} %get-tuple-element.88.ds_ref, bf16[32,64,1024]{2,1,0:T(8,128)(2,1)S(1)} %get-tuple-element.89.n1_ref, f32[4,128]{1,0:T(4,128)S(1)} %get-tuple-element.79.np_ref, bf16[1024,256]{1,0:T(8,128)(2,1)S(1)} %get-tuple-element.90.w_ref), custom_call_target="tpu_custom_call" | custom-call | bytes 21600000 | tf_op jit(solution)/shard_map/hidden_gradient/pallas_call | solution.py:855
  103.5 2.4 %hidden_gradient_ends.1 = (f32[32,64,256]{2,1,0:T(8,128)S(1)}, bf16[16,64,128]{2,1,0:T(8,128)(2,1)S(1)}, f32[32,2,128]{2,1,0:T(2,128)S(1)}) custom-call(bf16[34,64,896]{2,1,0:T(8,128)(2,1)S(1)} %get-tuple-element.88.ds_ref, bf16[17,64,128]{2,1,0:T(8,128)(2,1)S(1)} %collective-permute-done.8.left_ref, ...), custom_call_target="tpu_custom_call" | custom-call | bytes 10800000 | tf_op jit(solution)/shard_map/hidden_gradient_ends/pallas_call | solution.py:897
  105.9 1.3 collective-permute-start.10
  107.2 12.8 %all_to_all.33.sum_ref.s1_ref = f32[32,2,128]{2,1,0:T(2,128)S(1)} all-to-all(f32[32,2,128]{2,1,0:T(2,128)S(1)} %get-tuple-element.97), channel_id=1, replica_groups=mesh['gy'=4,'gx'=8] {'gy','gx'}, dimensions={0} | all-to-all | bytes 65536 | tf_op jit(solution)/shard_map/all_to_all | solution.py:1193
  120.1 13.6 %back_one.1 = (bf16[32,64,1024]{2,1,0:T(8,128)(2,1)}, bf16[32,24,128]{2,1,0:T(8,128)(2,1)}) custom-call(f32[32,64,768]{2,1,0:T(8,128)S(1)} %get-tuple-element.91.dp_ref, f32[32,64,256]{2,1,0:T(8,128)S(1)} %get-tuple-element.95.ends_ref, bf16[16,64,128]{2,1,0:T(8,128)(2,1)S(1)} %collective-permute-done.10.edge_ref, ...), custom_call_target="tpu_custom_call" | custom-call | bytes 57600000 | tf_op jit(solution)/shard_map/back_one/pallas_call | solution.py:1019
  133.7 2.6 %all-to-all-start.4 = ((bf16[32,24,128]{2,1,0:T(8,128)(2,1)}), bf16[32,24,128]{2,1,0:T(8,128)(2,1)S(1)}, u32[]{:S(2)}, u32[]{:S(2)}) async-start(bf16[32,24,128]{2,1,0:T(8,128)(2,1)} %get-tuple-element.101), calls=%async_computation.4 | async-start | bytes 393216 | tf_op jit(solution)/shard_map/all_to_all | solution.py:1193
  136.3 6.6 %input_gradient.2.rest_0_ = bf16[62,64,1792]{2,1,0:T(8,128)(2,1)} custom-call(bf16[32,64,1024]{2,1,0:T(8,128)(2,1)} %get-tuple-element.99.ds, s16[5,64,1792]{2,1,0:T(8,128)(2,1)} %copy-done.1, bf16[768,256]{1,0:T(8,128)(2,1)S(1)} %get-tuple-element.100.w_ref), custom_call_target="tpu_custom_call" | custom-call | bytes 25200000 | tf_op jit(solution)/shard_map/input_gradient/pallas_call | solution.py:1076
  142.9 1.9 %all-to-all-done.4.g_ref = bf16[32,24,128]{2,1,0:T(8,128)(2,1)S(1)} async-done(((bf16[32,24,128]{2,1,0:T(8,128)(2,1)}), bf16[32,24,128]{2,1,0:T(8,128)(2,1)S(1)}, u32[]{:S(2)}, u32[]{:S(2)}) %all-to-all-start.4) | async-done | bytes 196640 | tf_op jit(solution)/shard_map/all_to_all | solution.py:1193
  145.6 3.9 %all-to-all-start.5 = ((bf16[32,24,128]{2,1,0:T(8,128)(2,1)}), bf16[32,24,128]{2,1,0:T(8,128)(2,1)S(1)}, u32[]{:S(2)}, u32[]{:S(2)}) async-start(bf16[32,24,128]{2,1,0:T(8,128)(2,1)} %sum_share.1), calls=%async_computation.5 | async-start | bytes 393216 | tf_op jit(solution)/shard_map/all_to_all | solution.py:1193
  149.6 6.7 %input_gradient.3 = bf16[62,64,1792]{2,1,0:T(8,128)(2,1)} custom-call(bf16[32,64,1024]{2,1,0:T(8,128)(2,1)} %get-tuple-element.99.ds, s16[5,64,1792]{2,1,0:T(8,128)(2,1)} %copy-done.1, bf16[768,256]{1,0:T(8,128)(2,1)S(1)} %get-tuple-element.100.w_ref, bf16[62,64,1792]{2,1,0:T(8,128)(2,1)} %input_gradient.2.rest_0_), custom_call_target="tpu_custom_call", output_to_operand_aliasing={{}: (3, {})} | custom-call | bytes 25200000 | tf_op jit(solution)/shard_map/input_gradient/pallas_call | solution.py:1076
  156.3 1.8 %all-to-all-done.5.g_ref = bf16[32,24,128]{2,1,0:T(8,128)(2,1)S(1)} async-done(((bf16[32,24,128]{2,1,0:T(8,128)(2,1)}), bf16[32,24,128]{2,1,0:T(8,128)(2,1)S(1)}, u32[]{:S(2)}, u32[]{:S(2)}) %all-to-all-start.5) | async-done | bytes 196640 | tf_op jit(solution)/shard_map/all_to_all | solution.py:1193
  158.1 1.7 %update.1 = (f32[1,1]{1,0:T(1,128)}, f32[2,64,576]{2,1,0:T(8,128)}, f32[2,64,576]{2,1,0:T(8,128)}, f32[2,64,576]{2,1,0:T(8,128)}, bf16[2,64,576]{2,1,0:T(8,128)(...) custom-call(bf16[32,24,128]{2,1,0:T(8,128)(2,1)S(1)} %all-to-all-done.5.g_ref, ...), custom_call_target="tpu_custom_call" | custom-call | bytes 10800000 | tf_op jit(solution)/shard_map/update/pallas_call | solution.py:1173
  (39 shorter events, 3.9 us)
Async XLA Ops:
  0.6 18.9 %slice-start = ((s8[14221312]{0:T(1024)(128)(4,1)}), s8[4194304]{0:T(1024)(128)(4,1)S(1)}, s32[]{:S(2)}) async-start(s8[14221312]{0:T(1024)(128)(4,1)} %bitcast.22), calls=%async_computation.6 | async-start | bytes 8388608
  0.7 16.2 %copy-start.2 = (f32[2,576,64]{1,2,0:T(8,128)S(1)}, f32[2,576,64]{1,2,0:T(8,128)}, u32[]{:S(2)}) copy-start(f32[2,576,64]{1,2,0:T(8,128)} %param.11) | copy-start | bytes 884740
  0.7 16.2 %copy-start.5 = (f32[2,2,64]{2,1,0:T(2,128)S(1)}, f32[2,2,64]{2,1,0:T(2,128)}, u32[]{:S(2)}) copy-start(f32[2,2,64]{2,1,0:T(2,128)} %param.14) | copy-start | bytes 3076
  0.7 18.8 %slice-start.1 = ((s8[14221312]{0:T(1024)(128)(4,1)}), s8[4194304]{0:T(1024)(128)(4,1)S(1)}, s32[]{:S(2)}) async-start(s8[14221312]{0:T(1024)(128)(4,1)} %bitcast.22), calls=%async_computation.7 | async-start | bytes 8388608
  0.7 18.8 %slice-start.2 = ((s8[14221312]{0:T(1024)(128)(4,1)}), s8[4194304]{0:T(1024)(128)(4,1)S(1)}, s32[]{:S(2)}) async-start(s8[14221312]{0:T(1024)(128)(4,1)} %bitcast.22), calls=%async_computation.8 | async-start | bytes 8388608
  0.7 18.8 %slice-start.3 = ((s8[14221312]{0:T(1024)(128)(4,1)}), s8[1638400]{0:T(1024)(128)(4,1)S(1)}, s32[]{:S(2)}) async-start(s8[14221312]{0:T(1024)(128)(4,1)} %bitcast.22), calls=%async_computation.9 | async-start | bytes 3276800
  3.2 16.1 %collective-permute-start.1 = (bf16[31,64,128]{2,1,0:T(8,128)(2,1)S(1)}, bf16[31,64,128]{2,1,0:T(8,128)(2,1)S(1)}, u32[]{:S(2)}, u32[]{:S(2)}) collective-permute-start(bf16[31,64,128]{2,1,0:T(8,128)(2,1)S(1)} %get-tuple-element.63), channel_id=1, source_target_pairs={{0,1},{1,2},{2,3},{3,4},{4,5},{5,6},{6,7},{8,9},{9,10},{10,11},{11... | collective-permute-start | bytes 1523720 | tf_op jit(solution)/shard_map/ppermute | solution.py:1189
  8.4 11.1 %collective-permute-start = (bf16[64,2688]{1,0:T(8,128)(2,1)S(1)}, bf16[64,2688]{1,0:T(8,128)(2,1)S(1)}, u32[]{:S(2)}, u32[]{:S(2)}) collective-permute-start(bf16[64,2688]{1,0:T(8,128)(2,1)S(1)} %get-tuple-element.62), channel_id=1, source_target_pairs={{0,8},{8,16},{16,24},{1,9},{9,17},{17,25},{2,10},{10,18},{18,26},{... | collective-permute-start | bytes 1032200 | tf_op jit(solution)/shard_map/ppermute | solution.py:1189
  9.9 9.2 %collective-permute-start.2 = (bf16[2,64,896]{2,1,0:T(8,128)(2,1)S(1)}, bf16[2,64,896]{2,1,0:T(8,128)(2,1)S(1)}, u32[]{:S(2)}, u32[]{:S(2)}) collective-permute-start(bf16[2,64,896]{2,1,0:T(8,128)(2,1)S(1)} %get-tuple-element.64), channel_id=1, source_target_pairs={{8,0},{16,8},{24,16},{9,1},{17,9},{25,17},{10,2},{18,10},{26,18},{... | collective-permute-start | bytes 688136 | tf_op jit(solution)/shard_map/ppermute | solution.py:1189
  11.2 8.3 %collective-permute-start.3 = (bf16[64,128]{1,0:T(8,128)(2,1)S(1)}, bf16[64,128]{1,0:T(8,128)(2,1)S(1)}, u32[]{:S(2)}, u32[]{:S(2)}) collective-permute-start(bf16[64,128]{1,0:T(8,128)(2,1)S(1)} %get-tuple-element.66), channel_id=1, source_target_pairs={{0,9},{1,10},{2,11},{3,12},{4,13},{5,14},{6,15},{8,17},{9,18},{10,... | collective-permute-start | bytes 49160 | tf_op jit(solution)/shard_map/ppermute | solution.py:1214
  19.1 9.5 %copy-start.1 = (s16[5,64,1792]{2,1,0:T(8,128)(2,1)}, s16[5,64,1792]{2,1,0:T(8,128)(2,1)S(1)}, u32[]{:S(2)}) copy-start(s16[5,64,1792]{2,1,0:T(8,128)(2,1)S(1)} %get-tuple-element.61.bits_ref) | copy-start | bytes 3440644
  23.0 15.9 %collective-permute-start.4 = (bf16[16,64,128]{2,1,0:T(8,128)(2,1)S(1)}, bf16[16,64,128]{2,1,0:T(8,128)(2,1)S(1)}, u32[]{:S(2)}, u32[]{:S(2)}) collective-permute-start(bf16[16,64,128]{2,1,0:T(8,128)(2,1)S(1)} %get-tuple-element.74), channel_id=1, source_target_pairs={{0,1},{1,2},{2,3},{3,4},{4,5},{5,6},{6,7},{8,9},{9,10},{10,11},{11... | collective-permute-start | bytes 786440 | tf_op jit(solution)/shard_map/ppermute | solution.py:1189
  27.3 11.7 %collective-permute-start.5 = (bf16[16,64,128]{2,1,0:T(8,128)(2,1)S(1)}, bf16[16,64,128]{2,1,0:T(8,128)(2,1)S(1)}, u32[]{:S(2)}, u32[]{:S(2)}) collective-permute-start(bf16[16,64,128]{2,1,0:T(8,128)(2,1)S(1)} %get-tuple-element.75), channel_id=1, source_target_pairs={{1,0},{2,1},{3,2},{4,3},{5,4},{6,5},{7,6},{9,8},{10,9},{11,10},{12... | collective-permute-start | bytes 786440 | tf_op jit(solution)/shard_map/ppermute | solution.py:1189
  39.6 18.7 %collective-permute-start.7 = (bf16[3,64,1024]{2,1,0:T(8,128)(2,1)S(1)}, bf16[3,64,1024]{2,1,0:T(8,128)(2,1)S(1)}, u32[]{:S(2)}, u32[]{:S(2)}) collective-permute-start(bf16[3,64,1024]{2,1,0:T(8,128)(2,1)S(1)} %get-tuple-element.77), channel_id=1, source_target_pairs={{8,0},{16,8},{24,16},{9,1},{17,9},{25,17},{10,2},{18,10},{26,18},{... | collective-permute-start | bytes 1179656 | tf_op jit(solution)/shard_map/ppermute | solution.py:1189
  40.9 17.4 %collective-permute-start.6 = (bf16[2,64,1024]{2,1,0:T(8,128)(2,1)S(1)}, bf16[2,64,1024]{2,1,0:T(8,128)(2,1)S(1)}, u32[]{:S(2)}, u32[]{:S(2)}) collective-permute-start(bf16[2,64,1024]{2,1,0:T(8,128)(2,1)S(1)} %get-tuple-element.76), channel_id=1, source_target_pairs={{0,8},{8,16},{16,24},{1,9},{9,17},{17,25},{2,10},{10,18},{18,26},{... | collective-permute-start | bytes 786440 | tf_op jit(solution)/shard_map/ppermute | solution.py:1189
  58.2 15.6 %copy-start = (bf16[64,31,896]{2,0,1:T(8,128)(2,1)S(1)}, bf16[64,31,896]{2,0,1:T(8,128)(2,1)}, u32[]{:S(2)}) copy-start(bf16[64,31,896]{2,0,1:T(8,128)(2,1)} %param.17) | copy-start | bytes 10665988
  88.8 14.7 %collective-permute-start.8 = (bf16[17,64,128]{2,1,0:T(8,128)(2,1)S(1)}, bf16[17,64,128]{2,1,0:T(8,128)(2,1)S(1)}, u32[]{:S(2)}, u32[]{:S(2)}) collective-permute-start(bf16[17,64,128]{2,1,0:T(8,128)(2,1)S(1)} %get-tuple-element.92), channel_id=1, source_target_pairs={{0,1},{1,2},{2,3},{3,4},{4,5},{5,6},{6,7},{8,9},{9,10},{10,11},{11... | collective-permute-start | bytes 835592 | tf_op jit(solution)/shard_map/ppermute | solution.py:1189
  91.4 12.1 %collective-permute-start.9 = (bf16[17,64,128]{2,1,0:T(8,128)(2,1)S(1)}, bf16[17,64,128]{2,1,0:T(8,128)(2,1)S(1)}, u32[]{:S(2)}, u32[]{:S(2)}) collective-permute-start(bf16[17,64,128]{2,1,0:T(8,128)(2,1)S(1)} %get-tuple-element.93), channel_id=1, source_target_pairs={{1,0},{2,1},{3,2},{4,3},{5,4},{6,5},{7,6},{9,8},{10,9},{11,10},{12... | collective-permute-start | bytes 835592 | tf_op jit(solution)/shard_map/ppermute | solution.py:1189
  105.9 14.1 %collective-permute-start.10 = (bf16[16,64,128]{2,1,0:T(8,128)(2,1)S(1)}, bf16[16,64,128]{2,1,0:T(8,128)(2,1)S(1)}, u32[]{:S(2)}, u32[]{:S(2)}) collective-permute-start(bf16[16,64,128]{2,1,0:T(8,128)(2,1)S(1)} %get-tuple-element.96), channel_id=1, source_target_pairs={{1,0},{2,1},{3,2},{4,3},{5,4},{6,5},{7,6},{9,8},{10,9},{11,10},{12... | collective-permute-start | bytes 786440 | tf_op jit(solution)/shard_map/ppermute | solution.py:1189
  133.7 11.1 %all-to-all-start.4 = ((bf16[32,24,128]{2,1,0:T(8,128)(2,1)}), bf16[32,24,128]{2,1,0:T(8,128)(2,1)S(1)}, u32[]{:S(2)}, u32[]{:S(2)}) async-start(bf16[32,24,128]{2,1,0:T(8,128)(2,1)} %get-tuple-element.101), calls=%async_computation.4 | async-start | bytes 393216 | tf_op jit(solution)/shard_map/all_to_all | solution.py:1193
  145.6 12.5 %all-to-all-start.5 = ((bf16[32,24,128]{2,1,0:T(8,128)(2,1)}), bf16[32,24,128]{2,1,0:T(8,128)(2,1)S(1)}, u32[]{:S(2)}, u32[]{:S(2)}) async-start(bf16[32,24,128]{2,1,0:T(8,128)(2,1)} %sum_share.1), calls=%async_computation.5 | async-start | bytes 393216 | tf_op jit(solution)/shard_map/all_to_all | solution.py:1193
  149.5 8.6 %copy-start.3 = (f32[2,576,64]{1,2,0:T(8,128)S(1)}, f32[2,576,64]{1,2,0:T(8,128)}, u32[]{:S(2)}) copy-start(f32[2,576,64]{1,2,0:T(8,128)} %param.12) | copy-start | bytes 884740
  149.5 8.5 %copy-start.4 = (f32[2,576,64]{1,2,0:T(8,128)S(1)}, f32[2,576,64]{1,2,0:T(8,128)}, u32[]{:S(2)}) copy-start(f32[2,576,64]{1,2,0:T(8,128)} %param.13) | copy-start | bytes 884740
  149.5 8.5 %copy-start.6 = (f32[2,2,64]{2,1,0:T(2,128)S(1)}, f32[2,2,64]{2,1,0:T(2,128)}, u32[]{:S(2)}) copy-start(f32[2,2,64]{2,1,0:T(2,128)} %param.15) | copy-start | bytes 3076
  149.6 8.5 %copy-start.7 = (f32[2,2,64]{2,1,0:T(2,128)S(1)}, f32[2,2,64]{2,1,0:T(2,128)}, u32[]{:S(2)}) copy-start(f32[2,2,64]{2,1,0:T(2,128)} %param.16) | copy-start | bytes 3076

commit v7 on v6

--- a/solution.py
+++ b/solution.py
@@ -150,12 +150,27 @@
     return b if a is None else [x + y for x, y in zip(a, b)]
 
 
-def rim_of(first, second, row, low):
-    half = first.shape[0]
+def odd_place():
+    return lax.rem(lax.axis_index("gx"), 2) == 1
+
+
+def swapped(far, near, odd):
+    return lambda k: (
+        jnp.where(odd, far(k), near(k)),
+        jnp.where(odd, near(k), far(k)),
+    )
+
+
+def rim_of(far, near, row, low, left_first):
+    half = far.shape[0]
+    k = row % half
+    right, left = swapped(
+        lambda k: far[k].astype(f32), lambda k: near[k].astype(f32), odd_place()
+    )(k)
+    first, second = (left, right) if left_first else (right, left)
     if row < half:
-        return jnp.where(low, first[row].astype(f32), second[row].astype(f32))
-    row = row - half
-    return swap(jnp.where(low, second[row].astype(f32), first[row].astype(f32)))
+        return jnp.where(low, first, second)
+    return swap(jnp.where(low, second, first))
 
 
 def halves(x):
@@ -349,10 +364,12 @@
         edge_ref[i] = edge[i].astype(bf16)
     finish_stats(step, steps, pilot, off_sums(edge, pilot), float(r * S), run, st_ref)
     half = er_ref.shape[0]
+    odd = odd_place()
     for k in range(half):
         far = swap(edge[k + half]) if k + half < r else jnp.zeros((S, L), f32)
-        er_ref[k] = jnp.where(low, edge[k], far).astype(bf16)
-        el_ref[k] = jnp.where(low, far, edge[k]).astype(bf16)
+        right, left = (jnp.where(low, edge[k], far), jnp.where(low, far, edge[k]))
+        er_ref[k] = jnp.where(odd, right, left).astype(bf16)
+        el_ref[k] = jnp.where(odd, left, right).astype(bf16)
 
 
 def first_last(x, bits, down, xcol, corner, w):
@@ -471,7 +488,7 @@
         out[:, :, :wide] = src[...]
         for k in range(src.shape[0]):
             out[k, :, wide : wide + L] = edge_ref[first + k]
-            out[k, :, wide + L :] = rim_of(left_ref, right_ref, first + k, low).astype(bf16)
+            out[k, :, wide + L :] = rim_of(left_ref, right_ref, first + k, low, True).astype(bf16)
 
 
 def pack_rows(up, down, edge, left, right):
@@ -513,7 +530,7 @@
     left = jnp.where(low, f_left, 1.0)
     right = jnp.where(low, 1.0, f_right)
     for row in range(r):
-        rim[row] = rim_of(left_ref, right_ref, row, low)
+        rim[row] = rim_of(left_ref, right_ref, row, low, True)
 
     def act(row, t):
         at_end = t in (0, tiles - 1)
@@ -719,10 +736,12 @@
     half = rows // 2
     column = lambda row, t: back(row, pair(d_ref, row, t), pair(c_ref, row, t))
     both = lambda row: jnp.where(low, column(row, 0), column(row, last))
+    odd = odd_place()
     for k in range(half):
         near, far = (both(k), swap(both(k + half)))
-        el_ref[k] = jnp.where(low, near, far).astype(bf16)
-        er_ref[k] = jnp.where(low, far, near).astype(bf16)
+        right, left = (jnp.where(low, far, near), jnp.where(low, near, far))
+        er_ref[k] = jnp.where(odd, right, left).astype(bf16)
+        el_ref[k] = jnp.where(odd, left, right).astype(bf16)
 
 
 def rim_two(d, c2, st, sums, np2, count):
@@ -877,7 +896,7 @@
     r, tiles = (n1_ref.shape[0] - 1, n1_ref.shape[2] // L)
     low = low_half(S2)
     for row in range(r + 3):
-        rim[row] = rim_of(right_ref, left_ref, row, low).astype(bf16)
+        rim[row] = rim_of(left_ref, right_ref, row, low, False).astype(bf16)
     first, last = (ds_ref[:, :, k * L : (k + 1) * L] for k in (0, tiles - 2))
     args = (n1_ref, np_ref, w_ref, dp_ref)
     sums = hidden_tile(0, [rim[...], first], *args, 0, True, False)
@@ -1189,6 +1208,13 @@
     return lax.ppermute(block, axis, route)
 
 
+def partnered(block, first):
+    route = []
+    for i in range(first, lax.axis_size("gx") - 1, 2):
+        route += [(i, i + 1), (i + 1, i)]
+    return lax.ppermute(block, "gx", route)
+
+
 def exchange(rows):
     return lax.all_to_all(rows, BOTH, 0, 0, tiled=True)
 
@@ -1217,27 +1243,27 @@
     bits, w1, w2, w2b, w1b, np2 = prepare(occ, kt, norm_params)
 
     xcol, cot_down = lax.optimization_barrier((xcol, cot_down))
-    ends, st1, going_right, going_left, edge = first_last(x, bits, down, xcol, corner, w1)
-    left_in = shifted(going_right, "gx", 1)
-    right_in = shifted(going_left, "gx", -1)
+    ends, st1, for_far, for_near, edge = first_last(x, bits, down, xcol, corner, w1)
+    far_in = partnered(for_far, 1)
+    near_in = partnered(for_near, 0)
     c1, st1, up, low_rows = conv_one(x, bits, down, st1, w1, devices)
-    up, low_rows = pack_rows(up, low_rows, edge, left_in, right_in)
+    up, low_rows = pack_rows(up, low_rows, edge, far_in, near_in)
     down_in = shifted(up, "gy", -1)
     up_in = shifted(low_rows, "gy", 1)
     st1 = exchange(st1)
 
     c2, n1, hid, st2 = conv_two(
-        c1, ends, up_in, down_in, left_in, right_in, st1, np2, w2, count
+        c1, ends, up_in, down_in, far_in, near_in, st1, np2, w2, count
     )
     st2 = exchange(st2)
     features, d2, sums2 = output(c2, st2, np2, cot, down, cot_down, count)
     sums2 = exchange(sums2)
-    going_right, going_left = rim_two(d2, c2, st2, sums2, np2, count)
-    left_in = shifted(going_right, "gx", 1)
-    right_in = shifted(going_left, "gx", -1)
+    for_far, for_near = rim_two(d2, c2, st2, sums2, np2, count)
+    far_in = partnered(for_far, 1)
+    near_in = partnered(for_near, 0)
     ds, kg2 = back_two(d2, c2, hid, st2, sums2, np2, count)
     d1, sums1 = hidden_gradient(ds, n1, np2, w2b)
-    d1_ends, edge, sums1 = hidden_ends(ds, left_in, right_in, n1, np2, w2b, sums1, devices)
+    d1_ends, edge, sums1 = hidden_ends(ds, far_in, near_in, n1, np2, w2b, sums1, devices)
     edge = shifted(edge, "gx", -1)
     sums1 = exchange(sums1)
     d1, grads = back_one(d1, d1_ends, edge, n1, x, bits, st1, sums1, np2, kg2, count)

time: 160 us -> 160 us (level)
  blocking collectives: 44.9 us -> 42.5 us
    ppermute x0 -> x4, starting transfers between devices: none -> 10.9 us  [partnered(): return lax.ppermute(block, 'gx', route)]
    ppermute x10 -> x6, starting transfers between devices: 23.2 us -> 13.5 us  [shifted(): return lax.ppermute(block, axis, route)]
    all_to_all x4, blocking collectives: 44.9 us -> 42.5 us  [exchange(): return lax.all_to_all(rows, BOTH, 0, 0, tiled=True)]
    ppermute x0 -> x4, waiting for transfers between devices: none -> 1.92 us  [partnered(): return lax.ppermute(block, 'gx', route)]
where the time goes in v7:
time: 160 us; the launch traced here: 159 us
  Pallas kernels  73.1 us (46%)
  blocking collectives  42.5 us (27%)
  starting transfers between devices  36.6 us (23%)
  waiting for transfers between devices  6.06 us (4%)
    all_to_all x4, blocking collectives, exchange(): return lax.all_to_all(rows, BOTH, 0, 0, tiled=True)  42.5 us
    pallas_call x1, Pallas kernels, back_one(): pl.pallas_call(functools.partial(back_one_kernel, count=count), grid=(sca...  13.6 us
    ppermute x6, starting transfers between devices, shifted(): return lax.ppermute(block, axis, route)  13.5 us
    pallas_call x2, Pallas kernels, input_gradient(): pl.pallas_call(input_grad_kernel, grid=(steps,), in_specs=[at(r, wide), a...  13.3 us
    ppermute x4, starting transfers between devices, partnered(): return lax.ppermute(block, 'gx', route)  10.9 us
    pallas_call x1, Pallas kernels, conv_one(): pl.pallas_call(conv_one_kernel, grid=(scan_count // S,), in_specs=[held,...  9.62 us
    pallas_call x1, Pallas kernels, conv_two(): pl.pallas_call(functools.partial(conv_two_kernel, count=count), grid=(sca...  6.72 us
    all_to_all x2, starting transfers between devices, exchange(): return lax.all_to_all(rows, BOTH, 0, 0, tiled=True)  6.51 us
  transfers between devices with their start and end apart: 13, of which 6 were waited for; matrix products, arithmetic and copies ran while one was open for 0% of the time, Pallas kernels for 22%

profile of v7, /device:TPU:0, one launch (start us, length us, event | category | flops | bytes accessed | tf_op | source)
XLA Modules:
  0.0 159.3 jit_solution(1814138940982622094)
XLA Ops:
  0.7 2.5 %edges.1 = (bf16[64,2688]{1,0:T(8,128)(2,1)S(1)}, bf16[2,64,896]{2,1,0:T(8,128)(2,1)S(1)}, bf16[64,128]{1,0:T(8,128)(2,1)S(1)}, bf16[31,64,128]{2,1,0:T(8,128)(2,1)S(1)}) custom-call(bf16[62,64,1792]{2,1,0:T(8,128)(2,1)} %bitcast.19, bf16[62,64,1792]{2,1,0:T(8,128)(2,1)} %bitcast.20, s32[28,64,62]{2,1,0:T(8,128)} %bitcast.38, bf16[31,64,896]{2,1,0:T(8,128)(2,1)} %bitcast.26, ...), custom_call_target="tpu_custom_call" | custom-call | bytes 10800000 | tf_op jit(solution)/shard_map/edges/pallas_call | solution.py:231
  3.2 5.1 %collective-permute-start.1 = (bf16[31,64,128]{2,1,0:T(8,128)(2,1)S(1)}, bf16[31,64,128]{2,1,0:T(8,128)(2,1)S(1)}, u32[]{:S(2)}, u32[]{:S(2)}) collective-permute-start(bf16[31,64,128]{2,1,0:T(8,128)(2,1)S(1)} %get-tuple-element.63), channel_id=1, source_target_pairs={{0,1},{1,2},{2,3},{3,4},{4,5},{5,6},{6,7},{8,9},{9,10},{10,11},{11... | collective-permute-start | bytes 1523720 | tf_op jit(solution)/shard_map/ppermute | solution.py:1208
  8.4 1.5 collective-permute-start
  9.9 1.3 collective-permute-start.2
  11.2 5.7 %collective-permute-start.3 = (bf16[64,128]{1,0:T(8,128)(2,1)S(1)}, bf16[64,128]{1,0:T(8,128)(2,1)S(1)}, u32[]{:S(2)}, u32[]{:S(2)}) collective-permute-start(bf16[64,128]{1,0:T(8,128)(2,1)S(1)} %get-tuple-element.66), channel_id=1, source_target_pairs={{0,9},{1,10},{2,11},{3,12},{4,13},{5,14},{6,15},{8,17},{9,18},{10,... | collective-permute-start | bytes 49160 | tf_op jit(solution)/shard_map/ppermute | solution.py:1240
  16.9 2.2 %prepare.1 = (s16[5,64,1792]{2,1,0:T(8,128)(2,1)S(1)}, bf16[1920,256]{1,0:T(8,128)(2,1)S(1)}, bf16[1024,256]{1,0:T(8,128)(2,1)S(1)}, bf16[1024,256]{1,0:T(8,128)...) custom-call(s32[28,64,62]{2,1,0:T(8,128)} %bitcast.39, f32[2,64,576]{2,1,0:T(8,128)S(1)} %bitcast.29, ...), custom_call_target="tpu_custom_call" | custom-call | bytes 14400000 | tf_op jit(solution)/shard_map/prepare/pallas_call | solution.py:292
  19.5 3.5 %conv_one_ends.1 = (f32[31,64,256]{2,1,0:T(8,128)S(1)}, f32[1,2,128]{2,1,0:T(2,128)S(1)}, bf16[16,64,128]{2,1,0:T(8,128)(2,1)S(1)}, bf16[16,64,128]{2,1,0:T(8,128)(2,1)S(1)}, bf16[31,64,128]{2,1,0:T(8,128)(2,1)S(1)}) custom-call(bf16[62,64,1792]{2,1,0:T(8,128)(2,1)S(1)} %bitcast.24, s16[5,64,1792]{2,1,0:T(8,128)(2,1)S(1)} %get-tuple-element.61.bits_ref, ...), custom_call_target="tpu_custom_call" | custom-call | bytes 14400000 | tf_op jit(solution)/shard_map/conv_one_ends/pallas_call | solution.py:379
  23.8 6.1 %collective-permute-start.5 = (bf16[16,64,128]{2,1,0:T(8,128)(2,1)S(1)}, bf16[16,64,128]{2,1,0:T(8,128)(2,1)S(1)}, u32[]{:S(2)}, u32[]{:S(2)}) collective-permute-start(bf16[16,64,128]{2,1,0:T(8,128)(2,1)S(1)} %get-tuple-element.75), channel_id=1, source_target_pairs={{0,1},{1,0},{2,3},{3,2},{4,5},{5,4},{6,7},{7,6},{8,9},{9,8},{10,11... | collective-permute-start | bytes 786440 | tf_op jit(solution)/shard_map/ppermute | solution.py:1215
  29.8 9.6 %conv_one.1 = (f32[31,64,768]{2,1,0:T(8,128)S(1)}, f32[32,2,128]{2,1,0:T(2,128)S(1)}, bf16[3,64,768]{2,1,0:T(8,128)(2,1)S(1)}, bf16[2,64,768]{2,1,0:T(8,128)(2,1)S(1)}) custom-call(bf16[62,64,1792]{2,1,0:T(8,128)(2,1)S(1)} %bitcast.25, s16[5,64,1792]{2,1,0:T(8,128)(2,1)S(1)} %get-tuple-element.61.bits_ref, ...), custom_call_target="tpu_custom_call" | custom-call | bytes 39600000 | tf_op jit(solution)/shard_map/conv_one/pallas_call | solution.py:457
  40.5 1.3 collective-permute-start.7
  41.8 3.0 %collective-permute-start.6 = (bf16[2,64,1024]{2,1,0:T(8,128)(2,1)S(1)}, bf16[2,64,1024]{2,1,0:T(8,128)(2,1)S(1)}, u32[]{:S(2)}, u32[]{:S(2)}) collective-permute-start(bf16[2,64,1024]{2,1,0:T(8,128)(2,1)S(1)} %get-tuple-element.76), channel_id=1, source_target_pairs={{0,8},{8,16},{16,24},{1,9},{9,17},{17,25},{2,10},{10,18},{18,26},{... | collective-permute-start | bytes 786440 | tf_op jit(solution)/shard_map/ppermute | solution.py:1208
  44.9 12.8 %all_to_all.30.st_ref = f32[32,2,128]{2,1,0:T(2,128)S(1)} all-to-all(f32[32,2,128]{2,1,0:T(2,128)S(1)} %get-tuple-element.78), channel_id=1, replica_groups=mesh['gy'=4,'gx'=8] {'gy','gx'}, dimensions={0} | all-to-all | bytes 65536 | tf_op jit(solution)/shard_map/all_to_all | solution.py:1219
  57.7 6.7 %conv_two.1 = (f32[34,64,896]{2,1,0:T(8,128)S(1)}, bf16[32,64,1024]{2,1,0:T(8,128)(2,1)S(1)}, bf16[36,64,1024]{2,1,0:T(8,128)(2,1)S(1)}, f32[32,2,128]{2,1,0:T(2,128)S(1)}) custom-call(f32[31,64,768]{2,1,0:T(8,128)S(1)} %get-tuple-element.69.c_ref, f32[31,64,256]{2,1,0:T(8,128)S(1)} %get-tuple-element.70.ends_ref, ...), custom_call_target="tpu_custom_call" | custom-call | bytes 50400000 | tf_op jit(solution)/shard_map/conv_two/pallas_call | solution.py:594
  64.4 8.9 %all_to_all.31.st_ref = f32[32,2,128]{2,1,0:T(2,128)S(1)} all-to-all(f32[32,2,128]{2,1,0:T(2,128)S(1)} %get-tuple-element.82), channel_id=1, replica_groups=mesh['gy'=4,'gx'=8] {'gy','gx'}, dimensions={0} | all-to-all | bytes 65536 | tf_op jit(solution)/shard_map/all_to_all | solution.py:1219
  73.3 5.3 %output.1 = (bf16[31,64,896]{2,1,0:T(8,128)(2,1)}, f32[34,64,896]{2,1,0:T(8,128)S(1)}, f32[32,2,128]{2,1,0:T(2,128)S(1)}) custom-call(f32[34,64,896]{2,1,0:T(8,128)S(1)} %get-tuple-element.81.c2_ref.c_ref, f32[32,2,128]{2,1,0:T(2,128)S(1)} %all_to_all.31.st_ref, f32[4,128]{1,0:T(4,128)S(1)} %get-tuple-element.79.np_ref, bf16[31,64,896]{2,1,0:T(8,128)(2,1)S(1)} %bitcast.28, ...), custom_call_target="tpu_custom_call" | custom-call | bytes 43200000 | tf_op jit(solution)/shard_map/output/pallas_call | solution.py:683
  78.5 8.9 %all_to_all.32.sum_ref.s2_ref = f32[32,2,128]{2,1,0:T(2,128)S(1)} all-to-all(f32[32,2,128]{2,1,0:T(2,128)S(1)} %get-tuple-element.87), channel_id=1, replica_groups=mesh['gy'=4,'gx'=8] {'gy','gx'}, dimensions={0} | all-to-all | bytes 65536 | tf_op jit(solution)/shard_map/all_to_all | solution.py:1219
  87.4 0.9 rim_two.1
  89.1 3.3 %collective-permute-start.9 = (bf16[17,64,128]{2,1,0:T(8,128)(2,1)S(1)}, bf16[17,64,128]{2,1,0:T(8,128)(2,1)S(1)}, u32[]{:S(2)}, u32[]{:S(2)}) collective-permute-start(bf16[17,64,128]{2,1,0:T(8,128)(2,1)S(1)} %get-tuple-element.93), channel_id=1, source_target_pairs={{0,1},{1,0},{2,3},{3,2},{4,5},{5,4},{6,7},{7,6},{8,9},{9,8},{10,11... | collective-permute-start | bytes 835592 | tf_op jit(solution)/shard_map/ppermute | solution.py:1215
  92.4 5.1 %back_two.1 = (bf16[34,64,896]{2,1,0:T(8,128)(2,1)S(1)}, f32[9,64,64]{2,1,0:T(8,128)S(1)}) custom-call(f32[34,64,896]{2,1,0:T(8,128)S(1)} %get-tuple-element.85.d_ref, f32[34,64,896]{2,1,0:T(8,128)S(1)} %get-tuple-element.81.c2_ref.c_ref, bf16[36,64,1024]{2,1,0:T(8,128)(2,1)S(1)} %get-tuple-element.86.hid_ref, f32[32,2,128]{2,1,0:T(2,128)S(1)} %all_to_all.31.st_ref, ...), custom_call_target="tpu_custom_call" | custom-call | bytes 43200000 | tf_op jit(solution)/shard_map/back_two/pallas_call | solution.py:812
  97.5 4.9 %hidden_gradient.1 = (f32[32,64,768]{2,1,0:T(8,128)S(1)}, f32[1,2,128]{2,1,0:T(2,128)S(1)}) custom-call(bf16[34,64,896]{2,1,0:T(8,128)(2,1)S(1)} %get-tuple-element.88.ds_ref, bf16[32,64,1024]{2,1,0:T(8,128)(2,1)S(1)} %get-tuple-element.89.n1_ref, f32[4,128]{1,0:T(4,128)S(1)} %get-tuple-element.79.np_ref, bf16[1024,256]{1,0:T(8,128)(2,1)S(1)} %get-tuple-element.90.w_ref), custom_call_target="tpu_custom_call" | custom-call | bytes 21600000 | tf_op jit(solution)/shard_map/hidden_gradient/pallas_call | solution.py:874
  102.4 1.5 collective-permute-done.9.right_ref
  103.9 2.4 %hidden_gradient_ends.1 = (f32[32,64,256]{2,1,0:T(8,128)S(1)}, bf16[16,64,128]{2,1,0:T(8,128)(2,1)S(1)}, f32[32,2,128]{2,1,0:T(2,128)S(1)}) custom-call(bf16[34,64,896]{2,1,0:T(8,128)(2,1)S(1)} %get-tuple-element.88.ds_ref, bf16[17,64,128]{2,1,0:T(8,128)(2,1)S(1)} %collective-permute-done.8.left_ref, ...), custom_call_target="tpu_custom_call" | custom-call | bytes 10800000 | tf_op jit(solution)/shard_map/hidden_gradient_ends/pallas_call | solution.py:916
  106.3 1.3 collective-permute-start.10
  107.6 11.9 %all_to_all.33.sum_ref.s1_ref = f32[32,2,128]{2,1,0:T(2,128)S(1)} all-to-all(f32[32,2,128]{2,1,0:T(2,128)S(1)} %get-tuple-element.97), channel_id=1, replica_groups=mesh['gy'=4,'gx'=8] {'gy','gx'}, dimensions={0} | all-to-all | bytes 65536 | tf_op jit(solution)/shard_map/all_to_all | solution.py:1219
  119.6 13.6 %back_one.1 = (bf16[32,64,1024]{2,1,0:T(8,128)(2,1)}, bf16[32,24,128]{2,1,0:T(8,128)(2,1)}) custom-call(f32[32,64,768]{2,1,0:T(8,128)S(1)} %get-tuple-element.91.dp_ref, f32[32,64,256]{2,1,0:T(8,128)S(1)} %get-tuple-element.95.ends_ref, bf16[16,64,128]{2,1,0:T(8,128)(2,1)S(1)} %collective-permute-done.10.edge_ref, ...), custom_call_target="tpu_custom_call" | custom-call | bytes 57600000 | tf_op jit(solution)/shard_map/back_one/pallas_call | solution.py:1038
  133.2 2.6 %all-to-all-start.4 = ((bf16[32,24,128]{2,1,0:T(8,128)(2,1)}), bf16[32,24,128]{2,1,0:T(8,128)(2,1)S(1)}, u32[]{:S(2)}, u32[]{:S(2)}) async-start(bf16[32,24,128]{2,1,0:T(8,128)(2,1)} %get-tuple-element.101), calls=%async_computation.4 | async-start | bytes 393216 | tf_op jit(solution)/shard_map/all_to_all | solution.py:1219
  135.8 6.6 %input_gradient.2.rest_0_ = bf16[62,64,1792]{2,1,0:T(8,128)(2,1)} custom-call(bf16[32,64,1024]{2,1,0:T(8,128)(2,1)} %get-tuple-element.99.ds, s16[5,64,1792]{2,1,0:T(8,128)(2,1)} %copy-done.1, bf16[768,256]{1,0:T(8,128)(2,1)S(1)} %get-tuple-element.100.w_ref), custom_call_target="tpu_custom_call" | custom-call | bytes 25200000 | tf_op jit(solution)/shard_map/input_gradient/pallas_call | solution.py:1095
  142.5 1.9 %all-to-all-done.4.g_ref = bf16[32,24,128]{2,1,0:T(8,128)(2,1)S(1)} async-done(((bf16[32,24,128]{2,1,0:T(8,128)(2,1)}), bf16[32,24,128]{2,1,0:T(8,128)(2,1)S(1)}, u32[]{:S(2)}, u32[]{:S(2)}) %all-to-all-start.4) | async-done | bytes 196640 | tf_op jit(solution)/shard_map/all_to_all | solution.py:1219
  145.1 3.9 %all-to-all-start.5 = ((bf16[32,24,128]{2,1,0:T(8,128)(2,1)}), bf16[32,24,128]{2,1,0:T(8,128)(2,1)S(1)}, u32[]{:S(2)}, u32[]{:S(2)}) async-start(bf16[32,24,128]{2,1,0:T(8,128)(2,1)} %sum_share.1), calls=%async_computation.5 | async-start | bytes 393216 | tf_op jit(solution)/shard_map/all_to_all | solution.py:1219
  149.1 6.7 %input_gradient.3 = bf16[62,64,1792]{2,1,0:T(8,128)(2,1)} custom-call(bf16[32,64,1024]{2,1,0:T(8,128)(2,1)} %get-tuple-element.99.ds, s16[5,64,1792]{2,1,0:T(8,128)(2,1)} %copy-done.1, bf16[768,256]{1,0:T(8,128)(2,1)S(1)} %get-tuple-element.100.w_ref, bf16[62,64,1792]{2,1,0:T(8,128)(2,1)} %input_gradient.2.rest_0_), custom_call_target="tpu_custom_call", output_to_operand_aliasing={{}: (3, {})} | custom-call | bytes 25200000 | tf_op jit(solution)/shard_map/input_gradient/pallas_call | solution.py:1095
  155.8 1.8 %all-to-all-done.5.g_ref = bf16[32,24,128]{2,1,0:T(8,128)(2,1)S(1)} async-done(((bf16[32,24,128]{2,1,0:T(8,128)(2,1)}), bf16[32,24,128]{2,1,0:T(8,128)(2,1)S(1)}, u32[]{:S(2)}, u32[]{:S(2)}) %all-to-all-start.5) | async-done | bytes 196640 | tf_op jit(solution)/shard_map/all_to_all | solution.py:1219
  157.6 1.7 %update.1 = (f32[1,1]{1,0:T(1,128)}, f32[2,64,576]{2,1,0:T(8,128)}, f32[2,64,576]{2,1,0:T(8,128)}, f32[2,64,576]{2,1,0:T(8,128)}, bf16[2,64,576]{2,1,0:T(8,128)(...) custom-call(bf16[32,24,128]{2,1,0:T(8,128)(2,1)S(1)} %all-to-all-done.5.g_ref, ...), custom_call_target="tpu_custom_call" | custom-call | bytes 10800000 | tf_op jit(solution)/shard_map/update/pallas_call | solution.py:1192
  (39 shorter events, 3.8 us)
Async XLA Ops:
  0.6 18.9 %slice-start = ((s8[14221312]{0:T(1024)(128)(4,1)}), s8[4194304]{0:T(1024)(128)(4,1)S(1)}, s32[]{:S(2)}) async-start(s8[14221312]{0:T(1024)(128)(4,1)} %bitcast.22), calls=%async_computation.6 | async-start | bytes 8388608
  0.7 16.2 %copy-start.2 = (f32[2,576,64]{1,2,0:T(8,128)S(1)}, f32[2,576,64]{1,2,0:T(8,128)}, u32[]{:S(2)}) copy-start(f32[2,576,64]{1,2,0:T(8,128)} %param.11) | copy-start | bytes 884740
  0.7 16.2 %copy-start.5 = (f32[2,2,64]{2,1,0:T(2,128)S(1)}, f32[2,2,64]{2,1,0:T(2,128)}, u32[]{:S(2)}) copy-start(f32[2,2,64]{2,1,0:T(2,128)} %param.14) | copy-start | bytes 3076
  0.7 18.8 %slice-start.1 = ((s8[14221312]{0:T(1024)(128)(4,1)}), s8[4194304]{0:T(1024)(128)(4,1)S(1)}, s32[]{:S(2)}) async-start(s8[14221312]{0:T(1024)(128)(4,1)} %bitcast.22), calls=%async_computation.7 | async-start | bytes 8388608
  0.7 18.8 %slice-start.2 = ((s8[14221312]{0:T(1024)(128)(4,1)}), s8[4194304]{0:T(1024)(128)(4,1)S(1)}, s32[]{:S(2)}) async-start(s8[14221312]{0:T(1024)(128)(4,1)} %bitcast.22), calls=%async_computation.8 | async-start | bytes 8388608
  0.7 18.8 %slice-start.3 = ((s8[14221312]{0:T(1024)(128)(4,1)}), s8[1638400]{0:T(1024)(128)(4,1)S(1)}, s32[]{:S(2)}) async-start(s8[14221312]{0:T(1024)(128)(4,1)} %bitcast.22), calls=%async_computation.9 | async-start | bytes 3276800
  3.2 16.1 %collective-permute-start.1 = (bf16[31,64,128]{2,1,0:T(8,128)(2,1)S(1)}, bf16[31,64,128]{2,1,0:T(8,128)(2,1)S(1)}, u32[]{:S(2)}, u32[]{:S(2)}) collective-permute-start(bf16[31,64,128]{2,1,0:T(8,128)(2,1)S(1)} %get-tuple-element.63), channel_id=1, source_target_pairs={{0,1},{1,2},{2,3},{3,4},{4,5},{5,6},{6,7},{8,9},{9,10},{10,11},{11... | collective-permute-start | bytes 1523720 | tf_op jit(solution)/shard_map/ppermute | solution.py:1208
  8.4 11.1 %collective-permute-start = (bf16[64,2688]{1,0:T(8,128)(2,1)S(1)}, bf16[64,2688]{1,0:T(8,128)(2,1)S(1)}, u32[]{:S(2)}, u32[]{:S(2)}) collective-permute-start(bf16[64,2688]{1,0:T(8,128)(2,1)S(1)} %get-tuple-element.62), channel_id=1, source_target_pairs={{0,8},{8,16},{16,24},{1,9},{9,17},{17,25},{2,10},{10,18},{18,26},{... | collective-permute-start | bytes 1032200 | tf_op jit(solution)/shard_map/ppermute | solution.py:1208
  9.9 9.2 %collective-permute-start.2 = (bf16[2,64,896]{2,1,0:T(8,128)(2,1)S(1)}, bf16[2,64,896]{2,1,0:T(8,128)(2,1)S(1)}, u32[]{:S(2)}, u32[]{:S(2)}) collective-permute-start(bf16[2,64,896]{2,1,0:T(8,128)(2,1)S(1)} %get-tuple-element.64), channel_id=1, source_target_pairs={{8,0},{16,8},{24,16},{9,1},{17,9},{25,17},{10,2},{18,10},{26,18},{... | collective-permute-start | bytes 688136 | tf_op jit(solution)/shard_map/ppermute | solution.py:1208
  11.2 8.3 %collective-permute-start.3 = (bf16[64,128]{1,0:T(8,128)(2,1)S(1)}, bf16[64,128]{1,0:T(8,128)(2,1)S(1)}, u32[]{:S(2)}, u32[]{:S(2)}) collective-permute-start(bf16[64,128]{1,0:T(8,128)(2,1)S(1)} %get-tuple-element.66), channel_id=1, source_target_pairs={{0,9},{1,10},{2,11},{3,12},{4,13},{5,14},{6,15},{8,17},{9,18},{10,... | collective-permute-start | bytes 49160 | tf_op jit(solution)/shard_map/ppermute | solution.py:1240
  19.1 10.8 %copy-start.1 = (s16[5,64,1792]{2,1,0:T(8,128)(2,1)}, s16[5,64,1792]{2,1,0:T(8,128)(2,1)S(1)}, u32[]{:S(2)}) copy-start(s16[5,64,1792]{2,1,0:T(8,128)(2,1)S(1)} %get-tuple-element.61.bits_ref) | copy-start | bytes 3440644
  23.1 16.4 %collective-permute-start.4 = (bf16[16,64,128]{2,1,0:T(8,128)(2,1)S(1)}, bf16[16,64,128]{2,1,0:T(8,128)(2,1)S(1)}, u32[]{:S(2)}, u32[]{:S(2)}) collective-permute-start(bf16[16,64,128]{2,1,0:T(8,128)(2,1)S(1)} %get-tuple-element.74), channel_id=1, source_target_pairs={{1,2},{2,1},{3,4},{4,3},{5,6},{6,5},{9,10},{10,9},{11,12},{12,11},... | collective-permute-start | bytes 786440 | tf_op jit(solution)/shard_map/ppermute | solution.py:1215
  23.8 16.2 %collective-permute-start.5 = (bf16[16,64,128]{2,1,0:T(8,128)(2,1)S(1)}, bf16[16,64,128]{2,1,0:T(8,128)(2,1)S(1)}, u32[]{:S(2)}, u32[]{:S(2)}) collective-permute-start(bf16[16,64,128]{2,1,0:T(8,128)(2,1)S(1)} %get-tuple-element.75), channel_id=1, source_target_pairs={{0,1},{1,0},{2,3},{3,2},{4,5},{5,4},{6,7},{7,6},{8,9},{9,8},{10,11... | collective-permute-start | bytes 786440 | tf_op jit(solution)/shard_map/ppermute | solution.py:1215
  40.5 17.1 %collective-permute-start.7 = (bf16[3,64,1024]{2,1,0:T(8,128)(2,1)S(1)}, bf16[3,64,1024]{2,1,0:T(8,128)(2,1)S(1)}, u32[]{:S(2)}, u32[]{:S(2)}) collective-permute-start(bf16[3,64,1024]{2,1,0:T(8,128)(2,1)S(1)} %get-tuple-element.77), channel_id=1, source_target_pairs={{8,0},{16,8},{24,16},{9,1},{17,9},{25,17},{10,2},{18,10},{26,18},{... | collective-permute-start | bytes 1179656 | tf_op jit(solution)/shard_map/ppermute | solution.py:1208
  41.8 15.8 %collective-permute-start.6 = (bf16[2,64,1024]{2,1,0:T(8,128)(2,1)S(1)}, bf16[2,64,1024]{2,1,0:T(8,128)(2,1)S(1)}, u32[]{:S(2)}, u32[]{:S(2)}) collective-permute-start(bf16[2,64,1024]{2,1,0:T(8,128)(2,1)S(1)} %get-tuple-element.76), channel_id=1, source_target_pairs={{0,8},{8,16},{16,24},{1,9},{9,17},{17,25},{2,10},{10,18},{18,26},{... | collective-permute-start | bytes 786440 | tf_op jit(solution)/shard_map/ppermute | solution.py:1208
  57.7 15.6 %copy-start = (bf16[64,31,896]{2,0,1:T(8,128)(2,1)S(1)}, bf16[64,31,896]{2,0,1:T(8,128)(2,1)}, u32[]{:S(2)}) copy-start(bf16[64,31,896]{2,0,1:T(8,128)(2,1)} %param.17) | copy-start | bytes 10665988
  88.3 14.2 %collective-permute-start.8 = (bf16[17,64,128]{2,1,0:T(8,128)(2,1)S(1)}, bf16[17,64,128]{2,1,0:T(8,128)(2,1)S(1)}, u32[]{:S(2)}, u32[]{:S(2)}) collective-permute-start(bf16[17,64,128]{2,1,0:T(8,128)(2,1)S(1)} %get-tuple-element.92), channel_id=1, source_target_pairs={{1,2},{2,1},{3,4},{4,3},{5,6},{6,5},{9,10},{10,9},{11,12},{12,11},... | collective-permute-start | bytes 835592 | tf_op jit(solution)/shard_map/ppermute | solution.py:1215
  89.1 14.8 %collective-permute-start.9 = (bf16[17,64,128]{2,1,0:T(8,128)(2,1)S(1)}, bf16[17,64,128]{2,1,0:T(8,128)(2,1)S(1)}, u32[]{:S(2)}, u32[]{:S(2)}) collective-permute-start(bf16[17,64,128]{2,1,0:T(8,128)(2,1)S(1)} %get-tuple-element.93), channel_id=1, source_target_pairs={{0,1},{1,0},{2,3},{3,2},{4,5},{5,4},{6,7},{7,6},{8,9},{9,8},{10,11... | collective-permute-start | bytes 835592 | tf_op jit(solution)/shard_map/ppermute | solution.py:1215
  106.3 13.3 %collective-permute-start.10 = (bf16[16,64,128]{2,1,0:T(8,128)(2,1)S(1)}, bf16[16,64,128]{2,1,0:T(8,128)(2,1)S(1)}, u32[]{:S(2)}, u32[]{:S(2)}) collective-permute-start(bf16[16,64,128]{2,1,0:T(8,128)(2,1)S(1)} %get-tuple-element.96), channel_id=1, source_target_pairs={{1,0},{2,1},{3,2},{4,3},{5,4},{6,5},{7,6},{9,8},{10,9},{11,10},{12... | collective-permute-start | bytes 786440 | tf_op jit(solution)/shard_map/ppermute | solution.py:1208
  133.2 11.1 %all-to-all-start.4 = ((bf16[32,24,128]{2,1,0:T(8,128)(2,1)}), bf16[32,24,128]{2,1,0:T(8,128)(2,1)S(1)}, u32[]{:S(2)}, u32[]{:S(2)}) async-start(bf16[32,24,128]{2,1,0:T(8,128)(2,1)} %get-tuple-element.101), calls=%async_computation.4 | async-start | bytes 393216 | tf_op jit(solution)/shard_map/all_to_all | solution.py:1219
  145.1 12.5 %all-to-all-start.5 = ((bf16[32,24,128]{2,1,0:T(8,128)(2,1)}), bf16[32,24,128]{2,1,0:T(8,128)(2,1)S(1)}, u32[]{:S(2)}, u32[]{:S(2)}) async-start(bf16[32,24,128]{2,1,0:T(8,128)(2,1)} %sum_share.1), calls=%async_computation.5 | async-start | bytes 393216 | tf_op jit(solution)/shard_map/all_to_all | solution.py:1219
  149.0 8.6 %copy-start.3 = (f32[2,576,64]{1,2,0:T(8,128)S(1)}, f32[2,576,64]{1,2,0:T(8,128)}, u32[]{:S(2)}) copy-start(f32[2,576,64]{1,2,0:T(8,128)} %param.12) | copy-start | bytes 884740
  149.1 8.5 %copy-start.4 = (f32[2,576,64]{1,2,0:T(8,128)S(1)}, f32[2,576,64]{1,2,0:T(8,128)}, u32[]{:S(2)}) copy-start(f32[2,576,64]{1,2,0:T(8,128)} %param.13) | copy-start | bytes 884740
  149.1 8.5 %copy-start.6 = (f32[2,2,64]{2,1,0:T(2,128)S(1)}, f32[2,2,64]{2,1,0:T(2,128)}, u32[]{:S(2)}) copy-start(f32[2,2,64]{2,1,0:T(2,128)} %param.15) | copy-start | bytes 3076
  149.1 8.5 %copy-start.7 = (f32[2,2,64]{2,1,0:T(2,128)S(1)}, f32[2,2,64]{2,1,0:T(2,128)}, u32[]{:S(2)}) copy-start(f32[2,2,64]{2,1,0:T(2,128)} %param.16) | copy-start | bytes 3076
